TPU v7x, 32 devices: a whole 2x2x4 slice. The times are simulated.
32 devices in a mesh: groups: 2 (over x), clus: 8 (over z, y), blk: 2 (over core).
Axes of the slice: x: 2, y: 2, z: 4, core: 2. Of those that a mesh axis runs over, the one named last changes fastest.
Arguments:
- embeddings: bfloat16 [32768, 1024], P(('groups', 'clus', 'blk')), parts along dimension 0, may hold values from -120 to 120
- cluster_ids: int32 [32, 1024], P(('groups', 'clus', 'blk')), parts along dimension 0, may hold values from 0 to 15, as said below
Outputs:
- best_match: float32 [32, 2048], P(('groups', 'clus'), 'blk'), parts along dimension 0
There are 2 independent parts, one for each index of `groups`. A program takes and returns all parts, laid end to end along the dimension named above; each array names one. Nothing has to cross between parts.
Inputs may be any that keep to these rules, and one draw needn't show every extreme that they name: `cluster_ids`: each loader shard holds at most 128 rows of any one cluster, and in every draw some cluster has exactly 128 rows on every loader shard.
All inputs are finite; a program needn't handle non-finite values.
Results may differ from a plain program's by a relative error of at most 0.0005.
Values may be sent and summed in bfloat16 or wider, within the bound.
No kernel may reach another device: no remote copies, remote signals or barrier semaphores. Data moves between devices by JAX's collectives and lax.ppermute only.
A program may use at most 64 MiB of HBM per device.

v0:
```python
import jax
import jax.numpy as jnp
from jax import lax
from jax.sharding import PartitionSpec as P

CLUS_DEV = 2


def shifted(value, axis, steps):
    count = lax.axis_size(axis)
    leading, last = (max(0, -steps), min(count, count - steps))
    return lax.ppermute(value, axis, [(source, source + steps) for source in range(leading, last)])


def usable_slots(counts, per_source):
    slots = jnp.arange(per_source, dtype=jnp.int32)
    usable = slots[None, None, :] < counts[:, :, None]
    return usable.reshape(counts.shape[0], counts.shape[1] * per_source)


def masked_largest(own_rows, other_rows, other_usable, strict):
    width = own_rows.shape[1]
    later = (
        jnp.arange(width, dtype=jnp.int32)[:, None] > jnp.arange(width, dtype=jnp.int32)[None, :]
    )

    def per_item(parts):
        left, right, allowed_cols = parts
        similarity = lax.dot_general(
            left, right, (((1,), (1,)), ((), ())), preferred_element_type=jnp.float32
        )
        allowed = allowed_cols[None, :]
        if strict:
            allowed = allowed & later
        return jnp.max(jnp.where(allowed, similarity, jnp.float32(-1.0)), axis=1)

    return lax.map(per_item, (own_rows, other_rows, other_usable))


def score_blocks(items):
    arrived, arrived_counts = items
    own_rows = arrived[0]
    own_counts = arrived_counts[0]
    per_source = own_rows.shape[1] // own_counts.shape[1]
    own_usable = usable_slots(own_counts, per_source)
    result = masked_largest(own_rows, own_rows, own_usable, True)
    other_rows, other_counts = shifted((own_rows, own_counts), "blk", 1)
    other_usable = usable_slots(other_counts, per_source)
    result = jnp.maximum(result, masked_largest(own_rows, other_rows, other_usable, False))
    best = jnp.where(own_usable, result, jnp.float32(0.0))
    return best[None]


def local(embeddings, cluster_ids):
    values = embeddings.astype(jnp.float32)
    unit_rows = (
        values * lax.rsqrt(jnp.sum(values * values, axis=1, keepdims=True) + 1e-06)
    ).astype(jnp.bfloat16)
    owners = lax.axis_size("clus")
    clusters = CLUS_DEV * owners
    per_source = 2 * unit_rows.shape[0] // clusters
    row_ids = cluster_ids[0]
    onehot = (row_ids[:, None] == jnp.arange(clusters, dtype=jnp.int32)[None, :]).astype(jnp.int32)
    before = jnp.cumsum(onehot, axis=0) - onehot
    slot = jnp.sum(before * onehot, axis=1)
    counts = jnp.sum(onehot, axis=0)
    target = row_ids * per_source + slot
    outgoing = (
        jnp.zeros((clusters * per_source, unit_rows.shape[1]), jnp.bfloat16)
        .at[target]
        .set(unit_rows)
    )
    outgoing = outgoing.reshape(owners, CLUS_DEV, per_source, unit_rows.shape[1])
    count_out = counts.reshape(owners, CLUS_DEV, 1)
    best = score_blocks(
        (
            lax.all_to_all(outgoing, "clus", split_axis=0, concat_axis=2, tiled=True),
            lax.all_to_all(count_out, "clus", split_axis=0, concat_axis=2, tiled=True),
        )
    )
    return best.reshape(CLUS_DEV, best.shape[2])


def solution(mesh):
    placed = (P(("groups", "clus", "blk"), None), P(("groups", "clus", "blk"), None))
    return jax.shard_map(
        local, mesh=mesh, in_specs=placed, out_specs=P(("groups", "clus"), "blk"), check_vma=False
    )
```

profile of v0, /device:TPU:0, one launch (start us, length us, event | category | flops | bytes accessed | tf_op | source)
XLA Modules:
  0.0 156.3 jit_solution(17198674321320618444)
XLA Ops:
  0.0 0.8 fusion.27
  0.8 4.5 %reduce-window.6 = s32[16,8,128]{2,1,0:T(8,128)S(1)} reduce-window(s32[16,8,128]{2,1,0:T(8,128)S(1)} %fusion.27, s32[]{:T(128)} %constant.41.clone.1), window={size=1x1x128 pad=0_0x0_0x127_0}, to_apply=%region_1.0 | reduce-window | flops 2080768 | bytes 131076 | tf_op jit(solution)/shard_map/reduce-window
  5.3 0.1 slice.8
  5.4 0.1 copy.15
  5.6 0.1 copy.16
  5.7 0.1 broadcast_add_fusion
  5.8 0.8 fusion.26
  6.6 0.7 compare_select_fusion
  7.3 2.1 %fusion.19 = f32[1024]{0:T(1024)S(1)} fusion(bf16[1024,1024]{1,0:T(8,128)(2,1)} %param.6), kind=kLoop, calls=%fused_computation.20 | loop fusion | flops 3144704 | bytes 2101248 | tf_op jit(solution)/shard_map/reduce_sum | solution.py:57
  9.4 8.3 %scatter_custom_fusion = bf16[2048,1024]{1,0:T(8,128)(2,1)} fusion(s32[1024]{0:T(1024)S(1)} %bitcast.75, bf16[1024,1024]{1,0:T(8,128)(2,1)S(1)} %copy-done, f32[1024]{0:T(1024)S(1)} %add_rsqrt_fusion, bf16[]{:T(256)} %constant.43.clone.1), kind=kCustom, calls=%fused_computation.22 | custom fusion | flops 3145728 | bytes 6295554 | tf_op jit(solution)/shard_map/scatter | solution.py:71
  17.7 100.5 %all_to_all.30 = bf16[8,2,128,1024]{3,2,1,0:T(8,128)(2,1)S(1)} all-to-all(bf16[8,2,128,1024]{3,2,1,0:T(8,128)(2,1)} %bitcast.66), channel_id=1, replica_groups=mesh['groups'=2,'clus'=8,'blk'=2] {'clus'}, dimensions={0} | all-to-all | bytes 8388608 | tf_op jit(solution)/shard_map/all_to_all | solution.py:77
  118.1 2.4 %copy.17 = bf16[1,2,8,128,1024]{4,3,2,1,0:T(8,128)(2,1)} copy(bf16[1,2,8,128,1024]{4,3,1,2,0:T(8,128)(2,1)S(1)} %bitcast.67) | data formatting | bytes 8388608 | tf_op jit(solution)/shard_map/all_to_all | solution.py:77
  120.5 3.3 %collective-permute-start.1 = (bf16[2,1024,1024]{2,1,0:T(8,128)(2,1)}, bf16[2,1024,1024]{2,1,0:T(8,128)(2,1)}, u32[]{:S(2)}, u32[]{:S(2)}) collective-permute-start(bf16[2,1024,1024]{2,1,0:T(8,128)(2,1)} %bitcast.18), channel_id=1, source_target_pairs={{0,1},{2,3},{4,5},{6,7},{8,9},{10,11},{12,13},{14,15},{16,17},{18,... | collective-permute-start | bytes 12582920 | tf_op jit(solution)/shard_map/ppermute | solution.py:12
  123.7 0.7 reshape.68
  124.4 3.7 %all-to-all-start = ((s32[8,2,1]{1,2,0:T(1,128)}), s32[8,2,1]{1,2,0:T(1,128)S(1)}, u32[]{:S(2)}, u32[]{:S(2)}) async-start(s32[8,2,1]{1,2,0:T(1,128)} %bitcast.5), calls=%async_computation | async-start | bytes 8192 | tf_op jit(solution)/shard_map/all_to_all | solution.py:78
  128.1 6.4 %all-to-all-done = s32[8,2,1]{1,2,0:T(1,128)S(1)} async-done(((s32[8,2,1]{1,2,0:T(1,128)}), s32[8,2,1]{1,2,0:T(1,128)S(1)}, u32[]{:S(2)}, u32[]{:S(2)}) %all-to-all-start) | async-done | bytes 96 | tf_op jit(solution)/shard_map/all_to_all | solution.py:78
  134.5 0.1 copy.14
  134.6 1.3 collective-permute-start
  135.9 0.1 broadcast_bitcast_fusion.1
  135.9 0.7 collective-permute-done
  136.7 0.1 broadcast_bitcast_fusion
  136.8 9.5 %while.22 = (s32[]{:T(128)}, f32[2,1024]{1,0:T(2,128)S(1)}, pred[2,1024]{1,0:T(4,128)(4,1)S(1)}, bf16[2,1024,1024]{2,1,0:T(8,128)(2,1)}, s32[]{:T(128)}, /*index=5*/s32[]{:T(128)}) while((s32[]{:T(128)}, f32[2,1024]{1,0:T(2,128)S(1)}, pred[2,1024]{1,0:T(4,128)(4,1)S(1)}, bf16[2,1024,1024]{2,1,0:T(8,128)(2,1)}, s32[]{:T(128)}, ...), condition=%wide.region_8.9_spmd.clone, body=%wide.region_6.8_spmd.clone.sunk | while | flops 2151676928 | bytes 2113101 | solution.py:37
  136.8 4.6 %select_reduce_fusion.5 = f32[1024]{0:T(1024)S(1)} fusion(pred[1024]{0:T(1024)(128)(4,1)S(1)} %dynamic-slice_reduce_fusion.5, bf16[2,1024,1024]{2,1,0:T(8,128)(2,1)} %get-tuple-element.164, s32[]{:T(128)} %get-tuple-element.155), kind=kOutput, calls=%fused_computation.11.clone.1 | convolution fusion | flops 2151676928 | bytes 2102784 | tf_op jit(solution)/shard_map/while/body/eval_jaxpr/dot_general | solution.py:29
  141.4 0.1 dynamic_update_slice.11
  141.5 4.6 %select_reduce_fusion.5 = f32[1024]{0:T(1024)S(1)} fusion(pred[1024]{0:T(1024)(128)(4,1)S(1)} %dynamic-slice_reduce_fusion.5, bf16[2,1024,1024]{2,1,0:T(8,128)(2,1)} %get-tuple-element.164, s32[]{:T(128)} %get-tuple-element.155), kind=kOutput, calls=%fused_computation.11.clone.1 | convolution fusion | flops 2151676928 | bytes 2102784 | tf_op jit(solution)/shard_map/while/body/eval_jaxpr/dot_general | solution.py:29
  146.2 0.1 dynamic_update_slice.11
  146.3 9.4 %while.21 = (s32[]{:T(128)}, f32[2,1024]{1,0:T(2,128)S(1)}, pred[2,1024]{1,0:T(4,128)(4,1)S(1)}, bf16[2,1024,1024]{2,1,0:T(8,128)(2,1)}, bf16[2,1024,1024]{2,1,0:T(8,128)(2,1)}, /*index=5*/s32[]{:T(128)}, s32[]{:T(128)}) while((s32[]{:T(128)}, f32[2,1024]{1,0:T(2,128)S(1)}, pred[2,1024]{1,0:T(4,128)(4,1)S(1)}, ...), condition=%wide.region_11.12_spmd, body=%wide.region_9.11_spmd.sunk | while | flops 2149579776 | bytes 4210773 | solution.py:37
  146.3 4.6 %select_reduce_fusion.4 = f32[1024]{0:T(1024)S(1)} fusion(pred[1024]{0:T(1024)(128)(4,1)S(1)} %dynamic-slice_reduce_fusion.4, bf16[2,1024,1024]{2,1,0:T(8,128)(2,1)} %get-tuple-element.185, s32[]{:T(128)} %get-tuple-element.174, bf16[2,1024,1024]{2,1,0:T(8,128)(2,1)} %get-tuple-element.184), kind=kOutput, calls=%fused_computation.2.clone.1 | convolution fusion | flops 2149579776 | bytes 4200448 | tf_op jit(solution)/shard_map/while/body/eval_jaxpr/dot_general | solution.py:29
  150.9 0.1 dynamic_update_slice.10
  151.0 4.6 %select_reduce_fusion.4 = f32[1024]{0:T(1024)S(1)} fusion(pred[1024]{0:T(1024)(128)(4,1)S(1)} %dynamic-slice_reduce_fusion.4, bf16[2,1024,1024]{2,1,0:T(8,128)(2,1)} %get-tuple-element.185, s32[]{:T(128)} %get-tuple-element.174, bf16[2,1024,1024]{2,1,0:T(8,128)(2,1)} %get-tuple-element.184), kind=kOutput, calls=%fused_computation.2.clone.1 | convolution fusion | flops 2149579776 | bytes 4200448 | tf_op jit(solution)/shard_map/while/body/eval_jaxpr/dot_general | solution.py:29
  155.6 0.1 dynamic_update_slice.10
  155.7 0.6 maximum_select_fusion
  (14 shorter events, 0.2 us)
Async XLA Ops:
  0.0 9.4 %copy-start = (bf16[1024,1024]{1,0:T(8,128)(2,1)S(1)}, bf16[1024,1024]{1,0:T(8,128)(2,1)}, u32[]{:S(2)}) copy-start(bf16[1024,1024]{1,0:T(8,128)(2,1)} %param.6) | copy-start | bytes 6291460
  120.5 25.8 %collective-permute-start.1 = (bf16[2,1024,1024]{2,1,0:T(8,128)(2,1)}, bf16[2,1024,1024]{2,1,0:T(8,128)(2,1)}, u32[]{:S(2)}, u32[]{:S(2)}) collective-permute-start(bf16[2,1024,1024]{2,1,0:T(8,128)(2,1)} %bitcast.18), channel_id=1, source_target_pairs={{0,1},{2,3},{4,5},{6,7},{8,9},{10,11},{12,13},{14,15},{16,17},{18,... | collective-permute-start | bytes 12582920 | tf_op jit(solution)/shard_map/ppermute | solution.py:12
  124.4 10.1 %all-to-all-start = ((s32[8,2,1]{1,2,0:T(1,128)}), s32[8,2,1]{1,2,0:T(1,128)S(1)}, u32[]{:S(2)}, u32[]{:S(2)}) async-start(s32[8,2,1]{1,2,0:T(1,128)} %bitcast.5), calls=%async_computation | async-start | bytes 8192 | tf_op jit(solution)/shard_map/all_to_all | solution.py:78
  134.6 2.1 %collective-permute-start = (s32[2,8]{1,0:T(2,128)S(1)}, s32[2,8]{1,0:T(2,128)S(1)}, u32[]{:S(2)}, u32[]{:S(2)}) collective-permute-start(s32[2,8]{1,0:T(2,128)S(1)} %bitcast.76), channel_id=1, source_target_pairs={{0,1},{2,3},{4,5},{6,7},{8,9},{10,11},{12,13},{14,15},{16,17},{18,... | collective-permute-start | bytes 200 | tf_op jit(solution)/shard_map/ppermute | solution.py:12
where the time goes:
time: 157 us; the launch traced here: 156 us
  blocking collectives  100 us (64%)
  matrix products  18.5 us (12%)
  other arithmetic  18 us (11%)
  starting transfers between devices  8.22 us (5%)
  waiting for transfers between devices  7.12 us (5%)
  local copies, waits for them, and re-layouts  3.88 us (2%)
    all_to_all x1, blocking collectives, local(): lax.all_to_all(outgoing, 'clus', split_axis=0, concat_axis=2, tiled=True)  100 us
    dot_general x4, matrix products, per_item(): lax.dot_general(left, right, (((1,), (1,)), ((), ())), preferred_element_...  18.5 us
    scatter x1, other arithmetic, local(): outgoing = jnp.zeros((clusters * per_source, unit_rows.shape[1]), jnp.bfl...  8.29 us
    all_to_all x1, waiting for transfers between devices, local(): lax.all_to_all(count_out, 'clus', split_axis=0, concat_axis=2, tiled=True)  6.38 us
    another operation x3, other arithmetic  4.61 us
    ppermute x2, starting transfers between devices, shifted(): lax.ppermute(value, axis, [(source, source + steps) for source in range(l...  4.54 us
    all_to_all x1, starting transfers between devices, local(): lax.all_to_all(count_out, 'clus', split_axis=0, concat_axis=2, tiled=True)  3.69 us
  transfers between devices with their start and end apart: 3, of which 2 were waited for; matrix products, arithmetic and copies ran while one was open for 7% of the time, Pallas kernels for 0%

commit v1 on v0

v1 whole, which is shorter than its diff:
```python
import functools

import jax
import jax.numpy as jnp
from jax import lax
from jax.experimental import pallas as pl
from jax.experimental.pallas import tpu as pltpu
from jax.sharding import PartitionSpec as P

CLUS_DEV = 2
LANES = 128
MARK = 2.0
BF = jnp.bfloat16
F32 = jnp.float32


def iota(shape, dim):
    return lax.broadcasted_iota(jnp.int32, shape, dim)


def matmul(a, b, contract):
    return lax.dot_general(a, b, (contract, ((), ())), preferred_element_type=F32)


def targets(ids, clusters, per_source):
    groups = ids.shape[1] // LANES
    parts = [ids[:, g * LANES : (g + 1) * LANES] for g in range(groups)]
    hot = jnp.concatenate(
        [(iota((clusters, LANES), 0) == part).astype(F32) for part in parts], axis=0
    )
    stacked = groups * clusters
    earlier = (iota((LANES, LANES), 0) < iota((LANES, LANES), 1)).astype(F32).astype(BF)
    within = matmul(hot.astype(BF), earlier, ((1,), (0,)))
    totals = jnp.broadcast_to(jnp.sum(hot, axis=1, keepdims=True), (stacked, LANES))
    a, b = iota((stacked, stacked), 0), iota((stacked, stacked), 1)
    chunks_before = ((a % clusters == b % clusters) & (b < a)).astype(F32).astype(BF)
    before = within + matmul(chunks_before, totals.astype(BF), ((1,), (0,)))
    picked = hot * before
    out = [
        jnp.sum(picked[g * clusters : (g + 1) * clusters], axis=0, keepdims=True).astype(jnp.int32)
        + parts[g] * per_source
        for g in range(groups)
    ]
    return jnp.concatenate(out, axis=1)


def pack_block(unit, tgt, dest, width):
    hit = (tgt - dest * width) == iota((width, tgt.shape[1]), 0)
    hot = hit.astype(F32)
    rows = matmul(hot.astype(BF), unit, ((1,), (0,)))
    empty = jnp.max(hot, axis=1, keepdims=True) < 0.5
    head = jnp.where(empty, F32(MARK), rows[:, :LANES])
    return head.astype(BF), rows[:, LANES:].astype(BF)


def store_blocks(unit, tgt, steps, width, outs):
    me = lax.axis_index("clus")
    for step, out in zip(steps, outs):
        head, tail = pack_block(unit, tgt, me ^ step, width)
        out[:, :LANES] = head
        out[:, LANES:] = tail


def pack_first(steps, clusters, per_source, emb, ids, unit, tgt, *outs):
    values = emb[...].astype(F32)
    scale = lax.rsqrt(jnp.sum(values * values, axis=1, keepdims=True) + 1e-6)
    unit[...] = (values * scale).astype(BF)
    tgt[...] = targets(ids[...], clusters, per_source)
    store_blocks(unit[...], tgt[...], steps, CLUS_DEV * per_source, outs)


def pack_rest(steps, per_source, unit, tgt, *outs):
    store_blocks(unit[...], tgt[...], steps, CLUS_DEV * per_source, outs)


VMEM = pl.BlockSpec(memory_space=pltpu.VMEM)


def call_pack_first(emb, ids, steps, clusters, per_source):
    block = jax.ShapeDtypeStruct((CLUS_DEV * per_source, emb.shape[1]), BF)
    n = len(steps)
    return pl.pallas_call(
        functools.partial(pack_first, steps, clusters, per_source),
        out_shape=[
            jax.ShapeDtypeStruct(emb.shape, BF),
            jax.ShapeDtypeStruct(ids.shape, jnp.int32),
        ]
        + [block] * n,
        in_specs=[VMEM] * 2,
        out_specs=[VMEM] * (n + 2),
        compiler_params=pltpu.CompilerParams(vmem_limit_bytes=48 * 2**20),
        cost_estimate=pl.CostEstimate(
            flops=2 * n * block.shape[0] * emb.size, bytes_accessed=8 * 2**20, transcendentals=0
        ),
        name="pack_first",
    )(emb, ids)


def call_pack_rest(unit, tgt, steps, per_source):
    block = jax.ShapeDtypeStruct((CLUS_DEV * per_source, unit.shape[1]), BF)
    n = len(steps)
    return pl.pallas_call(
        functools.partial(pack_rest, steps, per_source),
        out_shape=[block] * n,
        in_specs=[VMEM] * 2,
        out_specs=[VMEM] * n,
        compiler_params=pltpu.CompilerParams(vmem_limit_bytes=48 * 2**20),
        cost_estimate=pl.CostEstimate(
            flops=2 * n * block.shape[0] * unit.size, bytes_accessed=8 * 2**20, transcendentals=0
        ),
        name="pack_rest",
    )(unit, tgt)


def load_half(blocks, scratch, me, half):
    per = blocks[0].shape[1]
    for step, block in enumerate(blocks):
        place = (me ^ step) & (half - 1)
        scratch[pl.ds(pl.multiple_of(place * per, per), per), :] = block[0]


CHUNK = 256


def best_over(keys, queries, start, triangular):
    chunk = queries[start : start + CHUNK, :]
    count = start + CHUNK if triangular else keys.shape[0]
    sims = matmul(keys[:count, :], chunk, ((1,), (1,)))
    filled = keys[:count, :LANES].astype(F32) < 1.5
    out = []
    for first in range(0, CHUNK, LANES):
        tile = sims[:, first : first + LANES]
        allowed = filled
        if triangular:
            allowed = filled & (
                iota((count, LANES), 0) < iota((count, LANES), 1) + (start + first)
            )
        out.append(jnp.max(jnp.where(allowed, tile, F32(-1.0)), axis=0, keepdims=True))
    return jnp.concatenate(out, axis=1)


def raise_best(best, keys, queries, triangular=False):
    for start in range(0, queries.shape[0], CHUNK):
        part = best_over(keys, queries, start, triangular)
        window = slice(start, start + CHUNK)
        best[:, window] = jnp.maximum(best[:, window], part)


def filled_queries(rows):
    ones = jnp.ones((8, LANES), BF)
    return matmul(ones, rows[:, :LANES], ((1,), (1,)))[:1] < 100.0


def near_kernel(half, *refs):
    own, other = refs[:half], refs[half : 2 * half]
    out, keys, others = refs[2 * half :]
    me = lax.axis_index("clus")
    load_half(own, keys, me, half)
    out[0] = jnp.full(out.shape[1:], -1.0, F32)
    raise_best(out.at[0], keys, keys, True)

    @pl.when(lax.axis_index("blk") == 1)
    def _():
        load_half(other, others, me, half)
        raise_best(out.at[0], others, keys)


def far_kernel(half, *refs):
    own, other = refs[: 2 * half], refs[2 * half : 4 * half]
    near_best, out, near, far, near_other, far_other, best_n, best_f = refs[4 * half :]
    me = lax.axis_index("clus")
    upper = me >= half
    load_half(own[:half], near, me, half)
    load_half(own[half:], far, me, half)
    best_n[...] = near_best[0]
    best_f[...] = jnp.full(best_f.shape, -1.0, F32)
    raise_best(best_f, far, far, True)

    @pl.when(upper)
    def _():
        raise_best(best_n, far, near)

    @pl.when(jnp.logical_not(upper))
    def _():
        raise_best(best_f, near, far)

    @pl.when(lax.axis_index("blk") == 1)
    def _():
        load_half(other[:half], near_other, me, half)
        load_half(other[half:], far_other, me, half)
        raise_best(best_f, near_other, far)
        raise_best(best_f, far_other, far)
        raise_best(best_n, far_other, near)

    rows = near.shape[0]
    at_near = pl.ds(pl.multiple_of(jnp.where(upper, rows, 0), rows), rows)
    at_far = pl.ds(pl.multiple_of(jnp.where(upper, 0, rows), rows), rows)
    out[0, :, at_near] = jnp.where(filled_queries(near), best_n[...], F32(0.0))
    out[0, :, at_far] = jnp.where(filled_queries(far), best_f[...], F32(0.0))


def call_near(own, other, half):
    _, per, width = own[0].shape
    rows = half * per
    spec = pl.BlockSpec((1, per, width), lambda c: (c, 0, 0))
    return pl.pallas_call(
        functools.partial(near_kernel, half),
        grid=(CLUS_DEV,),
        out_shape=jax.ShapeDtypeStruct((CLUS_DEV, 1, rows), F32),
        in_specs=[spec] * (2 * half),
        out_specs=pl.BlockSpec((1, 1, rows), lambda c: (c, 0, 0)),
        scratch_shapes=[pltpu.VMEM((rows, width), BF)] * 2,
        compiler_params=pltpu.CompilerParams(vmem_limit_bytes=48 * 2**20),
        cost_estimate=pl.CostEstimate(
            flops=2 * CLUS_DEV * 2 * rows * rows * width,
            bytes_accessed=8 * CLUS_DEV * rows * width,
            transcendentals=0,
        ),
        name="near",
    )(*own, *other)


def call_far(own, other, near_best, half):
    _, per, width = own[0].shape
    rows = half * per
    spec = pl.BlockSpec((1, per, width), lambda c: (c, 0, 0))
    return pl.pallas_call(
        functools.partial(far_kernel, half),
        grid=(CLUS_DEV,),
        out_shape=jax.ShapeDtypeStruct((CLUS_DEV, 1, 2 * rows), F32),
        in_specs=[spec] * (4 * half) + [pl.BlockSpec((1, 1, rows), lambda c: (c, 0, 0))],
        out_specs=pl.BlockSpec((1, 1, 2 * rows), lambda c: (c, 0, 0)),
        scratch_shapes=[pltpu.VMEM((rows, width), BF)] * 4 + [pltpu.VMEM((1, rows), F32)] * 2,
        compiler_params=pltpu.CompilerParams(vmem_limit_bytes=48 * 2**20),
        cost_estimate=pl.CostEstimate(
            flops=2 * CLUS_DEV * 5 * rows * rows * width,
            bytes_accessed=16 * CLUS_DEV * rows * width,
            transcendentals=0,
        ),
        name="far",
    )(*own, *other, near_best)


def local(embeddings, cluster_ids):
    owners = lax.axis_size("clus")
    clusters = CLUS_DEV * owners
    rows, width = embeddings.shape
    per_source = 2 * rows // clusters
    half = owners // 2
    far_steps = list(range(half, owners))
    near_steps = list(range(half))

    def to_owner(block, step):
        return lax.ppermute(block, "clus", [(i, i ^ step) for i in range(owners)])

    def to_later(block):
        return lax.ppermute(block, "blk", [(0, 1)])

    unit, tgt, *far_out = call_pack_first(embeddings, cluster_ids, far_steps, clusters, per_source)
    far_in = [to_owner(block, step) for step, block in zip(far_steps, far_out)]
    near_out = call_pack_rest(unit, tgt, near_steps, per_source)
    near_in = [near_out[0]] + [
        to_owner(block, step) for step, block in zip(near_steps[1:], near_out[1:])
    ]
    shape = (CLUS_DEV, per_source, width)
    near_in = [block.reshape(shape) for block in near_in]
    far_in = [block.reshape(shape) for block in far_in]
    near_other = [to_later(block) for block in near_in]
    far_other = [to_later(block) for block in far_in]
    near_best = call_near(near_in, near_other, half)
    best = call_far(near_in + far_in, near_other + far_other, near_best, half)
    return best.reshape(CLUS_DEV, rows)


def solution(mesh):
    placed = (P(("groups", "clus", "blk"), None), P(("groups", "clus", "blk"), None))
    return jax.shard_map(
        local, mesh=mesh, in_specs=placed, out_specs=P(("groups", "clus"), "blk"), check_vma=False
    )
```

time: 157 us -> 123 us (0.78)
  the two profiles are of different devices: /device:TPU:0 before, /device:TPU:17 now
where the time goes in v1:
time: 123 us
  waiting for transfers between devices  84.7 us (69%)
  Pallas kernels  19.2 us (16%)
  starting transfers between devices  16.5 us (13%)
  local copies, waits for them, and re-layouts  2.4 us (2%)
    ppermute x7, waiting for transfers between devices, to_owner(): return lax.ppermute(block, 'clus', [(i, i ^ step) for i in range(owners)])  83.9 us
    ppermute x8, starting transfers between devices, to_later(): return lax.ppermute(block, 'blk', [(0, 1)])  10.3 us
    pallas_call x1, Pallas kernels, call_far(): pl.pallas_call(functools.partial(far_kernel, half), grid=(CLUS_DEV,), out...  8.45 us
    ppermute x7, starting transfers between devices, to_owner(): return lax.ppermute(block, 'clus', [(i, i ^ step) for i in range(owners)])  6.23 us
    pallas_call x1, Pallas kernels, call_pack_first(): pl.pallas_call(functools.partial(pack_first, steps, clusters, per_source)...  5.15 us
    pallas_call x1, Pallas kernels, call_near(): pl.pallas_call(functools.partial(near_kernel, half), grid=(CLUS_DEV,), ou...  2.97 us
    pallas_call x1, Pallas kernels, call_pack_rest(): pl.pallas_call(functools.partial(pack_rest, steps, per_source), out_shape...  2.64 us
  transfers between devices with their start and end apart: 15, of which 7 were waited for; matrix products, arithmetic and copies ran while one was open for 0% of the time, Pallas kernels for 2%

profile of v1, /device:TPU:17, one launch (start us, length us, event | category | flops | bytes accessed | tf_op | source)
XLA Modules:
  0.0 123.1 jit_solution(16451568319634194162)
XLA Ops:
  0.0 0.7 copy-done.1
  0.7 5.1 %pack_first.1 = (bf16[1024,1024]{1,0:T(8,128)(2,1)S(1)}, s32[1,1024]{1,0:T(1,128)S(1)}, bf16[256,1024]{1,0:T(8,128)(2,1)S(1)}, bf16[256,1024]{1,0:T(8,128)(2,1)S...) custom-call(bf16[1024,1024]{1,0:T(8,128)(2,1)} %emb.1, s32[1,1024]{1,0:T(1,128)S(1)} %copy-done.1), custom_call_target="tpu_custom_call" | custom-call | flops 2147483648 | bytes 8388608 | tf_op jit(solution)/shard_map/pack_first/pallas_call | solution.py:82
  5.8 2.6 %pack_rest.1 = (bf16[256,1024]{1,0:T(8,128)(2,1)S(1)}, bf16[256,1024]{1,0:T(8,128)(2,1)S(1)}, bf16[256,1024]{1,0:T(8,128)(2,1)S(1)}, bf16[256,1024]{1,0:T(8,128)(2,1)S(1)}) custom-call(bf16[1024,1024]{1,0:T(8,128)(2,1)S(1)} %get-tuple-element.15.unit, s32[1,1024]{1,0:T(1,128)S(1)} %get-tuple-element.16.tgt), custom_call_target="tpu_custom_call" | custom-call | flops 2147483648 | bytes 8388608 | tf_op jit(solution)/shard_map/pack_rest/pallas_call | solution.py:102
  8.5 1.3 %collective-permute-start = (bf16[256,1024]{1,0:T(8,128)(2,1)S(1)}, bf16[256,1024]{1,0:T(8,128)(2,1)S(1)}, u32[]{:S(2)}, u32[]{:S(2)}) collective-permute-start(bf16[256,1024]{1,0:T(8,128)(2,1)S(1)} %get-tuple-element.18), channel_id=1, source_target_pairs={{0,2},{2,0},{4,6},{6,4},{8,10},{10,8},{12,14},{14,12},{1,3},{3,1},... | collective-permute-start | bytes 1572872 | tf_op jit(solution)/shard_map/ppermute | solution.py:254
  9.8 1.3 %collective-permute-start.1 = (bf16[256,1024]{1,0:T(8,128)(2,1)S(1)}, bf16[256,1024]{1,0:T(8,128)(2,1)S(1)}, u32[]{:S(2)}, u32[]{:S(2)}) collective-permute-start(bf16[256,1024]{1,0:T(8,128)(2,1)S(1)} %get-tuple-element.19), channel_id=1, source_target_pairs={{0,4},{2,6},{4,0},{6,2},{8,12},{10,14},{12,8},{14,10},{1,5},{3,7},... | collective-permute-start | bytes 1572872 | tf_op jit(solution)/shard_map/ppermute | solution.py:254
  11.1 0.1 collective-permute-start.2
  11.2 3.3 %collective-permute-start.4 = (bf16[256,1024]{1,0:T(8,128)(2,1)S(1)}, bf16[256,1024]{1,0:T(8,128)(2,1)S(1)}, u32[]{:S(2)}, u32[]{:S(2)}) collective-permute-start(bf16[256,1024]{1,0:T(8,128)(2,1)S(1)} %get-tuple-element.22), channel_id=1, source_target_pairs={{0,10},{2,8},{4,14},{6,12},{8,2},{10,0},{12,6},{14,4},{1,11},{3,9}... | collective-permute-start | bytes 1572872 | tf_op jit(solution)/shard_map/ppermute | solution.py:254
  14.5 6.8 %collective-permute-done = bf16[256,1024]{1,0:T(8,128)(2,1)S(1)} collective-permute-done((bf16[256,1024]{1,0:T(8,128)(2,1)S(1)}, bf16[256,1024]{1,0:T(8,128)(2,1)S(1)}, u32[]{:S(2)}, u32[]{:S(2)}) %collective-permute-start) | collective-permute-done | bytes 524320 | tf_op jit(solution)/shard_map/ppermute | solution.py:254
  21.4 0.2 collective-permute-start.5
  21.5 19.8 %collective-permute-done.1 = bf16[256,1024]{1,0:T(8,128)(2,1)S(1)} collective-permute-done((bf16[256,1024]{1,0:T(8,128)(2,1)S(1)}, bf16[256,1024]{1,0:T(8,128)(2,1)S(1)}, u32[]{:S(2)}, u32[]{:S(2)}) %collective-permute-start.1) | collective-permute-done | bytes 524320 | tf_op jit(solution)/shard_map/ppermute | solution.py:254
  41.4 0.0 collective-permute-start.6
  41.4 11.2 %collective-permute-done.2 = bf16[256,1024]{1,0:T(8,128)(2,1)S(1)} collective-permute-done((bf16[256,1024]{1,0:T(8,128)(2,1)S(1)}, bf16[256,1024]{1,0:T(8,128)(2,1)S(1)}, u32[]{:S(2)}, u32[]{:S(2)}) %collective-permute-start.2) | collective-permute-done | bytes 524320 | tf_op jit(solution)/shard_map/ppermute | solution.py:254
  52.6 1.3 %collective-permute-start.7 = (bf16[2,128,1024]{2,1,0:T(8,128)(2,1)S(1)}, bf16[2,128,1024]{2,1,0:T(8,128)(2,1)S(1)}, u32[]{:S(2)}, u32[]{:S(2)}) collective-permute-start(bf16[2,128,1024]{2,1,0:T(8,128)(2,1)S(1)} %bitcast.11), channel_id=1, source_target_pairs={{0,1},{2,3},{4,5},{6,7},{8,9},{10,11},{12,13},{14,15},{16,17},{18,... | collective-permute-start | bytes 1572872 | tf_op jit(solution)/shard_map/ppermute | solution.py:257
  53.9 0.0 collective-permute-done.3
  53.9 1.3 %collective-permute-start.8 = (bf16[2,128,1024]{2,1,0:T(8,128)(2,1)S(1)}, bf16[2,128,1024]{2,1,0:T(8,128)(2,1)S(1)}, u32[]{:S(2)}, u32[]{:S(2)}) collective-permute-start(bf16[2,128,1024]{2,1,0:T(8,128)(2,1)S(1)} %bitcast.14), channel_id=1, source_target_pairs={{0,1},{2,3},{4,5},{6,7},{8,9},{10,11},{12,13},{14,15},{16,17},{18,... | collective-permute-start | bytes 1572872 | tf_op jit(solution)/shard_map/ppermute | solution.py:257
  55.2 0.7 collective-permute-done.4
  55.9 1.3 %collective-permute-start.9 = (bf16[2,128,1024]{2,1,0:T(8,128)(2,1)S(1)}, bf16[2,128,1024]{2,1,0:T(8,128)(2,1)S(1)}, u32[]{:S(2)}, u32[]{:S(2)}) collective-permute-start(bf16[2,128,1024]{2,1,0:T(8,128)(2,1)S(1)} %bitcast.17), channel_id=1, source_target_pairs={{0,1},{2,3},{4,5},{6,7},{8,9},{10,11},{12,13},{14,15},{16,17},{18,... | collective-permute-start | bytes 1572872 | tf_op jit(solution)/shard_map/ppermute | solution.py:257
  57.1 34.5 %collective-permute-done.5 = bf16[256,1024]{1,0:T(8,128)(2,1)S(1)} collective-permute-done((bf16[256,1024]{1,0:T(8,128)(2,1)S(1)}, bf16[256,1024]{1,0:T(8,128)(2,1)S(1)}, u32[]{:S(2)}, u32[]{:S(2)}) %collective-permute-start.5) | collective-permute-done | bytes 524320 | tf_op jit(solution)/shard_map/ppermute | solution.py:254
  91.6 1.3 %collective-permute-start.10 = (bf16[2,128,1024]{2,1,0:T(8,128)(2,1)S(1)}, bf16[2,128,1024]{2,1,0:T(8,128)(2,1)S(1)}, u32[]{:S(2)}, u32[]{:S(2)}) collective-permute-start(bf16[2,128,1024]{2,1,0:T(8,128)(2,1)S(1)} %bitcast.20), channel_id=1, source_target_pairs={{0,1},{2,3},{4,5},{6,7},{8,9},{10,11},{12,13},{14,15},{16,17},{18,... | collective-permute-start | bytes 1572872 | tf_op jit(solution)/shard_map/ppermute | solution.py:257
  92.9 10.9 %collective-permute-done.6 = bf16[256,1024]{1,0:T(8,128)(2,1)S(1)} collective-permute-done((bf16[256,1024]{1,0:T(8,128)(2,1)S(1)}, bf16[256,1024]{1,0:T(8,128)(2,1)S(1)}, u32[]{:S(2)}, u32[]{:S(2)}) %collective-permute-start.6) | collective-permute-done | bytes 524320 | tf_op jit(solution)/shard_map/ppermute | solution.py:254
  103.8 1.3 %collective-permute-start.11 = (bf16[2,128,1024]{2,1,0:T(8,128)(2,1)S(1)}, bf16[2,128,1024]{2,1,0:T(8,128)(2,1)S(1)}, u32[]{:S(2)}, u32[]{:S(2)}) collective-permute-start(bf16[2,128,1024]{2,1,0:T(8,128)(2,1)S(1)} %bitcast.23), channel_id=1, source_target_pairs={{0,1},{2,3},{4,5},{6,7},{8,9},{10,11},{12,13},{14,15},{16,17},{18,... | collective-permute-start | bytes 1572872 | tf_op jit(solution)/shard_map/ppermute | solution.py:257
  105.1 0.0 collective-permute-done.7.refs_4_.refs_8_
  105.1 1.3 %collective-permute-start.12 = (bf16[2,128,1024]{2,1,0:T(8,128)(2,1)S(1)}, bf16[2,128,1024]{2,1,0:T(8,128)(2,1)S(1)}, u32[]{:S(2)}, u32[]{:S(2)}) collective-permute-start(bf16[2,128,1024]{2,1,0:T(8,128)(2,1)S(1)} %bitcast.25), channel_id=1, source_target_pairs={{0,1},{2,3},{4,5},{6,7},{8,9},{10,11},{12,13},{14,15},{16,17},{18,... | collective-permute-start | bytes 1572872 | tf_op jit(solution)/shard_map/ppermute | solution.py:257
  106.4 1.3 %collective-permute-start.13 = (bf16[2,128,1024]{2,1,0:T(8,128)(2,1)S(1)}, bf16[2,128,1024]{2,1,0:T(8,128)(2,1)S(1)}, u32[]{:S(2)}, u32[]{:S(2)}) collective-permute-start(bf16[2,128,1024]{2,1,0:T(8,128)(2,1)S(1)} %bitcast.27), channel_id=1, source_target_pairs={{0,1},{2,3},{4,5},{6,7},{8,9},{10,11},{12,13},{14,15},{16,17},{18,... | collective-permute-start | bytes 1572872 | tf_op jit(solution)/shard_map/ppermute | solution.py:257
  107.7 1.3 %collective-permute-start.14 = (bf16[2,128,1024]{2,1,0:T(8,128)(2,1)S(1)}, bf16[2,128,1024]{2,1,0:T(8,128)(2,1)S(1)}, u32[]{:S(2)}, u32[]{:S(2)}) collective-permute-start(bf16[2,128,1024]{2,1,0:T(8,128)(2,1)S(1)} %bitcast.29), channel_id=1, source_target_pairs={{0,1},{2,3},{4,5},{6,7},{8,9},{10,11},{12,13},{14,15},{16,17},{18,... | collective-permute-start | bytes 1572872 | tf_op jit(solution)/shard_map/ppermute | solution.py:257
  109.1 3.0 %near.1.refs_16_ = f32[2,1,512]{2,1,0:T(1,128)S(1)} custom-call(bf16[2,128,1024]{2,1,0:T(8,128)(2,1)S(1)} %bitcast.12, bf16[2,128,1024]{2,1,0:T(8,128)(2,1)S(1)} %bitcast.15, bf16[2,128,1024]{2,1,0:T(8,128)(2,1)S(1)} %bitcast.18, bf16[2,128,1024]{2,1,0:T(8,128)(2,1)S(1)} %bitcast.21, bf16[2,128,1024]{2,1,0:T(8,128)(2,1)S(1)} %collective-permute-done.7.refs_4_.refs_8_, ...), custom_call_target="tpu_custom_call" | custom-call | flops 2147483648 | bytes 8388608 | tf_op jit(solution)/shard_map/near/pallas_call | solution.py:206
  112.1 0.8 collective-permute-done.14.refs_15_
  112.9 0.1 copy-done.3
  113.1 0.2 copy-done.4
  113.2 0.8 copy-done.5
  114.0 8.4 %far.1 = f32[2,1,1024]{2,1,0:T(1,128)S(1)} custom-call(bf16[2,128,1024]{2,1,0:T(8,128)(2,1)S(1)} %bitcast.13, bf16[2,128,1024]{2,1,0:T(8,128)(2,1)S(1)} %bitcast.16, bf16[2,128,1024]{2,1,0:T(8,128)(2,1)S(1)} %bitcast.19, bf16[2,128,1024]{2,1,0:T(8,128)(2,1)S(1)} %bitcast.22, bf16[2,128,1024]{2,1,0:T(8,128)(2,1)S(1)} %bitcast.24, ...), custom_call_target="tpu_custom_call" | custom-call | flops 5368709120 | bytes 16777216 | tf_op jit(solution)/shard_map/far/pallas_call | solution.py:227
  122.5 0.6 copy.5
  (15 shorter events, 0.0 us)
Async XLA Ops:
  0.0 0.7 copy-start.1
  8.5 12.9 %collective-permute-start = (bf16[256,1024]{1,0:T(8,128)(2,1)S(1)}, bf16[256,1024]{1,0:T(8,128)(2,1)S(1)}, u32[]{:S(2)}, u32[]{:S(2)}) collective-permute-start(bf16[256,1024]{1,0:T(8,128)(2,1)S(1)} %get-tuple-element.18), channel_id=1, source_target_pairs={{0,2},{2,0},{4,6},{6,4},{8,10},{10,8},{12,14},{14,12},{1,3},{3,1},... | collective-permute-start | bytes 1572872 | tf_op jit(solution)/shard_map/ppermute | solution.py:254
  9.8 31.6 %collective-permute-start.1 = (bf16[256,1024]{1,0:T(8,128)(2,1)S(1)}, bf16[256,1024]{1,0:T(8,128)(2,1)S(1)}, u32[]{:S(2)}, u32[]{:S(2)}) collective-permute-start(bf16[256,1024]{1,0:T(8,128)(2,1)S(1)} %get-tuple-element.19), channel_id=1, source_target_pairs={{0,4},{2,6},{4,0},{6,2},{8,12},{10,14},{12,8},{14,10},{1,5},{3,7},... | collective-permute-start | bytes 1572872 | tf_op jit(solution)/shard_map/ppermute | solution.py:254
  11.1 41.5 %collective-permute-start.2 = (bf16[256,1024]{1,0:T(8,128)(2,1)S(1)}, bf16[256,1024]{1,0:T(8,128)(2,1)S(1)}, u32[]{:S(2)}, u32[]{:S(2)}) collective-permute-start(bf16[256,1024]{1,0:T(8,128)(2,1)S(1)} %get-tuple-element.20), channel_id=1, source_target_pairs={{0,6},{2,4},{4,2},{6,0},{8,14},{10,12},{12,10},{14,8},{1,7},{3,5},... | collective-permute-start | bytes 1572872 | tf_op jit(solution)/shard_map/ppermute | solution.py:254
  11.2 42.7 %collective-permute-start.3 = (bf16[256,1024]{1,0:T(8,128)(2,1)S(1)}, bf16[256,1024]{1,0:T(8,128)(2,1)S(1)}, u32[]{:S(2)}, u32[]{:S(2)}) collective-permute-start(bf16[256,1024]{1,0:T(8,128)(2,1)S(1)} %get-tuple-element.21), channel_id=1, source_target_pairs={{0,8},{2,10},{4,12},{6,14},{8,0},{10,2},{12,4},{14,6},{1,9},{3,11}... | collective-permute-start | bytes 1572872 | tf_op jit(solution)/shard_map/ppermute | solution.py:254
  11.2 44.6 %collective-permute-start.4 = (bf16[256,1024]{1,0:T(8,128)(2,1)S(1)}, bf16[256,1024]{1,0:T(8,128)(2,1)S(1)}, u32[]{:S(2)}, u32[]{:S(2)}) collective-permute-start(bf16[256,1024]{1,0:T(8,128)(2,1)S(1)} %get-tuple-element.22), channel_id=1, source_target_pairs={{0,10},{2,8},{4,14},{6,12},{8,2},{10,0},{12,6},{14,4},{1,11},{3,9}... | collective-permute-start | bytes 1572872 | tf_op jit(solution)/shard_map/ppermute | solution.py:254
  21.4 70.3 %collective-permute-start.5 = (bf16[256,1024]{1,0:T(8,128)(2,1)S(1)}, bf16[256,1024]{1,0:T(8,128)(2,1)S(1)}, u32[]{:S(2)}, u32[]{:S(2)}) collective-permute-start(bf16[256,1024]{1,0:T(8,128)(2,1)S(1)} %get-tuple-element.23), channel_id=1, source_target_pairs={{0,12},{2,14},{4,8},{6,10},{8,4},{10,6},{12,0},{14,2},{1,13},{3,15... | collective-permute-start | bytes 1572872 | tf_op jit(solution)/shard_map/ppermute | solution.py:254
  41.4 62.5 %collective-permute-start.6 = (bf16[256,1024]{1,0:T(8,128)(2,1)S(1)}, bf16[256,1024]{1,0:T(8,128)(2,1)S(1)}, u32[]{:S(2)}, u32[]{:S(2)}) collective-permute-start(bf16[256,1024]{1,0:T(8,128)(2,1)S(1)} %get-tuple-element.24), channel_id=1, source_target_pairs={{0,14},{2,12},{4,10},{6,8},{8,6},{10,4},{12,2},{14,0},{1,15},{3,13... | collective-permute-start | bytes 1572872 | tf_op jit(solution)/shard_map/ppermute | solution.py:254
  52.6 52.5 %collective-permute-start.7 = (bf16[2,128,1024]{2,1,0:T(8,128)(2,1)S(1)}, bf16[2,128,1024]{2,1,0:T(8,128)(2,1)S(1)}, u32[]{:S(2)}, u32[]{:S(2)}) collective-permute-start(bf16[2,128,1024]{2,1,0:T(8,128)(2,1)S(1)} %bitcast.11), channel_id=1, source_target_pairs={{0,1},{2,3},{4,5},{6,7},{8,9},{10,11},{12,13},{14,15},{16,17},{18,... | collective-permute-start | bytes 1572872 | tf_op jit(solution)/shard_map/ppermute | solution.py:257
  53.9 52.5 %collective-permute-start.8 = (bf16[2,128,1024]{2,1,0:T(8,128)(2,1)S(1)}, bf16[2,128,1024]{2,1,0:T(8,128)(2,1)S(1)}, u32[]{:S(2)}, u32[]{:S(2)}) collective-permute-start(bf16[2,128,1024]{2,1,0:T(8,128)(2,1)S(1)} %bitcast.14), channel_id=1, source_target_pairs={{0,1},{2,3},{4,5},{6,7},{8,9},{10,11},{12,13},{14,15},{16,17},{18,... | collective-permute-start | bytes 1572872 | tf_op jit(solution)/shard_map/ppermute | solution.py:257
  55.9 51.9 %collective-permute-start.9 = (bf16[2,128,1024]{2,1,0:T(8,128)(2,1)S(1)}, bf16[2,128,1024]{2,1,0:T(8,128)(2,1)S(1)}, u32[]{:S(2)}, u32[]{:S(2)}) collective-permute-start(bf16[2,128,1024]{2,1,0:T(8,128)(2,1)S(1)} %bitcast.17), channel_id=1, source_target_pairs={{0,1},{2,3},{4,5},{6,7},{8,9},{10,11},{12,13},{14,15},{16,17},{18,... | collective-permute-start | bytes 1572872 | tf_op jit(solution)/shard_map/ppermute | solution.py:257
  91.6 17.4 %collective-permute-start.10 = (bf16[2,128,1024]{2,1,0:T(8,128)(2,1)S(1)}, bf16[2,128,1024]{2,1,0:T(8,128)(2,1)S(1)}, u32[]{:S(2)}, u32[]{:S(2)}) collective-permute-start(bf16[2,128,1024]{2,1,0:T(8,128)(2,1)S(1)} %bitcast.20), channel_id=1, source_target_pairs={{0,1},{2,3},{4,5},{6,7},{8,9},{10,11},{12,13},{14,15},{16,17},{18,... | collective-permute-start | bytes 1572872 | tf_op jit(solution)/shard_map/ppermute | solution.py:257
  103.8 8.2 %collective-permute-start.11 = (bf16[2,128,1024]{2,1,0:T(8,128)(2,1)S(1)}, bf16[2,128,1024]{2,1,0:T(8,128)(2,1)S(1)}, u32[]{:S(2)}, u32[]{:S(2)}) collective-permute-start(bf16[2,128,1024]{2,1,0:T(8,128)(2,1)S(1)} %bitcast.23), channel_id=1, source_target_pairs={{0,1},{2,3},{4,5},{6,7},{8,9},{10,11},{12,13},{14,15},{16,17},{18,... | collective-permute-start | bytes 1572872 | tf_op jit(solution)/shard_map/ppermute | solution.py:257
  105.1 7.0 %collective-permute-start.12 = (bf16[2,128,1024]{2,1,0:T(8,128)(2,1)S(1)}, bf16[2,128,1024]{2,1,0:T(8,128)(2,1)S(1)}, u32[]{:S(2)}, u32[]{:S(2)}) collective-permute-start(bf16[2,128,1024]{2,1,0:T(8,128)(2,1)S(1)} %bitcast.25), channel_id=1, source_target_pairs={{0,1},{2,3},{4,5},{6,7},{8,9},{10,11},{12,13},{14,15},{16,17},{18,... | collective-permute-start | bytes 1572872 | tf_op jit(solution)/shard_map/ppermute | solution.py:257
  106.4 5.7 %collective-permute-start.13 = (bf16[2,128,1024]{2,1,0:T(8,128)(2,1)S(1)}, bf16[2,128,1024]{2,1,0:T(8,128)(2,1)S(1)}, u32[]{:S(2)}, u32[]{:S(2)}) collective-permute-start(bf16[2,128,1024]{2,1,0:T(8,128)(2,1)S(1)} %bitcast.27), channel_id=1, source_target_pairs={{0,1},{2,3},{4,5},{6,7},{8,9},{10,11},{12,13},{14,15},{16,17},{18,... | collective-permute-start | bytes 1572872 | tf_op jit(solution)/shard_map/ppermute | solution.py:257
  107.7 5.2 %collective-permute-start.14 = (bf16[2,128,1024]{2,1,0:T(8,128)(2,1)S(1)}, bf16[2,128,1024]{2,1,0:T(8,128)(2,1)S(1)}, u32[]{:S(2)}, u32[]{:S(2)}) collective-permute-start(bf16[2,128,1024]{2,1,0:T(8,128)(2,1)S(1)} %bitcast.29), channel_id=1, source_target_pairs={{0,1},{2,3},{4,5},{6,7},{8,9},{10,11},{12,13},{14,15},{16,17},{18,... | collective-permute-start | bytes 1572872 | tf_op jit(solution)/shard_map/ppermute | solution.py:257
  109.1 3.0 %copy-start = (bf16[2,128,1024]{2,1,0:T(8,128)(2,1)}, bf16[2,128,1024]{2,1,0:T(8,128)(2,1)S(1)}, u32[]{:S(2)}) copy-start(bf16[2,128,1024]{2,1,0:T(8,128)(2,1)S(1)} %collective-permute-done.10.refs_7_.refs_11_) | copy-start | bytes 1572868
  112.1 0.8 copy-start.2
  112.1 1.0 copy-start.3
  112.1 1.1 copy-start.4
  113.2 0.8 copy-start.5

commit v2 on v0

v2 whole, which is shorter than its diff:
```python
import functools

import jax
import jax.numpy as jnp
from jax import lax
from jax.experimental import pallas as pl
from jax.experimental.pallas import tpu as pltpu
from jax.sharding import PartitionSpec as P

CLUS_DEV = 2
LANES = 128
MARK = 2.0
BF = jnp.bfloat16
F32 = jnp.float32


def iota(shape, dim):
    return lax.broadcasted_iota(jnp.int32, shape, dim)


def matmul(a, b, contract):
    return lax.dot_general(a, b, (contract, ((), ())), preferred_element_type=F32)


def targets(ids, clusters, per_source):
    groups = ids.shape[1] // LANES
    parts = [ids[:, g * LANES : (g + 1) * LANES] for g in range(groups)]
    hot = jnp.concatenate(
        [(iota((clusters, LANES), 0) == part).astype(F32) for part in parts], axis=0
    )
    stacked = groups * clusters
    earlier = (iota((LANES, LANES), 0) < iota((LANES, LANES), 1)).astype(F32).astype(BF)
    within = matmul(hot.astype(BF), earlier, ((1,), (0,)))
    totals = jnp.broadcast_to(jnp.sum(hot, axis=1, keepdims=True), (stacked, LANES))
    a, b = iota((stacked, stacked), 0), iota((stacked, stacked), 1)
    chunks_before = ((a % clusters == b % clusters) & (b < a)).astype(F32).astype(BF)
    before = within + matmul(chunks_before, totals.astype(BF), ((1,), (0,)))
    picked = hot * before
    out = [
        jnp.sum(picked[g * clusters : (g + 1) * clusters], axis=0, keepdims=True).astype(jnp.int32)
        + parts[g] * per_source
        for g in range(groups)
    ]
    return jnp.concatenate(out, axis=1)


def pack_block(unit, tgt, dest, width):
    hit = (tgt - dest * width) == iota((width, tgt.shape[1]), 0)
    hot = hit.astype(F32)
    rows = matmul(hot.astype(BF), unit, ((1,), (0,)))
    empty = jnp.max(hot, axis=1, keepdims=True) < 0.5
    head = jnp.where(empty, F32(MARK), rows[:, :LANES])
    return head.astype(BF), rows[:, LANES:].astype(BF)


def store_blocks(unit, tgt, steps, width, outs):
    me = lax.axis_index("clus")
    for step, out in zip(steps, outs):
        head, tail = pack_block(unit, tgt, me ^ step, width)
        out[:, :LANES] = head
        out[:, LANES:] = tail


def pack_first(steps, clusters, per_source, emb, ids, unit, tgt, *outs):
    values = emb[...].astype(F32)
    scale = lax.rsqrt(jnp.sum(values * values, axis=1, keepdims=True) + 1e-6)
    unit[...] = (values * scale).astype(BF)
    tgt[...] = targets(ids[...], clusters, per_source)
    store_blocks(unit[...], tgt[...], steps, CLUS_DEV * per_source, outs)


def pack_rest(steps, per_source, unit, tgt, *outs):
    store_blocks(unit[...], tgt[...], steps, CLUS_DEV * per_source, outs)


VMEM = pl.BlockSpec(memory_space=pltpu.VMEM)


def kernel_call(kernel, shapes, inputs, flops, name, scratch=()):
    moved = sum(x.size * x.dtype.itemsize for x in list(inputs) + list(shapes))
    return pl.pallas_call(
        kernel,
        out_shape=shapes,
        in_specs=[VMEM] * len(inputs),
        out_specs=[VMEM] * len(shapes),
        scratch_shapes=scratch,
        compiler_params=pltpu.CompilerParams(vmem_limit_bytes=40 * 2**20),
        cost_estimate=pl.CostEstimate(flops=int(flops), bytes_accessed=moved, transcendentals=0),
        name=name,
    )(*inputs)


def call_pack_first(emb, ids, steps, clusters, per_source):
    block = jax.ShapeDtypeStruct((CLUS_DEV * per_source, emb.shape[1]), BF)
    shapes = [jax.ShapeDtypeStruct(emb.shape, BF), jax.ShapeDtypeStruct(ids.shape, jnp.int32)]
    return kernel_call(
        functools.partial(pack_first, steps, clusters, per_source),
        shapes + [block] * len(steps),
        [emb, ids],
        2 * len(steps) * block.shape[0] * emb.size,
        "pack_first",
    )


def call_pack_rest(unit, tgt, steps, per_source):
    block = jax.ShapeDtypeStruct((CLUS_DEV * per_source, unit.shape[1]), BF)
    return kernel_call(
        functools.partial(pack_rest, steps, per_source),
        [block] * len(steps),
        [unit, tgt],
        2 * len(steps) * block.shape[0] * unit.size,
        "pack_rest",
    )


CHUNK = 256


def raise_best(best, keys, queries, triangular=False):
    rows = queries.shape[0]
    chunk = min(CHUNK, rows)
    for start in range(0, rows, chunk):
        count = start + chunk if triangular else keys.shape[0]
        sims = matmul(keys[:count, :], queries[start : start + chunk, :], ((1,), (1,)))
        filled = keys[:count, :LANES].astype(F32) < 1.5
        for first in range(0, chunk, LANES):
            allowed = filled
            if triangular:
                allowed = filled & (
                    iota((count, LANES), 0) < iota((count, LANES), 1) + (start + first)
                )
            part = jnp.where(allowed, sims[:, first : first + LANES], F32(-1.0))
            window = slice(start + first, start + first + LANES)
            best[:, window] = jnp.maximum(best[:, window], jnp.max(part, axis=0, keepdims=True))


def gather_group(blocks, cluster, out, me):
    per = blocks[0].shape[0] // CLUS_DEV
    for step, block in enumerate(blocks):
        place = (me & (len(blocks) - 1)) ^ step
        rows = pl.ds(pl.multiple_of(place * per, per), per)
        out[rows, :] = block[cluster * per : (cluster + 1) * per, :]


def score_pair(bests, groups, new, old, bit, me):
    later = (me & bit) == 0

    @pl.when(later)
    def _():
        raise_best(bests[new], groups[old], groups[new])

    @pl.when(jnp.logical_not(later))
    def _():
        raise_best(bests[old], groups[new], groups[old])


def group_bits(owners):
    return [owners // 2, owners // 4, owners // 8]


def first_kernel(*refs):
    blocks, (cat, best) = refs[:-2], refs[-2:]
    me = lax.axis_index("clus")
    best[...] = jnp.full(best.shape, -1.0, F32)
    for c in range(CLUS_DEV):
        gather_group(blocks, c, cat.at[c], me)
        raise_best(best.at[c : c + 1], cat.at[c], cat.at[c], True)


def middle_kernel(bits, fresh, *refs):
    old = len(bits)
    cats, others, refs = refs[:old], refs[old : 2 * old], refs[2 * old :]
    old_bests, blocks = refs[:old], refs[old : old + fresh]
    cat, bests = refs[old + fresh], refs[old + fresh + 1 :]
    me = lax.axis_index("clus")
    for before, best in zip(old_bests, bests):
        best[...] = before[...]
    bests[old][...] = jnp.full(bests[old].shape, -1.0, F32)
    for c in range(CLUS_DEV):
        gather_group(blocks, c, cat.at[c], me)
        groups = [x.at[c] for x in cats] + [cat.at[c]]
        rows = [best.at[c : c + 1] for best in bests]
        raise_best(rows[old], groups[old], groups[old], True)
        for i, bit in enumerate(bits):
            score_pair(rows, groups, old, i, bit, me)

    @pl.when(lax.axis_index("blk") == 1)
    def _():
        for c in range(CLUS_DEV):
            rows = [best.at[c : c + 1] for best in bests]
            for i in range(old):
                raise_best(rows[i], others[old - 1].at[c], cats[i].at[c])
                raise_best(rows[old], others[i].at[c], cat.at[c])


def filled_queries(rows):
    ones = jnp.ones((8, LANES), BF)
    return matmul(ones, rows[:, :LANES], ((1,), (1,)))[:1] < 100.0


def last_kernel(bits, fresh, *refs):
    old = len(bits)
    cats, refs = refs[:old], refs[old:]
    others, refs = refs[: old - 1], refs[old - 1 :]
    late, refs = refs[:fresh], refs[fresh:]
    old_bests, refs = refs[:old], refs[old:]
    blocks, other_blocks, out = refs[:fresh], refs[fresh : 2 * fresh], refs[2 * fresh]
    cat, late_cat, *bests = refs[2 * fresh + 1 :]
    me = lax.axis_index("clus")
    for before, best in zip(old_bests, bests):
        best[...] = before[...]
    bests[old][...] = jnp.full(bests[old].shape, -1.0, F32)
    size = cat.shape[1]
    for c in range(CLUS_DEV):
        gather_group(blocks, c, cat.at[c], me)
        groups = [x.at[c] for x in cats] + [cat.at[c]]
        rows = [best.at[c : c + 1] for best in bests]
        raise_best(rows[old], groups[old], groups[old], True)
        for i, bit in enumerate(bits):
            score_pair(rows, groups, old, i, bit, me)

    @pl.when(lax.axis_index("blk") == 1)
    def _():
        for c in range(CLUS_DEV):
            rows = [best.at[c : c + 1] for best in bests]
            gather_group(late, c, late_cat.at[:size], me)
            gather_group(other_blocks, c, late_cat.at[size:], me)
            for i in range(old):
                raise_best(rows[i], late_cat, cats[i].at[c])
            raise_best(rows[old], late_cat, cat.at[c])
            for i in range(old - 1):
                raise_best(rows[old], others[i].at[c], cat.at[c])

    total = out.shape[1]
    start = 0
    for c in range(CLUS_DEV):
        start = 0
        for group, best in zip(list(cats) + [cat], bests):
            count = group.shape[1]
            per = blocks[0].shape[0] // CLUS_DEV
            sources = count // per
            base = (me ^ (start // per)) & ~(sources - 1)
            at = pl.ds(pl.multiple_of(base * per, LANES), count)
            kept = filled_queries(group.at[c])
            out[c : c + 1, at] = jnp.where(kept, best[c : c + 1, :], F32(0.0))
            start += count
    assert start == total


def shape_of(sources, per, width):
    return [
        jax.ShapeDtypeStruct((CLUS_DEV, sources * per, width), BF),
        jax.ShapeDtypeStruct((CLUS_DEV, sources * per), F32),
    ]


def local(embeddings, cluster_ids):
    owners = lax.axis_size("clus")
    clusters = CLUS_DEV * owners
    rows, width = embeddings.shape
    per = 2 * rows // clusters
    bits = group_bits(owners)
    bounds = [0, owners // 2, owners // 2 + owners // 4, owners - owners // 8, owners]
    steps = [list(range(a, b)) for a, b in zip(bounds, bounds[1:])]
    unit_flops = 2 * CLUS_DEV * per * per * width

    def to_owner(block, step):
        return lax.ppermute(block, "clus", [(i, i ^ step) for i in range(owners)])

    def to_later(block):
        return lax.ppermute(block, "blk", [(0, 1)])

    def after(block, done):
        return lax.optimization_barrier((block, done))

    unit, tgt, ahead = call_pack_first(embeddings, cluster_ids, steps[1][:1], clusters, per)
    far1 = [to_owner(ahead, steps[1][0])]
    near_out = call_pack_rest(unit, tgt, steps[0] + steps[1][1:], per)
    near = [near_out[0]] + [to_owner(b, s) for s, b in zip(steps[0][1:], near_out[1:])]
    far1 += [to_owner(b, s) for s, b in zip(steps[1][1:], near_out[len(steps[0]) :])]
    far_out = call_pack_rest(unit, tgt, steps[2] + steps[3], per)
    held, near[-1] = after(far_out[: len(steps[2])], near[-1])
    far2 = [to_owner(b, s) for s, b in zip(steps[2], held)]

    n0, n1, n2, n3 = [len(x) for x in steps]
    cat0, best0 = kernel_call(
        first_kernel, shape_of(n0, per, width), near, unit_flops * n0 * n0, "first"
    )
    oth0 = to_later(cat0)
    held, far1[0] = after(far_out[len(steps[2]) :], far1[0])
    far3 = [to_owner(b, s) for s, b in zip(steps[3], held)]
    cat1, best0, best1 = kernel_call(
        functools.partial(middle_kernel, bits[:1], n1),
        shape_of(n1, per, width)[:1] + [best0, shape_of(n1, per, width)[1]],
        [cat0, oth0, best0] + far1,
        unit_flops * (n0 * n0 + 2 * n0 * n1 + n1 * n1),
        "second",
    )
    oth1 = to_later(cat1)
    cat2, best0, best1, best2 = kernel_call(
        functools.partial(middle_kernel, bits[:2], n2),
        shape_of(n2, per, width)[:1] + [best0, best1, shape_of(n2, per, width)[1]],
        [cat0, cat1, oth0, oth1, best0, best1] + far2,
        unit_flops * (n0 * n1 + n1 * n1 + 2 * n2 * (n0 + n1)),
        "third",
    )
    oth2 = [to_later(b) for b in far2]
    oth3 = [to_later(b) for b in far3]
    (best,) = kernel_call(
        functools.partial(last_kernel, bits, n3),
        [jax.ShapeDtypeStruct((CLUS_DEV, rows), F32)],
        [cat0, cat1, cat2, oth0, oth1] + oth2 + [best0, best1, best2] + far3 + oth3,
        unit_flops * 4 * n3 * (n0 + n1 + n2),
        "last",
        [
            pltpu.VMEM((CLUS_DEV, n3 * per, width), BF),
            pltpu.VMEM((2 * n3 * per, width), BF),
        ]
        + [pltpu.VMEM((CLUS_DEV, n * per), F32) for n in (n0, n1, n2, n3)],
    )
    return best


def solution(mesh):
    placed = (P(("groups", "clus", "blk"), None), P(("groups", "clus", "blk"), None))
    return jax.shard_map(
        local, mesh=mesh, in_specs=placed, out_specs=P(("groups", "clus"), "blk"), check_vma=False
    )
```

time: 157 us -> 146 us (0.930)
  the two profiles are of different devices: /device:TPU:0 before, /device:TPU:17 now
where the time goes in v2:
time: 146 us; the launch traced here: 144 us
  waiting for transfers between devices  105 us (72%)
  Pallas kernels  21.1 us (14%)
  starting transfers between devices  14.8 us (10%)
  local copies, waits for them, and re-layouts  2.28 us (2%)
    ppermute x7, waiting for transfers between devices, to_owner(): return lax.ppermute(block, 'clus', [(i, i ^ step) for i in range(owners)])  105 us
    pallas_call x7, Pallas kernels, kernel_call(): pl.pallas_call(kernel, out_shape=shapes, in_specs=[VMEM] * len(inputs), o...  21.1 us
    ppermute x7, starting transfers between devices, to_owner(): return lax.ppermute(block, 'clus', [(i, i ^ step) for i in range(owners)])  9.65 us
    ppermute x4, starting transfers between devices, to_later(): return lax.ppermute(block, 'blk', [(0, 1)])  5.15 us
  transfers between devices with their start and end apart: 11, of which 6 were waited for; matrix products, arithmetic and copies ran while one was open for 0% of the time, Pallas kernels for 4%

profile of v2, /device:TPU:17, one launch (start us, length us, event | category | flops | bytes accessed | tf_op | source)
XLA Modules:
  0.0 143.7 jit_solution(7922798608074576068)
XLA Ops:
  0.0 0.0 copy-start
  0.0 1.6 %copy-done = bf16[1024,1024]{1,0:T(8,128)(2,1)S(1)} copy-done((bf16[1024,1024]{1,0:T(8,128)(2,1)S(1)}, bf16[1024,1024]{1,0:T(8,128)(2,1)}, u32[]{:S(2)}) %copy-start) | copy-done | bytes 2097176
  1.6 0.7 copy-done.1
  2.3 1.5 %pack_first.1 = (bf16[1024,1024]{1,0:T(8,128)(2,1)S(1)}, s32[1,1024]{1,0:T(1,128)S(1)}, bf16[256,1024]{1,0:T(8,128)(2,1)S(1)}) custom-call(bf16[1024,1024]{1,0:T(8,128)(2,1)S(1)} %copy-done, s32[1,1024]{1,0:T(1,128)S(1)} %copy-done.1), custom_call_target="tpu_custom_call" | custom-call | flops 536870912 | bytes 4726784 | tf_op jit(solution)/shard_map/pack_first/pallas_call | solution.py:81
  3.7 3.2 %pack_rest.2 = (bf16[256,1024]{1,0:T(8,128)(2,1)S(1)}, bf16[256,1024]{1,0:T(8,128)(2,1)S(1)}, bf16[256,1024]{1,0:T(8,128)(2,1)S(1)}, bf16[256,1024]{1,0:T(8,128)(2,1)S(1)}, bf16[256,1024]{1,0:T(8,128)(2,1)S(1)}) custom-call(bf16[1024,1024]{1,0:T(8,128)(2,1)S(1)} %get-tuple-element.28.unit, s32[1,1024]{1,0:T(1,128)S(1)} %get-tuple-element.29.tgt), custom_call_target="tpu_custom_call" | custom-call | flops 2684354560 | bytes 4722688 | tf_op jit(solution)/shard_map/pack_rest/pallas_call | solution.py:81
  7.0 2.3 %collective-permute-start.2 = (bf16[256,1024]{1,0:T(8,128)(2,1)S(1)}, bf16[256,1024]{1,0:T(8,128)(2,1)S(1)}, u32[]{:S(2)}, u32[]{:S(2)}) collective-permute-start(bf16[256,1024]{1,0:T(8,128)(2,1)S(1)} %get-tuple-element.34), channel_id=1, source_target_pairs={{0,6},{2,4},{4,2},{6,0},{8,14},{10,12},{12,10},{14,8},{1,7},{3,5},... | collective-permute-start | bytes 1572872 | tf_op jit(solution)/shard_map/ppermute | solution.py:268
  9.3 0.2 collective-permute-start
  9.5 0.2 collective-permute-start.1
  9.7 1.4 pack_rest.3
  11.1 9.6 %collective-permute-done.2.refs_3_ = bf16[256,1024]{1,0:T(8,128)(2,1)S(1)} collective-permute-done((bf16[256,1024]{1,0:T(8,128)(2,1)S(1)}, bf16[256,1024]{1,0:T(8,128)(2,1)S(1)}, u32[]{:S(2)}, u32[]{:S(2)}) %collective-permute-start.2) | collective-permute-done | bytes 524320 | tf_op jit(solution)/shard_map/ppermute | solution.py:268
  20.8 12.3 %collective-permute-done.refs_1_ = bf16[256,1024]{1,0:T(8,128)(2,1)S(1)} collective-permute-done((bf16[256,1024]{1,0:T(8,128)(2,1)S(1)}, bf16[256,1024]{1,0:T(8,128)(2,1)S(1)}, u32[]{:S(2)}, u32[]{:S(2)}) %collective-permute-start) | collective-permute-done | bytes 524320 | tf_op jit(solution)/shard_map/ppermute | solution.py:268
  33.0 0.0 collective-permute-done.1.refs_2_
  33.0 1.2 first.1
  34.3 1.3 collective-permute-start.3
  35.6 0.1 collective-permute-start.4
  35.7 3.3 %collective-permute-start.5 = (bf16[256,1024]{1,0:T(8,128)(2,1)S(1)}, bf16[256,1024]{1,0:T(8,128)(2,1)S(1)}, u32[]{:S(2)}, u32[]{:S(2)}) collective-permute-start(bf16[256,1024]{1,0:T(8,128)(2,1)S(1)} %get-tuple-element.41), channel_id=1, source_target_pairs={{0,10},{2,8},{4,14},{6,12},{8,2},{10,0},{12,6},{14,4},{1,11},{3,9}... | collective-permute-start | bytes 1572872 | tf_op jit(solution)/shard_map/ppermute | solution.py:268
  39.0 29.7 %collective-permute-done.4.refs_3_ = bf16[256,1024]{1,0:T(8,128)(2,1)S(1)} collective-permute-done((bf16[256,1024]{1,0:T(8,128)(2,1)S(1)}, bf16[256,1024]{1,0:T(8,128)(2,1)S(1)}, u32[]{:S(2)}, u32[]{:S(2)}) %collective-permute-start.4) | collective-permute-done | bytes 524320 | tf_op jit(solution)/shard_map/ppermute | solution.py:268
  68.6 11.2 %collective-permute-done.5.refs_4_ = bf16[256,1024]{1,0:T(8,128)(2,1)S(1)} collective-permute-done((bf16[256,1024]{1,0:T(8,128)(2,1)S(1)}, bf16[256,1024]{1,0:T(8,128)(2,1)S(1)}, u32[]{:S(2)}, u32[]{:S(2)}) %collective-permute-start.5) | collective-permute-done | bytes 524320 | tf_op jit(solution)/shard_map/ppermute | solution.py:268
  79.9 0.0 collective-permute-done.3.refs_1_.refs_2_.refs_3_
  79.9 3.6 %second.1 = (bf16[2,256,1024]{2,1,0:T(8,128)(2,1)S(1)}, f32[2,512]{1,0:T(2,128)S(1)}, f32[2,256]{1,0:T(2,128)S(1)}) custom-call(bf16[2,512,1024]{2,1,0:T(8,128)(2,1)S(1)} %get-tuple-element.36.refs_0_, bf16[2,512,1024]{2,1,0:T(8,128)(2,1)S(1)} %collective-permute-done.3.refs_1_.refs_2_.refs_3_, f32[2,512]{1,0:T(2,128)S(1)} %get-tuple-element.37.refs_2_, ...), custom_call_target="tpu_custom_call" | custom-call | flops 2415919104 | bytes 6301696 | tf_op jit(solution)/shard_map/second/pallas_call | solution.py:81
  83.5 1.3 collective-permute-start.6
  84.8 3.5 %collective-permute-start.7 = (bf16[256,1024]{1,0:T(8,128)(2,1)S(1)}, bf16[256,1024]{1,0:T(8,128)(2,1)S(1)}, u32[]{:S(2)}, u32[]{:S(2)}) collective-permute-start(bf16[256,1024]{1,0:T(8,128)(2,1)S(1)} %get-tuple-element.45), channel_id=1, source_target_pairs={{0,12},{2,14},{4,8},{6,10},{8,4},{10,6},{12,0},{14,2},{1,13},{3,15... | collective-permute-start | bytes 1572872 | tf_op jit(solution)/shard_map/ppermute | solution.py:268
  88.3 0.0 collective-permute-start.9
  88.3 33.5 %collective-permute-done.7.refs_6_ = bf16[256,1024]{1,0:T(8,128)(2,1)S(1)} collective-permute-done((bf16[256,1024]{1,0:T(8,128)(2,1)S(1)}, bf16[256,1024]{1,0:T(8,128)(2,1)S(1)}, u32[]{:S(2)}, u32[]{:S(2)}) %collective-permute-start.7) | collective-permute-done | bytes 524320 | tf_op jit(solution)/shard_map/ppermute | solution.py:268
  121.9 1.3 collective-permute-start.8
  123.1 9.1 %collective-permute-done.9.refs_9_ = bf16[256,1024]{1,0:T(8,128)(2,1)S(1)} collective-permute-done((bf16[256,1024]{1,0:T(8,128)(2,1)S(1)}, bf16[256,1024]{1,0:T(8,128)(2,1)S(1)}, u32[]{:S(2)}, u32[]{:S(2)}) %collective-permute-start.9) | collective-permute-done | bytes 524320 | tf_op jit(solution)/shard_map/ppermute | solution.py:268
  132.3 1.3 collective-permute-start.10
  133.6 0.0 collective-permute-done.6.refs_3_.refs_4_
  133.6 4.2 %third.1 = (bf16[2,128,1024]{2,1,0:T(8,128)(2,1)S(1)}, f32[2,512]{1,0:T(2,128)S(1)}, f32[2,256]{1,0:T(2,128)S(1)}, f32[2,128]{1,0:T(2,128)S(1)}) custom-call(bf16[2,512,1024]{2,1,0:T(8,128)(2,1)S(1)} %get-tuple-element.36.refs_0_, bf16[2,256,1024]{2,1,0:T(8,128)(2,1)S(1)} %get-tuple-element.42.refs_1_, ...), custom_call_target="tpu_custom_call" | custom-call | flops 1610612736 | bytes 7353344 | tf_op jit(solution)/shard_map/third/pallas_call | solution.py:81
  137.7 0.0 collective-permute-done.8.refs_5_
  137.8 0.0 collective-permute-done.10.refs_10_
  137.8 6.0 %last.1 = f32[2,1024]{1,0:T(2,128)} custom-call(bf16[2,512,1024]{2,1,0:T(8,128)(2,1)S(1)} %get-tuple-element.36.refs_0_, bf16[2,256,1024]{2,1,0:T(8,128)(2,1)S(1)} %get-tuple-element.42.refs_1_, bf16[2,128,1024]{2,1,0:T(8,128)(2,1)S(1)} %get-tuple-element.46.refs_2_, bf16[2,512,1024]{2,1,0:T(8,128)(2,1)S(1)} %collective-permute-done.3.refs_1_.refs_2_.refs_3_, ...), custom_call_target="tpu_custom_call" | custom-call | flops 1879048192 | bytes 8403968 | tf_op jit(solution)/shard_map/last/pallas_call | solution.py:81
  (1 shorter events, 0.0 us)
Async XLA Ops:
  0.0 1.6 %copy-start = (bf16[1024,1024]{1,0:T(8,128)(2,1)S(1)}, bf16[1024,1024]{1,0:T(8,128)(2,1)}, u32[]{:S(2)}) copy-start(bf16[1024,1024]{1,0:T(8,128)(2,1)} %emb.1) | copy-start | bytes 6291460
  1.6 0.7 copy-start.1
  7.0 13.8 %collective-permute-start.2 = (bf16[256,1024]{1,0:T(8,128)(2,1)S(1)}, bf16[256,1024]{1,0:T(8,128)(2,1)S(1)}, u32[]{:S(2)}, u32[]{:S(2)}) collective-permute-start(bf16[256,1024]{1,0:T(8,128)(2,1)S(1)} %get-tuple-element.34), channel_id=1, source_target_pairs={{0,6},{2,4},{4,2},{6,0},{8,14},{10,12},{12,10},{14,8},{1,7},{3,5},... | collective-permute-start | bytes 1572872 | tf_op jit(solution)/shard_map/ppermute | solution.py:268
  9.3 23.7 %collective-permute-start = (bf16[256,1024]{1,0:T(8,128)(2,1)S(1)}, bf16[256,1024]{1,0:T(8,128)(2,1)S(1)}, u32[]{:S(2)}, u32[]{:S(2)}) collective-permute-start(bf16[256,1024]{1,0:T(8,128)(2,1)S(1)} %get-tuple-element.31), channel_id=1, source_target_pairs={{0,2},{2,0},{4,6},{6,4},{8,10},{10,8},{12,14},{14,12},{1,3},{3,1},... | collective-permute-start | bytes 1572872 | tf_op jit(solution)/shard_map/ppermute | solution.py:268
  9.5 23.5 %collective-permute-start.1 = (bf16[256,1024]{1,0:T(8,128)(2,1)S(1)}, bf16[256,1024]{1,0:T(8,128)(2,1)S(1)}, u32[]{:S(2)}, u32[]{:S(2)}) collective-permute-start(bf16[256,1024]{1,0:T(8,128)(2,1)S(1)} %get-tuple-element.32), channel_id=1, source_target_pairs={{0,4},{2,6},{4,0},{6,2},{8,12},{10,14},{12,8},{14,10},{1,5},{3,7},... | collective-permute-start | bytes 1572872 | tf_op jit(solution)/shard_map/ppermute | solution.py:268
  34.3 45.6 %collective-permute-start.3 = (bf16[2,512,1024]{2,1,0:T(8,128)(2,1)S(1)}, bf16[2,512,1024]{2,1,0:T(8,128)(2,1)S(1)}, u32[]{:S(2)}, u32[]{:S(2)}) collective-permute-start(bf16[2,512,1024]{2,1,0:T(8,128)(2,1)S(1)} %get-tuple-element.36.refs_0_), channel_id=1, source_target_pairs={{0,1},{2,3},{4,5},{6,7},{8,9},{10,11},{12,13},{14,15},{16,17},{18,... | collective-permute-start | bytes 6291464 | tf_op jit(solution)/shard_map/ppermute | solution.py:271
  35.6 33.0 %collective-permute-start.4 = (bf16[256,1024]{1,0:T(8,128)(2,1)S(1)}, bf16[256,1024]{1,0:T(8,128)(2,1)S(1)}, u32[]{:S(2)}, u32[]{:S(2)}) collective-permute-start(bf16[256,1024]{1,0:T(8,128)(2,1)S(1)} %get-tuple-element.39), channel_id=1, source_target_pairs={{0,8},{2,10},{4,12},{6,14},{8,0},{10,2},{12,4},{14,6},{1,9},{3,11}... | collective-permute-start | bytes 1572872 | tf_op jit(solution)/shard_map/ppermute | solution.py:268
  35.7 44.2 %collective-permute-start.5 = (bf16[256,1024]{1,0:T(8,128)(2,1)S(1)}, bf16[256,1024]{1,0:T(8,128)(2,1)S(1)}, u32[]{:S(2)}, u32[]{:S(2)}) collective-permute-start(bf16[256,1024]{1,0:T(8,128)(2,1)S(1)} %get-tuple-element.41), channel_id=1, source_target_pairs={{0,10},{2,8},{4,14},{6,12},{8,2},{10,0},{12,6},{14,4},{1,11},{3,9}... | collective-permute-start | bytes 1572872 | tf_op jit(solution)/shard_map/ppermute | solution.py:268
  83.5 50.1 %collective-permute-start.6 = (bf16[2,256,1024]{2,1,0:T(8,128)(2,1)S(1)}, bf16[2,256,1024]{2,1,0:T(8,128)(2,1)S(1)}, u32[]{:S(2)}, u32[]{:S(2)}) collective-permute-start(bf16[2,256,1024]{2,1,0:T(8,128)(2,1)S(1)} %get-tuple-element.42.refs_1_), channel_id=1, source_target_pairs={{0,1},{2,3},{4,5},{6,7},{8,9},{10,11},{12,13},{14,15},{16,17},{18,... | collective-permute-start | bytes 3145736 | tf_op jit(solution)/shard_map/ppermute | solution.py:271
  84.8 37.1 %collective-permute-start.7 = (bf16[256,1024]{1,0:T(8,128)(2,1)S(1)}, bf16[256,1024]{1,0:T(8,128)(2,1)S(1)}, u32[]{:S(2)}, u32[]{:S(2)}) collective-permute-start(bf16[256,1024]{1,0:T(8,128)(2,1)S(1)} %get-tuple-element.45), channel_id=1, source_target_pairs={{0,12},{2,14},{4,8},{6,10},{8,4},{10,6},{12,0},{14,2},{1,13},{3,15... | collective-permute-start | bytes 1572872 | tf_op jit(solution)/shard_map/ppermute | solution.py:268
  88.3 43.9 %collective-permute-start.9 = (bf16[256,1024]{1,0:T(8,128)(2,1)S(1)}, bf16[256,1024]{1,0:T(8,128)(2,1)S(1)}, u32[]{:S(2)}, u32[]{:S(2)}) collective-permute-start(bf16[256,1024]{1,0:T(8,128)(2,1)S(1)} %get-tuple-element.50), channel_id=1, source_target_pairs={{0,14},{2,12},{4,10},{6,8},{8,6},{10,4},{12,2},{14,0},{1,15},{3,13... | collective-permute-start | bytes 1572872 | tf_op jit(solution)/shard_map/ppermute | solution.py:268
  121.9 15.9 %collective-permute-start.8 = (bf16[256,1024]{1,0:T(8,128)(2,1)S(1)}, bf16[256,1024]{1,0:T(8,128)(2,1)S(1)}, u32[]{:S(2)}, u32[]{:S(2)}) collective-permute-start(bf16[256,1024]{1,0:T(8,128)(2,1)S(1)} %collective-permute-done.7.refs_6_), channel_id=1, source_target_pairs={{0,1},{2,3},{4,5},{6,7},{8,9},{10,11},{12,13},{14,15},{16,17},{18,... | collective-permute-start | bytes 1572872 | tf_op jit(solution)/shard_map/ppermute | solution.py:271
  132.3 5.5 %collective-permute-start.10 = (bf16[256,1024]{1,0:T(8,128)(2,1)S(1)}, bf16[256,1024]{1,0:T(8,128)(2,1)S(1)}, u32[]{:S(2)}, u32[]{:S(2)}) collective-permute-start(bf16[256,1024]{1,0:T(8,128)(2,1)S(1)} %collective-permute-done.9.refs_9_), channel_id=1, source_target_pairs={{0,1},{2,3},{4,5},{6,7},{8,9},{10,11},{12,13},{14,15},{16,17},{18,... | collective-permute-start | bytes 1572872 | tf_op jit(solution)/shard_map/ppermute | solution.py:271

commit v3 on v2

v3 whole, which is shorter than its diff:
```python
import functools

import jax
import jax.numpy as jnp
from jax import lax
from jax.experimental import pallas as pl
from jax.experimental.pallas import tpu as pltpu
from jax.sharding import PartitionSpec as P

CLUS_DEV = 2
LANES = 128
MARK = 2.0
BF = jnp.bfloat16
F32 = jnp.float32


def iota(shape, dim):
    return lax.broadcasted_iota(jnp.int32, shape, dim)


def matmul(a, b, contract):
    return lax.dot_general(a, b, (contract, ((), ())), preferred_element_type=F32)


def targets(ids, clusters, per_source):
    groups = ids.shape[1] // LANES
    parts = [ids[:, g * LANES : (g + 1) * LANES] for g in range(groups)]
    hot = jnp.concatenate(
        [(iota((clusters, LANES), 0) == part).astype(F32) for part in parts], axis=0
    )
    stacked = groups * clusters
    earlier = (iota((LANES, LANES), 0) < iota((LANES, LANES), 1)).astype(F32).astype(BF)
    within = matmul(hot.astype(BF), earlier, ((1,), (0,)))
    totals = jnp.broadcast_to(jnp.sum(hot, axis=1, keepdims=True), (stacked, LANES))
    a, b = iota((stacked, stacked), 0), iota((stacked, stacked), 1)
    chunks_before = ((a % clusters == b % clusters) & (b < a)).astype(F32).astype(BF)
    before = within + matmul(chunks_before, totals.astype(BF), ((1,), (0,)))
    picked = hot * before
    out = [
        jnp.sum(picked[g * clusters : (g + 1) * clusters], axis=0, keepdims=True).astype(jnp.int32)
        + parts[g] * per_source
        for g in range(groups)
    ]
    return jnp.concatenate(out, axis=1)


def pack_block(unit, tgt, dest, width):
    hit = (tgt - dest * width) == iota((width, tgt.shape[1]), 0)
    hot = hit.astype(F32)
    rows = matmul(hot.astype(BF), unit, ((1,), (0,)))
    empty = jnp.max(hot, axis=1, keepdims=True) < 0.5
    head = jnp.where(empty, F32(MARK), rows[:, :LANES])
    return head.astype(BF), rows[:, LANES:].astype(BF)


def store_blocks(unit, tgt, steps, width, outs):
    me = lax.axis_index("clus")
    for step, out in zip(steps, outs):
        head, tail = pack_block(unit, tgt, me ^ step, width)
        out[:, :LANES] = head
        out[:, LANES:] = tail


def pack_first(steps, clusters, per_source, emb, ids, unit, tgt, *outs):
    values = emb[...].astype(F32)
    scale = lax.rsqrt(jnp.sum(values * values, axis=1, keepdims=True) + 1e-6)
    unit[...] = (values * scale).astype(BF)
    tgt[...] = targets(ids[...], clusters, per_source)
    store_blocks(unit[...], tgt[...], steps, CLUS_DEV * per_source, outs)


def pack_rest(steps, per_source, unit, tgt, *outs):
    store_blocks(unit[...], tgt[...], steps, CLUS_DEV * per_source, outs)


VMEM = pl.BlockSpec(memory_space=pltpu.VMEM)


def kernel_call(kernel, shapes, inputs, name, scratch=()):
    return pl.pallas_call(
        kernel,
        out_shape=shapes,
        in_specs=[VMEM] * len(inputs),
        out_specs=[VMEM] * len(shapes),
        scratch_shapes=scratch,
        compiler_params=pltpu.CompilerParams(vmem_limit_bytes=40 * 2**20),
        cost_estimate=pl.CostEstimate(flops=1000, bytes_accessed=1000, transcendentals=0),
        name=name,
    )(*inputs)


def call_pack_first(emb, ids, steps, clusters, per_source):
    block = jax.ShapeDtypeStruct((CLUS_DEV * per_source, emb.shape[1]), BF)
    shapes = [jax.ShapeDtypeStruct(emb.shape, BF), jax.ShapeDtypeStruct(ids.shape, jnp.int32)]
    return kernel_call(
        functools.partial(pack_first, steps, clusters, per_source),
        shapes + [block] * len(steps),
        [emb, ids],
        "pack_first",
    )


def call_pack_rest(unit, tgt, steps, per_source):
    block = jax.ShapeDtypeStruct((CLUS_DEV * per_source, unit.shape[1]), BF)
    return kernel_call(
        functools.partial(pack_rest, steps, per_source),
        [block] * len(steps),
        [unit, tgt],
        "pack_rest",
    )


CHUNK = 256


def raise_best(best, keys, queries, triangular=False):
    rows = queries.shape[0]
    chunk = min(CHUNK, rows)
    for start in range(0, rows, chunk):
        count = start + chunk if triangular else keys.shape[0]
        sims = matmul(keys[:count, :], queries[start : start + chunk, :], ((1,), (1,)))
        filled = keys[:count, :LANES].astype(F32) < 1.5
        for first in range(0, chunk, LANES):
            allowed = filled
            if triangular:
                allowed = filled & (
                    iota((count, LANES), 0) < iota((count, LANES), 1) + (start + first)
                )
            part = jnp.where(allowed, sims[:, first : first + LANES], F32(-1.0))
            window = slice(start + first, start + first + LANES)
            best[:, window] = jnp.maximum(best[:, window], jnp.max(part, axis=0, keepdims=True))


def gather_group(blocks, cluster, out, me):
    per = blocks[0].shape[0] // CLUS_DEV
    for step, block in enumerate(blocks):
        place = (me & (len(blocks) - 1)) ^ step
        rows = pl.ds(pl.multiple_of(place * per, per), per)
        out[rows, :] = block[cluster * per : (cluster + 1) * per, :]


def score_pair(bests, groups, new, old, bit, me):
    later = (me & bit) == 0

    @pl.when(later)
    def _():
        raise_best(bests[new], groups[old], groups[new])

    @pl.when(jnp.logical_not(later))
    def _():
        raise_best(bests[old], groups[new], groups[old])


def own_early(split, bit, *refs):
    blocks, (send, best) = refs[:-2], refs[-2:]
    per = blocks[0].shape[0] // CLUS_DEV
    cut = split * per
    me = lax.axis_index("clus")
    best[...] = jnp.full(best.shape, -1.0, F32)
    for c in range(CLUS_DEV):
        near, far = send.at[1, c, :cut], send.at[1, c, cut:]
        gather_group(blocks[:split], c, near, me)
        gather_group(blocks[split:], c, far, me)
        rows = [best.at[c : c + 1, :cut], best.at[c : c + 1, cut:]]
        raise_best(rows[0], near, near, True)
        raise_best(rows[1], far, far, True)
        score_pair(rows, [near, far], 1, 0, bit, me)


def cross_early(send, received, before, best):
    best[...] = before[...]

    @pl.when(lax.axis_index("blk") == 1)
    def _():
        for c in range(CLUS_DEV):
            raise_best(best.at[c : c + 1], received.at[0, c], send.at[1, c])


def own_late(cuts, bits, *refs):
    send, before = refs[:2]
    blocks, (cat, best, best_late) = refs[2:-3], refs[-3:]
    me = lax.axis_index("clus")
    best[...] = before[...]
    best_late[...] = jnp.full(best_late.shape, -1.0, F32)
    for c in range(CLUS_DEV):
        late = cat.at[c]
        gather_group(blocks, c, late, me)
        groups, rows = [late], [best_late.at[c : c + 1]]
        for a, b in zip(cuts, cuts[1:]):
            groups.append(send.at[1, c, a:b])
            rows.append(best.at[c : c + 1, a:b])
        raise_best(rows[0], late, late, True)
        for i, bit in enumerate(bits):
            score_pair(rows, groups, 0, i + 1, bit, me)


def filled_queries(rows):
    ones = jnp.ones((8, LANES), BF)
    return matmul(ones, rows[:, :LANES], ((1,), (1,)))[:1] < 100.0


def cross_late(cuts, send, received, cat, before, before_late, *refs):
    others, (out, keys, best, best_late) = refs[:-4], refs[-4:]
    per = others[0].shape[0] // CLUS_DEV
    me = lax.axis_index("clus")
    best[...] = before[...]
    best_late[...] = before_late[...]

    @pl.when(lax.axis_index("blk") == 1)
    def _():
        for c in range(CLUS_DEV):
            for i, other in enumerate(others):
                keys[i * per : (i + 1) * per, :] = other[c * per : (c + 1) * per, :]
            raise_best(best.at[c : c + 1], keys, send.at[1, c])
            raise_best(best_late.at[c : c + 1], keys, cat.at[c])
            raise_best(best_late.at[c : c + 1], received.at[0, c], cat.at[c])

    for c in range(CLUS_DEV):
        parts = [
            (a, b - a, send.at[1, c, a:b], best.at[c : c + 1, a:b]) for a, b in zip(cuts, cuts[1:])
        ]
        parts.append((cuts[-1], cat.shape[1], cat.at[c], best_late.at[c : c + 1]))
        for start, count, rows, value in parts:
            sources = count // per
            base = (me ^ (start // per)) & ~(sources - 1)
            at = pl.ds(pl.multiple_of(base * per, LANES), count)
            out[c : c + 1, at] = jnp.where(filled_queries(rows), value[...], F32(0.0))


def local(embeddings, cluster_ids):
    owners = lax.axis_size("clus")
    clusters = CLUS_DEV * owners
    rows, width = embeddings.shape
    per = 2 * rows // clusters
    bits = [owners // 2, owners // 4]
    bounds = [0, owners // 2, owners // 2 + owners // 4, owners]
    cuts = [x * per for x in bounds[:3]]
    near, mid, late = [list(range(a, b)) for a, b in zip(bounds, bounds[1:])]

    def to_owner(block, step):
        return lax.ppermute(block, "clus", [(i, i ^ step) for i in range(owners)])

    unit, tgt, ahead = call_pack_first(embeddings, cluster_ids, mid[:1], clusters, per)
    sent = [to_owner(ahead, mid[0])]
    order = mid[1:] + near
    packed = dict(zip(order, call_pack_rest(unit, tgt, order, per)))
    arrived = {0: packed.pop(0), mid[0]: sent[0]}
    for step, block in packed.items():
        arrived[step] = to_owner(block, step)
    for step, block in zip(late, call_pack_rest(unit, tgt, late, per)):
        arrived[step] = to_owner(block, step)

    early = cuts[-1]
    late_rows = rows - early
    send, best = kernel_call(
        functools.partial(own_early, len(near), bits[0]),
        [
            jax.ShapeDtypeStruct((2, CLUS_DEV, early, width), BF),
            jax.ShapeDtypeStruct((CLUS_DEV, early), F32),
        ],
        [arrived[s] for s in near + mid],
        "own_early",
    )
    received = lax.all_to_all(send, "blk", split_axis=0, concat_axis=0, tiled=True)
    (best,) = kernel_call(cross_early, [best], [send, received, best], "cross_early")
    *last, best = lax.optimization_barrier((*[arrived[s] for s in late], best))
    cat, best, best_late = kernel_call(
        functools.partial(own_late, cuts, bits),
        [
            jax.ShapeDtypeStruct((CLUS_DEV, late_rows, width), BF),
            best,
            jax.ShapeDtypeStruct((CLUS_DEV, late_rows), F32),
        ],
        [send, best] + last,
        "own_late",
    )
    others = [lax.ppermute(block, "blk", [(0, 1)]) for block in last]
    (out,) = kernel_call(
        functools.partial(cross_late, cuts),
        [jax.ShapeDtypeStruct((CLUS_DEV, rows), F32)],
        [send, received, cat, best, best_late] + others,
        "cross_late",
        [
            pltpu.VMEM((late_rows, width), BF),
            pltpu.VMEM((CLUS_DEV, early), F32),
            pltpu.VMEM((CLUS_DEV, late_rows), F32),
        ],
    )
    return out


def solution(mesh):
    placed = (P(("groups", "clus", "blk"), None), P(("groups", "clus", "blk"), None))
    return jax.shard_map(
        local, mesh=mesh, in_specs=placed, out_specs=P(("groups", "clus"), "blk"), check_vma=False
    )
```

time: 146 us -> 115 us (0.79); the launches traced: 144 us -> 114 us
  waiting for transfers between devices: 105 us -> 47.1 us
  blocking collectives: 0 us -> 35.1 us
  starting transfers between devices: 14.8 us -> 9.91 us
    ppermute x7, waiting for transfers between devices: 105 us -> 46 us  [to_owner(): return lax.ppermute(block, 'clus', [(i, i ^ step) for i in range(owners)])]
    all_to_all x0 -> x1, blocking collectives: none -> 35.1 us  [local(): lax.all_to_all(send, 'blk', split_axis=0, concat_axis=0, tiled=True)]
    ppermute x4 -> x2, starting transfers between devices: 5.15 us -> 2.57 us  [local(): others = [lax.ppermute(block, 'blk', [(0, 1)]) for block in last]]
    ppermute x7, starting transfers between devices: 9.65 us -> 7.34 us  [to_owner(): return lax.ppermute(block, 'clus', [(i, i ^ step) for i in range(owners)])]
  transfers between devices with their start and end apart: 11 -> 9, of which waited for: 6 -> 6; matrix products, arithmetic and copies ran while one was open for 0% -> 0% of each run, Pallas kernels for 4% -> 8%
where the time goes in v3:
time: 115 us; the launch traced here: 114 us
  waiting for transfers between devices  47.1 us (41%)
  blocking collectives  35.1 us (31%)
  Pallas kernels  20 us (17%)
  starting transfers between devices  9.91 us (9%)
  local copies, waits for them, and re-layouts  2.28 us (2%)
    ppermute x7, waiting for transfers between devices, to_owner(): return lax.ppermute(block, 'clus', [(i, i ^ step) for i in range(owners)])  46 us
    all_to_all x1, blocking collectives, local(): lax.all_to_all(send, 'blk', split_axis=0, concat_axis=0, tiled=True)  35.1 us
    pallas_call x7, Pallas kernels, kernel_call(): pl.pallas_call(kernel, out_shape=shapes, in_specs=[VMEM] * len(inputs), o...  20 us
    ppermute x7, starting transfers between devices, to_owner(): return lax.ppermute(block, 'clus', [(i, i ^ step) for i in range(owners)])  7.34 us
    ppermute x2, starting transfers between devices, local(): others = [lax.ppermute(block, 'blk', [(0, 1)]) for block in last]  2.57 us
  transfers between devices with their start and end apart: 9, of which 6 were waited for; matrix products, arithmetic and copies ran while one was open for 0% of the time, Pallas kernels for 8%

profile of v3, /device:TPU:17, one launch (start us, length us, event | category | flops | bytes accessed | tf_op | source)
XLA Modules:
  0.0 114.5 jit_solution(6836244543297868706)
XLA Ops:
  0.0 0.0 copy-start.1
  0.0 1.6 %copy-done.1 = bf16[1024,1024]{1,0:T(8,128)(2,1)S(1)} copy-done((bf16[1024,1024]{1,0:T(8,128)(2,1)S(1)}, bf16[1024,1024]{1,0:T(8,128)(2,1)}, u32[]{:S(2)}) %copy-start.1) | copy-done | bytes 2097176
  1.6 0.0 copy-start.2
  1.6 0.7 copy-done.2
  2.3 1.5 %pack_first.1 = (bf16[1024,1024]{1,0:T(8,128)(2,1)S(1)}, s32[1,1024]{1,0:T(1,128)S(1)}, bf16[256,1024]{1,0:T(8,128)(2,1)S(1)}) custom-call(bf16[1024,1024]{1,0:T(8,128)(2,1)S(1)} %copy-done.1, s32[1,1024]{1,0:T(1,128)S(1)} %copy-done.2), custom_call_target="tpu_custom_call" | custom-call | flops 1000 | bytes 1000 | tf_op jit(solution)/shard_map/pack_first/pallas_call | solution.py:80
  3.7 3.3 %pack_rest.2 = (bf16[256,1024]{1,0:T(8,128)(2,1)S(1)}, bf16[256,1024]{1,0:T(8,128)(2,1)S(1)}, bf16[256,1024]{1,0:T(8,128)(2,1)S(1)}, bf16[256,1024]{1,0:T(8,128)(2,1)S(1)}, bf16[256,1024]{1,0:T(8,128)(2,1)S(1)}) custom-call(bf16[1024,1024]{1,0:T(8,128)(2,1)S(1)} %get-tuple-element.23.unit, s32[1,1024]{1,0:T(1,128)S(1)} %get-tuple-element.24.tgt), custom_call_target="tpu_custom_call" | custom-call | flops 1000 | bytes 1000 | tf_op jit(solution)/shard_map/pack_rest/pallas_call | solution.py:80
  7.0 1.3 %collective-permute-start = (bf16[256,1024]{1,0:T(8,128)(2,1)S(1)}, bf16[256,1024]{1,0:T(8,128)(2,1)S(1)}, u32[]{:S(2)}, u32[]{:S(2)}) collective-permute-start(bf16[256,1024]{1,0:T(8,128)(2,1)S(1)} %get-tuple-element.26), channel_id=1, source_target_pairs={{0,2},{2,0},{4,6},{6,4},{8,10},{10,8},{12,14},{14,12},{1,3},{3,1},... | collective-permute-start | bytes 1572872 | tf_op jit(solution)/shard_map/ppermute | solution.py:241
  8.3 1.3 %collective-permute-start.1 = (bf16[256,1024]{1,0:T(8,128)(2,1)S(1)}, bf16[256,1024]{1,0:T(8,128)(2,1)S(1)}, u32[]{:S(2)}, u32[]{:S(2)}) collective-permute-start(bf16[256,1024]{1,0:T(8,128)(2,1)S(1)} %get-tuple-element.27), channel_id=1, source_target_pairs={{0,4},{2,6},{4,0},{6,2},{8,12},{10,14},{12,8},{14,10},{1,5},{3,7},... | collective-permute-start | bytes 1572872 | tf_op jit(solution)/shard_map/ppermute | solution.py:241
  9.6 0.1 collective-permute-start.2
  9.7 1.0 collective-permute-start.4
  10.7 2.3 %collective-permute-start.3 = (bf16[256,1024]{1,0:T(8,128)(2,1)S(1)}, bf16[256,1024]{1,0:T(8,128)(2,1)S(1)}, u32[]{:S(2)}, u32[]{:S(2)}) collective-permute-start(bf16[256,1024]{1,0:T(8,128)(2,1)S(1)} %get-tuple-element.29), channel_id=1, source_target_pairs={{0,8},{2,10},{4,12},{6,14},{8,0},{10,2},{12,4},{14,6},{1,9},{3,11}... | collective-permute-start | bytes 1572872 | tf_op jit(solution)/shard_map/ppermute | solution.py:241
  13.0 1.4 %pack_rest.3 = (bf16[256,1024]{1,0:T(8,128)(2,1)S(1)}, bf16[256,1024]{1,0:T(8,128)(2,1)S(1)}) custom-call(bf16[1024,1024]{1,0:T(8,128)(2,1)S(1)} %get-tuple-element.23.unit, s32[1,1024]{1,0:T(1,128)S(1)} %get-tuple-element.24.tgt), custom_call_target="tpu_custom_call" | custom-call | flops 1000 | bytes 1000 | tf_op jit(solution)/shard_map/pack_rest/pallas_call | solution.py:80
  14.5 5.4 %collective-permute-done.refs_1_ = bf16[256,1024]{1,0:T(8,128)(2,1)S(1)} collective-permute-done((bf16[256,1024]{1,0:T(8,128)(2,1)S(1)}, bf16[256,1024]{1,0:T(8,128)(2,1)S(1)}, u32[]{:S(2)}, u32[]{:S(2)}) %collective-permute-start) | collective-permute-done | bytes 524320 | tf_op jit(solution)/shard_map/ppermute | solution.py:241
  19.9 0.2 collective-permute-start.5
  20.0 18.9 %collective-permute-done.1.refs_2_ = bf16[256,1024]{1,0:T(8,128)(2,1)S(1)} collective-permute-done((bf16[256,1024]{1,0:T(8,128)(2,1)S(1)}, bf16[256,1024]{1,0:T(8,128)(2,1)S(1)}, u32[]{:S(2)}, u32[]{:S(2)}) %collective-permute-start.1) | collective-permute-done | bytes 524320 | tf_op jit(solution)/shard_map/ppermute | solution.py:241
  38.9 1.1 collective-permute-start.6
  40.0 10.1 %collective-permute-done.2.refs_3_ = bf16[256,1024]{1,0:T(8,128)(2,1)S(1)} collective-permute-done((bf16[256,1024]{1,0:T(8,128)(2,1)S(1)}, bf16[256,1024]{1,0:T(8,128)(2,1)S(1)}, u32[]{:S(2)}, u32[]{:S(2)}) %collective-permute-start.2) | collective-permute-done | bytes 524320 | tf_op jit(solution)/shard_map/ppermute | solution.py:241
  50.1 0.0 collective-permute-done.4.refs_5_
  50.1 4.3 %collective-permute-done.3.refs_4_ = bf16[256,1024]{1,0:T(8,128)(2,1)S(1)} collective-permute-done((bf16[256,1024]{1,0:T(8,128)(2,1)S(1)}, bf16[256,1024]{1,0:T(8,128)(2,1)S(1)}, u32[]{:S(2)}, u32[]{:S(2)}) %collective-permute-start.3) | collective-permute-done | bytes 524320 | tf_op jit(solution)/shard_map/ppermute | solution.py:241
  54.4 2.7 %own_early.1 = (bf16[2,2,768,1024]{3,2,1,0:T(8,128)(2,1)S(1)}, f32[2,768]{1,0:T(2,128)S(1)}) custom-call(bf16[256,1024]{1,0:T(8,128)(2,1)S(1)} %get-tuple-element.25.refs_0_, bf16[256,1024]{1,0:T(8,128)(2,1)S(1)} %collective-permute-done.refs_1_, bf16[256,1024]{1,0:T(8,128)(2,1)S(1)} %collective-permute-done.1.refs_2_, ...), custom_call_target="tpu_custom_call" | custom-call | flops 1000 | bytes 1000 | tf_op jit(solution)/shard_map/own_early/pallas_call | solution.py:80
  57.1 35.1 %all_to_all.5.received = bf16[2,2,768,1024]{3,2,1,0:T(8,128)(2,1)S(1)} all-to-all(bf16[2,2,768,1024]{3,2,1,0:T(8,128)(2,1)S(1)} %get-tuple-element.31.send.refs_0_), channel_id=1, replica_groups=mesh['groups'=2,'clus'=8,'blk'=2] {'blk'}, dimensions={0} | all-to-all | bytes 12582912 | tf_op jit(solution)/shard_map/all_to_all | solution.py:264
  92.2 0.0 copy-start
  92.2 2.7 %cross_early.1.refs_1_ = f32[2,768]{1,0:T(2,128)S(1)} custom-call(bf16[2,2,768,1024]{3,2,1,0:T(8,128)(2,1)S(1)} %get-tuple-element.31.send.refs_0_, bf16[2,2,768,1024]{3,2,1,0:T(8,128)(2,1)S(1)} %all_to_all.5.received, f32[2,768]{1,0:T(2,128)S(1)} %get-tuple-element.34.before), custom_call_target="tpu_custom_call" | custom-call | flops 1000 | bytes 1000 | tf_op jit(solution)/shard_map/cross_early/pallas_call | solution.py:80
  94.9 0.0 copy-done
  94.9 0.0 collective-permute-done.5.refs_2_
  94.9 7.4 %collective-permute-done.6.refs_3_ = bf16[256,1024]{1,0:T(8,128)(2,1)S(1)} collective-permute-done((bf16[256,1024]{1,0:T(8,128)(2,1)S(1)}, bf16[256,1024]{1,0:T(8,128)(2,1)S(1)}, u32[]{:S(2)}, u32[]{:S(2)}) %collective-permute-start.6) | collective-permute-done | bytes 524320 | tf_op jit(solution)/shard_map/ppermute | solution.py:241
  102.3 1.3 %collective-permute-start.7 = (bf16[256,1024]{1,0:T(8,128)(2,1)S(1)}, bf16[256,1024]{1,0:T(8,128)(2,1)S(1)}, u32[]{:S(2)}, u32[]{:S(2)}) collective-permute-start(bf16[256,1024]{1,0:T(8,128)(2,1)S(1)} %collective-permute-done.5.refs_2_), channel_id=1, source_target_pairs={{0,1},{2,3},{4,5},{6,7},{8,9},{10,11},{12,13},{14,15},{16,17},{18,... | collective-permute-start | bytes 1572872 | tf_op jit(solution)/shard_map/ppermute | solution.py:277
  103.6 1.3 %collective-permute-start.8 = (bf16[256,1024]{1,0:T(8,128)(2,1)S(1)}, bf16[256,1024]{1,0:T(8,128)(2,1)S(1)}, u32[]{:S(2)}, u32[]{:S(2)}) collective-permute-start(bf16[256,1024]{1,0:T(8,128)(2,1)S(1)} %collective-permute-done.6.refs_3_), channel_id=1, source_target_pairs={{0,1},{2,3},{4,5},{6,7},{8,9},{10,11},{12,13},{14,15},{16,17},{18,... | collective-permute-start | bytes 1572872 | tf_op jit(solution)/shard_map/ppermute | solution.py:277
  104.9 2.6 %own_late.1 = (bf16[2,256,1024]{2,1,0:T(8,128)(2,1)S(1)}, f32[2,768]{1,0:T(2,128)S(1)}, f32[2,256]{1,0:T(2,128)S(1)}) custom-call(bf16[2,2,768,1024]{3,2,1,0:T(8,128)(2,1)S(1)} %get-tuple-element.31.send.refs_0_, f32[2,768]{1,0:T(2,128)S(1)} %cross_early.1.refs_1_, bf16[256,1024]{1,0:T(8,128)(2,1)S(1)} %collective-permute-done.5.refs_2_, ...), custom_call_target="tpu_custom_call" | custom-call | flops 1000 | bytes 1000 | tf_op jit(solution)/shard_map/own_late/pallas_call | solution.py:80
  107.5 0.0 collective-permute-done.7.refs_0_
  107.5 1.1 collective-permute-done.8.refs_1_
  108.7 5.8 %cross_late.1 = f32[2,1024]{1,0:T(2,128)} custom-call(bf16[2,2,768,1024]{3,2,1,0:T(8,128)(2,1)S(1)} %get-tuple-element.31.send.refs_0_, bf16[2,2,768,1024]{3,2,1,0:T(8,128)(2,1)} %copy-done, bf16[2,256,1024]{2,1,0:T(8,128)(2,1)S(1)} %get-tuple-element.38.cat, f32[2,768]{1,0:T(2,128)S(1)} %get-tuple-element.39.before, ...), custom_call_target="tpu_custom_call" | custom-call | flops 1000 | bytes 1000 | tf_op jit(solution)/shard_map/cross_late/pallas_call | solution.py:80
Async XLA Ops:
  0.0 1.6 %copy-start.1 = (bf16[1024,1024]{1,0:T(8,128)(2,1)S(1)}, bf16[1024,1024]{1,0:T(8,128)(2,1)}, u32[]{:S(2)}) copy-start(bf16[1024,1024]{1,0:T(8,128)(2,1)} %emb.1) | copy-start | bytes 6291460
  1.6 0.7 copy-start.2
  7.0 12.9 %collective-permute-start = (bf16[256,1024]{1,0:T(8,128)(2,1)S(1)}, bf16[256,1024]{1,0:T(8,128)(2,1)S(1)}, u32[]{:S(2)}, u32[]{:S(2)}) collective-permute-start(bf16[256,1024]{1,0:T(8,128)(2,1)S(1)} %get-tuple-element.26), channel_id=1, source_target_pairs={{0,2},{2,0},{4,6},{6,4},{8,10},{10,8},{12,14},{14,12},{1,3},{3,1},... | collective-permute-start | bytes 1572872 | tf_op jit(solution)/shard_map/ppermute | solution.py:241
  8.3 30.6 %collective-permute-start.1 = (bf16[256,1024]{1,0:T(8,128)(2,1)S(1)}, bf16[256,1024]{1,0:T(8,128)(2,1)S(1)}, u32[]{:S(2)}, u32[]{:S(2)}) collective-permute-start(bf16[256,1024]{1,0:T(8,128)(2,1)S(1)} %get-tuple-element.27), channel_id=1, source_target_pairs={{0,4},{2,6},{4,0},{6,2},{8,12},{10,14},{12,8},{14,10},{1,5},{3,7},... | collective-permute-start | bytes 1572872 | tf_op jit(solution)/shard_map/ppermute | solution.py:241
  9.6 40.5 %collective-permute-start.2 = (bf16[256,1024]{1,0:T(8,128)(2,1)S(1)}, bf16[256,1024]{1,0:T(8,128)(2,1)S(1)}, u32[]{:S(2)}, u32[]{:S(2)}) collective-permute-start(bf16[256,1024]{1,0:T(8,128)(2,1)S(1)} %get-tuple-element.28), channel_id=1, source_target_pairs={{0,6},{2,4},{4,2},{6,0},{8,14},{10,12},{12,10},{14,8},{1,7},{3,5},... | collective-permute-start | bytes 1572872 | tf_op jit(solution)/shard_map/ppermute | solution.py:241
  9.7 40.4 %collective-permute-start.4 = (bf16[256,1024]{1,0:T(8,128)(2,1)S(1)}, bf16[256,1024]{1,0:T(8,128)(2,1)S(1)}, u32[]{:S(2)}, u32[]{:S(2)}) collective-permute-start(bf16[256,1024]{1,0:T(8,128)(2,1)S(1)} %get-tuple-element.30), channel_id=1, source_target_pairs={{0,10},{2,8},{4,14},{6,12},{8,2},{10,0},{12,6},{14,4},{1,11},{3,9}... | collective-permute-start | bytes 1572872 | tf_op jit(solution)/shard_map/ppermute | solution.py:241
  10.7 43.7 %collective-permute-start.3 = (bf16[256,1024]{1,0:T(8,128)(2,1)S(1)}, bf16[256,1024]{1,0:T(8,128)(2,1)S(1)}, u32[]{:S(2)}, u32[]{:S(2)}) collective-permute-start(bf16[256,1024]{1,0:T(8,128)(2,1)S(1)} %get-tuple-element.29), channel_id=1, source_target_pairs={{0,8},{2,10},{4,12},{6,14},{8,0},{10,2},{12,4},{14,6},{1,9},{3,11}... | collective-permute-start | bytes 1572872 | tf_op jit(solution)/shard_map/ppermute | solution.py:241
  19.9 75.0 %collective-permute-start.5 = (bf16[256,1024]{1,0:T(8,128)(2,1)S(1)}, bf16[256,1024]{1,0:T(8,128)(2,1)S(1)}, u32[]{:S(2)}, u32[]{:S(2)}) collective-permute-start(bf16[256,1024]{1,0:T(8,128)(2,1)S(1)} %get-tuple-element.32), channel_id=1, source_target_pairs={{0,12},{2,14},{4,8},{6,10},{8,4},{10,6},{12,0},{14,2},{1,13},{3,15... | collective-permute-start | bytes 1572872 | tf_op jit(solution)/shard_map/ppermute | solution.py:241
  38.9 63.4 %collective-permute-start.6 = (bf16[256,1024]{1,0:T(8,128)(2,1)S(1)}, bf16[256,1024]{1,0:T(8,128)(2,1)S(1)}, u32[]{:S(2)}, u32[]{:S(2)}) collective-permute-start(bf16[256,1024]{1,0:T(8,128)(2,1)S(1)} %get-tuple-element.33), channel_id=1, source_target_pairs={{0,14},{2,12},{4,10},{6,8},{8,6},{10,4},{12,2},{14,0},{1,15},{3,13... | collective-permute-start | bytes 1572872 | tf_op jit(solution)/shard_map/ppermute | solution.py:241
  92.2 2.7 %copy-start = (bf16[2,2,768,1024]{3,2,1,0:T(8,128)(2,1)}, bf16[2,2,768,1024]{3,2,1,0:T(8,128)(2,1)S(1)}, u32[]{:S(2)}) copy-start(bf16[2,2,768,1024]{3,2,1,0:T(8,128)(2,1)S(1)} %all_to_all.5.received) | copy-start | bytes 18874372
  102.3 5.2 %collective-permute-start.7 = (bf16[256,1024]{1,0:T(8,128)(2,1)S(1)}, bf16[256,1024]{1,0:T(8,128)(2,1)S(1)}, u32[]{:S(2)}, u32[]{:S(2)}) collective-permute-start(bf16[256,1024]{1,0:T(8,128)(2,1)S(1)} %collective-permute-done.5.refs_2_), channel_id=1, source_target_pairs={{0,1},{2,3},{4,5},{6,7},{8,9},{10,11},{12,13},{14,15},{16,17},{18,... | collective-permute-start | bytes 1572872 | tf_op jit(solution)/shard_map/ppermute | solution.py:277
  103.6 5.1 %collective-permute-start.8 = (bf16[256,1024]{1,0:T(8,128)(2,1)S(1)}, bf16[256,1024]{1,0:T(8,128)(2,1)S(1)}, u32[]{:S(2)}, u32[]{:S(2)}) collective-permute-start(bf16[256,1024]{1,0:T(8,128)(2,1)S(1)} %collective-permute-done.6.refs_3_), channel_id=1, source_target_pairs={{0,1},{2,3},{4,5},{6,7},{8,9},{10,11},{12,13},{14,15},{16,17},{18,... | collective-permute-start | bytes 1572872 | tf_op jit(solution)/shard_map/ppermute | solution.py:277

commit v4 on v3

--- a/solution.py
+++ b/solution.py
@@ -83,7 +83,7 @@
         in_specs=[VMEM] * len(inputs),
         out_specs=[VMEM] * len(shapes),
         scratch_shapes=scratch,
-        compiler_params=pltpu.CompilerParams(vmem_limit_bytes=40 * 2**20),
+        compiler_params=pltpu.CompilerParams(vmem_limit_bytes=20 * 2**20),
         cost_estimate=pl.CostEstimate(flops=1000, bytes_accessed=1000, transcendentals=0),
         name=name,
     )(*inputs)
@@ -115,8 +115,8 @@
 
 def raise_best(best, keys, queries, triangular=False):
     rows = queries.shape[0]
-    chunk = min(CHUNK, rows)
-    for start in range(0, rows, chunk):
+    for start in range(0, rows, CHUNK):
+        chunk = min(CHUNK, rows - start)
         count = start + chunk if triangular else keys.shape[0]
         sims = matmul(keys[:count, :], queries[start : start + chunk, :], ((1,), (1,)))
         filled = keys[:count, :LANES].astype(F32) < 1.5
@@ -151,47 +151,54 @@
         raise_best(bests[old], groups[new], groups[old])
 
 
-def own_early(split, bit, *refs):
-    blocks, (send, best) = refs[:-2], refs[-2:]
+def own_stage(cuts, bits, held, first, *refs):
+    stages, refs = refs[:held], refs[held:]
+    blocks, (send, best) = list(refs[:-2]), refs[-2:]
+    before = blocks.pop(0) if held else None
     per = blocks[0].shape[0] // CLUS_DEV
-    cut = split * per
     me = lax.axis_index("clus")
-    best[...] = jnp.full(best.shape, -1.0, F32)
+    core = lax.axis_index("blk")
+    spans = list(zip(cuts, cuts[1:]))
+    base = spans[first][0]
+    if held:
+        best[:, :base] = before[:, :base]
+    best[:, base:] = jnp.full((CLUS_DEV, best.shape[1] - base), -1.0, F32)
     for c in range(CLUS_DEV):
-        near, far = send.at[1, c, :cut], send.at[1, c, cut:]
-        gather_group(blocks[:split], c, near, me)
-        gather_group(blocks[split:], c, far, me)
-        rows = [best.at[c : c + 1, :cut], best.at[c : c + 1, cut:]]
-        raise_best(rows[0], near, near, True)
-        raise_best(rows[1], far, far, True)
-        score_pair(rows, [near, far], 1, 0, bit, me)
-
-
-def cross_early(send, received, before, best):
+        rows = [best.at[c : c + 1, a:b] for a, b in spans]
+        groups = []
+        for stage in stages:
+            start = spans[len(groups)][0]
+            end = start + stage.shape[2]
+            while len(groups) < first and spans[len(groups)][0] < end:
+                a, b = spans[len(groups)]
+                groups.append(stage.at[core, c, a - start : b - start])
+        for i in range(first, len(spans)):
+            a, b = spans[i]
+            group = send.at[1, c, a - base : b - base]
+            gather_group(blocks[(a - base) // per : (b - base) // per], c, group, me)
+            groups.append(group)
+            raise_best(rows[i], group, group, True)
+            for j in range(i):
+                score_pair(rows, groups, i, j, bits[j], me)
+        send[0, c] = send[1, c]
+
+
+def cross_stage(cuts, held, *refs):
+    stages, before, best = refs[: held + 1], refs[held + 1], refs[held + 2]
     best[...] = before[...]
 
     @pl.when(lax.axis_index("blk") == 1)
     def _():
+        new = stages[-1]
         for c in range(CLUS_DEV):
-            raise_best(best.at[c : c + 1], received.at[0, c], send.at[1, c])
-
-
-def own_late(cuts, bits, *refs):
-    send, before = refs[:2]
-    blocks, (cat, best, best_late) = refs[2:-3], refs[-3:]
-    me = lax.axis_index("clus")
-    best[...] = before[...]
-    best_late[...] = jnp.full(best_late.shape, -1.0, F32)
-    for c in range(CLUS_DEV):
-        late = cat.at[c]
-        gather_group(blocks, c, late, me)
-        groups, rows = [late], [best_late.at[c : c + 1]]
-        for a, b in zip(cuts, cuts[1:]):
-            groups.append(send.at[1, c, a:b])
-            rows.append(best.at[c : c + 1, a:b])
-        raise_best(rows[0], late, late, True)
-        for i, bit in enumerate(bits):
-            score_pair(rows, groups, 0, i + 1, bit, me)
+            base = 0
+            for stage in stages:
+                end = base + stage.shape[2]
+                raise_best(best.at[c : c + 1, base:end], new.at[0, c], stage.at[1, c])
+                base = end
+            start = base - new.shape[2]
+            for stage in stages[:-1]:
+                raise_best(best.at[c : c + 1, start:base], stage.at[0, c], new.at[1, c])
 
 
 def filled_queries(rows):
@@ -199,32 +206,40 @@
     return matmul(ones, rows[:, :LANES], ((1,), (1,)))[:1] < 100.0
 
 
-def cross_late(cuts, send, received, cat, before, before_late, *refs):
-    others, (out, keys, best, best_late) = refs[:-4], refs[-4:]
+def cross_last(cuts, held, *refs):
+    stages, (send, before), refs = refs[:held], refs[held : held + 2], refs[held + 2 :]
+    others, (out, keys, best) = refs[:-3], refs[-3:]
     per = others[0].shape[0] // CLUS_DEV
     me = lax.axis_index("clus")
+    core = lax.axis_index("blk")
     best[...] = before[...]
-    best_late[...] = before_late[...]
-
-    @pl.when(lax.axis_index("blk") == 1)
+    start = best.shape[1] - send.shape[2]
+
+    @pl.when(core == 1)
     def _():
         for c in range(CLUS_DEV):
             for i, other in enumerate(others):
                 keys[i * per : (i + 1) * per, :] = other[c * per : (c + 1) * per, :]
-            raise_best(best.at[c : c + 1], keys, send.at[1, c])
-            raise_best(best_late.at[c : c + 1], keys, cat.at[c])
-            raise_best(best_late.at[c : c + 1], received.at[0, c], cat.at[c])
+            base = 0
+            for stage in stages:
+                end = base + stage.shape[2]
+                raise_best(best.at[c : c + 1, base:end], keys, stage.at[1, c])
+                raise_best(best.at[c : c + 1, start:], stage.at[0, c], send.at[1, c])
+                base = end
+            raise_best(best.at[c : c + 1, start:], keys, send.at[1, c])
 
     for c in range(CLUS_DEV):
-        parts = [
-            (a, b - a, send.at[1, c, a:b], best.at[c : c + 1, a:b]) for a, b in zip(cuts, cuts[1:])
-        ]
-        parts.append((cuts[-1], cat.shape[1], cat.at[c], best_late.at[c : c + 1]))
-        for start, count, rows, value in parts:
-            sources = count // per
-            base = (me ^ (start // per)) & ~(sources - 1)
-            at = pl.ds(pl.multiple_of(base * per, LANES), count)
-            out[c : c + 1, at] = jnp.where(filled_queries(rows), value[...], F32(0.0))
+        whole = [(stage.shape[2], stage.at[core, c]) for stage in stages]
+        whole.append((send.shape[2], send.at[1, c]))
+        base = 0
+        for size, rows in whole:
+            kept = jnp.where(filled_queries(rows), best[c : c + 1, base : base + size], F32(0.0))
+            for a, b in zip(cuts, cuts[1:]):
+                if base <= a < base + size:
+                    place = (me ^ (a // per)) & ~((b - a) // per - 1)
+                    at = pl.ds(pl.multiple_of(place * per, LANES), b - a)
+                    out[c : c + 1, at] = kept[:, a - base : b - base]
+            base += size
 
 
 def local(embeddings, cluster_ids):
@@ -232,59 +247,65 @@
     clusters = CLUS_DEV * owners
     rows, width = embeddings.shape
     per = 2 * rows // clusters
-    bits = [owners // 2, owners // 4]
-    bounds = [0, owners // 2, owners // 2 + owners // 4, owners]
-    cuts = [x * per for x in bounds[:3]]
-    near, mid, late = [list(range(a, b)) for a, b in zip(bounds, bounds[1:])]
+    bits = [owners // 2, owners // 4, owners // 8]
+    bounds = [0, owners // 2, owners // 2 + owners // 4, owners - owners // 8, owners]
+    cuts = [x * per for x in bounds]
+    near, far1, far2, far3 = [list(range(a, b)) for a, b in zip(bounds, bounds[1:])]
+    best_shape = jax.ShapeDtypeStruct((CLUS_DEV, rows), F32)
 
     def to_owner(block, step):
         return lax.ppermute(block, "clus", [(i, i ^ step) for i in range(owners)])
 
-    unit, tgt, ahead = call_pack_first(embeddings, cluster_ids, mid[:1], clusters, per)
-    sent = [to_owner(ahead, mid[0])]
-    order = mid[1:] + near
-    packed = dict(zip(order, call_pack_rest(unit, tgt, order, per)))
-    arrived = {0: packed.pop(0), mid[0]: sent[0]}
-    for step, block in packed.items():
-        arrived[step] = to_owner(block, step)
-    for step, block in zip(late, call_pack_rest(unit, tgt, late, per)):
-        arrived[step] = to_owner(block, step)
-
-    early = cuts[-1]
-    late_rows = rows - early
+    def stage_shape(sources):
+        return jax.ShapeDtypeStruct((2, CLUS_DEV, sources * per, width), BF)
+
+    def to_both(send):
+        return lax.all_to_all(send, "blk", split_axis=0, concat_axis=0, tiled=True)
+
+    arrived = {}
+    lead = near[1 : 1 + len(far2) + len(far3)]
+    unit, tgt, *packed = call_pack_first(embeddings, cluster_ids, lead, clusters, per)
+    for steps in (far1, near[len(lead) + 1 :] + [0], far2 + far3, []):
+        for step, block in zip(lead, packed):
+            arrived[step] = to_owner(block, step) if step else block
+        lead, packed = steps, call_pack_rest(unit, tgt, steps, per) if steps else []
+
+    early = near + far1
     send, best = kernel_call(
-        functools.partial(own_early, len(near), bits[0]),
-        [
-            jax.ShapeDtypeStruct((2, CLUS_DEV, early, width), BF),
-            jax.ShapeDtypeStruct((CLUS_DEV, early), F32),
-        ],
-        [arrived[s] for s in near + mid],
+        functools.partial(own_stage, cuts[:3], bits, 0, 0),
+        [stage_shape(len(early)), best_shape],
+        [arrived[s] for s in early],
         "own_early",
     )
-    received = lax.all_to_all(send, "blk", split_axis=0, concat_axis=0, tiled=True)
-    (best,) = kernel_call(cross_early, [best], [send, received, best], "cross_early")
-    *last, best = lax.optimization_barrier((*[arrived[s] for s in late], best))
-    cat, best, best_late = kernel_call(
-        functools.partial(own_late, cuts, bits),
-        [
-            jax.ShapeDtypeStruct((CLUS_DEV, late_rows, width), BF),
-            best,
-            jax.ShapeDtypeStruct((CLUS_DEV, late_rows), F32),
-        ],
-        [send, best] + last,
-        "own_late",
-    )
-    others = [lax.ppermute(block, "blk", [(0, 1)]) for block in last]
+    stages = [to_both(send)]
+    (best,) = kernel_call(
+        functools.partial(cross_stage, cuts, 0), [best_shape], stages + [best], "cross_early"
+    )
+    *new, best = lax.optimization_barrier((*[arrived[s] for s in far2], best))
+    send, best = kernel_call(
+        functools.partial(own_stage, cuts[:4], bits, 1, 2),
+        [stage_shape(len(far2)), best_shape],
+        stages + [best] + new,
+        "own_middle",
+    )
+    stages.append(to_both(send))
+    (best,) = kernel_call(
+        functools.partial(cross_stage, cuts, 1), [best_shape], stages + [best], "cross_middle"
+    )
+    *new, best = lax.optimization_barrier((*[arrived[s] for s in far3], best))
+    send, best = kernel_call(
+        functools.partial(own_stage, cuts, bits, 2, 3),
+        [stage_shape(len(far3)), best_shape],
+        stages + [best] + new,
+        "own_last",
+    )
+    others = [lax.ppermute(block, "blk", [(0, 1)]) for block in new]
     (out,) = kernel_call(
-        functools.partial(cross_late, cuts),
-        [jax.ShapeDtypeStruct((CLUS_DEV, rows), F32)],
-        [send, received, cat, best, best_late] + others,
-        "cross_late",
-        [
-            pltpu.VMEM((late_rows, width), BF),
-            pltpu.VMEM((CLUS_DEV, early), F32),
-            pltpu.VMEM((CLUS_DEV, late_rows), F32),
-        ],
+        functools.partial(cross_last, cuts, 2),
+        [best_shape],
+        stages + [send, best] + others,
+        "cross_last",
+        [pltpu.VMEM((len(far3) * per, width), BF), pltpu.VMEM((CLUS_DEV, rows), F32)],
     )
     return out
 

time: 115 us -> 112 us (0.974)
  the two profiles are of different devices: /device:TPU:17 before, /device:TPU:1 now
where the time goes in v4:
time: 112 us
  blocking collectives  37.5 us (33%)
  waiting for transfers between devices  36.5 us (33%)
  Pallas kernels  22.1 us (20%)
  starting transfers between devices  13.7 us (12%)
  local copies, waits for them, and re-layouts  2.28 us (2%)
    all_to_all x2, blocking collectives, to_both(): return lax.all_to_all(send, 'blk', split_axis=0, concat_axis=0, tiled=True)  37.5 us
    ppermute x7, waiting for transfers between devices, to_owner(): return lax.ppermute(block, 'clus', [(i, i ^ step) for i in range(owners)])  36.5 us
    pallas_call x10, Pallas kernels, kernel_call(): pl.pallas_call(kernel, out_shape=shapes, in_specs=[VMEM] * len(inputs), o...  22.1 us
    ppermute x7, starting transfers between devices, to_owner(): return lax.ppermute(block, 'clus', [(i, i ^ step) for i in range(owners)])  12.4 us
    unnamed x4, local copies, waits for them, and re-layouts  2.28 us
  transfers between devices with their start and end apart: 8, of which 3 were waited for; matrix products, arithmetic and copies ran while one was open for 0% of the time, Pallas kernels for 15%

profile of v4, /device:TPU:1, one launch (start us, length us, event | category | flops | bytes accessed | tf_op | source)
XLA Modules:
  0.0 112.1 jit_solution(3282228542018642230)
XLA Ops:
  0.0 0.0 copy-start
  0.0 1.6 %copy-done = bf16[1024,1024]{1,0:T(8,128)(2,1)S(1)} copy-done((bf16[1024,1024]{1,0:T(8,128)(2,1)S(1)}, bf16[1024,1024]{1,0:T(8,128)(2,1)}, u32[]{:S(2)}) %copy-start) | copy-done | bytes 2097176
  1.6 0.0 copy-start.1
  1.6 0.7 copy-done.1
  2.3 2.1 %pack_first.1 = (bf16[1024,1024]{1,0:T(8,128)(2,1)S(1)}, s32[1,1024]{1,0:T(1,128)S(1)}, bf16[256,1024]{1,0:T(8,128)(2,1)S(1)}, bf16[256,1024]{1,0:T(8,128)(2,1)S(1)}) custom-call(bf16[1024,1024]{1,0:T(8,128)(2,1)S(1)} %copy-done, s32[1,1024]{1,0:T(1,128)S(1)} %copy-done.1), custom_call_target="tpu_custom_call" | custom-call | flops 1000 | bytes 1000 | tf_op jit(solution)/shard_map/pack_first/pallas_call | solution.py:80
  4.4 2.1 %collective-permute-start = (bf16[256,1024]{1,0:T(8,128)(2,1)S(1)}, bf16[256,1024]{1,0:T(8,128)(2,1)S(1)}, u32[]{:S(2)}, u32[]{:S(2)}) collective-permute-start(bf16[256,1024]{1,0:T(8,128)(2,1)S(1)} %get-tuple-element.28), channel_id=1, source_target_pairs={{0,2},{2,0},{4,6},{6,4},{8,10},{10,8},{12,14},{14,12},{1,3},{3,1},... | collective-permute-start | bytes 1572872 | tf_op jit(solution)/shard_map/ppermute | solution.py:257
  6.5 1.3 %collective-permute-start.1 = (bf16[256,1024]{1,0:T(8,128)(2,1)S(1)}, bf16[256,1024]{1,0:T(8,128)(2,1)S(1)}, u32[]{:S(2)}, u32[]{:S(2)}) collective-permute-start(bf16[256,1024]{1,0:T(8,128)(2,1)S(1)} %get-tuple-element.29), channel_id=1, source_target_pairs={{0,4},{2,6},{4,0},{6,2},{8,12},{10,14},{12,8},{14,10},{1,5},{3,7},... | collective-permute-start | bytes 1572872 | tf_op jit(solution)/shard_map/ppermute | solution.py:257
  7.8 1.4 %pack_rest.4 = (bf16[256,1024]{1,0:T(8,128)(2,1)S(1)}, bf16[256,1024]{1,0:T(8,128)(2,1)S(1)}) custom-call(bf16[1024,1024]{1,0:T(8,128)(2,1)S(1)} %get-tuple-element.25.unit, s32[1,1024]{1,0:T(1,128)S(1)} %get-tuple-element.26.tgt), custom_call_target="tpu_custom_call" | custom-call | flops 1000 | bytes 1000 | tf_op jit(solution)/shard_map/pack_rest/pallas_call | solution.py:80
  9.3 2.4 %collective-permute-start.3 = (bf16[256,1024]{1,0:T(8,128)(2,1)S(1)}, bf16[256,1024]{1,0:T(8,128)(2,1)S(1)}, u32[]{:S(2)}, u32[]{:S(2)}) collective-permute-start(bf16[256,1024]{1,0:T(8,128)(2,1)S(1)} %get-tuple-element.31), channel_id=1, source_target_pairs={{0,8},{2,10},{4,12},{6,14},{8,0},{10,2},{12,4},{14,6},{1,9},{3,11}... | collective-permute-start | bytes 1572872 | tf_op jit(solution)/shard_map/ppermute | solution.py:257
  11.7 0.0 collective-permute-start.4
  11.7 1.4 %pack_rest.3 = (bf16[256,1024]{1,0:T(8,128)(2,1)S(1)}, bf16[256,1024]{1,0:T(8,128)(2,1)S(1)}) custom-call(bf16[1024,1024]{1,0:T(8,128)(2,1)S(1)} %get-tuple-element.25.unit, s32[1,1024]{1,0:T(1,128)S(1)} %get-tuple-element.26.tgt), custom_call_target="tpu_custom_call" | custom-call | flops 1000 | bytes 1000 | tf_op jit(solution)/shard_map/pack_rest/pallas_call | solution.py:80
  13.1 1.2 %collective-permute-start.2 = (bf16[256,1024]{1,0:T(8,128)(2,1)S(1)}, bf16[256,1024]{1,0:T(8,128)(2,1)S(1)}, u32[]{:S(2)}, u32[]{:S(2)}) collective-permute-start(bf16[256,1024]{1,0:T(8,128)(2,1)S(1)} %get-tuple-element.30), channel_id=1, source_target_pairs={{0,6},{2,4},{4,2},{6,0},{8,14},{10,12},{12,10},{14,8},{1,7},{3,5},... | collective-permute-start | bytes 1572872 | tf_op jit(solution)/shard_map/ppermute | solution.py:257
  14.3 1.4 %pack_rest.5 = (bf16[256,1024]{1,0:T(8,128)(2,1)S(1)}, bf16[256,1024]{1,0:T(8,128)(2,1)S(1)}) custom-call(bf16[1024,1024]{1,0:T(8,128)(2,1)S(1)} %get-tuple-element.25.unit, s32[1,1024]{1,0:T(1,128)S(1)} %get-tuple-element.26.tgt), custom_call_target="tpu_custom_call" | custom-call | flops 1000 | bytes 1000 | tf_op jit(solution)/shard_map/pack_rest/pallas_call | solution.py:80
  15.7 2.5 %collective-permute-done.refs_1_ = bf16[256,1024]{1,0:T(8,128)(2,1)S(1)} collective-permute-done((bf16[256,1024]{1,0:T(8,128)(2,1)S(1)}, bf16[256,1024]{1,0:T(8,128)(2,1)S(1)}, u32[]{:S(2)}, u32[]{:S(2)}) %collective-permute-start) | collective-permute-done | bytes 524320 | tf_op jit(solution)/shard_map/ppermute | solution.py:257
  18.2 3.2 %collective-permute-start.5 = (bf16[256,1024]{1,0:T(8,128)(2,1)S(1)}, bf16[256,1024]{1,0:T(8,128)(2,1)S(1)}, u32[]{:S(2)}, u32[]{:S(2)}) collective-permute-start(bf16[256,1024]{1,0:T(8,128)(2,1)S(1)} %get-tuple-element.34), channel_id=1, source_target_pairs={{0,12},{2,14},{4,8},{6,10},{8,4},{10,6},{12,0},{14,2},{1,13},{3,15... | collective-permute-start | bytes 1572872 | tf_op jit(solution)/shard_map/ppermute | solution.py:257
  21.4 7.2 %collective-permute-done.1.refs_2_ = bf16[256,1024]{1,0:T(8,128)(2,1)S(1)} collective-permute-done((bf16[256,1024]{1,0:T(8,128)(2,1)S(1)}, bf16[256,1024]{1,0:T(8,128)(2,1)S(1)}, u32[]{:S(2)}, u32[]{:S(2)}) %collective-permute-start.1) | collective-permute-done | bytes 524320 | tf_op jit(solution)/shard_map/ppermute | solution.py:257
  28.6 2.1 %collective-permute-start.6 = (bf16[256,1024]{1,0:T(8,128)(2,1)S(1)}, bf16[256,1024]{1,0:T(8,128)(2,1)S(1)}, u32[]{:S(2)}, u32[]{:S(2)}) collective-permute-start(bf16[256,1024]{1,0:T(8,128)(2,1)S(1)} %get-tuple-element.39), channel_id=1, source_target_pairs={{0,14},{2,12},{4,10},{6,8},{8,6},{10,4},{12,2},{14,0},{1,15},{3,13... | collective-permute-start | bytes 1572872 | tf_op jit(solution)/shard_map/ppermute | solution.py:257
  30.8 0.0 collective-permute-done.3.refs_4_
  30.8 26.8 %collective-permute-done.4.refs_5_ = bf16[256,1024]{1,0:T(8,128)(2,1)S(1)} collective-permute-done((bf16[256,1024]{1,0:T(8,128)(2,1)S(1)}, bf16[256,1024]{1,0:T(8,128)(2,1)S(1)}, u32[]{:S(2)}, u32[]{:S(2)}) %collective-permute-start.4) | collective-permute-done | bytes 524320 | tf_op jit(solution)/shard_map/ppermute | solution.py:257
  57.6 0.0 collective-permute-done.2.refs_3_
  57.6 3.0 %own_early.1 = (bf16[2,2,768,1024]{3,2,1,0:T(8,128)(2,1)S(1)}, f32[2,1024]{1,0:T(2,128)S(1)}) custom-call(bf16[256,1024]{1,0:T(8,128)(2,1)S(1)} %get-tuple-element.27.refs_0_, bf16[256,1024]{1,0:T(8,128)(2,1)S(1)} %collective-permute-done.refs_1_, bf16[256,1024]{1,0:T(8,128)(2,1)S(1)} %collective-permute-done.1.refs_2_, ...), custom_call_target="tpu_custom_call" | custom-call | flops 1000 | bytes 1000 | tf_op jit(solution)/shard_map/own_early/pallas_call | solution.py:80
  60.6 33.3 %all_to_all.10.refs_0_ = bf16[2,2,768,1024]{3,2,1,0:T(8,128)(2,1)S(1)} all-to-all(bf16[2,2,768,1024]{3,2,1,0:T(8,128)(2,1)S(1)} %get-tuple-element.33), channel_id=1, replica_groups=mesh['groups'=2,'clus'=8,'blk'=2] {'blk'}, dimensions={0} | all-to-all | bytes 12582912 | tf_op jit(solution)/shard_map/all_to_all | solution.py:263
  93.9 2.7 %cross_early.1.refs_1_ = f32[2,1024]{1,0:T(2,128)S(1)} custom-call(bf16[2,2,768,1024]{3,2,1,0:T(8,128)(2,1)S(1)} %all_to_all.10.refs_0_, f32[2,1024]{1,0:T(2,128)S(1)} %get-tuple-element.35.refs_1_), custom_call_target="tpu_custom_call" | custom-call | flops 1000 | bytes 1000 | tf_op jit(solution)/shard_map/cross_early/pallas_call | solution.py:80
  96.6 0.0 collective-permute-done.5.refs_2_
  96.6 2.2 %own_middle.1 = (bf16[2,2,128,1024]{3,2,1,0:T(8,128)(2,1)S(1)}, f32[2,1024]{1,0:T(2,128)S(1)}) custom-call(bf16[2,2,768,1024]{3,2,1,0:T(8,128)(2,1)S(1)} %all_to_all.10.refs_0_, f32[2,1024]{1,0:T(2,128)S(1)} %cross_early.1.refs_1_, bf16[256,1024]{1,0:T(8,128)(2,1)S(1)} %collective-permute-done.5.refs_2_), custom_call_target="tpu_custom_call" | custom-call | flops 1000 | bytes 1000 | tf_op jit(solution)/shard_map/own_middle/pallas_call | solution.py:80
  98.8 4.2 %all_to_all.11.refs_1_ = bf16[2,2,128,1024]{3,2,1,0:T(8,128)(2,1)S(1)} all-to-all(bf16[2,2,128,1024]{3,2,1,0:T(8,128)(2,1)S(1)} %get-tuple-element.38), channel_id=1, replica_groups=mesh['groups'=2,'clus'=8,'blk'=2] {'blk'}, dimensions={0} | all-to-all | bytes 2097152 | tf_op jit(solution)/shard_map/all_to_all | solution.py:263
  103.0 2.0 %cross_middle.1.refs_2_ = f32[2,1024]{1,0:T(2,128)S(1)} custom-call(bf16[2,2,768,1024]{3,2,1,0:T(8,128)(2,1)S(1)} %all_to_all.10.refs_0_, bf16[2,2,128,1024]{3,2,1,0:T(8,128)(2,1)S(1)} %all_to_all.11.refs_1_, f32[2,1024]{1,0:T(2,128)S(1)} %get-tuple-element.40.refs_2_), custom_call_target="tpu_custom_call" | custom-call | flops 1000 | bytes 1000 | tf_op jit(solution)/shard_map/cross_middle/pallas_call | solution.py:80
  105.0 0.0 collective-permute-done.6.refs_3_
  105.0 1.3 %collective-permute-start.7 = (bf16[256,1024]{1,0:T(8,128)(2,1)S(1)}, bf16[256,1024]{1,0:T(8,128)(2,1)S(1)}, u32[]{:S(2)}, u32[]{:S(2)}) collective-permute-start(bf16[256,1024]{1,0:T(8,128)(2,1)S(1)} %collective-permute-done.6.refs_3_), channel_id=1, source_target_pairs={{0,1},{2,3},{4,5},{6,7},{8,9},{10,11},{12,13},{14,15},{16,17},{18,... | collective-permute-start | bytes 1572872 | tf_op jit(solution)/shard_map/ppermute | solution.py:302
  106.3 2.5 %own_last.1 = (bf16[2,2,128,1024]{3,2,1,0:T(8,128)(2,1)S(1)}, f32[2,1024]{1,0:T(2,128)S(1)}) custom-call(bf16[2,2,768,1024]{3,2,1,0:T(8,128)(2,1)S(1)} %all_to_all.10.refs_0_, bf16[2,2,128,1024]{3,2,1,0:T(8,128)(2,1)S(1)} %all_to_all.11.refs_1_, f32[2,1024]{1,0:T(2,128)S(1)} %cross_middle.1.refs_2_, bf16[256,1024]{1,0:T(8,128)(2,1)S(1)} %collective-permute-done.6.refs_3_), custom_call_target="tpu_custom_call" | custom-call | flops 1000 | bytes 1000 | tf_op jit(solution)/shard_map/own_last/pallas_call | solution.py:80
  108.9 0.0 collective-permute-done.7.refs_4_
  108.9 3.2 %cross_last.1 = f32[2,1024]{1,0:T(2,128)} custom-call(bf16[2,2,768,1024]{3,2,1,0:T(8,128)(2,1)S(1)} %all_to_all.10.refs_0_, bf16[2,2,128,1024]{3,2,1,0:T(8,128)(2,1)S(1)} %all_to_all.11.refs_1_, bf16[2,2,128,1024]{3,2,1,0:T(8,128)(2,1)S(1)} %get-tuple-element.43.refs_2_, f32[2,1024]{1,0:T(2,128)S(1)} %get-tuple-element.44.refs_3_, ...), custom_call_target="tpu_custom_call" | custom-call | flops 1000 | bytes 1000 | tf_op jit(solution)/shard_map/cross_last/pallas_call | solution.py:80
Async XLA Ops:
  0.0 1.6 %copy-start = (bf16[1024,1024]{1,0:T(8,128)(2,1)S(1)}, bf16[1024,1024]{1,0:T(8,128)(2,1)}, u32[]{:S(2)}) copy-start(bf16[1024,1024]{1,0:T(8,128)(2,1)} %emb.1) | copy-start | bytes 6291460
  1.6 0.7 copy-start.1
  4.4 13.8 %collective-permute-start = (bf16[256,1024]{1,0:T(8,128)(2,1)S(1)}, bf16[256,1024]{1,0:T(8,128)(2,1)S(1)}, u32[]{:S(2)}, u32[]{:S(2)}) collective-permute-start(bf16[256,1024]{1,0:T(8,128)(2,1)S(1)} %get-tuple-element.28), channel_id=1, source_target_pairs={{0,2},{2,0},{4,6},{6,4},{8,10},{10,8},{12,14},{14,12},{1,3},{3,1},... | collective-permute-start | bytes 1572872 | tf_op jit(solution)/shard_map/ppermute | solution.py:257
  6.5 22.1 %collective-permute-start.1 = (bf16[256,1024]{1,0:T(8,128)(2,1)S(1)}, bf16[256,1024]{1,0:T(8,128)(2,1)S(1)}, u32[]{:S(2)}, u32[]{:S(2)}) collective-permute-start(bf16[256,1024]{1,0:T(8,128)(2,1)S(1)} %get-tuple-element.29), channel_id=1, source_target_pairs={{0,4},{2,6},{4,0},{6,2},{8,12},{10,14},{12,8},{14,10},{1,5},{3,7},... | collective-permute-start | bytes 1572872 | tf_op jit(solution)/shard_map/ppermute | solution.py:257
  9.3 21.5 %collective-permute-start.3 = (bf16[256,1024]{1,0:T(8,128)(2,1)S(1)}, bf16[256,1024]{1,0:T(8,128)(2,1)S(1)}, u32[]{:S(2)}, u32[]{:S(2)}) collective-permute-start(bf16[256,1024]{1,0:T(8,128)(2,1)S(1)} %get-tuple-element.31), channel_id=1, source_target_pairs={{0,8},{2,10},{4,12},{6,14},{8,0},{10,2},{12,4},{14,6},{1,9},{3,11}... | collective-permute-start | bytes 1572872 | tf_op jit(solution)/shard_map/ppermute | solution.py:257
  11.7 45.9 %collective-permute-start.4 = (bf16[256,1024]{1,0:T(8,128)(2,1)S(1)}, bf16[256,1024]{1,0:T(8,128)(2,1)S(1)}, u32[]{:S(2)}, u32[]{:S(2)}) collective-permute-start(bf16[256,1024]{1,0:T(8,128)(2,1)S(1)} %get-tuple-element.32), channel_id=1, source_target_pairs={{0,10},{2,8},{4,14},{6,12},{8,2},{10,0},{12,6},{14,4},{1,11},{3,9}... | collective-permute-start | bytes 1572872 | tf_op jit(solution)/shard_map/ppermute | solution.py:257
  13.1 44.5 %collective-permute-start.2 = (bf16[256,1024]{1,0:T(8,128)(2,1)S(1)}, bf16[256,1024]{1,0:T(8,128)(2,1)S(1)}, u32[]{:S(2)}, u32[]{:S(2)}) collective-permute-start(bf16[256,1024]{1,0:T(8,128)(2,1)S(1)} %get-tuple-element.30), channel_id=1, source_target_pairs={{0,6},{2,4},{4,2},{6,0},{8,14},{10,12},{12,10},{14,8},{1,7},{3,5},... | collective-permute-start | bytes 1572872 | tf_op jit(solution)/shard_map/ppermute | solution.py:257
  18.2 78.4 %collective-permute-start.5 = (bf16[256,1024]{1,0:T(8,128)(2,1)S(1)}, bf16[256,1024]{1,0:T(8,128)(2,1)S(1)}, u32[]{:S(2)}, u32[]{:S(2)}) collective-permute-start(bf16[256,1024]{1,0:T(8,128)(2,1)S(1)} %get-tuple-element.34), channel_id=1, source_target_pairs={{0,12},{2,14},{4,8},{6,10},{8,4},{10,6},{12,0},{14,2},{1,13},{3,15... | collective-permute-start | bytes 1572872 | tf_op jit(solution)/shard_map/ppermute | solution.py:257
  28.6 76.4 %collective-permute-start.6 = (bf16[256,1024]{1,0:T(8,128)(2,1)S(1)}, bf16[256,1024]{1,0:T(8,128)(2,1)S(1)}, u32[]{:S(2)}, u32[]{:S(2)}) collective-permute-start(bf16[256,1024]{1,0:T(8,128)(2,1)S(1)} %get-tuple-element.39), channel_id=1, source_target_pairs={{0,14},{2,12},{4,10},{6,8},{8,6},{10,4},{12,2},{14,0},{1,15},{3,13... | collective-permute-start | bytes 1572872 | tf_op jit(solution)/shard_map/ppermute | solution.py:257
  105.0 3.8 %collective-permute-start.7 = (bf16[256,1024]{1,0:T(8,128)(2,1)S(1)}, bf16[256,1024]{1,0:T(8,128)(2,1)S(1)}, u32[]{:S(2)}, u32[]{:S(2)}) collective-permute-start(bf16[256,1024]{1,0:T(8,128)(2,1)S(1)} %collective-permute-done.6.refs_3_), channel_id=1, source_target_pairs={{0,1},{2,3},{4,5},{6,7},{8,9},{10,11},{12,13},{14,15},{16,17},{18,... | collective-permute-start | bytes 1572872 | tf_op jit(solution)/shard_map/ppermute | solution.py:302

commit v5 on v4

--- a/solution.py
+++ b/solution.py
@@ -263,12 +263,20 @@
         return lax.all_to_all(send, "blk", split_axis=0, concat_axis=0, tiled=True)
 
     arrived = {}
-    lead = near[1 : 1 + len(far2) + len(far3)]
+    lead = [near[-1], far1[0]]
     unit, tgt, *packed = call_pack_first(embeddings, cluster_ids, lead, clusters, per)
-    for steps in (far1, near[len(lead) + 1 :] + [0], far2 + far3, []):
+    for steps in (near[1:-1] + far1[1:] + [0], []):
         for step, block in zip(lead, packed):
             arrived[step] = to_owner(block, step) if step else block
         lead, packed = steps, call_pack_rest(unit, tgt, steps, per) if steps else []
+    packed = call_pack_rest(unit, tgt, far2 + far3, per)
+    for steps, gate in ((far2, near[-1]), (far3, far1[0])):
+        *held, arrived[gate] = lax.optimization_barrier(
+            (*packed[: len(steps)], arrived[gate])
+        )
+        packed = packed[len(steps) :]
+        for step, block in zip(steps, held):
+            arrived[step] = to_owner(block, step)
 
     early = near + far1
     send, best = kernel_call(

time: 112 us -> 110 us (0.982)
  waiting for transfers between devices: 36.5 us -> 32.6 us
  blocking collectives: 37.5 us -> 41 us
  starting transfers between devices: 13.7 us -> 12.2 us
    ppermute x7, waiting for transfers between devices: 36.5 us -> 32.6 us  [to_owner(): return lax.ppermute(block, 'clus', [(i, i ^ step) for i in range(owners)])]
    all_to_all x2, blocking collectives: 37.5 us -> 41 us  [to_both(): return lax.all_to_all(send, 'blk', split_axis=0, concat_axis=0, tiled=True)]
    ppermute x7, starting transfers between devices: 12.4 us -> 10.9 us  [to_owner(): return lax.ppermute(block, 'clus', [(i, i ^ step) for i in range(owners)])]
    pallas_call x10 -> x9, Pallas kernels: 22.1 us -> 21.9 us  [kernel_call(): pl.pallas_call(kernel, out_shape=shapes, in_specs=[VMEM] * len(inputs), o...]
where the time goes in v5:
time: 110 us
  blocking collectives  41 us (37%)
  waiting for transfers between devices  32.6 us (30%)
  Pallas kernels  21.9 us (20%)
  starting transfers between devices  12.2 us (11%)
  local copies, waits for them, and re-layouts  2.28 us (2%)
    all_to_all x2, blocking collectives, to_both(): return lax.all_to_all(send, 'blk', split_axis=0, concat_axis=0, tiled=True)  41 us
    ppermute x7, waiting for transfers between devices, to_owner(): return lax.ppermute(block, 'clus', [(i, i ^ step) for i in range(owners)])  32.6 us
    pallas_call x9, Pallas kernels, kernel_call(): pl.pallas_call(kernel, out_shape=shapes, in_specs=[VMEM] * len(inputs), o...  21.9 us
    ppermute x7, starting transfers between devices, to_owner(): return lax.ppermute(block, 'clus', [(i, i ^ step) for i in range(owners)])  10.9 us
    unnamed x4, local copies, waits for them, and re-layouts  2.28 us
  transfers between devices with their start and end apart: 8, of which 3 were waited for; matrix products, arithmetic and copies ran while one was open for 0% of the time, Pallas kernels for 15%

profile of v5, /device:TPU:1, one launch (start us, length us, event | category | flops | bytes accessed | tf_op | source)
XLA Modules:
  0.0 110.1 jit_solution(8899540488455742583)
XLA Ops:
  0.0 0.0 copy-start
  0.0 1.6 %copy-done = bf16[1024,1024]{1,0:T(8,128)(2,1)S(1)} copy-done((bf16[1024,1024]{1,0:T(8,128)(2,1)S(1)}, bf16[1024,1024]{1,0:T(8,128)(2,1)}, u32[]{:S(2)}) %copy-start) | copy-done | bytes 2097176
  1.6 0.0 copy-start.1
  1.6 0.7 copy-done.1
  2.3 2.1 %pack_first.1 = (bf16[1024,1024]{1,0:T(8,128)(2,1)S(1)}, s32[1,1024]{1,0:T(1,128)S(1)}, bf16[256,1024]{1,0:T(8,128)(2,1)S(1)}, bf16[256,1024]{1,0:T(8,128)(2,1)S(1)}) custom-call(bf16[1024,1024]{1,0:T(8,128)(2,1)S(1)} %copy-done, s32[1,1024]{1,0:T(1,128)S(1)} %copy-done.1), custom_call_target="tpu_custom_call" | custom-call | flops 1000 | bytes 1000 | tf_op jit(solution)/shard_map/pack_first/pallas_call | solution.py:80
  4.4 3.1 %collective-permute-start.2 = (bf16[256,1024]{1,0:T(8,128)(2,1)S(1)}, bf16[256,1024]{1,0:T(8,128)(2,1)S(1)}, u32[]{:S(2)}, u32[]{:S(2)}) collective-permute-start(bf16[256,1024]{1,0:T(8,128)(2,1)S(1)} %get-tuple-element.35), channel_id=1, source_target_pairs={{0,6},{2,4},{4,2},{6,0},{8,14},{10,12},{12,10},{14,8},{1,7},{3,5},... | collective-permute-start | bytes 1572872 | tf_op jit(solution)/shard_map/ppermute | solution.py:257
  7.6 2.3 %collective-permute-start.3 = (bf16[256,1024]{1,0:T(8,128)(2,1)S(1)}, bf16[256,1024]{1,0:T(8,128)(2,1)S(1)}, u32[]{:S(2)}, u32[]{:S(2)}) collective-permute-start(bf16[256,1024]{1,0:T(8,128)(2,1)S(1)} %get-tuple-element.38), channel_id=1, source_target_pairs={{0,8},{2,10},{4,12},{6,14},{8,0},{10,2},{12,4},{14,6},{1,9},{3,11}... | collective-permute-start | bytes 1572872 | tf_op jit(solution)/shard_map/ppermute | solution.py:257
  9.9 2.6 %pack_rest.2 = (bf16[256,1024]{1,0:T(8,128)(2,1)S(1)}, bf16[256,1024]{1,0:T(8,128)(2,1)S(1)}, bf16[256,1024]{1,0:T(8,128)(2,1)S(1)}, bf16[256,1024]{1,0:T(8,128)(2,1)S(1)}) custom-call(bf16[1024,1024]{1,0:T(8,128)(2,1)S(1)} %get-tuple-element.29.unit, s32[1,1024]{1,0:T(1,128)S(1)} %get-tuple-element.30.tgt), custom_call_target="tpu_custom_call" | custom-call | flops 1000 | bytes 1000 | tf_op jit(solution)/shard_map/pack_rest/pallas_call | solution.py:80
  12.5 0.3 collective-permute-start
  12.8 0.2 collective-permute-start.1
  13.0 1.0 collective-permute-start.4
  14.0 1.4 %pack_rest.3 = (bf16[256,1024]{1,0:T(8,128)(2,1)S(1)}, bf16[256,1024]{1,0:T(8,128)(2,1)S(1)}) custom-call(bf16[1024,1024]{1,0:T(8,128)(2,1)S(1)} %get-tuple-element.29.unit, s32[1,1024]{1,0:T(1,128)S(1)} %get-tuple-element.30.tgt), custom_call_target="tpu_custom_call" | custom-call | flops 1000 | bytes 1000 | tf_op jit(solution)/shard_map/pack_rest/pallas_call | solution.py:80
  15.4 14.9 %collective-permute-done.2.refs_3_ = bf16[256,1024]{1,0:T(8,128)(2,1)S(1)} collective-permute-done((bf16[256,1024]{1,0:T(8,128)(2,1)S(1)}, bf16[256,1024]{1,0:T(8,128)(2,1)S(1)}, u32[]{:S(2)}, u32[]{:S(2)}) %collective-permute-start.2) | collective-permute-done | bytes 524320 | tf_op jit(solution)/shard_map/ppermute | solution.py:257
  30.4 2.0 %collective-permute-start.5 = (bf16[256,1024]{1,0:T(8,128)(2,1)S(1)}, bf16[256,1024]{1,0:T(8,128)(2,1)S(1)}, u32[]{:S(2)}, u32[]{:S(2)}) collective-permute-start(bf16[256,1024]{1,0:T(8,128)(2,1)S(1)} %get-tuple-element.42), channel_id=1, source_target_pairs={{0,12},{2,14},{4,8},{6,10},{8,4},{10,6},{12,0},{14,2},{1,13},{3,15... | collective-permute-start | bytes 1572872 | tf_op jit(solution)/shard_map/ppermute | solution.py:257
  32.4 0.0 collective-permute-done.3.refs_4_
  32.4 2.0 %collective-permute-start.6 = (bf16[256,1024]{1,0:T(8,128)(2,1)S(1)}, bf16[256,1024]{1,0:T(8,128)(2,1)S(1)}, u32[]{:S(2)}, u32[]{:S(2)}) collective-permute-start(bf16[256,1024]{1,0:T(8,128)(2,1)S(1)} %get-tuple-element.47), channel_id=1, source_target_pairs={{0,14},{2,12},{4,10},{6,8},{8,6},{10,4},{12,2},{14,0},{1,15},{3,13... | collective-permute-start | bytes 1572872 | tf_op jit(solution)/shard_map/ppermute | solution.py:257
  34.4 0.5 collective-permute-done.refs_1_
  34.9 17.1 %collective-permute-done.1.refs_2_ = bf16[256,1024]{1,0:T(8,128)(2,1)S(1)} collective-permute-done((bf16[256,1024]{1,0:T(8,128)(2,1)S(1)}, bf16[256,1024]{1,0:T(8,128)(2,1)S(1)}, u32[]{:S(2)}, u32[]{:S(2)}) %collective-permute-start.1) | collective-permute-done | bytes 524320 | tf_op jit(solution)/shard_map/ppermute | solution.py:257
  52.0 0.0 collective-permute-done.4.refs_5_
  52.0 3.0 %own_early.1 = (bf16[2,2,768,1024]{3,2,1,0:T(8,128)(2,1)S(1)}, f32[2,1024]{1,0:T(2,128)S(1)}) custom-call(bf16[256,1024]{1,0:T(8,128)(2,1)S(1)} %get-tuple-element.31.refs_0_, bf16[256,1024]{1,0:T(8,128)(2,1)S(1)} %collective-permute-done.refs_1_, bf16[256,1024]{1,0:T(8,128)(2,1)S(1)} %collective-permute-done.1.refs_2_, ...), custom_call_target="tpu_custom_call" | custom-call | flops 1000 | bytes 1000 | tf_op jit(solution)/shard_map/own_early/pallas_call | solution.py:80
  55.0 36.8 %all_to_all.10.refs_0_ = bf16[2,2,768,1024]{3,2,1,0:T(8,128)(2,1)S(1)} all-to-all(bf16[2,2,768,1024]{3,2,1,0:T(8,128)(2,1)S(1)} %get-tuple-element.41), channel_id=1, replica_groups=mesh['groups'=2,'clus'=8,'blk'=2] {'blk'}, dimensions={0} | all-to-all | bytes 12582912 | tf_op jit(solution)/shard_map/all_to_all | solution.py:263
  91.8 2.7 %cross_early.1.refs_1_ = f32[2,1024]{1,0:T(2,128)S(1)} custom-call(bf16[2,2,768,1024]{3,2,1,0:T(8,128)(2,1)S(1)} %all_to_all.10.refs_0_, f32[2,1024]{1,0:T(2,128)S(1)} %get-tuple-element.43.refs_1_), custom_call_target="tpu_custom_call" | custom-call | flops 1000 | bytes 1000 | tf_op jit(solution)/shard_map/cross_early/pallas_call | solution.py:80
  94.5 0.0 collective-permute-done.5.refs_2_
  94.6 2.2 %own_middle.1 = (bf16[2,2,128,1024]{3,2,1,0:T(8,128)(2,1)S(1)}, f32[2,1024]{1,0:T(2,128)S(1)}) custom-call(bf16[2,2,768,1024]{3,2,1,0:T(8,128)(2,1)S(1)} %all_to_all.10.refs_0_, f32[2,1024]{1,0:T(2,128)S(1)} %cross_early.1.refs_1_, bf16[256,1024]{1,0:T(8,128)(2,1)S(1)} %collective-permute-done.5.refs_2_), custom_call_target="tpu_custom_call" | custom-call | flops 1000 | bytes 1000 | tf_op jit(solution)/shard_map/own_middle/pallas_call | solution.py:80
  96.8 4.2 %all_to_all.11.refs_1_ = bf16[2,2,128,1024]{3,2,1,0:T(8,128)(2,1)S(1)} all-to-all(bf16[2,2,128,1024]{3,2,1,0:T(8,128)(2,1)S(1)} %get-tuple-element.46), channel_id=1, replica_groups=mesh['groups'=2,'clus'=8,'blk'=2] {'blk'}, dimensions={0} | all-to-all | bytes 2097152 | tf_op jit(solution)/shard_map/all_to_all | solution.py:263
  101.0 2.0 %cross_middle.1.refs_2_ = f32[2,1024]{1,0:T(2,128)S(1)} custom-call(bf16[2,2,768,1024]{3,2,1,0:T(8,128)(2,1)S(1)} %all_to_all.10.refs_0_, bf16[2,2,128,1024]{3,2,1,0:T(8,128)(2,1)S(1)} %all_to_all.11.refs_1_, f32[2,1024]{1,0:T(2,128)S(1)} %get-tuple-element.48.refs_2_), custom_call_target="tpu_custom_call" | custom-call | flops 1000 | bytes 1000 | tf_op jit(solution)/shard_map/cross_middle/pallas_call | solution.py:80
  103.0 0.0 collective-permute-done.6.refs_3_
  103.0 1.3 %collective-permute-start.7 = (bf16[256,1024]{1,0:T(8,128)(2,1)S(1)}, bf16[256,1024]{1,0:T(8,128)(2,1)S(1)}, u32[]{:S(2)}, u32[]{:S(2)}) collective-permute-start(bf16[256,1024]{1,0:T(8,128)(2,1)S(1)} %collective-permute-done.6.refs_3_), channel_id=1, source_target_pairs={{0,1},{2,3},{4,5},{6,7},{8,9},{10,11},{12,13},{14,15},{16,17},{18,... | collective-permute-start | bytes 1572872 | tf_op jit(solution)/shard_map/ppermute | solution.py:310
  104.3 2.5 %own_last.1 = (bf16[2,2,128,1024]{3,2,1,0:T(8,128)(2,1)S(1)}, f32[2,1024]{1,0:T(2,128)S(1)}) custom-call(bf16[2,2,768,1024]{3,2,1,0:T(8,128)(2,1)S(1)} %all_to_all.10.refs_0_, bf16[2,2,128,1024]{3,2,1,0:T(8,128)(2,1)S(1)} %all_to_all.11.refs_1_, f32[2,1024]{1,0:T(2,128)S(1)} %cross_middle.1.refs_2_, bf16[256,1024]{1,0:T(8,128)(2,1)S(1)} %collective-permute-done.6.refs_3_), custom_call_target="tpu_custom_call" | custom-call | flops 1000 | bytes 1000 | tf_op jit(solution)/shard_map/own_last/pallas_call | solution.py:80
  106.8 0.0 collective-permute-done.7.refs_4_
  106.8 3.2 %cross_last.1 = f32[2,1024]{1,0:T(2,128)} custom-call(bf16[2,2,768,1024]{3,2,1,0:T(8,128)(2,1)S(1)} %all_to_all.10.refs_0_, bf16[2,2,128,1024]{3,2,1,0:T(8,128)(2,1)S(1)} %all_to_all.11.refs_1_, bf16[2,2,128,1024]{3,2,1,0:T(8,128)(2,1)S(1)} %get-tuple-element.51.refs_2_, f32[2,1024]{1,0:T(2,128)S(1)} %get-tuple-element.52.refs_3_, ...), custom_call_target="tpu_custom_call" | custom-call | flops 1000 | bytes 1000 | tf_op jit(solution)/shard_map/cross_last/pallas_call | solution.py:80
Async XLA Ops:
  0.0 1.6 %copy-start = (bf16[1024,1024]{1,0:T(8,128)(2,1)S(1)}, bf16[1024,1024]{1,0:T(8,128)(2,1)}, u32[]{:S(2)}) copy-start(bf16[1024,1024]{1,0:T(8,128)(2,1)} %emb.1) | copy-start | bytes 6291460
  1.6 0.7 copy-start.1
  4.4 26.0 %collective-permute-start.2 = (bf16[256,1024]{1,0:T(8,128)(2,1)S(1)}, bf16[256,1024]{1,0:T(8,128)(2,1)S(1)}, u32[]{:S(2)}, u32[]{:S(2)}) collective-permute-start(bf16[256,1024]{1,0:T(8,128)(2,1)S(1)} %get-tuple-element.35), channel_id=1, source_target_pairs={{0,6},{2,4},{4,2},{6,0},{8,14},{10,12},{12,10},{14,8},{1,7},{3,5},... | collective-permute-start | bytes 1572872 | tf_op jit(solution)/shard_map/ppermute | solution.py:257
  7.6 24.8 %collective-permute-start.3 = (bf16[256,1024]{1,0:T(8,128)(2,1)S(1)}, bf16[256,1024]{1,0:T(8,128)(2,1)S(1)}, u32[]{:S(2)}, u32[]{:S(2)}) collective-permute-start(bf16[256,1024]{1,0:T(8,128)(2,1)S(1)} %get-tuple-element.38), channel_id=1, source_target_pairs={{0,8},{2,10},{4,12},{6,14},{8,0},{10,2},{12,4},{14,6},{1,9},{3,11}... | collective-permute-start | bytes 1572872 | tf_op jit(solution)/shard_map/ppermute | solution.py:257
  12.5 22.4 %collective-permute-start = (bf16[256,1024]{1,0:T(8,128)(2,1)S(1)}, bf16[256,1024]{1,0:T(8,128)(2,1)S(1)}, u32[]{:S(2)}, u32[]{:S(2)}) collective-permute-start(bf16[256,1024]{1,0:T(8,128)(2,1)S(1)} %get-tuple-element.32), channel_id=1, source_target_pairs={{0,2},{2,0},{4,6},{6,4},{8,10},{10,8},{12,14},{14,12},{1,3},{3,1},... | collective-permute-start | bytes 1572872 | tf_op jit(solution)/shard_map/ppermute | solution.py:257
  12.8 39.2 %collective-permute-start.1 = (bf16[256,1024]{1,0:T(8,128)(2,1)S(1)}, bf16[256,1024]{1,0:T(8,128)(2,1)S(1)}, u32[]{:S(2)}, u32[]{:S(2)}) collective-permute-start(bf16[256,1024]{1,0:T(8,128)(2,1)S(1)} %get-tuple-element.33), channel_id=1, source_target_pairs={{0,4},{2,6},{4,0},{6,2},{8,12},{10,14},{12,8},{14,10},{1,5},{3,7},... | collective-permute-start | bytes 1572872 | tf_op jit(solution)/shard_map/ppermute | solution.py:257
  13.0 39.0 %collective-permute-start.4 = (bf16[256,1024]{1,0:T(8,128)(2,1)S(1)}, bf16[256,1024]{1,0:T(8,128)(2,1)S(1)}, u32[]{:S(2)}, u32[]{:S(2)}) collective-permute-start(bf16[256,1024]{1,0:T(8,128)(2,1)S(1)} %get-tuple-element.40), channel_id=1, source_target_pairs={{0,10},{2,8},{4,14},{6,12},{8,2},{10,0},{12,6},{14,4},{1,11},{3,9}... | collective-permute-start | bytes 1572872 | tf_op jit(solution)/shard_map/ppermute | solution.py:257
  30.4 64.2 %collective-permute-start.5 = (bf16[256,1024]{1,0:T(8,128)(2,1)S(1)}, bf16[256,1024]{1,0:T(8,128)(2,1)S(1)}, u32[]{:S(2)}, u32[]{:S(2)}) collective-permute-start(bf16[256,1024]{1,0:T(8,128)(2,1)S(1)} %get-tuple-element.42), channel_id=1, source_target_pairs={{0,12},{2,14},{4,8},{6,10},{8,4},{10,6},{12,0},{14,2},{1,13},{3,15... | collective-permute-start | bytes 1572872 | tf_op jit(solution)/shard_map/ppermute | solution.py:257
  32.4 70.7 %collective-permute-start.6 = (bf16[256,1024]{1,0:T(8,128)(2,1)S(1)}, bf16[256,1024]{1,0:T(8,128)(2,1)S(1)}, u32[]{:S(2)}, u32[]{:S(2)}) collective-permute-start(bf16[256,1024]{1,0:T(8,128)(2,1)S(1)} %get-tuple-element.47), channel_id=1, source_target_pairs={{0,14},{2,12},{4,10},{6,8},{8,6},{10,4},{12,2},{14,0},{1,15},{3,13... | collective-permute-start | bytes 1572872 | tf_op jit(solution)/shard_map/ppermute | solution.py:257
  103.0 3.8 %collective-permute-start.7 = (bf16[256,1024]{1,0:T(8,128)(2,1)S(1)}, bf16[256,1024]{1,0:T(8,128)(2,1)S(1)}, u32[]{:S(2)}, u32[]{:S(2)}) collective-permute-start(bf16[256,1024]{1,0:T(8,128)(2,1)S(1)} %collective-permute-done.6.refs_3_), channel_id=1, source_target_pairs={{0,1},{2,3},{4,5},{6,7},{8,9},{10,11},{12,13},{14,15},{16,17},{18,... | collective-permute-start | bytes 1572872 | tf_op jit(solution)/shard_map/ppermute | solution.py:310

commit v6 on v5

--- a/solution.py
+++ b/solution.py
@@ -61,11 +61,28 @@
         out[:, LANES:] = tail
 
 
-def pack_first(steps, clusters, per_source, emb, ids, unit, tgt, *outs):
-    values = emb[...].astype(F32)
-    scale = lax.rsqrt(jnp.sum(values * values, axis=1, keepdims=True) + 1e-6)
-    unit[...] = (values * scale).astype(BF)
-    tgt[...] = targets(ids[...], clusters, per_source)
+PIECES = 4
+
+
+def pack_first(steps, clusters, per_source, emb, ids, unit, tgt, *refs):
+    outs, (raw, raw_ids, sems, ids_sem) = refs[:-4], refs[-4:]
+    size = emb.shape[0] // PIECES
+    ids_copy = pltpu.make_async_copy(ids, raw_ids, ids_sem)
+    ids_copy.start()
+    windows = [pl.ds(piece * size, size) for piece in range(PIECES)]
+    copies = [
+        pltpu.make_async_copy(emb.at[window], raw.at[window], sems.at[piece])
+        for piece, window in enumerate(windows)
+    ]
+    for copy in copies:
+        copy.start()
+    ids_copy.wait()
+    tgt[...] = targets(raw_ids[...], clusters, per_source)
+    for copy, window in zip(copies, windows):
+        copy.wait()
+        values = raw[window, :].astype(F32)
+        scale = lax.rsqrt(jnp.sum(values * values, axis=1, keepdims=True) + 1e-6)
+        unit[window, :] = (values * scale).astype(BF)
     store_blocks(unit[...], tgt[...], steps, CLUS_DEV * per_source, outs)
 
 
@@ -76,11 +93,11 @@
 VMEM = pl.BlockSpec(memory_space=pltpu.VMEM)
 
 
-def kernel_call(kernel, shapes, inputs, name, scratch=()):
+def kernel_call(kernel, shapes, inputs, name, scratch=(), inputs_in=VMEM):
     return pl.pallas_call(
         kernel,
         out_shape=shapes,
-        in_specs=[VMEM] * len(inputs),
+        in_specs=[inputs_in] * len(inputs),
         out_specs=[VMEM] * len(shapes),
         scratch_shapes=scratch,
         compiler_params=pltpu.CompilerParams(vmem_limit_bytes=20 * 2**20),
@@ -96,7 +113,14 @@
         functools.partial(pack_first, steps, clusters, per_source),
         shapes + [block] * len(steps),
         [emb, ids],
-        "pack_first",
+        inputs_in=pl.BlockSpec(memory_space=pltpu.HBM),
+        name="pack_first",
+        scratch=[
+            pltpu.VMEM(emb.shape, BF),
+            pltpu.VMEM(ids.shape, jnp.int32),
+            pltpu.SemaphoreType.DMA((PIECES,)),
+            pltpu.SemaphoreType.DMA,
+        ],
     )
 
 
@@ -270,7 +294,7 @@
             arrived[step] = to_owner(block, step) if step else block
         lead, packed = steps, call_pack_rest(unit, tgt, steps, per) if steps else []
     packed = call_pack_rest(unit, tgt, far2 + far3, per)
-    for steps, gate in ((far2, near[-1]), (far3, far1[0])):
+    for steps, gate in ((far2, near[-1]), (far3, far1[-1])):
         *held, arrived[gate] = lax.optimization_barrier(
             (*packed[: len(steps)], arrived[gate])
         )

time: 110 us -> 113 us (1.027)
  waiting for transfers between devices: 32.6 us -> 60.4 us
  blocking collectives: 41 us -> 15.8 us
    ppermute x7, waiting for transfers between devices: 32.6 us -> 60.4 us  [to_owner(): return lax.ppermute(block, 'clus', [(i, i ^ step) for i in range(owners)])]
    all_to_all x2, blocking collectives: 41 us -> 15.8 us  [to_both(): return lax.all_to_all(send, 'blk', split_axis=0, concat_axis=0, tiled=True)]
where the time goes in v6:
time: 113 us
  waiting for transfers between devices  60.4 us (53%)
  Pallas kernels  22.3 us (20%)
  blocking collectives  15.8 us (14%)
  starting transfers between devices  12.4 us (11%)
  local copies, waits for them, and re-layouts  2.28 us (2%)
    ppermute x7, waiting for transfers between devices, to_owner(): return lax.ppermute(block, 'clus', [(i, i ^ step) for i in range(owners)])  60.4 us
    pallas_call x9, Pallas kernels, kernel_call(): pl.pallas_call(kernel, out_shape=shapes, in_specs=[inputs_in] * len(input...  22.3 us
    all_to_all x2, blocking collectives, to_both(): return lax.all_to_all(send, 'blk', split_axis=0, concat_axis=0, tiled=True)  15.8 us
    ppermute x7, starting transfers between devices, to_owner(): return lax.ppermute(block, 'clus', [(i, i ^ step) for i in range(owners)])  11.1 us
    unnamed x4, local copies, waits for them, and re-layouts  2.28 us
  transfers between devices with their start and end apart: 8, of which 3 were waited for; matrix products, arithmetic and copies ran while one was open for 0% of the time, Pallas kernels for 15%

profile of v6, /device:TPU:1, one launch (start us, length us, event | category | flops | bytes accessed | tf_op | source)
XLA Modules:
  0.0 113.2 jit_solution(14321180884172996428)
XLA Ops:
  0.0 0.0 copy-start
  0.0 1.6 %copy-done = bf16[1024,1024]{1,0:T(8,128)(2,1)S(1)} copy-done((bf16[1024,1024]{1,0:T(8,128)(2,1)S(1)}, bf16[1024,1024]{1,0:T(8,128)(2,1)}, u32[]{:S(2)}) %copy-start) | copy-done | bytes 2097176
  1.6 0.0 copy-start.1
  1.6 0.7 copy-done.1
  2.3 2.5 %pack_first.1 = (bf16[1024,1024]{1,0:T(8,128)(2,1)S(1)}, s32[1,1024]{1,0:T(1,128)S(1)}, bf16[256,1024]{1,0:T(8,128)(2,1)S(1)}, bf16[256,1024]{1,0:T(8,128)(2,1)S(1)}) custom-call(bf16[1024,1024]{1,0:T(8,128)(2,1)S(1)} %copy-done, s32[1,1024]{1,0:T(1,128)S(1)} %copy-done.1), custom_call_target="tpu_custom_call" | custom-call | flops 1000 | bytes 1000 | tf_op jit(solution)/shard_map/pack_first/pallas_call | solution.py:97
  4.8 3.1 %collective-permute-start.2 = (bf16[256,1024]{1,0:T(8,128)(2,1)S(1)}, bf16[256,1024]{1,0:T(8,128)(2,1)S(1)}, u32[]{:S(2)}, u32[]{:S(2)}) collective-permute-start(bf16[256,1024]{1,0:T(8,128)(2,1)S(1)} %get-tuple-element.35), channel_id=1, source_target_pairs={{0,6},{2,4},{4,2},{6,0},{8,14},{10,12},{12,10},{14,8},{1,7},{3,5},... | collective-permute-start | bytes 1572872 | tf_op jit(solution)/shard_map/ppermute | solution.py:281
  8.0 2.6 %pack_rest.2 = (bf16[256,1024]{1,0:T(8,128)(2,1)S(1)}, bf16[256,1024]{1,0:T(8,128)(2,1)S(1)}, bf16[256,1024]{1,0:T(8,128)(2,1)S(1)}, bf16[256,1024]{1,0:T(8,128)(2,1)S(1)}) custom-call(bf16[1024,1024]{1,0:T(8,128)(2,1)S(1)} %get-tuple-element.29.unit, s32[1,1024]{1,0:T(1,128)S(1)} %get-tuple-element.30.tgt), custom_call_target="tpu_custom_call" | custom-call | flops 1000 | bytes 1000 | tf_op jit(solution)/shard_map/pack_rest/pallas_call | solution.py:97
  10.6 2.3 %collective-permute-start.4 = (bf16[256,1024]{1,0:T(8,128)(2,1)S(1)}, bf16[256,1024]{1,0:T(8,128)(2,1)S(1)}, u32[]{:S(2)}, u32[]{:S(2)}) collective-permute-start(bf16[256,1024]{1,0:T(8,128)(2,1)S(1)} %get-tuple-element.39), channel_id=1, source_target_pairs={{0,10},{2,8},{4,14},{6,12},{8,2},{10,0},{12,6},{14,4},{1,11},{3,9}... | collective-permute-start | bytes 1572872 | tf_op jit(solution)/shard_map/ppermute | solution.py:281
  13.0 0.1 collective-permute-start.3
  13.1 1.2 %collective-permute-start = (bf16[256,1024]{1,0:T(8,128)(2,1)S(1)}, bf16[256,1024]{1,0:T(8,128)(2,1)S(1)}, u32[]{:S(2)}, u32[]{:S(2)}) collective-permute-start(bf16[256,1024]{1,0:T(8,128)(2,1)S(1)} %get-tuple-element.32), channel_id=1, source_target_pairs={{0,2},{2,0},{4,6},{6,4},{8,10},{10,8},{12,14},{14,12},{1,3},{3,1},... | collective-permute-start | bytes 1572872 | tf_op jit(solution)/shard_map/ppermute | solution.py:281
  14.2 0.2 collective-permute-start.1
  14.4 1.4 %pack_rest.3 = (bf16[256,1024]{1,0:T(8,128)(2,1)S(1)}, bf16[256,1024]{1,0:T(8,128)(2,1)S(1)}) custom-call(bf16[1024,1024]{1,0:T(8,128)(2,1)S(1)} %get-tuple-element.29.unit, s32[1,1024]{1,0:T(1,128)S(1)} %get-tuple-element.30.tgt), custom_call_target="tpu_custom_call" | custom-call | flops 1000 | bytes 1000 | tf_op jit(solution)/shard_map/pack_rest/pallas_call | solution.py:97
  15.8 11.3 %collective-permute-done.2.refs_3_ = bf16[256,1024]{1,0:T(8,128)(2,1)S(1)} collective-permute-done((bf16[256,1024]{1,0:T(8,128)(2,1)S(1)}, bf16[256,1024]{1,0:T(8,128)(2,1)S(1)}, u32[]{:S(2)}, u32[]{:S(2)}) %collective-permute-start.2) | collective-permute-done | bytes 524320 | tf_op jit(solution)/shard_map/ppermute | solution.py:281
  27.1 2.0 %collective-permute-start.5 = (bf16[256,1024]{1,0:T(8,128)(2,1)S(1)}, bf16[256,1024]{1,0:T(8,128)(2,1)S(1)}, u32[]{:S(2)}, u32[]{:S(2)}) collective-permute-start(bf16[256,1024]{1,0:T(8,128)(2,1)S(1)} %get-tuple-element.42), channel_id=1, source_target_pairs={{0,12},{2,14},{4,8},{6,10},{8,4},{10,6},{12,0},{14,2},{1,13},{3,15... | collective-permute-start | bytes 1572872 | tf_op jit(solution)/shard_map/ppermute | solution.py:281
  29.1 18.5 %collective-permute-done.4.refs_5_ = bf16[256,1024]{1,0:T(8,128)(2,1)S(1)} collective-permute-done((bf16[256,1024]{1,0:T(8,128)(2,1)S(1)}, bf16[256,1024]{1,0:T(8,128)(2,1)S(1)}, u32[]{:S(2)}, u32[]{:S(2)}) %collective-permute-start.4) | collective-permute-done | bytes 524320 | tf_op jit(solution)/shard_map/ppermute | solution.py:281
  47.6 2.2 %collective-permute-start.6 = (bf16[256,1024]{1,0:T(8,128)(2,1)S(1)}, bf16[256,1024]{1,0:T(8,128)(2,1)S(1)}, u32[]{:S(2)}, u32[]{:S(2)}) collective-permute-start(bf16[256,1024]{1,0:T(8,128)(2,1)S(1)} %get-tuple-element.47), channel_id=1, source_target_pairs={{0,14},{2,12},{4,10},{6,8},{8,6},{10,4},{12,2},{14,0},{1,15},{3,13... | collective-permute-start | bytes 1572872 | tf_op jit(solution)/shard_map/ppermute | solution.py:281
  49.7 30.6 %collective-permute-done.3.refs_4_ = bf16[256,1024]{1,0:T(8,128)(2,1)S(1)} collective-permute-done((bf16[256,1024]{1,0:T(8,128)(2,1)S(1)}, bf16[256,1024]{1,0:T(8,128)(2,1)S(1)}, u32[]{:S(2)}, u32[]{:S(2)}) %collective-permute-start.3) | collective-permute-done | bytes 524320 | tf_op jit(solution)/shard_map/ppermute | solution.py:281
  80.3 0.0 collective-permute-done.refs_1_
  80.3 0.0 collective-permute-done.1.refs_2_
  80.4 3.0 %own_early.1 = (bf16[2,2,768,1024]{3,2,1,0:T(8,128)(2,1)S(1)}, f32[2,1024]{1,0:T(2,128)S(1)}) custom-call(bf16[256,1024]{1,0:T(8,128)(2,1)S(1)} %get-tuple-element.31.refs_0_, bf16[256,1024]{1,0:T(8,128)(2,1)S(1)} %collective-permute-done.refs_1_, bf16[256,1024]{1,0:T(8,128)(2,1)S(1)} %collective-permute-done.1.refs_2_, ...), custom_call_target="tpu_custom_call" | custom-call | flops 1000 | bytes 1000 | tf_op jit(solution)/shard_map/own_early/pallas_call | solution.py:97
  83.4 11.6 %all_to_all.10.refs_0_ = bf16[2,2,768,1024]{3,2,1,0:T(8,128)(2,1)S(1)} all-to-all(bf16[2,2,768,1024]{3,2,1,0:T(8,128)(2,1)S(1)} %get-tuple-element.41), channel_id=1, replica_groups=mesh['groups'=2,'clus'=8,'blk'=2] {'blk'}, dimensions={0} | all-to-all | bytes 12582912 | tf_op jit(solution)/shard_map/all_to_all | solution.py:287
  95.0 2.7 %cross_early.1.refs_1_ = f32[2,1024]{1,0:T(2,128)S(1)} custom-call(bf16[2,2,768,1024]{3,2,1,0:T(8,128)(2,1)S(1)} %all_to_all.10.refs_0_, f32[2,1024]{1,0:T(2,128)S(1)} %get-tuple-element.43.refs_1_), custom_call_target="tpu_custom_call" | custom-call | flops 1000 | bytes 1000 | tf_op jit(solution)/shard_map/cross_early/pallas_call | solution.py:97
  97.7 0.0 collective-permute-done.5.refs_2_
  97.7 2.2 %own_middle.1 = (bf16[2,2,128,1024]{3,2,1,0:T(8,128)(2,1)S(1)}, f32[2,1024]{1,0:T(2,128)S(1)}) custom-call(bf16[2,2,768,1024]{3,2,1,0:T(8,128)(2,1)S(1)} %all_to_all.10.refs_0_, f32[2,1024]{1,0:T(2,128)S(1)} %cross_early.1.refs_1_, bf16[256,1024]{1,0:T(8,128)(2,1)S(1)} %collective-permute-done.5.refs_2_), custom_call_target="tpu_custom_call" | custom-call | flops 1000 | bytes 1000 | tf_op jit(solution)/shard_map/own_middle/pallas_call | solution.py:97
  99.9 4.2 %all_to_all.11.refs_1_ = bf16[2,2,128,1024]{3,2,1,0:T(8,128)(2,1)S(1)} all-to-all(bf16[2,2,128,1024]{3,2,1,0:T(8,128)(2,1)S(1)} %get-tuple-element.46), channel_id=1, replica_groups=mesh['groups'=2,'clus'=8,'blk'=2] {'blk'}, dimensions={0} | all-to-all | bytes 2097152 | tf_op jit(solution)/shard_map/all_to_all | solution.py:287
  104.1 2.0 %cross_middle.1.refs_2_ = f32[2,1024]{1,0:T(2,128)S(1)} custom-call(bf16[2,2,768,1024]{3,2,1,0:T(8,128)(2,1)S(1)} %all_to_all.10.refs_0_, bf16[2,2,128,1024]{3,2,1,0:T(8,128)(2,1)S(1)} %all_to_all.11.refs_1_, f32[2,1024]{1,0:T(2,128)S(1)} %get-tuple-element.48.refs_2_), custom_call_target="tpu_custom_call" | custom-call | flops 1000 | bytes 1000 | tf_op jit(solution)/shard_map/cross_middle/pallas_call | solution.py:97
  106.1 0.0 collective-permute-done.6.refs_3_
  106.2 1.3 %collective-permute-start.7 = (bf16[256,1024]{1,0:T(8,128)(2,1)S(1)}, bf16[256,1024]{1,0:T(8,128)(2,1)S(1)}, u32[]{:S(2)}, u32[]{:S(2)}) collective-permute-start(bf16[256,1024]{1,0:T(8,128)(2,1)S(1)} %collective-permute-done.6.refs_3_), channel_id=1, source_target_pairs={{0,1},{2,3},{4,5},{6,7},{8,9},{10,11},{12,13},{14,15},{16,17},{18,... | collective-permute-start | bytes 1572872 | tf_op jit(solution)/shard_map/ppermute | solution.py:334
  107.5 2.5 %own_last.1 = (bf16[2,2,128,1024]{3,2,1,0:T(8,128)(2,1)S(1)}, f32[2,1024]{1,0:T(2,128)S(1)}) custom-call(bf16[2,2,768,1024]{3,2,1,0:T(8,128)(2,1)S(1)} %all_to_all.10.refs_0_, bf16[2,2,128,1024]{3,2,1,0:T(8,128)(2,1)S(1)} %all_to_all.11.refs_1_, f32[2,1024]{1,0:T(2,128)S(1)} %cross_middle.1.refs_2_, bf16[256,1024]{1,0:T(8,128)(2,1)S(1)} %collective-permute-done.6.refs_3_), custom_call_target="tpu_custom_call" | custom-call | flops 1000 | bytes 1000 | tf_op jit(solution)/shard_map/own_last/pallas_call | solution.py:97
  110.0 0.0 collective-permute-done.7.refs_4_
  110.0 3.2 %cross_last.1 = f32[2,1024]{1,0:T(2,128)} custom-call(bf16[2,2,768,1024]{3,2,1,0:T(8,128)(2,1)S(1)} %all_to_all.10.refs_0_, bf16[2,2,128,1024]{3,2,1,0:T(8,128)(2,1)S(1)} %all_to_all.11.refs_1_, bf16[2,2,128,1024]{3,2,1,0:T(8,128)(2,1)S(1)} %get-tuple-element.51.refs_2_, f32[2,1024]{1,0:T(2,128)S(1)} %get-tuple-element.52.refs_3_, ...), custom_call_target="tpu_custom_call" | custom-call | flops 1000 | bytes 1000 | tf_op jit(solution)/shard_map/cross_last/pallas_call | solution.py:97
Async XLA Ops:
  0.0 1.6 %copy-start = (bf16[1024,1024]{1,0:T(8,128)(2,1)S(1)}, bf16[1024,1024]{1,0:T(8,128)(2,1)}, u32[]{:S(2)}) copy-start(bf16[1024,1024]{1,0:T(8,128)(2,1)} %emb.1) | copy-start | bytes 6291460
  1.6 0.7 copy-start.1
  4.8 22.3 %collective-permute-start.2 = (bf16[256,1024]{1,0:T(8,128)(2,1)S(1)}, bf16[256,1024]{1,0:T(8,128)(2,1)S(1)}, u32[]{:S(2)}, u32[]{:S(2)}) collective-permute-start(bf16[256,1024]{1,0:T(8,128)(2,1)S(1)} %get-tuple-element.35), channel_id=1, source_target_pairs={{0,6},{2,4},{4,2},{6,0},{8,14},{10,12},{12,10},{14,8},{1,7},{3,5},... | collective-permute-start | bytes 1572872 | tf_op jit(solution)/shard_map/ppermute | solution.py:281
  10.6 36.9 %collective-permute-start.4 = (bf16[256,1024]{1,0:T(8,128)(2,1)S(1)}, bf16[256,1024]{1,0:T(8,128)(2,1)S(1)}, u32[]{:S(2)}, u32[]{:S(2)}) collective-permute-start(bf16[256,1024]{1,0:T(8,128)(2,1)S(1)} %get-tuple-element.39), channel_id=1, source_target_pairs={{0,10},{2,8},{4,14},{6,12},{8,2},{10,0},{12,6},{14,4},{1,11},{3,9}... | collective-permute-start | bytes 1572872 | tf_op jit(solution)/shard_map/ppermute | solution.py:281
  13.0 67.4 %collective-permute-start.3 = (bf16[256,1024]{1,0:T(8,128)(2,1)S(1)}, bf16[256,1024]{1,0:T(8,128)(2,1)S(1)}, u32[]{:S(2)}, u32[]{:S(2)}) collective-permute-start(bf16[256,1024]{1,0:T(8,128)(2,1)S(1)} %get-tuple-element.37), channel_id=1, source_target_pairs={{0,8},{2,10},{4,12},{6,14},{8,0},{10,2},{12,4},{14,6},{1,9},{3,11}... | collective-permute-start | bytes 1572872 | tf_op jit(solution)/shard_map/ppermute | solution.py:281
  13.1 67.3 %collective-permute-start = (bf16[256,1024]{1,0:T(8,128)(2,1)S(1)}, bf16[256,1024]{1,0:T(8,128)(2,1)S(1)}, u32[]{:S(2)}, u32[]{:S(2)}) collective-permute-start(bf16[256,1024]{1,0:T(8,128)(2,1)S(1)} %get-tuple-element.32), channel_id=1, source_target_pairs={{0,2},{2,0},{4,6},{6,4},{8,10},{10,8},{12,14},{14,12},{1,3},{3,1},... | collective-permute-start | bytes 1572872 | tf_op jit(solution)/shard_map/ppermute | solution.py:281
  14.2 66.1 %collective-permute-start.1 = (bf16[256,1024]{1,0:T(8,128)(2,1)S(1)}, bf16[256,1024]{1,0:T(8,128)(2,1)S(1)}, u32[]{:S(2)}, u32[]{:S(2)}) collective-permute-start(bf16[256,1024]{1,0:T(8,128)(2,1)S(1)} %get-tuple-element.33), channel_id=1, source_target_pairs={{0,4},{2,6},{4,0},{6,2},{8,12},{10,14},{12,8},{14,10},{1,5},{3,7},... | collective-permute-start | bytes 1572872 | tf_op jit(solution)/shard_map/ppermute | solution.py:281
  27.1 70.6 %collective-permute-start.5 = (bf16[256,1024]{1,0:T(8,128)(2,1)S(1)}, bf16[256,1024]{1,0:T(8,128)(2,1)S(1)}, u32[]{:S(2)}, u32[]{:S(2)}) collective-permute-start(bf16[256,1024]{1,0:T(8,128)(2,1)S(1)} %get-tuple-element.42), channel_id=1, source_target_pairs={{0,12},{2,14},{4,8},{6,10},{8,4},{10,6},{12,0},{14,2},{1,13},{3,15... | collective-permute-start | bytes 1572872 | tf_op jit(solution)/shard_map/ppermute | solution.py:281
  47.6 58.6 %collective-permute-start.6 = (bf16[256,1024]{1,0:T(8,128)(2,1)S(1)}, bf16[256,1024]{1,0:T(8,128)(2,1)S(1)}, u32[]{:S(2)}, u32[]{:S(2)}) collective-permute-start(bf16[256,1024]{1,0:T(8,128)(2,1)S(1)} %get-tuple-element.47), channel_id=1, source_target_pairs={{0,14},{2,12},{4,10},{6,8},{8,6},{10,4},{12,2},{14,0},{1,15},{3,13... | collective-permute-start | bytes 1572872 | tf_op jit(solution)/shard_map/ppermute | solution.py:281
  106.2 3.8 %collective-permute-start.7 = (bf16[256,1024]{1,0:T(8,128)(2,1)S(1)}, bf16[256,1024]{1,0:T(8,128)(2,1)S(1)}, u32[]{:S(2)}, u32[]{:S(2)}) collective-permute-start(bf16[256,1024]{1,0:T(8,128)(2,1)S(1)} %collective-permute-done.6.refs_3_), channel_id=1, source_target_pairs={{0,1},{2,3},{4,5},{6,7},{8,9},{10,11},{12,13},{14,15},{16,17},{18,... | collective-permute-start | bytes 1572872 | tf_op jit(solution)/shard_map/ppermute | solution.py:334

commit v7 on v5

--- a/solution.py
+++ b/solution.py
@@ -263,14 +263,14 @@
         return lax.all_to_all(send, "blk", split_axis=0, concat_axis=0, tiled=True)
 
     arrived = {}
-    lead = [near[-1], far1[0]]
+    lead = far1
     unit, tgt, *packed = call_pack_first(embeddings, cluster_ids, lead, clusters, per)
-    for steps in (near[1:-1] + far1[1:] + [0], []):
+    for steps in (near[1:] + [0], []):
         for step, block in zip(lead, packed):
             arrived[step] = to_owner(block, step) if step else block
         lead, packed = steps, call_pack_rest(unit, tgt, steps, per) if steps else []
     packed = call_pack_rest(unit, tgt, far2 + far3, per)
-    for steps, gate in ((far2, near[-1]), (far3, far1[0])):
+    for steps, gate in ((far2, far1[0]), (far3, far1[-1])):
         *held, arrived[gate] = lax.optimization_barrier(
             (*packed[: len(steps)], arrived[gate])
         )

time: 110 us -> 112 us (1.018)
  the two profiles are of different devices: /device:TPU:1 before, /device:TPU:17 now
where the time goes in v7:
time: 112 us; the launch traced here: 110 us
  waiting for transfers between devices  55.6 us (50%)
  Pallas kernels  22.1 us (20%)
  blocking collectives  15.1 us (13%)
  starting transfers between devices  15 us (13%)
  local copies, waits for them, and re-layouts  2.28 us (2%)
    ppermute x7, waiting for transfers between devices, to_owner(): return lax.ppermute(block, 'clus', [(i, i ^ step) for i in range(owners)])  55.6 us
    pallas_call x9, Pallas kernels, kernel_call(): pl.pallas_call(kernel, out_shape=shapes, in_specs=[VMEM] * len(inputs), o...  22.1 us
    all_to_all x2, blocking collectives, to_both(): return lax.all_to_all(send, 'blk', split_axis=0, concat_axis=0, tiled=True)  15.1 us
    ppermute x7, starting transfers between devices, to_owner(): return lax.ppermute(block, 'clus', [(i, i ^ step) for i in range(owners)])  13.7 us
    unnamed x4, local copies, waits for them, and re-layouts  2.28 us
  transfers between devices with their start and end apart: 8, of which 3 were waited for; matrix products, arithmetic and copies ran while one was open for 0% of the time, Pallas kernels for 15%

profile of v7, /device:TPU:17, one launch (start us, length us, event | category | flops | bytes accessed | tf_op | source)
XLA Modules:
  0.0 110.2 jit_solution(7443241713290409340)
XLA Ops:
  0.0 0.0 copy-start
  0.0 1.6 %copy-done = bf16[1024,1024]{1,0:T(8,128)(2,1)S(1)} copy-done((bf16[1024,1024]{1,0:T(8,128)(2,1)S(1)}, bf16[1024,1024]{1,0:T(8,128)(2,1)}, u32[]{:S(2)}) %copy-start) | copy-done | bytes 2097176
  1.6 0.0 copy-start.1
  1.6 0.7 copy-done.1
  2.3 2.1 %pack_first.1 = (bf16[1024,1024]{1,0:T(8,128)(2,1)S(1)}, s32[1,1024]{1,0:T(1,128)S(1)}, bf16[256,1024]{1,0:T(8,128)(2,1)S(1)}, bf16[256,1024]{1,0:T(8,128)(2,1)S(1)}) custom-call(bf16[1024,1024]{1,0:T(8,128)(2,1)S(1)} %copy-done, s32[1,1024]{1,0:T(1,128)S(1)} %copy-done.1), custom_call_target="tpu_custom_call" | custom-call | flops 1000 | bytes 1000 | tf_op jit(solution)/shard_map/pack_first/pallas_call | solution.py:80
  4.4 0.1 collective-permute-start.3
  4.5 3.3 %collective-permute-start.4 = (bf16[256,1024]{1,0:T(8,128)(2,1)S(1)}, bf16[256,1024]{1,0:T(8,128)(2,1)S(1)}, u32[]{:S(2)}, u32[]{:S(2)}) collective-permute-start(bf16[256,1024]{1,0:T(8,128)(2,1)S(1)} %get-tuple-element.39), channel_id=1, source_target_pairs={{0,10},{2,8},{4,14},{6,12},{8,2},{10,0},{12,6},{14,4},{1,11},{3,9}... | collective-permute-start | bytes 1572872 | tf_op jit(solution)/shard_map/ppermute | solution.py:257
  7.8 2.7 %pack_rest.2 = (bf16[256,1024]{1,0:T(8,128)(2,1)S(1)}, bf16[256,1024]{1,0:T(8,128)(2,1)S(1)}, bf16[256,1024]{1,0:T(8,128)(2,1)S(1)}, bf16[256,1024]{1,0:T(8,128)(2,1)S(1)}) custom-call(bf16[1024,1024]{1,0:T(8,128)(2,1)S(1)} %get-tuple-element.29.unit, s32[1,1024]{1,0:T(1,128)S(1)} %get-tuple-element.30.tgt), custom_call_target="tpu_custom_call" | custom-call | flops 1000 | bytes 1000 | tf_op jit(solution)/shard_map/pack_rest/pallas_call | solution.py:80
  10.5 0.3 collective-permute-start
  10.7 1.3 %collective-permute-start.1 = (bf16[256,1024]{1,0:T(8,128)(2,1)S(1)}, bf16[256,1024]{1,0:T(8,128)(2,1)S(1)}, u32[]{:S(2)}, u32[]{:S(2)}) collective-permute-start(bf16[256,1024]{1,0:T(8,128)(2,1)S(1)} %get-tuple-element.33), channel_id=1, source_target_pairs={{0,4},{2,6},{4,0},{6,2},{8,12},{10,14},{12,8},{14,10},{1,5},{3,7},... | collective-permute-start | bytes 1572872 | tf_op jit(solution)/shard_map/ppermute | solution.py:257
  12.0 1.1 %collective-permute-start.2 = (bf16[256,1024]{1,0:T(8,128)(2,1)S(1)}, bf16[256,1024]{1,0:T(8,128)(2,1)S(1)}, u32[]{:S(2)}, u32[]{:S(2)}) collective-permute-start(bf16[256,1024]{1,0:T(8,128)(2,1)S(1)} %get-tuple-element.34), channel_id=1, source_target_pairs={{0,6},{2,4},{4,2},{6,0},{8,14},{10,12},{12,10},{14,8},{1,7},{3,5},... | collective-permute-start | bytes 1572872 | tf_op jit(solution)/shard_map/ppermute | solution.py:257
  13.2 1.4 %pack_rest.3 = (bf16[256,1024]{1,0:T(8,128)(2,1)S(1)}, bf16[256,1024]{1,0:T(8,128)(2,1)S(1)}) custom-call(bf16[1024,1024]{1,0:T(8,128)(2,1)S(1)} %get-tuple-element.29.unit, s32[1,1024]{1,0:T(1,128)S(1)} %get-tuple-element.30.tgt), custom_call_target="tpu_custom_call" | custom-call | flops 1000 | bytes 1000 | tf_op jit(solution)/shard_map/pack_rest/pallas_call | solution.py:80
  14.6 23.3 %collective-permute-done.3.refs_4_ = bf16[256,1024]{1,0:T(8,128)(2,1)S(1)} collective-permute-done((bf16[256,1024]{1,0:T(8,128)(2,1)S(1)}, bf16[256,1024]{1,0:T(8,128)(2,1)S(1)}, u32[]{:S(2)}, u32[]{:S(2)}) %collective-permute-start.3) | collective-permute-done | bytes 524320 | tf_op jit(solution)/shard_map/ppermute | solution.py:257
  37.9 3.1 %collective-permute-start.5 = (bf16[256,1024]{1,0:T(8,128)(2,1)S(1)}, bf16[256,1024]{1,0:T(8,128)(2,1)S(1)}, u32[]{:S(2)}, u32[]{:S(2)}) collective-permute-start(bf16[256,1024]{1,0:T(8,128)(2,1)S(1)} %get-tuple-element.42), channel_id=1, source_target_pairs={{0,12},{2,14},{4,8},{6,10},{8,4},{10,6},{12,0},{14,2},{1,13},{3,15... | collective-permute-start | bytes 1572872 | tf_op jit(solution)/shard_map/ppermute | solution.py:257
  41.0 8.1 %collective-permute-done.4.refs_5_ = bf16[256,1024]{1,0:T(8,128)(2,1)S(1)} collective-permute-done((bf16[256,1024]{1,0:T(8,128)(2,1)S(1)}, bf16[256,1024]{1,0:T(8,128)(2,1)S(1)}, u32[]{:S(2)}, u32[]{:S(2)}) %collective-permute-start.4) | collective-permute-done | bytes 524320 | tf_op jit(solution)/shard_map/ppermute | solution.py:257
  49.1 4.6 %collective-permute-start.6 = (bf16[256,1024]{1,0:T(8,128)(2,1)S(1)}, bf16[256,1024]{1,0:T(8,128)(2,1)S(1)}, u32[]{:S(2)}, u32[]{:S(2)}) collective-permute-start(bf16[256,1024]{1,0:T(8,128)(2,1)S(1)} %get-tuple-element.47), channel_id=1, source_target_pairs={{0,14},{2,12},{4,10},{6,8},{8,6},{10,4},{12,2},{14,0},{1,15},{3,13... | collective-permute-start | bytes 1572872 | tf_op jit(solution)/shard_map/ppermute | solution.py:257
  53.7 0.0 collective-permute-done.refs_1_
  53.7 0.0 collective-permute-done.1.refs_2_
  53.7 24.1 %collective-permute-done.2.refs_3_ = bf16[256,1024]{1,0:T(8,128)(2,1)S(1)} collective-permute-done((bf16[256,1024]{1,0:T(8,128)(2,1)S(1)}, bf16[256,1024]{1,0:T(8,128)(2,1)S(1)}, u32[]{:S(2)}, u32[]{:S(2)}) %collective-permute-start.2) | collective-permute-done | bytes 524320 | tf_op jit(solution)/shard_map/ppermute | solution.py:257
  77.8 3.0 %own_early.1 = (bf16[2,2,768,1024]{3,2,1,0:T(8,128)(2,1)S(1)}, f32[2,1024]{1,0:T(2,128)S(1)}) custom-call(bf16[256,1024]{1,0:T(8,128)(2,1)S(1)} %get-tuple-element.31.refs_0_, bf16[256,1024]{1,0:T(8,128)(2,1)S(1)} %collective-permute-done.refs_1_, bf16[256,1024]{1,0:T(8,128)(2,1)S(1)} %collective-permute-done.1.refs_2_, ...), custom_call_target="tpu_custom_call" | custom-call | flops 1000 | bytes 1000 | tf_op jit(solution)/shard_map/own_early/pallas_call | solution.py:80
  80.8 10.9 %all_to_all.10.refs_0_ = bf16[2,2,768,1024]{3,2,1,0:T(8,128)(2,1)S(1)} all-to-all(bf16[2,2,768,1024]{3,2,1,0:T(8,128)(2,1)S(1)} %get-tuple-element.41), channel_id=1, replica_groups=mesh['groups'=2,'clus'=8,'blk'=2] {'blk'}, dimensions={0} | all-to-all | bytes 12582912 | tf_op jit(solution)/shard_map/all_to_all | solution.py:263
  91.7 2.7 %cross_early.1.refs_1_ = f32[2,1024]{1,0:T(2,128)S(1)} custom-call(bf16[2,2,768,1024]{3,2,1,0:T(8,128)(2,1)S(1)} %all_to_all.10.refs_0_, f32[2,1024]{1,0:T(2,128)S(1)} %get-tuple-element.43.refs_1_), custom_call_target="tpu_custom_call" | custom-call | flops 1000 | bytes 1000 | tf_op jit(solution)/shard_map/cross_early/pallas_call | solution.py:80
  94.4 0.0 collective-permute-done.5.refs_2_
  94.4 2.3 %own_middle.1 = (bf16[2,2,128,1024]{3,2,1,0:T(8,128)(2,1)S(1)}, f32[2,1024]{1,0:T(2,128)S(1)}) custom-call(bf16[2,2,768,1024]{3,2,1,0:T(8,128)(2,1)S(1)} %all_to_all.10.refs_0_, f32[2,1024]{1,0:T(2,128)S(1)} %cross_early.1.refs_1_, bf16[256,1024]{1,0:T(8,128)(2,1)S(1)} %collective-permute-done.5.refs_2_), custom_call_target="tpu_custom_call" | custom-call | flops 1000 | bytes 1000 | tf_op jit(solution)/shard_map/own_middle/pallas_call | solution.py:80
  96.7 4.2 %all_to_all.11.refs_1_ = bf16[2,2,128,1024]{3,2,1,0:T(8,128)(2,1)S(1)} all-to-all(bf16[2,2,128,1024]{3,2,1,0:T(8,128)(2,1)S(1)} %get-tuple-element.46), channel_id=1, replica_groups=mesh['groups'=2,'clus'=8,'blk'=2] {'blk'}, dimensions={0} | all-to-all | bytes 2097152 | tf_op jit(solution)/shard_map/all_to_all | solution.py:263
  100.9 2.0 %cross_middle.1.refs_2_ = f32[2,1024]{1,0:T(2,128)S(1)} custom-call(bf16[2,2,768,1024]{3,2,1,0:T(8,128)(2,1)S(1)} %all_to_all.10.refs_0_, bf16[2,2,128,1024]{3,2,1,0:T(8,128)(2,1)S(1)} %all_to_all.11.refs_1_, f32[2,1024]{1,0:T(2,128)S(1)} %get-tuple-element.48.refs_2_), custom_call_target="tpu_custom_call" | custom-call | flops 1000 | bytes 1000 | tf_op jit(solution)/shard_map/cross_middle/pallas_call | solution.py:80
  103.0 0.0 collective-permute-done.6.refs_3_
  103.0 1.3 %collective-permute-start.7 = (bf16[256,1024]{1,0:T(8,128)(2,1)S(1)}, bf16[256,1024]{1,0:T(8,128)(2,1)S(1)}, u32[]{:S(2)}, u32[]{:S(2)}) collective-permute-start(bf16[256,1024]{1,0:T(8,128)(2,1)S(1)} %collective-permute-done.6.refs_3_), channel_id=1, source_target_pairs={{0,1},{2,3},{4,5},{6,7},{8,9},{10,11},{12,13},{14,15},{16,17},{18,... | collective-permute-start | bytes 1572872 | tf_op jit(solution)/shard_map/ppermute | solution.py:310
  104.3 2.6 %own_last.1 = (bf16[2,2,128,1024]{3,2,1,0:T(8,128)(2,1)S(1)}, f32[2,1024]{1,0:T(2,128)S(1)}) custom-call(bf16[2,2,768,1024]{3,2,1,0:T(8,128)(2,1)S(1)} %all_to_all.10.refs_0_, bf16[2,2,128,1024]{3,2,1,0:T(8,128)(2,1)S(1)} %all_to_all.11.refs_1_, f32[2,1024]{1,0:T(2,128)S(1)} %cross_middle.1.refs_2_, bf16[256,1024]{1,0:T(8,128)(2,1)S(1)} %collective-permute-done.6.refs_3_), custom_call_target="tpu_custom_call" | custom-call | flops 1000 | bytes 1000 | tf_op jit(solution)/shard_map/own_last/pallas_call | solution.py:80
  106.9 0.0 collective-permute-done.7.refs_4_
  106.9 3.2 %cross_last.1 = f32[2,1024]{1,0:T(2,128)} custom-call(bf16[2,2,768,1024]{3,2,1,0:T(8,128)(2,1)S(1)} %all_to_all.10.refs_0_, bf16[2,2,128,1024]{3,2,1,0:T(8,128)(2,1)S(1)} %all_to_all.11.refs_1_, bf16[2,2,128,1024]{3,2,1,0:T(8,128)(2,1)S(1)} %get-tuple-element.51.refs_2_, f32[2,1024]{1,0:T(2,128)S(1)} %get-tuple-element.52.refs_3_, ...), custom_call_target="tpu_custom_call" | custom-call | flops 1000 | bytes 1000 | tf_op jit(solution)/shard_map/cross_last/pallas_call | solution.py:80
Async XLA Ops:
  0.0 1.6 %copy-start = (bf16[1024,1024]{1,0:T(8,128)(2,1)S(1)}, bf16[1024,1024]{1,0:T(8,128)(2,1)}, u32[]{:S(2)}) copy-start(bf16[1024,1024]{1,0:T(8,128)(2,1)} %emb.1) | copy-start | bytes 6291460
  1.6 0.7 copy-start.1
  4.4 33.5 %collective-permute-start.3 = (bf16[256,1024]{1,0:T(8,128)(2,1)S(1)}, bf16[256,1024]{1,0:T(8,128)(2,1)S(1)}, u32[]{:S(2)}, u32[]{:S(2)}) collective-permute-start(bf16[256,1024]{1,0:T(8,128)(2,1)S(1)} %get-tuple-element.36), channel_id=1, source_target_pairs={{0,8},{2,10},{4,12},{6,14},{8,0},{10,2},{12,4},{14,6},{1,9},{3,11}... | collective-permute-start | bytes 1572872 | tf_op jit(solution)/shard_map/ppermute | solution.py:257
  4.5 44.7 %collective-permute-start.4 = (bf16[256,1024]{1,0:T(8,128)(2,1)S(1)}, bf16[256,1024]{1,0:T(8,128)(2,1)S(1)}, u32[]{:S(2)}, u32[]{:S(2)}) collective-permute-start(bf16[256,1024]{1,0:T(8,128)(2,1)S(1)} %get-tuple-element.39), channel_id=1, source_target_pairs={{0,10},{2,8},{4,14},{6,12},{8,2},{10,0},{12,6},{14,4},{1,11},{3,9}... | collective-permute-start | bytes 1572872 | tf_op jit(solution)/shard_map/ppermute | solution.py:257
  10.5 43.2 %collective-permute-start = (bf16[256,1024]{1,0:T(8,128)(2,1)S(1)}, bf16[256,1024]{1,0:T(8,128)(2,1)S(1)}, u32[]{:S(2)}, u32[]{:S(2)}) collective-permute-start(bf16[256,1024]{1,0:T(8,128)(2,1)S(1)} %get-tuple-element.32), channel_id=1, source_target_pairs={{0,2},{2,0},{4,6},{6,4},{8,10},{10,8},{12,14},{14,12},{1,3},{3,1},... | collective-permute-start | bytes 1572872 | tf_op jit(solution)/shard_map/ppermute | solution.py:257
  10.7 43.0 %collective-permute-start.1 = (bf16[256,1024]{1,0:T(8,128)(2,1)S(1)}, bf16[256,1024]{1,0:T(8,128)(2,1)S(1)}, u32[]{:S(2)}, u32[]{:S(2)}) collective-permute-start(bf16[256,1024]{1,0:T(8,128)(2,1)S(1)} %get-tuple-element.33), channel_id=1, source_target_pairs={{0,4},{2,6},{4,0},{6,2},{8,12},{10,14},{12,8},{14,10},{1,5},{3,7},... | collective-permute-start | bytes 1572872 | tf_op jit(solution)/shard_map/ppermute | solution.py:257
  12.0 65.8 %collective-permute-start.2 = (bf16[256,1024]{1,0:T(8,128)(2,1)S(1)}, bf16[256,1024]{1,0:T(8,128)(2,1)S(1)}, u32[]{:S(2)}, u32[]{:S(2)}) collective-permute-start(bf16[256,1024]{1,0:T(8,128)(2,1)S(1)} %get-tuple-element.34), channel_id=1, source_target_pairs={{0,6},{2,4},{4,2},{6,0},{8,14},{10,12},{12,10},{14,8},{1,7},{3,5},... | collective-permute-start | bytes 1572872 | tf_op jit(solution)/shard_map/ppermute | solution.py:257
  37.9 56.5 %collective-permute-start.5 = (bf16[256,1024]{1,0:T(8,128)(2,1)S(1)}, bf16[256,1024]{1,0:T(8,128)(2,1)S(1)}, u32[]{:S(2)}, u32[]{:S(2)}) collective-permute-start(bf16[256,1024]{1,0:T(8,128)(2,1)S(1)} %get-tuple-element.42), channel_id=1, source_target_pairs={{0,12},{2,14},{4,8},{6,10},{8,4},{10,6},{12,0},{14,2},{1,13},{3,15... | collective-permute-start | bytes 1572872 | tf_op jit(solution)/shard_map/ppermute | solution.py:257
  49.1 53.8 %collective-permute-start.6 = (bf16[256,1024]{1,0:T(8,128)(2,1)S(1)}, bf16[256,1024]{1,0:T(8,128)(2,1)S(1)}, u32[]{:S(2)}, u32[]{:S(2)}) collective-permute-start(bf16[256,1024]{1,0:T(8,128)(2,1)S(1)} %get-tuple-element.47), channel_id=1, source_target_pairs={{0,14},{2,12},{4,10},{6,8},{8,6},{10,4},{12,2},{14,0},{1,15},{3,13... | collective-permute-start | bytes 1572872 | tf_op jit(solution)/shard_map/ppermute | solution.py:257
  103.0 3.9 %collective-permute-start.7 = (bf16[256,1024]{1,0:T(8,128)(2,1)S(1)}, bf16[256,1024]{1,0:T(8,128)(2,1)S(1)}, u32[]{:S(2)}, u32[]{:S(2)}) collective-permute-start(bf16[256,1024]{1,0:T(8,128)(2,1)S(1)} %collective-permute-done.6.refs_3_), channel_id=1, source_target_pairs={{0,1},{2,3},{4,5},{6,7},{8,9},{10,11},{12,13},{14,15},{16,17},{18,... | collective-permute-start | bytes 1572872 | tf_op jit(solution)/shard_map/ppermute | solution.py:310

commit v8 on v4

v8 whole, which is shorter than its diff:
```python
import functools

import jax
import jax.numpy as jnp
from jax import lax
from jax.experimental import pallas as pl
from jax.experimental.pallas import tpu as pltpu
from jax.sharding import PartitionSpec as P

CLUS_DEV = 2
LANES = 128
MARK = 2.0
BF = jnp.bfloat16
F32 = jnp.float32


def iota(shape, dim):
    return lax.broadcasted_iota(jnp.int32, shape, dim)


def matmul(a, b, contract):
    return lax.dot_general(a, b, (contract, ((), ())), preferred_element_type=F32)


def targets(ids, clusters, per_source):
    groups = ids.shape[1] // LANES
    parts = [ids[:, g * LANES : (g + 1) * LANES] for g in range(groups)]
    hot = jnp.concatenate(
        [(iota((clusters, LANES), 0) == part).astype(F32) for part in parts], axis=0
    )
    stacked = groups * clusters
    earlier = (iota((LANES, LANES), 0) < iota((LANES, LANES), 1)).astype(F32).astype(BF)
    within = matmul(hot.astype(BF), earlier, ((1,), (0,)))
    totals = jnp.broadcast_to(jnp.sum(hot, axis=1, keepdims=True), (stacked, LANES))
    a, b = iota((stacked, stacked), 0), iota((stacked, stacked), 1)
    chunks_before = ((a % clusters == b % clusters) & (b < a)).astype(F32).astype(BF)
    before = within + matmul(chunks_before, totals.astype(BF), ((1,), (0,)))
    picked = hot * before
    out = [
        jnp.sum(picked[g * clusters : (g + 1) * clusters], axis=0, keepdims=True).astype(jnp.int32)
        + parts[g] * per_source
        for g in range(groups)
    ]
    return jnp.concatenate(out, axis=1)


def store_blocks(unit, tgt, picks, outs):
    me = lax.axis_index("clus")
    per = outs[0].shape[0]
    hits = [
        (tgt - ((me ^ step) * CLUS_DEV + cluster) * per == iota((per, tgt.shape[1]), 0)).astype(F32)
        for step, cluster in picks
    ]
    hot = jnp.concatenate(hits, axis=0) if len(hits) > 1 else hits[0]
    rows = matmul(hot.astype(BF), unit, ((1,), (0,)))
    empty = jnp.max(hot, axis=1, keepdims=True) < 0.5
    marked = jnp.where(empty, F32(MARK), rows[:, :LANES])
    for k, out in enumerate(outs):
        window = slice(k * per, (k + 1) * per)
        out[:, :LANES] = marked[window].astype(BF)
        out[:, LANES:] = rows[window, LANES:].astype(BF)


def pack_first(picks, clusters, emb, ids, unit, tgt, *outs):
    values = emb[...].astype(F32)
    scale = lax.rsqrt(jnp.sum(values * values, axis=1, keepdims=True) + 1e-6)
    unit[...] = (values * scale).astype(BF)
    tgt[...] = targets(ids[...], clusters, outs[0].shape[0])
    store_blocks(unit[...], tgt[...], picks, outs)


def pack_rest(picks, unit, tgt, *outs):
    store_blocks(unit[...], tgt[...], picks, outs)


VMEM = pl.BlockSpec(memory_space=pltpu.VMEM)


def kernel_call(kernel, shapes, inputs, name, scratch=()):
    return pl.pallas_call(
        kernel,
        out_shape=shapes,
        in_specs=[VMEM] * len(inputs),
        out_specs=[VMEM] * len(shapes),
        scratch_shapes=scratch,
        compiler_params=pltpu.CompilerParams(vmem_limit_bytes=20 * 2**20),
        cost_estimate=pl.CostEstimate(flops=1000, bytes_accessed=1000, transcendentals=0),
        name=name,
    )(*inputs)


CHUNK = 256


def raise_best(best, keys, queries, triangular=False):
    rows = queries.shape[0]
    for start in range(0, rows, CHUNK):
        chunk = min(CHUNK, rows - start)
        count = start + chunk if triangular else keys.shape[0]
        sims = matmul(keys[:count, :], queries[start : start + chunk, :], ((1,), (1,)))
        filled = keys[:count, :LANES].astype(F32) < 1.5
        for first in range(0, chunk, LANES):
            allowed = filled
            if triangular:
                allowed = filled & (
                    iota((count, LANES), 0) < iota((count, LANES), 1) + (start + first)
                )
            part = jnp.where(allowed, sims[:, first : first + LANES], F32(-1.0))
            window = slice(start + first, start + first + LANES)
            best[:, window] = jnp.maximum(best[:, window], jnp.max(part, axis=0, keepdims=True))


def gather_group(blocks, out, me):
    per = blocks[0].shape[0]
    for step, block in enumerate(blocks):
        place = (me & (len(blocks) - 1)) ^ step
        out[pl.ds(pl.multiple_of(place * per, per), per), :] = block[...]


def score_pair(bests, groups, new, old, bit, me):
    later = (me & bit) == 0

    @pl.when(later)
    def _():
        raise_best(bests[new], groups[old], groups[new])

    @pl.when(jnp.logical_not(later))
    def _():
        raise_best(bests[old], groups[new], groups[old])


def own_stage(cuts, bits, held, first, *refs):
    stages, refs = refs[:held], refs[held:]
    blocks, (send, best) = list(refs[:-2]), refs[-2:]
    before = blocks.pop(0) if held else None
    per = blocks[0].shape[0]
    me = lax.axis_index("clus")
    core = lax.axis_index("blk")
    spans = list(zip(cuts, cuts[1:]))
    base = spans[first][0]
    if held:
        best[:, :base] = before[:, :base]
    best[:, base:] = jnp.full((1, best.shape[1] - base), -1.0, F32)
    rows = [best.at[:, a:b] for a, b in spans]
    groups = []
    for stage in stages:
        start = spans[len(groups)][0]
        end = start + stage.shape[1]
        while len(groups) < first and spans[len(groups)][0] < end:
            a, b = spans[len(groups)]
            groups.append(stage.at[core, a - start : b - start])
    for i in range(first, len(spans)):
        a, b = spans[i]
        group = send.at[1, a - base : b - base]
        gather_group(blocks[(a - base) // per : (b - base) // per], group, me)
        groups.append(group)
        raise_best(rows[i], group, group, True)
        for j in range(i):
            score_pair(rows, groups, i, j, bits[j], me)
    send[0] = send[1]


def cross_stage(received, before, best):
    best[...] = before[...]

    @pl.when(lax.axis_index("blk") == 1)
    def _():
        raise_best(best.at[:, : received.shape[1]], received.at[0], received.at[1])


def filled_queries(rows):
    ones = jnp.ones((8, LANES), BF)
    return matmul(ones, rows[:, :LANES], ((1,), (1,)))[:1] < 100.0


def finish(cuts, per, whole, best, out, row):
    me = lax.axis_index("clus")
    base = 0
    for rows in whole:
        size = rows.shape[0]
        kept = jnp.where(filled_queries(rows), best[:, base : base + size], F32(0.0))
        for a, b in zip(cuts, cuts[1:]):
            if base <= a < base + size:
                place = (me ^ (a // per)) & ~((b - a) // per - 1)
                at = pl.ds(pl.multiple_of(place * per, LANES), b - a)
                out[row : row + 1, at] = kept[:, a - base : b - base]
        base += size


def cross_whole(cuts, per, received, before, out, best):
    cross_stage(received, before, best)
    finish(cuts, per, [received.at[lax.axis_index("blk")]], best, out, 0)


def cross_last(cuts, received, send, before, ready, *refs):
    others, (out, keys, best) = refs[:-3], refs[-3:]
    per = others[0].shape[0]
    core = lax.axis_index("blk")
    best[...] = before[...]
    start = received.shape[1]

    @pl.when(core == 1)
    def _():
        for i, other in enumerate(others):
            keys[i * per : (i + 1) * per, :] = other[...]
        raise_best(best.at[:, :start], keys, received.at[1])
        raise_best(best.at[:, start:], received.at[0], send.at[1])
        raise_best(best.at[:, start:], keys, send.at[1])

    out[0:1, :] = ready[...]
    finish(cuts, per, [received.at[core], send.at[1]], best, out, 1)


def local(embeddings, cluster_ids):
    owners = lax.axis_size("clus")
    clusters = CLUS_DEV * owners
    rows, width = embeddings.shape
    per = 2 * rows // clusters
    bits = [owners // 2, owners // 4, owners // 8]
    bounds = [0, owners // 2, owners // 2 + owners // 4, owners - owners // 8, owners]
    cuts = [x * per for x in bounds]
    near, far1, far2, far3 = [list(range(a, b)) for a, b in zip(bounds, bounds[1:])]
    best_shape = jax.ShapeDtypeStruct((1, rows), F32)
    block = jax.ShapeDtypeStruct((per, width), BF)

    def to_owner(block, step):
        return lax.ppermute(block, "clus", [(i, i ^ step) for i in range(owners)])

    def stage_shape(sources):
        return jax.ShapeDtypeStruct((2, sources * per, width), BF)

    def to_both(send):
        return lax.all_to_all(send, "blk", split_axis=0, concat_axis=0, tiled=True)

    arrived = [{}, {}]

    def dispatch(picks, packed):
        for (step, cluster), block in zip(picks, packed):
            arrived[cluster][step] = to_owner(block, step) if step else block

    picks = [(step, 0) for step in far1]
    unit, tgt, *packed = kernel_call(
        functools.partial(pack_first, picks, clusters),
        [
            jax.ShapeDtypeStruct(embeddings.shape, BF),
            jax.ShapeDtypeStruct(cluster_ids.shape, jnp.int32),
        ]
        + [block] * len(picks),
        [embeddings, cluster_ids],
        "pack_first",
    )
    dispatch(picks, packed)
    for steps, cluster in (
        (near[1:] + [0], 0),
        (far2 + far3, 0),
        (far1 + near, 1),
        (far2 + far3, 1),
    ):
        picks = [(step, cluster) for step in steps]
        packed = kernel_call(
            functools.partial(pack_rest, picks), [block] * len(picks), [unit, tgt], "pack_rest"
        )
        dispatch(picks, packed)

    send, best = kernel_call(
        functools.partial(own_stage, cuts, bits, 0, 0),
        [stage_shape(owners), best_shape],
        [arrived[0][s] for s in near + far1 + far2 + far3],
        "own_whole",
    )
    (ready,) = kernel_call(
        functools.partial(cross_whole, cuts, per),
        [best_shape],
        [to_both(send), best],
        "cross_whole",
        [pltpu.VMEM((1, rows), F32)],
    )
    order = far1 + near
    *early, ready = lax.optimization_barrier((*[arrived[1][s] for s in order], ready))
    early = [early[order.index(s)] for s in near + far1]
    send, best = kernel_call(
        functools.partial(own_stage, cuts[:3], bits, 0, 0),
        [stage_shape(len(early)), best_shape],
        early,
        "own_early",
    )
    received = to_both(send)
    (best,) = kernel_call(cross_stage, [best_shape], [received, best], "cross_early")
    *late, best = lax.optimization_barrier((*[arrived[1][s] for s in far2 + far3], best))
    send, best = kernel_call(
        functools.partial(own_stage, cuts, bits, 1, 2),
        [stage_shape(len(late)), best_shape],
        [received, best] + late,
        "own_last",
    )
    others = [lax.ppermute(block, "blk", [(0, 1)]) for block in late]
    (out,) = kernel_call(
        functools.partial(cross_last, cuts),
        [jax.ShapeDtypeStruct((CLUS_DEV, rows), F32)],
        [received, send, best, ready] + others,
        "cross_last",
        [pltpu.VMEM((len(late) * per, width), BF), pltpu.VMEM((1, rows), F32)],
    )
    return out


def solution(mesh):
    placed = (P(("groups", "clus", "blk"), None), P(("groups", "clus", "blk"), None))
    return jax.shard_map(
        local, mesh=mesh, in_specs=placed, out_specs=P(("groups", "clus"), "blk"), check_vma=False
    )
```

time: 112 us -> 114 us (1.018)
  starting transfers between devices: 13.7 us -> 43.3 us
  blocking collectives: 37.5 us -> 14.9 us
  waiting for transfers between devices: 36.5 us -> 32.7 us
  Pallas kernels: 22.1 us -> 20 us
    ppermute x7 -> x14, starting transfers between devices: 12.4 us -> 40.8 us  [to_owner(): return lax.ppermute(block, 'clus', [(i, i ^ step) for i in range(owners)])]
    all_to_all x2, blocking collectives: 37.5 us -> 14.9 us  [to_both(): return lax.all_to_all(send, 'blk', split_axis=0, concat_axis=0, tiled=True)]
    ppermute x7 -> x14, waiting for transfers between devices: 36.5 us -> 32.7 us  [to_owner(): return lax.ppermute(block, 'clus', [(i, i ^ step) for i in range(owners)])]
    pallas_call x10 -> x11, Pallas kernels: 22.1 us -> 20 us  [kernel_call(): pl.pallas_call(kernel, out_shape=shapes, in_specs=[VMEM] * len(inputs), o...]
    ppermute x1 -> x2, starting transfers between devices: 1.29 us -> 2.58 us  [local(): others = [lax.ppermute(block, 'blk', [(0, 1)]) for block in late]]
  transfers between devices with their start and end apart: 8 -> 16, of which waited for: 3 -> 5; matrix products, arithmetic and copies ran while one was open for 0% -> 0% of each run, Pallas kernels for 15% -> 15%
where the time goes in v8:
time: 114 us; the launch traced here: 113 us
  starting transfers between devices  43.3 us (38%)
  waiting for transfers between devices  32.7 us (29%)
  Pallas kernels  20 us (18%)
  blocking collectives  14.9 us (13%)
  local copies, waits for them, and re-layouts  2.28 us (2%)
    ppermute x14, starting transfers between devices, to_owner(): return lax.ppermute(block, 'clus', [(i, i ^ step) for i in range(owners)])  40.8 us
    ppermute x14, waiting for transfers between devices, to_owner(): return lax.ppermute(block, 'clus', [(i, i ^ step) for i in range(owners)])  32.7 us
    pallas_call x11, Pallas kernels, kernel_call(): pl.pallas_call(kernel, out_shape=shapes, in_specs=[VMEM] * len(inputs), o...  20 us
    all_to_all x2, blocking collectives, to_both(): return lax.all_to_all(send, 'blk', split_axis=0, concat_axis=0, tiled=True)  14.9 us
    ppermute x2, starting transfers between devices, local(): others = [lax.ppermute(block, 'blk', [(0, 1)]) for block in late]  2.58 us
  transfers between devices with their start and end apart: 16, of which 5 were waited for; matrix products, arithmetic and copies ran while one was open for 0% of the time, Pallas kernels for 15%

profile of v8, /device:TPU:1, one launch (start us, length us, event | category | flops | bytes accessed | tf_op | source)
XLA Modules:
  0.0 113.4 jit_solution(11191099136640088657)
XLA Ops:
  0.0 1.6 %copy-done = bf16[1024,1024]{1,0:T(8,128)(2,1)S(1)} copy-done((bf16[1024,1024]{1,0:T(8,128)(2,1)S(1)}, bf16[1024,1024]{1,0:T(8,128)(2,1)}, u32[]{:S(2)}) %copy-start) | copy-done | bytes 2097176
  2.3 1.5 %pack_first.1 = (bf16[1024,1024]{1,0:T(8,128)(2,1)S(1)}, s32[1,1024]{1,0:T(1,128)S(1)}, bf16[128,1024]{1,0:T(8,128)(2,1)S(1)}, bf16[128,1024]{1,0:T(8,128)(2,1)S(1)}) custom-call(bf16[1024,1024]{1,0:T(8,128)(2,1)S(1)} %copy-done, s32[1,1024]{1,0:T(1,128)S(1)} %copy-done.1), custom_call_target="tpu_custom_call" | custom-call | flops 1000 | bytes 1000 | tf_op jit(solution)/shard_map/pack_first/pallas_call | solution.py:80
  3.7 3.2 %collective-permute-start.8 = (bf16[128,1024]{1,0:T(8,128)(2,1)S(1)}, bf16[128,1024]{1,0:T(8,128)(2,1)S(1)}, u32[]{:S(2)}, u32[]{:S(2)}) collective-permute-start(bf16[128,1024]{1,0:T(8,128)(2,1)S(1)} %get-tuple-element.51), channel_id=1, source_target_pairs={{0,8},{2,10},{4,12},{6,14},{8,0},{10,2},{12,4},{14,6},{1,9},{3,11}... | collective-permute-start | bytes 786440 | tf_op jit(solution)/shard_map/ppermute | solution.py:227
  7.0 1.0 collective-permute-start.9
  8.0 0.8 pack_rest.6
  8.8 3.3 %collective-permute-start.10 = (bf16[128,1024]{1,0:T(8,128)(2,1)S(1)}, bf16[128,1024]{1,0:T(8,128)(2,1)S(1)}, u32[]{:S(2)}, u32[]{:S(2)}) collective-permute-start(bf16[128,1024]{1,0:T(8,128)(2,1)S(1)} %get-tuple-element.53), channel_id=1, source_target_pairs={{0,12},{2,14},{4,8},{6,10},{8,4},{10,6},{12,0},{14,2},{1,13},{3,15... | collective-permute-start | bytes 786440 | tf_op jit(solution)/shard_map/ppermute | solution.py:227
  12.2 1.4 %pack_rest.5 = (bf16[128,1024]{1,0:T(8,128)(2,1)S(1)}, bf16[128,1024]{1,0:T(8,128)(2,1)S(1)}, bf16[128,1024]{1,0:T(8,128)(2,1)S(1)}, bf16[128,1024]{1,0:T(8,128)(2,1)S(1)}) custom-call(bf16[1024,1024]{1,0:T(8,128)(2,1)S(1)} %get-tuple-element.39.unit, s32[1,1024]{1,0:T(1,128)S(1)} %get-tuple-element.40.tgt), custom_call_target="tpu_custom_call" | custom-call | flops 1000 | bytes 1000 | tf_op jit(solution)/shard_map/pack_rest/pallas_call | solution.py:80
  13.6 1.3 %collective-permute-start.5 = (bf16[128,1024]{1,0:T(8,128)(2,1)S(1)}, bf16[128,1024]{1,0:T(8,128)(2,1)S(1)}, u32[]{:S(2)}, u32[]{:S(2)}) collective-permute-start(bf16[128,1024]{1,0:T(8,128)(2,1)S(1)} %get-tuple-element.48), channel_id=1, source_target_pairs={{0,2},{2,0},{4,6},{6,4},{8,10},{10,8},{12,14},{14,12},{1,3},{3,1},... | collective-permute-start | bytes 786440 | tf_op jit(solution)/shard_map/ppermute | solution.py:227
  14.9 20.5 %collective-permute-done.8.refs_4_ = bf16[128,1024]{1,0:T(8,128)(2,1)S(1)} collective-permute-done((bf16[128,1024]{1,0:T(8,128)(2,1)S(1)}, bf16[128,1024]{1,0:T(8,128)(2,1)S(1)}, u32[]{:S(2)}, u32[]{:S(2)}) %collective-permute-start.8) | collective-permute-done | bytes 262176 | tf_op jit(solution)/shard_map/ppermute | solution.py:227
  35.5 1.2 %collective-permute-start.6 = (bf16[128,1024]{1,0:T(8,128)(2,1)S(1)}, bf16[128,1024]{1,0:T(8,128)(2,1)S(1)}, u32[]{:S(2)}, u32[]{:S(2)}) collective-permute-start(bf16[128,1024]{1,0:T(8,128)(2,1)S(1)} %get-tuple-element.49), channel_id=1, source_target_pairs={{0,4},{2,6},{4,0},{6,2},{8,12},{10,14},{12,8},{14,10},{1,5},{3,7},... | collective-permute-start | bytes 786440 | tf_op jit(solution)/shard_map/ppermute | solution.py:227
  36.6 5.2 %collective-permute-done.9.refs_5_ = bf16[128,1024]{1,0:T(8,128)(2,1)S(1)} collective-permute-done((bf16[128,1024]{1,0:T(8,128)(2,1)S(1)}, bf16[128,1024]{1,0:T(8,128)(2,1)S(1)}, u32[]{:S(2)}, u32[]{:S(2)}) %collective-permute-start.9) | collective-permute-done | bytes 262176 | tf_op jit(solution)/shard_map/ppermute | solution.py:227
  41.8 1.4 %collective-permute-start.7 = (bf16[128,1024]{1,0:T(8,128)(2,1)S(1)}, bf16[128,1024]{1,0:T(8,128)(2,1)S(1)}, u32[]{:S(2)}, u32[]{:S(2)}) collective-permute-start(bf16[128,1024]{1,0:T(8,128)(2,1)S(1)} %get-tuple-element.50), channel_id=1, source_target_pairs={{0,6},{2,4},{4,2},{6,0},{8,14},{10,12},{12,10},{14,8},{1,7},{3,5},... | collective-permute-start | bytes 786440 | tf_op jit(solution)/shard_map/ppermute | solution.py:227
  43.3 2.0 %pack_rest.4 = (bf16[128,1024]{1,0:T(8,128)(2,1)S(1)}, bf16[128,1024]{1,0:T(8,128)(2,1)S(1)}, bf16[128,1024]{1,0:T(8,128)(2,1)S(1)}, bf16[128,1024]{1,0:T(8,128)...) custom-call(bf16[1024,1024]{1,0:T(8,128)(2,1)S(1)} %get-tuple-element.39.unit, ...), custom_call_target="tpu_custom_call" | custom-call | flops 1000 | bytes 1000 | tf_op jit(solution)/shard_map/pack_rest/pallas_call | solution.py:80
  45.3 4.5 %collective-permute-start = (bf16[128,1024]{1,0:T(8,128)(2,1)S(1)}, bf16[128,1024]{1,0:T(8,128)(2,1)S(1)}, u32[]{:S(2)}, u32[]{:S(2)}) collective-permute-start(bf16[128,1024]{1,0:T(8,128)(2,1)S(1)} %get-tuple-element.41), channel_id=1, source_target_pairs={{0,8},{2,10},{4,12},{6,14},{8,0},{10,2},{12,4},{14,6},{1,9},{3,11}... | collective-permute-start | bytes 786440 | tf_op jit(solution)/shard_map/ppermute | solution.py:227
  49.8 13.5 %collective-permute-start.1 = (bf16[128,1024]{1,0:T(8,128)(2,1)S(1)}, bf16[128,1024]{1,0:T(8,128)(2,1)S(1)}, u32[]{:S(2)}, u32[]{:S(2)}) collective-permute-start(bf16[128,1024]{1,0:T(8,128)(2,1)S(1)} %get-tuple-element.42), channel_id=1, source_target_pairs={{0,10},{2,8},{4,14},{6,12},{8,2},{10,0},{12,6},{14,4},{1,11},{3,9}... | collective-permute-start | bytes 786440 | tf_op jit(solution)/shard_map/ppermute | solution.py:227
  63.3 1.2 %collective-permute-start.2 = (bf16[128,1024]{1,0:T(8,128)(2,1)S(1)}, bf16[128,1024]{1,0:T(8,128)(2,1)S(1)}, u32[]{:S(2)}, u32[]{:S(2)}) collective-permute-start(bf16[128,1024]{1,0:T(8,128)(2,1)S(1)} %get-tuple-element.44), channel_id=1, source_target_pairs={{0,2},{2,0},{4,6},{6,4},{8,10},{10,8},{12,14},{14,12},{1,3},{3,1},... | collective-permute-start | bytes 786440 | tf_op jit(solution)/shard_map/ppermute | solution.py:227
  64.5 1.5 %collective-permute-start.4 = (bf16[128,1024]{1,0:T(8,128)(2,1)S(1)}, bf16[128,1024]{1,0:T(8,128)(2,1)S(1)}, u32[]{:S(2)}, u32[]{:S(2)}) collective-permute-start(bf16[128,1024]{1,0:T(8,128)(2,1)S(1)} %get-tuple-element.46), channel_id=1, source_target_pairs={{0,6},{2,4},{4,2},{6,0},{8,14},{10,12},{12,10},{14,8},{1,7},{3,5},... | collective-permute-start | bytes 786440 | tf_op jit(solution)/shard_map/ppermute | solution.py:227
  66.8 3.4 %collective-permute-done.refs_4_ = bf16[128,1024]{1,0:T(8,128)(2,1)S(1)} collective-permute-done((bf16[128,1024]{1,0:T(8,128)(2,1)S(1)}, bf16[128,1024]{1,0:T(8,128)(2,1)S(1)}, u32[]{:S(2)}, u32[]{:S(2)}) %collective-permute-start) | collective-permute-done | bytes 262176 | tf_op jit(solution)/shard_map/ppermute | solution.py:227
  70.2 4.3 %collective-permute-start.12 = (bf16[128,1024]{1,0:T(8,128)(2,1)S(1)}, bf16[128,1024]{1,0:T(8,128)(2,1)S(1)}, u32[]{:S(2)}, u32[]{:S(2)}) collective-permute-start(bf16[128,1024]{1,0:T(8,128)(2,1)S(1)} %get-tuple-element.64), channel_id=1, source_target_pairs={{0,12},{2,14},{4,8},{6,10},{8,4},{10,6},{12,0},{14,2},{1,13},{3,15... | collective-permute-start | bytes 786440 | tf_op jit(solution)/shard_map/ppermute | solution.py:227
  74.6 2.3 %collective-permute-done.1.refs_5_ = bf16[128,1024]{1,0:T(8,128)(2,1)S(1)} collective-permute-done((bf16[128,1024]{1,0:T(8,128)(2,1)S(1)}, bf16[128,1024]{1,0:T(8,128)(2,1)S(1)}, u32[]{:S(2)}, u32[]{:S(2)}) %collective-permute-start.1) | collective-permute-done | bytes 262176 | tf_op jit(solution)/shard_map/ppermute | solution.py:227
  76.9 4.2 %collective-permute-start.13 = (bf16[128,1024]{1,0:T(8,128)(2,1)S(1)}, bf16[128,1024]{1,0:T(8,128)(2,1)S(1)}, u32[]{:S(2)}, u32[]{:S(2)}) collective-permute-start(bf16[128,1024]{1,0:T(8,128)(2,1)S(1)} %get-tuple-element.65), channel_id=1, source_target_pairs={{0,14},{2,12},{4,10},{6,8},{8,6},{10,4},{12,2},{14,0},{1,15},{3,13... | collective-permute-start | bytes 786440 | tf_op jit(solution)/shard_map/ppermute | solution.py:227
  81.1 3.7 %own_whole.1 = (bf16[2,1024,1024]{2,1,0:T(8,128)(2,1)S(1)}, f32[1,1024]{1,0:T(1,128)S(1)}) custom-call(bf16[128,1024]{1,0:T(8,128)(2,1)S(1)} %get-tuple-element.47.refs_0_, bf16[128,1024]{1,0:T(8,128)(2,1)S(1)} %collective-permute-done.5.refs_1_, bf16[128,1024]{1,0:T(8,128)(2,1)S(1)} %collective-permute-done.6.refs_2_, ...), custom_call_target="tpu_custom_call" | custom-call | flops 1000 | bytes 1000 | tf_op jit(solution)/shard_map/own_whole/pallas_call | solution.py:80
  84.9 7.6 %all_to_all.10.received = bf16[2,1024,1024]{2,1,0:T(8,128)(2,1)S(1)} all-to-all(bf16[2,1024,1024]{2,1,0:T(8,128)(2,1)S(1)} %get-tuple-element.55), channel_id=1, replica_groups=mesh['groups'=2,'clus'=8,'blk'=2] {'blk'}, dimensions={0} | all-to-all | bytes 8388608 | tf_op jit(solution)/shard_map/all_to_all | solution.py:233
  92.5 2.6 %cross_whole.1.ready = f32[1,1024]{1,0:T(1,128)S(1)} custom-call(bf16[2,1024,1024]{2,1,0:T(8,128)(2,1)S(1)} %all_to_all.10.received, f32[1,1024]{1,0:T(1,128)S(1)} %get-tuple-element.56.before), custom_call_target="tpu_custom_call" | custom-call | flops 1000 | bytes 1000 | tf_op jit(solution)/shard_map/cross_whole/pallas_call | solution.py:80
  95.0 1.2 %collective-permute-done.4.refs_3_ = bf16[128,1024]{1,0:T(8,128)(2,1)S(1)} collective-permute-done((bf16[128,1024]{1,0:T(8,128)(2,1)S(1)}, bf16[128,1024]{1,0:T(8,128)(2,1)S(1)}, u32[]{:S(2)}, u32[]{:S(2)}) %collective-permute-start.4) | collective-permute-done | bytes 262176 | tf_op jit(solution)/shard_map/ppermute | solution.py:227
  96.2 1.5 %own_early.1 = (bf16[2,768,1024]{2,1,0:T(8,128)(2,1)S(1)}, f32[1,1024]{1,0:T(1,128)S(1)}) custom-call(bf16[128,1024]{1,0:T(8,128)(2,1)S(1)} %get-tuple-element.57.refs_0_, bf16[128,1024]{1,0:T(8,128)(2,1)S(1)} %collective-permute-done.2.refs_1_, bf16[128,1024]{1,0:T(8,128)(2,1)S(1)} %collective-permute-done.3.refs_2_, ...), custom_call_target="tpu_custom_call" | custom-call | flops 1000 | bytes 1000 | tf_op jit(solution)/shard_map/own_early/pallas_call | solution.py:80
  97.7 7.3 %all_to_all.11.received.refs_0_ = bf16[2,768,1024]{2,1,0:T(8,128)(2,1)S(1)} all-to-all(bf16[2,768,1024]{2,1,0:T(8,128)(2,1)S(1)} %get-tuple-element.63), channel_id=1, replica_groups=mesh['groups'=2,'clus'=8,'blk'=2] {'blk'}, dimensions={0} | all-to-all | bytes 6291456 | tf_op jit(solution)/shard_map/all_to_all | solution.py:233
  105.1 1.4 %cross_early.1.refs_1_ = f32[1,1024]{1,0:T(1,128)S(1)} custom-call(bf16[2,768,1024]{2,1,0:T(8,128)(2,1)S(1)} %all_to_all.11.received.refs_0_, f32[1,1024]{1,0:T(1,128)S(1)} %get-tuple-element.66.before), custom_call_target="tpu_custom_call" | custom-call | flops 1000 | bytes 1000 | tf_op jit(solution)/shard_map/cross_early/pallas_call | solution.py:80
  106.5 1.3 %collective-permute-start.14 = (bf16[128,1024]{1,0:T(8,128)(2,1)S(1)}, bf16[128,1024]{1,0:T(8,128)(2,1)S(1)}, u32[]{:S(2)}, u32[]{:S(2)}) collective-permute-start(bf16[128,1024]{1,0:T(8,128)(2,1)S(1)} %collective-permute-done.12.refs_2_), channel_id=1, source_target_pairs={{0,1},{2,3},{4,5},{6,7},{8,9},{10,11},{12,13},{14,15},{16,17},{18,... | collective-permute-start | bytes 786440 | tf_op jit(solution)/shard_map/ppermute | solution.py:296
  107.8 1.3 %collective-permute-start.15 = (bf16[128,1024]{1,0:T(8,128)(2,1)S(1)}, bf16[128,1024]{1,0:T(8,128)(2,1)S(1)}, u32[]{:S(2)}, u32[]{:S(2)}) collective-permute-start(bf16[128,1024]{1,0:T(8,128)(2,1)S(1)} %collective-permute-done.13.refs_3_), channel_id=1, source_target_pairs={{0,1},{2,3},{4,5},{6,7},{8,9},{10,11},{12,13},{14,15},{16,17},{18,... | collective-permute-start | bytes 786440 | tf_op jit(solution)/shard_map/ppermute | solution.py:296
  109.1 2.3 %own_last.1 = (bf16[2,256,1024]{2,1,0:T(8,128)(2,1)S(1)}, f32[1,1024]{1,0:T(1,128)S(1)}) custom-call(bf16[2,768,1024]{2,1,0:T(8,128)(2,1)S(1)} %all_to_all.11.received.refs_0_, f32[1,1024]{1,0:T(1,128)S(1)} %cross_early.1.refs_1_, bf16[128,1024]{1,0:T(8,128)(2,1)S(1)} %collective-permute-done.12.refs_2_, bf16[128,1024]{1,0:T(8,128)(2,1)S(1)} %collective-permute-done.13.refs_3_), custom_call_target="tpu_custom_call" | custom-call | flops 1000 | bytes 1000 | tf_op jit(solution)/shard_map/own_last/pallas_call | solution.py:80
  111.4 2.0 %cross_last.1 = f32[2,1024]{1,0:T(2,128)} custom-call(bf16[2,768,1024]{2,1,0:T(8,128)(2,1)S(1)} %all_to_all.11.received.refs_0_, bf16[2,256,1024]{2,1,0:T(8,128)(2,1)S(1)} %get-tuple-element.70.send, f32[1,1024]{1,0:T(1,128)S(1)} %get-tuple-element.71.before, f32[1,1024]{1,0:T(1,128)S(1)} %cross_whole.1.ready, ...), custom_call_target="tpu_custom_call" | custom-call | flops 1000 | bytes 1000 | tf_op jit(solution)/shard_map/cross_last/pallas_call | solution.py:80
  (17 shorter events, 1.6 us)
Async XLA Ops:
  0.0 1.6 %copy-start = (bf16[1024,1024]{1,0:T(8,128)(2,1)S(1)}, bf16[1024,1024]{1,0:T(8,128)(2,1)}, u32[]{:S(2)}) copy-start(bf16[1024,1024]{1,0:T(8,128)(2,1)} %emb.1) | copy-start | bytes 6291460
  1.6 0.7 copy-start.1
  3.7 31.7 %collective-permute-start.8 = (bf16[128,1024]{1,0:T(8,128)(2,1)S(1)}, bf16[128,1024]{1,0:T(8,128)(2,1)S(1)}, u32[]{:S(2)}, u32[]{:S(2)}) collective-permute-start(bf16[128,1024]{1,0:T(8,128)(2,1)S(1)} %get-tuple-element.51), channel_id=1, source_target_pairs={{0,8},{2,10},{4,12},{6,14},{8,0},{10,2},{12,4},{14,6},{1,9},{3,11}... | collective-permute-start | bytes 786440 | tf_op jit(solution)/shard_map/ppermute | solution.py:227
  7.0 34.9 %collective-permute-start.9 = (bf16[128,1024]{1,0:T(8,128)(2,1)S(1)}, bf16[128,1024]{1,0:T(8,128)(2,1)S(1)}, u32[]{:S(2)}, u32[]{:S(2)}) collective-permute-start(bf16[128,1024]{1,0:T(8,128)(2,1)S(1)} %get-tuple-element.52), channel_id=1, source_target_pairs={{0,10},{2,8},{4,14},{6,12},{8,2},{10,0},{12,6},{14,4},{1,11},{3,9}... | collective-permute-start | bytes 786440 | tf_op jit(solution)/shard_map/ppermute | solution.py:227
  8.8 36.5 %collective-permute-start.10 = (bf16[128,1024]{1,0:T(8,128)(2,1)S(1)}, bf16[128,1024]{1,0:T(8,128)(2,1)S(1)}, u32[]{:S(2)}, u32[]{:S(2)}) collective-permute-start(bf16[128,1024]{1,0:T(8,128)(2,1)S(1)} %get-tuple-element.53), channel_id=1, source_target_pairs={{0,12},{2,14},{4,8},{6,10},{8,4},{10,6},{12,0},{14,2},{1,13},{3,15... | collective-permute-start | bytes 786440 | tf_op jit(solution)/shard_map/ppermute | solution.py:227
  12.2 37.7 %collective-permute-start.11 = (bf16[128,1024]{1,0:T(8,128)(2,1)S(1)}, bf16[128,1024]{1,0:T(8,128)(2,1)S(1)}, u32[]{:S(2)}, u32[]{:S(2)}) collective-permute-start(bf16[128,1024]{1,0:T(8,128)(2,1)S(1)} %get-tuple-element.54), channel_id=1, source_target_pairs={{0,14},{2,12},{4,10},{6,8},{8,6},{10,4},{12,2},{14,0},{1,15},{3,13... | collective-permute-start | bytes 786440 | tf_op jit(solution)/shard_map/ppermute | solution.py:227
  13.6 49.7 %collective-permute-start.5 = (bf16[128,1024]{1,0:T(8,128)(2,1)S(1)}, bf16[128,1024]{1,0:T(8,128)(2,1)S(1)}, u32[]{:S(2)}, u32[]{:S(2)}) collective-permute-start(bf16[128,1024]{1,0:T(8,128)(2,1)S(1)} %get-tuple-element.48), channel_id=1, source_target_pairs={{0,2},{2,0},{4,6},{6,4},{8,10},{10,8},{12,14},{14,12},{1,3},{3,1},... | collective-permute-start | bytes 786440 | tf_op jit(solution)/shard_map/ppermute | solution.py:227
  35.5 29.1 %collective-permute-start.6 = (bf16[128,1024]{1,0:T(8,128)(2,1)S(1)}, bf16[128,1024]{1,0:T(8,128)(2,1)S(1)}, u32[]{:S(2)}, u32[]{:S(2)}) collective-permute-start(bf16[128,1024]{1,0:T(8,128)(2,1)S(1)} %get-tuple-element.49), channel_id=1, source_target_pairs={{0,4},{2,6},{4,0},{6,2},{8,12},{10,14},{12,8},{14,10},{1,5},{3,7},... | collective-permute-start | bytes 786440 | tf_op jit(solution)/shard_map/ppermute | solution.py:227
  41.8 22.7 %collective-permute-start.7 = (bf16[128,1024]{1,0:T(8,128)(2,1)S(1)}, bf16[128,1024]{1,0:T(8,128)(2,1)S(1)}, u32[]{:S(2)}, u32[]{:S(2)}) collective-permute-start(bf16[128,1024]{1,0:T(8,128)(2,1)S(1)} %get-tuple-element.50), channel_id=1, source_target_pairs={{0,6},{2,4},{4,2},{6,0},{8,14},{10,12},{12,10},{14,8},{1,7},{3,5},... | collective-permute-start | bytes 786440 | tf_op jit(solution)/shard_map/ppermute | solution.py:227
  45.3 24.9 %collective-permute-start = (bf16[128,1024]{1,0:T(8,128)(2,1)S(1)}, bf16[128,1024]{1,0:T(8,128)(2,1)S(1)}, u32[]{:S(2)}, u32[]{:S(2)}) collective-permute-start(bf16[128,1024]{1,0:T(8,128)(2,1)S(1)} %get-tuple-element.41), channel_id=1, source_target_pairs={{0,8},{2,10},{4,12},{6,14},{8,0},{10,2},{12,4},{14,6},{1,9},{3,11}... | collective-permute-start | bytes 786440 | tf_op jit(solution)/shard_map/ppermute | solution.py:227
  49.8 27.1 %collective-permute-start.1 = (bf16[128,1024]{1,0:T(8,128)(2,1)S(1)}, bf16[128,1024]{1,0:T(8,128)(2,1)S(1)}, u32[]{:S(2)}, u32[]{:S(2)}) collective-permute-start(bf16[128,1024]{1,0:T(8,128)(2,1)S(1)} %get-tuple-element.42), channel_id=1, source_target_pairs={{0,10},{2,8},{4,14},{6,12},{8,2},{10,0},{12,6},{14,4},{1,11},{3,9}... | collective-permute-start | bytes 786440 | tf_op jit(solution)/shard_map/ppermute | solution.py:227
  63.3 31.7 %collective-permute-start.2 = (bf16[128,1024]{1,0:T(8,128)(2,1)S(1)}, bf16[128,1024]{1,0:T(8,128)(2,1)S(1)}, u32[]{:S(2)}, u32[]{:S(2)}) collective-permute-start(bf16[128,1024]{1,0:T(8,128)(2,1)S(1)} %get-tuple-element.44), channel_id=1, source_target_pairs={{0,2},{2,0},{4,6},{6,4},{8,10},{10,8},{12,14},{14,12},{1,3},{3,1},... | collective-permute-start | bytes 786440 | tf_op jit(solution)/shard_map/ppermute | solution.py:227
  64.5 30.5 %collective-permute-start.3 = (bf16[128,1024]{1,0:T(8,128)(2,1)S(1)}, bf16[128,1024]{1,0:T(8,128)(2,1)S(1)}, u32[]{:S(2)}, u32[]{:S(2)}) collective-permute-start(bf16[128,1024]{1,0:T(8,128)(2,1)S(1)} %get-tuple-element.45), channel_id=1, source_target_pairs={{0,4},{2,6},{4,0},{6,2},{8,12},{10,14},{12,8},{14,10},{1,5},{3,7},... | collective-permute-start | bytes 786440 | tf_op jit(solution)/shard_map/ppermute | solution.py:227
  64.5 31.7 %collective-permute-start.4 = (bf16[128,1024]{1,0:T(8,128)(2,1)S(1)}, bf16[128,1024]{1,0:T(8,128)(2,1)S(1)}, u32[]{:S(2)}, u32[]{:S(2)}) collective-permute-start(bf16[128,1024]{1,0:T(8,128)(2,1)S(1)} %get-tuple-element.46), channel_id=1, source_target_pairs={{0,6},{2,4},{4,2},{6,0},{8,14},{10,12},{12,10},{14,8},{1,7},{3,5},... | collective-permute-start | bytes 786440 | tf_op jit(solution)/shard_map/ppermute | solution.py:227
  70.2 36.3 %collective-permute-start.12 = (bf16[128,1024]{1,0:T(8,128)(2,1)S(1)}, bf16[128,1024]{1,0:T(8,128)(2,1)S(1)}, u32[]{:S(2)}, u32[]{:S(2)}) collective-permute-start(bf16[128,1024]{1,0:T(8,128)(2,1)S(1)} %get-tuple-element.64), channel_id=1, source_target_pairs={{0,12},{2,14},{4,8},{6,10},{8,4},{10,6},{12,0},{14,2},{1,13},{3,15... | collective-permute-start | bytes 786440 | tf_op jit(solution)/shard_map/ppermute | solution.py:227
  76.9 29.6 %collective-permute-start.13 = (bf16[128,1024]{1,0:T(8,128)(2,1)S(1)}, bf16[128,1024]{1,0:T(8,128)(2,1)S(1)}, u32[]{:S(2)}, u32[]{:S(2)}) collective-permute-start(bf16[128,1024]{1,0:T(8,128)(2,1)S(1)} %get-tuple-element.65), channel_id=1, source_target_pairs={{0,14},{2,12},{4,10},{6,8},{8,6},{10,4},{12,2},{14,0},{1,15},{3,13... | collective-permute-start | bytes 786440 | tf_op jit(solution)/shard_map/ppermute | solution.py:227
  106.5 4.9 %collective-permute-start.14 = (bf16[128,1024]{1,0:T(8,128)(2,1)S(1)}, bf16[128,1024]{1,0:T(8,128)(2,1)S(1)}, u32[]{:S(2)}, u32[]{:S(2)}) collective-permute-start(bf16[128,1024]{1,0:T(8,128)(2,1)S(1)} %collective-permute-done.12.refs_2_), channel_id=1, source_target_pairs={{0,1},{2,3},{4,5},{6,7},{8,9},{10,11},{12,13},{14,15},{16,17},{18,... | collective-permute-start | bytes 786440 | tf_op jit(solution)/shard_map/ppermute | solution.py:296
  107.8 3.6 %collective-permute-start.15 = (bf16[128,1024]{1,0:T(8,128)(2,1)S(1)}, bf16[128,1024]{1,0:T(8,128)(2,1)S(1)}, u32[]{:S(2)}, u32[]{:S(2)}) collective-permute-start(bf16[128,1024]{1,0:T(8,128)(2,1)S(1)} %collective-permute-done.13.refs_3_), channel_id=1, source_target_pairs={{0,1},{2,3},{4,5},{6,7},{8,9},{10,11},{12,13},{14,15},{16,17},{18,... | collective-permute-start | bytes 786440 | tf_op jit(solution)/shard_map/ppermute | solution.py:296

commit v9 on v8

--- a/solution.py
+++ b/solution.py
@@ -44,33 +44,34 @@
     return jnp.concatenate(out, axis=1)
 
 
-def store_blocks(unit, tgt, picks, outs):
+def store_blocks(unit, tgt, per, picks, outs):
     me = lax.axis_index("clus")
-    per = outs[0].shape[0]
-    hits = [
-        (tgt - ((me ^ step) * CLUS_DEV + cluster) * per == iota((per, tgt.shape[1]), 0)).astype(F32)
-        for step, cluster in picks
-    ]
+    hits = []
+    for (step, cluster), out in zip(picks, outs):
+        base = ((me ^ step) * CLUS_DEV + cluster) * per
+        hits.append((tgt - base == iota((out.shape[0], tgt.shape[1]), 0)).astype(F32))
     hot = jnp.concatenate(hits, axis=0) if len(hits) > 1 else hits[0]
     rows = matmul(hot.astype(BF), unit, ((1,), (0,)))
     empty = jnp.max(hot, axis=1, keepdims=True) < 0.5
     marked = jnp.where(empty, F32(MARK), rows[:, :LANES])
-    for k, out in enumerate(outs):
-        window = slice(k * per, (k + 1) * per)
+    first = 0
+    for out in outs:
+        window = slice(first, first + out.shape[0])
         out[:, :LANES] = marked[window].astype(BF)
         out[:, LANES:] = rows[window, LANES:].astype(BF)
-
-
-def pack_first(picks, clusters, emb, ids, unit, tgt, *outs):
+        first += out.shape[0]
+
+
+def pack_first(per, picks, clusters, emb, ids, unit, tgt, *outs):
     values = emb[...].astype(F32)
     scale = lax.rsqrt(jnp.sum(values * values, axis=1, keepdims=True) + 1e-6)
     unit[...] = (values * scale).astype(BF)
-    tgt[...] = targets(ids[...], clusters, outs[0].shape[0])
-    store_blocks(unit[...], tgt[...], picks, outs)
-
-
-def pack_rest(picks, unit, tgt, *outs):
-    store_blocks(unit[...], tgt[...], picks, outs)
+    tgt[...] = targets(ids[...], clusters, per)
+    store_blocks(unit[...], tgt[...], per, picks, outs)
+
+
+def pack_rest(per, picks, unit, tgt, *outs):
+    store_blocks(unit[...], tgt[...], per, picks, outs)
 
 
 VMEM = pl.BlockSpec(memory_space=pltpu.VMEM)
@@ -110,11 +111,12 @@
             best[:, window] = jnp.maximum(best[:, window], jnp.max(part, axis=0, keepdims=True))
 
 
-def gather_group(blocks, out, me):
-    per = blocks[0].shape[0]
+def gather_group(blocks, per, cluster, out, me):
     for step, block in enumerate(blocks):
         place = (me & (len(blocks) - 1)) ^ step
-        out[pl.ds(pl.multiple_of(place * per, per), per), :] = block[...]
+        first = cluster * per if block.shape[0] > per else 0
+        rows = pl.ds(pl.multiple_of(place * per, per), per)
+        out[rows, :] = block[first : first + per, :]
 
 
 def score_pair(bests, groups, new, old, bit, me):
@@ -129,11 +131,10 @@
         raise_best(bests[old], groups[new], groups[old])
 
 
-def own_stage(cuts, bits, held, first, *refs):
+def own_stage(per, cluster, cuts, bits, held, first, *refs):
     stages, refs = refs[:held], refs[held:]
     blocks, (send, best) = list(refs[:-2]), refs[-2:]
     before = blocks.pop(0) if held else None
-    per = blocks[0].shape[0]
     me = lax.axis_index("clus")
     core = lax.axis_index("blk")
     spans = list(zip(cuts, cuts[1:]))
@@ -152,7 +153,7 @@
     for i in range(first, len(spans)):
         a, b = spans[i]
         group = send.at[1, a - base : b - base]
-        gather_group(blocks[(a - base) // per : (b - base) // per], group, me)
+        gather_group(blocks[(a - base) // per : (b - base) // per], per, cluster, group, me)
         groups.append(group)
         raise_best(rows[i], group, group, True)
         for j in range(i):
@@ -240,7 +241,7 @@
 
     picks = [(step, 0) for step in far1]
     unit, tgt, *packed = kernel_call(
-        functools.partial(pack_first, picks, clusters),
+        functools.partial(pack_first, per, picks, clusters),
         [
             jax.ShapeDtypeStruct(embeddings.shape, BF),
             jax.ShapeDtypeStruct(cluster_ids.shape, jnp.int32),
@@ -250,20 +251,20 @@
         "pack_first",
     )
     dispatch(picks, packed)
-    for steps, cluster in (
-        (near[1:] + [0], 0),
-        (far2 + far3, 0),
-        (far1 + near, 1),
-        (far2 + far3, 1),
+    both = jax.ShapeDtypeStruct((CLUS_DEV * per, width), BF)
+    for picks, shape in (
+        ([(step, 0) for step in far2 + far3], block),
+        ([(step, 0) for step in near[1:] + [0]], both),
+        ([(step, 1) for step in far1], block),
+        ([(step, 1) for step in far2 + far3], block),
     ):
-        picks = [(step, cluster) for step in steps]
         packed = kernel_call(
-            functools.partial(pack_rest, picks), [block] * len(picks), [unit, tgt], "pack_rest"
+            functools.partial(pack_rest, per, picks), [shape] * len(picks), [unit, tgt], "pack_rest"
         )
         dispatch(picks, packed)
 
     send, best = kernel_call(
-        functools.partial(own_stage, cuts, bits, 0, 0),
+        functools.partial(own_stage, per, 0, cuts, bits, 0, 0),
         [stage_shape(owners), best_shape],
         [arrived[0][s] for s in near + far1 + far2 + far3],
         "own_whole",
@@ -275,12 +276,11 @@
         "cross_whole",
         [pltpu.VMEM((1, rows), F32)],
     )
-    order = far1 + near
-    *early, ready = lax.optimization_barrier((*[arrived[1][s] for s in order], ready))
-    early = [early[order.index(s)] for s in near + far1]
+    *early, ready = lax.optimization_barrier((*[arrived[1][s] for s in far1], ready))
+    early = [arrived[0][s] for s in near] + early
     send, best = kernel_call(
-        functools.partial(own_stage, cuts[:3], bits, 0, 0),
-        [stage_shape(len(early)), best_shape],
+        functools.partial(own_stage, per, 1, cuts[:3], bits, 0, 0),
+        [stage_shape(len(near + far1)), best_shape],
         early,
         "own_early",
     )
@@ -288,7 +288,7 @@
     (best,) = kernel_call(cross_stage, [best_shape], [received, best], "cross_early")
     *late, best = lax.optimization_barrier((*[arrived[1][s] for s in far2 + far3], best))
     send, best = kernel_call(
-        functools.partial(own_stage, cuts, bits, 1, 2),
+        functools.partial(own_stage, per, 1, cuts, bits, 1, 2),
         [stage_shape(len(late)), best_shape],
         [received, best] + late,
         "own_last",

time: 114 us -> 111 us (0.974)
  the two profiles are of different devices: /device:TPU:1 before, /device:TPU:17 now
where the time goes in v9:
time: 111 us; the launch traced here: 110 us
  starting transfers between devices  41.3 us (37%)
  waiting for transfers between devices  30.2 us (27%)
  Pallas kernels  20.3 us (18%)
  blocking collectives  16.3 us (15%)
  local copies, waits for them, and re-layouts  2.28 us (2%)
    ppermute x11, starting transfers between devices, to_owner(): return lax.ppermute(block, 'clus', [(i, i ^ step) for i in range(owners)])  38.7 us
    ppermute x11, waiting for transfers between devices, to_owner(): return lax.ppermute(block, 'clus', [(i, i ^ step) for i in range(owners)])  30.1 us
    pallas_call x11, Pallas kernels, kernel_call(): pl.pallas_call(kernel, out_shape=shapes, in_specs=[VMEM] * len(inputs), o...  20.3 us
    all_to_all x2, blocking collectives, to_both(): return lax.all_to_all(send, 'blk', split_axis=0, concat_axis=0, tiled=True)  16.3 us
    ppermute x2, starting transfers between devices, local(): others = [lax.ppermute(block, 'blk', [(0, 1)]) for block in late]  2.57 us
    unnamed x4, local copies, waits for them, and re-layouts  2.28 us
  transfers between devices with their start and end apart: 13, of which 7 were waited for; matrix products, arithmetic and copies ran while one was open for 0% of the time, Pallas kernels for 15%

profile of v9, /device:TPU:17, one launch (start us, length us, event | category | flops | bytes accessed | tf_op | source)
XLA Modules:
  0.0 110.4 jit_solution(16556625798467189756)
XLA Ops:
  0.0 1.6 %copy-done = bf16[1024,1024]{1,0:T(8,128)(2,1)S(1)} copy-done((bf16[1024,1024]{1,0:T(8,128)(2,1)S(1)}, bf16[1024,1024]{1,0:T(8,128)(2,1)}, u32[]{:S(2)}) %copy-start) | copy-done | bytes 2097176
  2.3 1.5 %pack_first.1 = (bf16[1024,1024]{1,0:T(8,128)(2,1)S(1)}, s32[1,1024]{1,0:T(1,128)S(1)}, bf16[128,1024]{1,0:T(8,128)(2,1)S(1)}, bf16[128,1024]{1,0:T(8,128)(2,1)S(1)}) custom-call(bf16[1024,1024]{1,0:T(8,128)(2,1)S(1)} %copy-done, s32[1,1024]{1,0:T(1,128)S(1)} %copy-done.1), custom_call_target="tpu_custom_call" | custom-call | flops 1000 | bytes 1000 | tf_op jit(solution)/shard_map/pack_first/pallas_call | solution.py:81
  3.8 3.3 %collective-permute-start.6 = (bf16[128,1024]{1,0:T(8,128)(2,1)S(1)}, bf16[128,1024]{1,0:T(8,128)(2,1)S(1)}, u32[]{:S(2)}, u32[]{:S(2)}) collective-permute-start(bf16[128,1024]{1,0:T(8,128)(2,1)S(1)} %get-tuple-element.40), channel_id=1, source_target_pairs={{0,10},{2,8},{4,14},{6,12},{8,2},{10,0},{12,6},{14,4},{1,11},{3,9}... | collective-permute-start | bytes 786440 | tf_op jit(solution)/shard_map/ppermute | solution.py:228
  7.1 2.6 %pack_rest.4 = (bf16[256,1024]{1,0:T(8,128)(2,1)S(1)}, bf16[256,1024]{1,0:T(8,128)(2,1)S(1)}, bf16[256,1024]{1,0:T(8,128)(2,1)S(1)}, bf16[256,1024]{1,0:T(8,128)(2,1)S(1)}) custom-call(bf16[1024,1024]{1,0:T(8,128)(2,1)S(1)} %get-tuple-element.31.unit, s32[1,1024]{1,0:T(1,128)S(1)} %get-tuple-element.32.tgt), custom_call_target="tpu_custom_call" | custom-call | flops 1000 | bytes 1000 | tf_op jit(solution)/shard_map/pack_rest/pallas_call | solution.py:81
  10.1 1.3 %collective-permute-start.1 = (bf16[256,1024]{1,0:T(8,128)(2,1)S(1)}, bf16[256,1024]{1,0:T(8,128)(2,1)S(1)}, u32[]{:S(2)}, u32[]{:S(2)}) collective-permute-start(bf16[256,1024]{1,0:T(8,128)(2,1)S(1)} %get-tuple-element.35), channel_id=1, source_target_pairs={{0,4},{2,6},{4,0},{6,2},{8,12},{10,14},{12,8},{14,10},{1,5},{3,7},... | collective-permute-start | bytes 1572872 | tf_op jit(solution)/shard_map/ppermute | solution.py:228
  11.4 1.1 %collective-permute-start.2 = (bf16[256,1024]{1,0:T(8,128)(2,1)S(1)}, bf16[256,1024]{1,0:T(8,128)(2,1)S(1)}, u32[]{:S(2)}, u32[]{:S(2)}) collective-permute-start(bf16[256,1024]{1,0:T(8,128)(2,1)S(1)} %get-tuple-element.36), channel_id=1, source_target_pairs={{0,6},{2,4},{4,2},{6,0},{8,14},{10,12},{12,10},{14,8},{1,7},{3,5},... | collective-permute-start | bytes 1572872 | tf_op jit(solution)/shard_map/ppermute | solution.py:228
  12.5 0.8 pack_rest.6
  13.3 7.1 %collective-permute-done.5.refs_4_ = bf16[128,1024]{1,0:T(8,128)(2,1)S(1)} collective-permute-done((bf16[128,1024]{1,0:T(8,128)(2,1)S(1)}, bf16[128,1024]{1,0:T(8,128)(2,1)S(1)}, u32[]{:S(2)}, u32[]{:S(2)}) %collective-permute-start.5) | collective-permute-done | bytes 262176 | tf_op jit(solution)/shard_map/ppermute | solution.py:228
  20.4 3.1 %collective-permute-start.7 = (bf16[128,1024]{1,0:T(8,128)(2,1)S(1)}, bf16[128,1024]{1,0:T(8,128)(2,1)S(1)}, u32[]{:S(2)}, u32[]{:S(2)}) collective-permute-start(bf16[128,1024]{1,0:T(8,128)(2,1)S(1)} %get-tuple-element.41), channel_id=1, source_target_pairs={{0,12},{2,14},{4,8},{6,10},{8,4},{10,6},{12,0},{14,2},{1,13},{3,15... | collective-permute-start | bytes 786440 | tf_op jit(solution)/shard_map/ppermute | solution.py:228
  23.5 2.5 %collective-permute-done.6.refs_5_ = bf16[128,1024]{1,0:T(8,128)(2,1)S(1)} collective-permute-done((bf16[128,1024]{1,0:T(8,128)(2,1)S(1)}, bf16[128,1024]{1,0:T(8,128)(2,1)S(1)}, u32[]{:S(2)}, u32[]{:S(2)}) %collective-permute-start.6) | collective-permute-done | bytes 262176 | tf_op jit(solution)/shard_map/ppermute | solution.py:228
  26.0 4.0 %collective-permute-start.8 = (bf16[128,1024]{1,0:T(8,128)(2,1)S(1)}, bf16[128,1024]{1,0:T(8,128)(2,1)S(1)}, u32[]{:S(2)}, u32[]{:S(2)}) collective-permute-start(bf16[128,1024]{1,0:T(8,128)(2,1)S(1)} %get-tuple-element.42), channel_id=1, source_target_pairs={{0,14},{2,12},{4,10},{6,8},{8,6},{10,4},{12,2},{14,0},{1,15},{3,13... | collective-permute-start | bytes 786440 | tf_op jit(solution)/shard_map/ppermute | solution.py:228
  30.1 0.8 pack_rest.5
  30.9 4.6 %collective-permute-done.7.refs_6_ = bf16[128,1024]{1,0:T(8,128)(2,1)S(1)} collective-permute-done((bf16[128,1024]{1,0:T(8,128)(2,1)S(1)}, bf16[128,1024]{1,0:T(8,128)(2,1)S(1)}, u32[]{:S(2)}, u32[]{:S(2)}) %collective-permute-start.7) | collective-permute-done | bytes 262176 | tf_op jit(solution)/shard_map/ppermute | solution.py:228
  35.5 14.5 %collective-permute-start.3 = (bf16[128,1024]{1,0:T(8,128)(2,1)S(1)}, bf16[128,1024]{1,0:T(8,128)(2,1)S(1)}, u32[]{:S(2)}, u32[]{:S(2)}) collective-permute-start(bf16[128,1024]{1,0:T(8,128)(2,1)S(1)} %get-tuple-element.37), channel_id=1, source_target_pairs={{0,8},{2,10},{4,12},{6,14},{8,0},{10,2},{12,4},{14,6},{1,9},{3,11}... | collective-permute-start | bytes 786440 | tf_op jit(solution)/shard_map/ppermute | solution.py:228
  49.9 6.8 %collective-permute-start.4 = (bf16[128,1024]{1,0:T(8,128)(2,1)S(1)}, bf16[128,1024]{1,0:T(8,128)(2,1)S(1)}, u32[]{:S(2)}, u32[]{:S(2)}) collective-permute-start(bf16[128,1024]{1,0:T(8,128)(2,1)S(1)} %get-tuple-element.38), channel_id=1, source_target_pairs={{0,10},{2,8},{4,14},{6,12},{8,2},{10,0},{12,6},{14,4},{1,11},{3,9}... | collective-permute-start | bytes 786440 | tf_op jit(solution)/shard_map/ppermute | solution.py:228
  56.8 0.8 pack_rest.7
  57.6 2.9 %collective-permute-start.9 = (bf16[128,1024]{1,0:T(8,128)(2,1)S(1)}, bf16[128,1024]{1,0:T(8,128)(2,1)S(1)}, u32[]{:S(2)}, u32[]{:S(2)}) collective-permute-start(bf16[128,1024]{1,0:T(8,128)(2,1)S(1)} %get-tuple-element.48), channel_id=1, source_target_pairs={{0,12},{2,14},{4,8},{6,10},{8,4},{10,6},{12,0},{14,2},{1,13},{3,15... | collective-permute-start | bytes 786440 | tf_op jit(solution)/shard_map/ppermute | solution.py:228
  60.6 1.2 %collective-permute-start.10 = (bf16[128,1024]{1,0:T(8,128)(2,1)S(1)}, bf16[128,1024]{1,0:T(8,128)(2,1)S(1)}, u32[]{:S(2)}, u32[]{:S(2)}) collective-permute-start(bf16[128,1024]{1,0:T(8,128)(2,1)S(1)} %get-tuple-element.49), channel_id=1, source_target_pairs={{0,14},{2,12},{4,10},{6,8},{8,6},{10,4},{12,2},{14,0},{1,15},{3,13... | collective-permute-start | bytes 786440 | tf_op jit(solution)/shard_map/ppermute | solution.py:228
  61.7 3.9 %own_whole.1 = (bf16[2,1024,1024]{2,1,0:T(8,128)(2,1)S(1)}, f32[1,1024]{1,0:T(1,128)S(1)}) custom-call(bf16[256,1024]{1,0:T(8,128)(2,1)S(1)} %get-tuple-element.33.refs_0_, bf16[256,1024]{1,0:T(8,128)(2,1)S(1)} %collective-permute-done.refs_1_, bf16[256,1024]{1,0:T(8,128)(2,1)S(1)} %collective-permute-done.1.refs_2_, ...), custom_call_target="tpu_custom_call" | custom-call | flops 1000 | bytes 1000 | tf_op jit(solution)/shard_map/own_whole/pallas_call | solution.py:81
  65.7 10.0 %all_to_all.10.received = bf16[2,1024,1024]{2,1,0:T(8,128)(2,1)S(1)} all-to-all(bf16[2,1024,1024]{2,1,0:T(8,128)(2,1)S(1)} %get-tuple-element.43), channel_id=1, replica_groups=mesh['groups'=2,'clus'=8,'blk'=2] {'blk'}, dimensions={0} | all-to-all | bytes 8388608 | tf_op jit(solution)/shard_map/all_to_all | solution.py:234
  75.7 2.6 %cross_whole.1.ready = f32[1,1024]{1,0:T(1,128)S(1)} custom-call(bf16[2,1024,1024]{2,1,0:T(8,128)(2,1)S(1)} %all_to_all.10.received, f32[1,1024]{1,0:T(1,128)S(1)} %get-tuple-element.44.before), custom_call_target="tpu_custom_call" | custom-call | flops 1000 | bytes 1000 | tf_op jit(solution)/shard_map/cross_whole/pallas_call | solution.py:81
  78.3 2.9 %collective-permute-done.3.refs_4_ = bf16[128,1024]{1,0:T(8,128)(2,1)S(1)} collective-permute-done((bf16[128,1024]{1,0:T(8,128)(2,1)S(1)}, bf16[128,1024]{1,0:T(8,128)(2,1)S(1)}, u32[]{:S(2)}, u32[]{:S(2)}) %collective-permute-start.3) | collective-permute-done | bytes 262176 | tf_op jit(solution)/shard_map/ppermute | solution.py:228
  81.1 5.6 %collective-permute-done.4.refs_5_ = bf16[128,1024]{1,0:T(8,128)(2,1)S(1)} collective-permute-done((bf16[128,1024]{1,0:T(8,128)(2,1)S(1)}, bf16[128,1024]{1,0:T(8,128)(2,1)S(1)}, u32[]{:S(2)}, u32[]{:S(2)}) %collective-permute-start.4) | collective-permute-done | bytes 262176 | tf_op jit(solution)/shard_map/ppermute | solution.py:228
  86.7 1.5 %own_early.1 = (bf16[2,768,1024]{2,1,0:T(8,128)(2,1)S(1)}, f32[1,1024]{1,0:T(1,128)S(1)}) custom-call(bf16[256,1024]{1,0:T(8,128)(2,1)S(1)} %get-tuple-element.33.refs_0_, bf16[256,1024]{1,0:T(8,128)(2,1)S(1)} %collective-permute-done.refs_1_, bf16[256,1024]{1,0:T(8,128)(2,1)S(1)} %collective-permute-done.1.refs_2_, ...), custom_call_target="tpu_custom_call" | custom-call | flops 1000 | bytes 1000 | tf_op jit(solution)/shard_map/own_early/pallas_call | solution.py:81
  88.2 6.3 %all_to_all.11.received.refs_0_ = bf16[2,768,1024]{2,1,0:T(8,128)(2,1)S(1)} all-to-all(bf16[2,768,1024]{2,1,0:T(8,128)(2,1)S(1)} %get-tuple-element.47), channel_id=1, replica_groups=mesh['groups'=2,'clus'=8,'blk'=2] {'blk'}, dimensions={0} | all-to-all | bytes 6291456 | tf_op jit(solution)/shard_map/all_to_all | solution.py:234
  94.5 1.4 %cross_early.1.refs_1_ = f32[1,1024]{1,0:T(1,128)S(1)} custom-call(bf16[2,768,1024]{2,1,0:T(8,128)(2,1)S(1)} %all_to_all.11.received.refs_0_, f32[1,1024]{1,0:T(1,128)S(1)} %get-tuple-element.50.before), custom_call_target="tpu_custom_call" | custom-call | flops 1000 | bytes 1000 | tf_op jit(solution)/shard_map/cross_early/pallas_call | solution.py:81
  96.0 0.8 collective-permute-done.9.refs_2_
  96.7 6.7 %collective-permute-done.10.refs_3_ = bf16[128,1024]{1,0:T(8,128)(2,1)S(1)} collective-permute-done((bf16[128,1024]{1,0:T(8,128)(2,1)S(1)}, bf16[128,1024]{1,0:T(8,128)(2,1)S(1)}, u32[]{:S(2)}, u32[]{:S(2)}) %collective-permute-start.10) | collective-permute-done | bytes 262176 | tf_op jit(solution)/shard_map/ppermute | solution.py:228
  103.4 1.3 %collective-permute-start.11 = (bf16[128,1024]{1,0:T(8,128)(2,1)S(1)}, bf16[128,1024]{1,0:T(8,128)(2,1)S(1)}, u32[]{:S(2)}, u32[]{:S(2)}) collective-permute-start(bf16[128,1024]{1,0:T(8,128)(2,1)S(1)} %collective-permute-done.9.refs_2_), channel_id=1, source_target_pairs={{0,1},{2,3},{4,5},{6,7},{8,9},{10,11},{12,13},{14,15},{16,17},{18,... | collective-permute-start | bytes 786440 | tf_op jit(solution)/shard_map/ppermute | solution.py:296
  104.7 1.3 %collective-permute-start.12 = (bf16[128,1024]{1,0:T(8,128)(2,1)S(1)}, bf16[128,1024]{1,0:T(8,128)(2,1)S(1)}, u32[]{:S(2)}, u32[]{:S(2)}) collective-permute-start(bf16[128,1024]{1,0:T(8,128)(2,1)S(1)} %collective-permute-done.10.refs_3_), channel_id=1, source_target_pairs={{0,1},{2,3},{4,5},{6,7},{8,9},{10,11},{12,13},{14,15},{16,17},{18,... | collective-permute-start | bytes 786440 | tf_op jit(solution)/shard_map/ppermute | solution.py:296
  106.0 2.4 %own_last.1 = (bf16[2,256,1024]{2,1,0:T(8,128)(2,1)S(1)}, f32[1,1024]{1,0:T(1,128)S(1)}) custom-call(bf16[2,768,1024]{2,1,0:T(8,128)(2,1)S(1)} %all_to_all.11.received.refs_0_, f32[1,1024]{1,0:T(1,128)S(1)} %cross_early.1.refs_1_, bf16[128,1024]{1,0:T(8,128)(2,1)S(1)} %collective-permute-done.9.refs_2_, bf16[128,1024]{1,0:T(8,128)(2,1)S(1)} %collective-permute-done.10.refs_3_), custom_call_target="tpu_custom_call" | custom-call | flops 1000 | bytes 1000 | tf_op jit(solution)/shard_map/own_last/pallas_call | solution.py:81
  108.4 2.0 %cross_last.1 = f32[2,1024]{1,0:T(2,128)} custom-call(bf16[2,768,1024]{2,1,0:T(8,128)(2,1)S(1)} %all_to_all.11.received.refs_0_, bf16[2,256,1024]{2,1,0:T(8,128)(2,1)S(1)} %get-tuple-element.54.send, f32[1,1024]{1,0:T(1,128)S(1)} %get-tuple-element.55.before, f32[1,1024]{1,0:T(1,128)S(1)} %cross_whole.1.ready, ...), custom_call_target="tpu_custom_call" | custom-call | flops 1000 | bytes 1000 | tf_op jit(solution)/shard_map/cross_last/pallas_call | solution.py:81
  (11 shorter events, 1.1 us)
Async XLA Ops:
  0.0 1.6 %copy-start = (bf16[1024,1024]{1,0:T(8,128)(2,1)S(1)}, bf16[1024,1024]{1,0:T(8,128)(2,1)}, u32[]{:S(2)}) copy-start(bf16[1024,1024]{1,0:T(8,128)(2,1)} %emb.1) | copy-start | bytes 6291460
  1.6 0.7 copy-start.1
  3.7 16.6 %collective-permute-start.5 = (bf16[128,1024]{1,0:T(8,128)(2,1)S(1)}, bf16[128,1024]{1,0:T(8,128)(2,1)S(1)}, u32[]{:S(2)}, u32[]{:S(2)}) collective-permute-start(bf16[128,1024]{1,0:T(8,128)(2,1)S(1)} %get-tuple-element.39), channel_id=1, source_target_pairs={{0,8},{2,10},{4,12},{6,14},{8,0},{10,2},{12,4},{14,6},{1,9},{3,11}... | collective-permute-start | bytes 786440 | tf_op jit(solution)/shard_map/ppermute | solution.py:228
  3.8 22.2 %collective-permute-start.6 = (bf16[128,1024]{1,0:T(8,128)(2,1)S(1)}, bf16[128,1024]{1,0:T(8,128)(2,1)S(1)}, u32[]{:S(2)}, u32[]{:S(2)}) collective-permute-start(bf16[128,1024]{1,0:T(8,128)(2,1)S(1)} %get-tuple-element.40), channel_id=1, source_target_pairs={{0,10},{2,8},{4,14},{6,12},{8,2},{10,0},{12,6},{14,4},{1,11},{3,9}... | collective-permute-start | bytes 786440 | tf_op jit(solution)/shard_map/ppermute | solution.py:228
  9.8 47.8 %collective-permute-start = (bf16[256,1024]{1,0:T(8,128)(2,1)S(1)}, bf16[256,1024]{1,0:T(8,128)(2,1)S(1)}, u32[]{:S(2)}, u32[]{:S(2)}) collective-permute-start(bf16[256,1024]{1,0:T(8,128)(2,1)S(1)} %get-tuple-element.34), channel_id=1, source_target_pairs={{0,2},{2,0},{4,6},{6,4},{8,10},{10,8},{12,14},{14,12},{1,3},{3,1},... | collective-permute-start | bytes 1572872 | tf_op jit(solution)/shard_map/ppermute | solution.py:228
  10.1 50.5 %collective-permute-start.1 = (bf16[256,1024]{1,0:T(8,128)(2,1)S(1)}, bf16[256,1024]{1,0:T(8,128)(2,1)S(1)}, u32[]{:S(2)}, u32[]{:S(2)}) collective-permute-start(bf16[256,1024]{1,0:T(8,128)(2,1)S(1)} %get-tuple-element.35), channel_id=1, source_target_pairs={{0,4},{2,6},{4,0},{6,2},{8,12},{10,14},{12,8},{14,10},{1,5},{3,7},... | collective-permute-start | bytes 1572872 | tf_op jit(solution)/shard_map/ppermute | solution.py:228
  11.4 50.4 %collective-permute-start.2 = (bf16[256,1024]{1,0:T(8,128)(2,1)S(1)}, bf16[256,1024]{1,0:T(8,128)(2,1)S(1)}, u32[]{:S(2)}, u32[]{:S(2)}) collective-permute-start(bf16[256,1024]{1,0:T(8,128)(2,1)S(1)} %get-tuple-element.36), channel_id=1, source_target_pairs={{0,6},{2,4},{4,2},{6,0},{8,14},{10,12},{12,10},{14,8},{1,7},{3,5},... | collective-permute-start | bytes 1572872 | tf_op jit(solution)/shard_map/ppermute | solution.py:228
  20.4 15.1 %collective-permute-start.7 = (bf16[128,1024]{1,0:T(8,128)(2,1)S(1)}, bf16[128,1024]{1,0:T(8,128)(2,1)S(1)}, u32[]{:S(2)}, u32[]{:S(2)}) collective-permute-start(bf16[128,1024]{1,0:T(8,128)(2,1)S(1)} %get-tuple-element.41), channel_id=1, source_target_pairs={{0,12},{2,14},{4,8},{6,10},{8,4},{10,6},{12,0},{14,2},{1,13},{3,15... | collective-permute-start | bytes 786440 | tf_op jit(solution)/shard_map/ppermute | solution.py:228
  26.0 23.9 %collective-permute-start.8 = (bf16[128,1024]{1,0:T(8,128)(2,1)S(1)}, bf16[128,1024]{1,0:T(8,128)(2,1)S(1)}, u32[]{:S(2)}, u32[]{:S(2)}) collective-permute-start(bf16[128,1024]{1,0:T(8,128)(2,1)S(1)} %get-tuple-element.42), channel_id=1, source_target_pairs={{0,14},{2,12},{4,10},{6,8},{8,6},{10,4},{12,2},{14,0},{1,15},{3,13... | collective-permute-start | bytes 786440 | tf_op jit(solution)/shard_map/ppermute | solution.py:228
  35.5 45.7 %collective-permute-start.3 = (bf16[128,1024]{1,0:T(8,128)(2,1)S(1)}, bf16[128,1024]{1,0:T(8,128)(2,1)S(1)}, u32[]{:S(2)}, u32[]{:S(2)}) collective-permute-start(bf16[128,1024]{1,0:T(8,128)(2,1)S(1)} %get-tuple-element.37), channel_id=1, source_target_pairs={{0,8},{2,10},{4,12},{6,14},{8,0},{10,2},{12,4},{14,6},{1,9},{3,11}... | collective-permute-start | bytes 786440 | tf_op jit(solution)/shard_map/ppermute | solution.py:228
  49.9 36.8 %collective-permute-start.4 = (bf16[128,1024]{1,0:T(8,128)(2,1)S(1)}, bf16[128,1024]{1,0:T(8,128)(2,1)S(1)}, u32[]{:S(2)}, u32[]{:S(2)}) collective-permute-start(bf16[128,1024]{1,0:T(8,128)(2,1)S(1)} %get-tuple-element.38), channel_id=1, source_target_pairs={{0,10},{2,8},{4,14},{6,12},{8,2},{10,0},{12,6},{14,4},{1,11},{3,9}... | collective-permute-start | bytes 786440 | tf_op jit(solution)/shard_map/ppermute | solution.py:228
  57.6 39.1 %collective-permute-start.9 = (bf16[128,1024]{1,0:T(8,128)(2,1)S(1)}, bf16[128,1024]{1,0:T(8,128)(2,1)S(1)}, u32[]{:S(2)}, u32[]{:S(2)}) collective-permute-start(bf16[128,1024]{1,0:T(8,128)(2,1)S(1)} %get-tuple-element.48), channel_id=1, source_target_pairs={{0,12},{2,14},{4,8},{6,10},{8,4},{10,6},{12,0},{14,2},{1,13},{3,15... | collective-permute-start | bytes 786440 | tf_op jit(solution)/shard_map/ppermute | solution.py:228
  60.6 42.9 %collective-permute-start.10 = (bf16[128,1024]{1,0:T(8,128)(2,1)S(1)}, bf16[128,1024]{1,0:T(8,128)(2,1)S(1)}, u32[]{:S(2)}, u32[]{:S(2)}) collective-permute-start(bf16[128,1024]{1,0:T(8,128)(2,1)S(1)} %get-tuple-element.49), channel_id=1, source_target_pairs={{0,14},{2,12},{4,10},{6,8},{8,6},{10,4},{12,2},{14,0},{1,15},{3,13... | collective-permute-start | bytes 786440 | tf_op jit(solution)/shard_map/ppermute | solution.py:228
  103.4 5.0 %collective-permute-start.11 = (bf16[128,1024]{1,0:T(8,128)(2,1)S(1)}, bf16[128,1024]{1,0:T(8,128)(2,1)S(1)}, u32[]{:S(2)}, u32[]{:S(2)}) collective-permute-start(bf16[128,1024]{1,0:T(8,128)(2,1)S(1)} %collective-permute-done.9.refs_2_), channel_id=1, source_target_pairs={{0,1},{2,3},{4,5},{6,7},{8,9},{10,11},{12,13},{14,15},{16,17},{18,... | collective-permute-start | bytes 786440 | tf_op jit(solution)/shard_map/ppermute | solution.py:296
  104.7 3.7 %collective-permute-start.12 = (bf16[128,1024]{1,0:T(8,128)(2,1)S(1)}, bf16[128,1024]{1,0:T(8,128)(2,1)S(1)}, u32[]{:S(2)}, u32[]{:S(2)}) collective-permute-start(bf16[128,1024]{1,0:T(8,128)(2,1)S(1)} %collective-permute-done.10.refs_3_), channel_id=1, source_target_pairs={{0,1},{2,3},{4,5},{6,7},{8,9},{10,11},{12,13},{14,15},{16,17},{18,... | collective-permute-start | bytes 786440 | tf_op jit(solution)/shard_map/ppermute | solution.py:296

commit v10 on v4

--- a/solution.py
+++ b/solution.py
@@ -206,40 +206,52 @@
     return matmul(ones, rows[:, :LANES], ((1,), (1,)))[:1] < 100.0
 
 
-def cross_last(cuts, held, *refs):
-    stages, (send, before), refs = refs[:held], refs[held : held + 2], refs[held + 2 :]
-    others, (out, keys, best) = refs[:-3], refs[-3:]
-    per = others[0].shape[0] // CLUS_DEV
+def gather_late(*refs):
+    blocks, out = refs[:-1], refs[-1]
+    for c in range(CLUS_DEV):
+        gather_group(blocks, c, out.at[c], lax.axis_index("clus"))
+
+
+def own_late(cuts, bits, held, *refs):
+    stages, (cat, before, best) = refs[:held], refs[held:]
     me = lax.axis_index("clus")
     core = lax.axis_index("blk")
+    spans = list(zip(cuts, cuts[1:]))
+    last = len(spans) - 1
+    start = spans[last][0]
+    best[:, :start] = before[:, :start]
+    best[:, start:] = jnp.full((CLUS_DEV, best.shape[1] - start), -1.0, F32)
+    for c in range(CLUS_DEV):
+        rows = [best.at[c : c + 1, a:b] for a, b in spans]
+        groups = [stage.at[core, c] for stage in stages] + [cat.at[c]]
+        raise_best(rows[last], groups[last], groups[last], True)
+        for i in range(last):
+            score_pair(rows, groups, last, i, bits[i], me)
+
+
+def cross_late(cuts, per, held, *refs):
+    stages, (cat, before, other, out, best) = refs[:held], refs[held:]
+    me = lax.axis_index("clus")
+    core = lax.axis_index("blk")
+    spans = list(zip(cuts, cuts[1:]))
     best[...] = before[...]
-    start = best.shape[1] - send.shape[2]
 
     @pl.when(core == 1)
     def _():
         for c in range(CLUS_DEV):
-            for i, other in enumerate(others):
-                keys[i * per : (i + 1) * per, :] = other[c * per : (c + 1) * per, :]
-            base = 0
-            for stage in stages:
-                end = base + stage.shape[2]
-                raise_best(best.at[c : c + 1, base:end], keys, stage.at[1, c])
-                raise_best(best.at[c : c + 1, start:], stage.at[0, c], send.at[1, c])
-                base = end
-            raise_best(best.at[c : c + 1, start:], keys, send.at[1, c])
+            rows = [best.at[c : c + 1, a:b] for a, b in spans]
+            for row, stage in zip(rows, stages):
+                raise_best(row, other.at[c], stage.at[1, c])
+                raise_best(rows[held], stage.at[0, c], cat.at[c])
+            raise_best(rows[held], other.at[c], cat.at[c])
 
     for c in range(CLUS_DEV):
-        whole = [(stage.shape[2], stage.at[core, c]) for stage in stages]
-        whole.append((send.shape[2], send.at[1, c]))
-        base = 0
-        for size, rows in whole:
-            kept = jnp.where(filled_queries(rows), best[c : c + 1, base : base + size], F32(0.0))
-            for a, b in zip(cuts, cuts[1:]):
-                if base <= a < base + size:
-                    place = (me ^ (a // per)) & ~((b - a) // per - 1)
-                    at = pl.ds(pl.multiple_of(place * per, LANES), b - a)
-                    out[c : c + 1, at] = kept[:, a - base : b - base]
-            base += size
+        groups = [stage.at[core, c] for stage in stages] + [cat.at[c]]
+        for (a, b), group in zip(spans, groups):
+            place = (me ^ (a // per)) & ~((b - a) // per - 1)
+            at = pl.ds(pl.multiple_of(place * per, LANES), b - a)
+            value = best[c : c + 1, a:b]
+            out[c : c + 1, at] = jnp.where(filled_queries(group), value, F32(0.0))
 
 
 def local(embeddings, cluster_ids):
@@ -247,10 +259,10 @@
     clusters = CLUS_DEV * owners
     rows, width = embeddings.shape
     per = 2 * rows // clusters
-    bits = [owners // 2, owners // 4, owners // 8]
-    bounds = [0, owners // 2, owners // 2 + owners // 4, owners - owners // 8, owners]
+    bits = [owners // 2, owners // 4]
+    bounds = [0, owners // 2, owners // 2 + owners // 4, owners]
     cuts = [x * per for x in bounds]
-    near, far1, far2, far3 = [list(range(a, b)) for a, b in zip(bounds, bounds[1:])]
+    near, far, late = [list(range(a, b)) for a, b in zip(bounds, bounds[1:])]
     best_shape = jax.ShapeDtypeStruct((CLUS_DEV, rows), F32)
 
     def to_owner(block, step):
@@ -263,49 +275,52 @@
         return lax.all_to_all(send, "blk", split_axis=0, concat_axis=0, tiled=True)
 
     arrived = {}
-    lead = near[1 : 1 + len(far2) + len(far3)]
+    lead = [near[-1], far[0]]
     unit, tgt, *packed = call_pack_first(embeddings, cluster_ids, lead, clusters, per)
-    for steps in (far1, near[len(lead) + 1 :] + [0], far2 + far3, []):
+    for steps in (near[1:-1] + far[1:] + [0], []):
         for step, block in zip(lead, packed):
             arrived[step] = to_owner(block, step) if step else block
         lead, packed = steps, call_pack_rest(unit, tgt, steps, per) if steps else []
-
-    early = near + far1
+    packed = call_pack_rest(unit, tgt, late, per)
+    for part, gate in ((slice(0, len(late) // 2), near[-1]), (slice(len(late) // 2, None), far[0])):
+        *held, arrived[gate] = lax.optimization_barrier((*packed[part], arrived[gate]))
+        for step, block in zip(late[part], held):
+            arrived[step] = to_owner(block, step)
+
     send, best = kernel_call(
-        functools.partial(own_stage, cuts[:3], bits, 0, 0),
-        [stage_shape(len(early)), best_shape],
-        [arrived[s] for s in early],
-        "own_early",
+        functools.partial(own_stage, cuts[:2], bits, 0, 0),
+        [stage_shape(len(near)), best_shape],
+        [arrived[s] for s in near],
+        "own_near",
     )
     stages = [to_both(send)]
     (best,) = kernel_call(
-        functools.partial(cross_stage, cuts, 0), [best_shape], stages + [best], "cross_early"
-    )
-    *new, best = lax.optimization_barrier((*[arrived[s] for s in far2], best))
+        functools.partial(cross_stage, cuts, 0), [best_shape], stages + [best], "cross_near"
+    )
+    arrived[far[-1]], best = lax.optimization_barrier((arrived[far[-1]], best))
     send, best = kernel_call(
-        functools.partial(own_stage, cuts[:4], bits, 1, 2),
-        [stage_shape(len(far2)), best_shape],
-        stages + [best] + new,
-        "own_middle",
+        functools.partial(own_stage, cuts[:3], bits, 1, 1),
+        [stage_shape(len(far)), best_shape],
+        stages + [best] + [arrived[s] for s in far],
+        "own_far",
     )
     stages.append(to_both(send))
     (best,) = kernel_call(
-        functools.partial(cross_stage, cuts, 1), [best_shape], stages + [best], "cross_middle"
-    )
-    *new, best = lax.optimization_barrier((*[arrived[s] for s in far3], best))
-    send, best = kernel_call(
-        functools.partial(own_stage, cuts, bits, 2, 3),
-        [stage_shape(len(far3)), best_shape],
-        stages + [best] + new,
-        "own_last",
-    )
-    others = [lax.ppermute(block, "blk", [(0, 1)]) for block in new]
+        functools.partial(cross_stage, cuts, 1), [best_shape], stages + [best], "cross_far"
+    )
+    *new, best = lax.optimization_barrier((*[arrived[s] for s in late], best))
+    cat_shape = jax.ShapeDtypeStruct((CLUS_DEV, len(late) * per, width), BF)
+    (cat,) = kernel_call(gather_late, [cat_shape], new, "gather_late")
+    other = lax.ppermute(cat, "blk", [(0, 1)])
+    (best,) = kernel_call(
+        functools.partial(own_late, cuts, bits, 2), [best_shape], stages + [cat, best], "own_late"
+    )
     (out,) = kernel_call(
-        functools.partial(cross_last, cuts, 2),
+        functools.partial(cross_late, cuts, per, 2),
         [best_shape],
-        stages + [send, best] + others,
-        "cross_last",
-        [pltpu.VMEM((len(far3) * per, width), BF), pltpu.VMEM((CLUS_DEV, rows), F32)],
+        stages + [cat, best, other],
+        "cross_late",
+        [pltpu.VMEM((CLUS_DEV, rows), F32)],
     )
     return out
 

time: 112 us -> 106 us (0.946)
  the two profiles are of different devices: /device:TPU:1 before, /device:TPU:17 now
where the time goes in v10:
time: 106 us
  waiting for transfers between devices  47.9 us (45%)
  blocking collectives  29.3 us (28%)
  Pallas kernels  17.6 us (17%)
  starting transfers between devices  8.98 us (8%)
  local copies, waits for them, and re-layouts  2.28 us (2%)
    ppermute x7, waiting for transfers between devices, to_owner(): return lax.ppermute(block, 'clus', [(i, i ^ step) for i in range(owners)])  46.5 us
    all_to_all x2, blocking collectives, to_both(): return lax.all_to_all(send, 'blk', split_axis=0, concat_axis=0, tiled=True)  29.3 us
    pallas_call x10, Pallas kernels, kernel_call(): pl.pallas_call(kernel, out_shape=shapes, in_specs=[VMEM] * len(inputs), o...  17.6 us
    ppermute x7, starting transfers between devices, to_owner(): return lax.ppermute(block, 'clus', [(i, i ^ step) for i in range(owners)])  7.5 us
    unnamed x4, local copies, waits for them, and re-layouts  2.28 us
  transfers between devices with their start and end apart: 8, of which 6 were waited for; matrix products, arithmetic and copies ran while one was open for 0% of the time, Pallas kernels for 12%

profile of v10, /device:TPU:17, one launch (start us, length us, event | category | flops | bytes accessed | tf_op | source)
XLA Modules:
  0.0 106.2 jit_solution(12936851991317279066)
XLA Ops:
  0.0 0.0 copy-start
  0.0 1.6 %copy-done = bf16[1024,1024]{1,0:T(8,128)(2,1)S(1)} copy-done((bf16[1024,1024]{1,0:T(8,128)(2,1)S(1)}, bf16[1024,1024]{1,0:T(8,128)(2,1)}, u32[]{:S(2)}) %copy-start) | copy-done | bytes 2097176
  1.6 0.0 copy-start.1
  1.6 0.7 copy-done.1
  2.3 2.1 %pack_first.1 = (bf16[1024,1024]{1,0:T(8,128)(2,1)S(1)}, s32[1,1024]{1,0:T(1,128)S(1)}, bf16[256,1024]{1,0:T(8,128)(2,1)S(1)}, bf16[256,1024]{1,0:T(8,128)(2,1)S(1)}) custom-call(bf16[1024,1024]{1,0:T(8,128)(2,1)S(1)} %copy-done, s32[1,1024]{1,0:T(1,128)S(1)} %copy-done.1), custom_call_target="tpu_custom_call" | custom-call | flops 1000 | bytes 1000 | tf_op jit(solution)/shard_map/pack_first/pallas_call | solution.py:80
  4.4 2.3 %collective-permute-start.2 = (bf16[256,1024]{1,0:T(8,128)(2,1)S(1)}, bf16[256,1024]{1,0:T(8,128)(2,1)S(1)}, u32[]{:S(2)}, u32[]{:S(2)}) collective-permute-start(bf16[256,1024]{1,0:T(8,128)(2,1)S(1)} %get-tuple-element.34), channel_id=1, source_target_pairs={{0,6},{2,4},{4,2},{6,0},{8,14},{10,12},{12,10},{14,8},{1,7},{3,5},... | collective-permute-start | bytes 1572872 | tf_op jit(solution)/shard_map/ppermute | solution.py:269
  6.7 0.1 collective-permute-start.4
  6.8 2.6 %pack_rest.2 = (bf16[256,1024]{1,0:T(8,128)(2,1)S(1)}, bf16[256,1024]{1,0:T(8,128)(2,1)S(1)}, bf16[256,1024]{1,0:T(8,128)(2,1)S(1)}, bf16[256,1024]{1,0:T(8,128)(2,1)S(1)}) custom-call(bf16[1024,1024]{1,0:T(8,128)(2,1)S(1)} %get-tuple-element.28.unit, s32[1,1024]{1,0:T(1,128)S(1)} %get-tuple-element.29.tgt), custom_call_target="tpu_custom_call" | custom-call | flops 1000 | bytes 1000 | tf_op jit(solution)/shard_map/pack_rest/pallas_call | solution.py:80
  9.4 0.3 collective-permute-start
  9.7 0.1 collective-permute-start.1
  9.9 3.3 %collective-permute-start.3 = (bf16[256,1024]{1,0:T(8,128)(2,1)S(1)}, bf16[256,1024]{1,0:T(8,128)(2,1)S(1)}, u32[]{:S(2)}, u32[]{:S(2)}) collective-permute-start(bf16[256,1024]{1,0:T(8,128)(2,1)S(1)} %get-tuple-element.37), channel_id=1, source_target_pairs={{0,10},{2,8},{4,14},{6,12},{8,2},{10,0},{12,6},{14,4},{1,11},{3,9}... | collective-permute-start | bytes 1572872 | tf_op jit(solution)/shard_map/ppermute | solution.py:269
  13.2 1.4 %pack_rest.3 = (bf16[256,1024]{1,0:T(8,128)(2,1)S(1)}, bf16[256,1024]{1,0:T(8,128)(2,1)S(1)}) custom-call(bf16[1024,1024]{1,0:T(8,128)(2,1)S(1)} %get-tuple-element.28.unit, s32[1,1024]{1,0:T(1,128)S(1)} %get-tuple-element.29.tgt), custom_call_target="tpu_custom_call" | custom-call | flops 1000 | bytes 1000 | tf_op jit(solution)/shard_map/pack_rest/pallas_call | solution.py:80
  14.6 12.8 %collective-permute-done.2.refs_3_ = bf16[256,1024]{1,0:T(8,128)(2,1)S(1)} collective-permute-done((bf16[256,1024]{1,0:T(8,128)(2,1)S(1)}, bf16[256,1024]{1,0:T(8,128)(2,1)S(1)}, u32[]{:S(2)}, u32[]{:S(2)}) %collective-permute-start.2) | collective-permute-done | bytes 524320 | tf_op jit(solution)/shard_map/ppermute | solution.py:269
  27.4 2.1 %collective-permute-done.4.refs_2_ = bf16[256,1024]{1,0:T(8,128)(2,1)S(1)} collective-permute-done((bf16[256,1024]{1,0:T(8,128)(2,1)S(1)}, bf16[256,1024]{1,0:T(8,128)(2,1)S(1)}, u32[]{:S(2)}, u32[]{:S(2)}) %collective-permute-start.4) | collective-permute-done | bytes 524320 | tf_op jit(solution)/shard_map/ppermute | solution.py:269
  29.4 1.2 %collective-permute-start.6 = (bf16[256,1024]{1,0:T(8,128)(2,1)S(1)}, bf16[256,1024]{1,0:T(8,128)(2,1)S(1)}, u32[]{:S(2)}, u32[]{:S(2)}) collective-permute-start(bf16[256,1024]{1,0:T(8,128)(2,1)S(1)} %get-tuple-element.46), channel_id=1, source_target_pairs={{0,14},{2,12},{4,10},{6,8},{8,6},{10,4},{12,2},{14,0},{1,15},{3,13... | collective-permute-start | bytes 1572872 | tf_op jit(solution)/shard_map/ppermute | solution.py:269
  30.7 0.2 collective-permute-start.5
  30.8 0.0 collective-permute-done.refs_1_
  30.8 18.9 %collective-permute-done.1.refs_2_ = bf16[256,1024]{1,0:T(8,128)(2,1)S(1)} collective-permute-done((bf16[256,1024]{1,0:T(8,128)(2,1)S(1)}, bf16[256,1024]{1,0:T(8,128)(2,1)S(1)}, u32[]{:S(2)}, u32[]{:S(2)}) %collective-permute-start.1) | collective-permute-done | bytes 524320 | tf_op jit(solution)/shard_map/ppermute | solution.py:269
  49.7 1.3 %own_near.1 = (bf16[2,2,512,1024]{3,2,1,0:T(8,128)(2,1)S(1)}, f32[2,1024]{1,0:T(2,128)S(1)}) custom-call(bf16[256,1024]{1,0:T(8,128)(2,1)S(1)} %get-tuple-element.30.refs_0_, bf16[256,1024]{1,0:T(8,128)(2,1)S(1)} %collective-permute-done.refs_1_, bf16[256,1024]{1,0:T(8,128)(2,1)S(1)} %collective-permute-done.1.refs_2_, ...), custom_call_target="tpu_custom_call" | custom-call | flops 1000 | bytes 1000 | tf_op jit(solution)/shard_map/own_near/pallas_call | solution.py:80
  51.0 8.3 %all_to_all.10.refs_0_ = bf16[2,2,512,1024]{3,2,1,0:T(8,128)(2,1)S(1)} all-to-all(bf16[2,2,512,1024]{3,2,1,0:T(8,128)(2,1)S(1)} %get-tuple-element.36), channel_id=1, replica_groups=mesh['groups'=2,'clus'=8,'blk'=2] {'blk'}, dimensions={0} | all-to-all | bytes 8388608 | tf_op jit(solution)/shard_map/all_to_all | solution.py:275
  59.3 1.3 %cross_near.1.refs_1_ = f32[2,1024]{1,0:T(2,128)S(1)} custom-call(bf16[2,2,512,1024]{3,2,1,0:T(8,128)(2,1)S(1)} %all_to_all.10.refs_0_, f32[2,1024]{1,0:T(2,128)S(1)} %get-tuple-element.38.refs_1_), custom_call_target="tpu_custom_call" | custom-call | flops 1000 | bytes 1000 | tf_op jit(solution)/shard_map/cross_near/pallas_call | solution.py:80
  60.6 0.0 collective-permute-done.3.refs_3_
  60.6 1.8 %own_far.1 = (bf16[2,2,256,1024]{3,2,1,0:T(8,128)(2,1)S(1)}, f32[2,1024]{1,0:T(2,128)S(1)}) custom-call(bf16[2,2,512,1024]{3,2,1,0:T(8,128)(2,1)S(1)} %all_to_all.10.refs_0_, f32[2,1024]{1,0:T(2,128)S(1)} %cross_near.1.refs_1_, bf16[256,1024]{1,0:T(8,128)(2,1)S(1)} %collective-permute-done.4.refs_2_, bf16[256,1024]{1,0:T(8,128)(2,1)S(1)} %collective-permute-done.3.refs_3_), custom_call_target="tpu_custom_call" | custom-call | flops 1000 | bytes 1000 | tf_op jit(solution)/shard_map/own_far/pallas_call | solution.py:80
  62.4 21.1 %all_to_all.11.refs_1_ = bf16[2,2,256,1024]{3,2,1,0:T(8,128)(2,1)S(1)} all-to-all(bf16[2,2,256,1024]{3,2,1,0:T(8,128)(2,1)S(1)} %get-tuple-element.44), channel_id=1, replica_groups=mesh['groups'=2,'clus'=8,'blk'=2] {'blk'}, dimensions={0} | all-to-all | bytes 4194304 | tf_op jit(solution)/shard_map/all_to_all | solution.py:275
  83.5 1.6 %cross_far.1.refs_3_ = f32[2,1024]{1,0:T(2,128)S(1)} custom-call(bf16[2,2,512,1024]{3,2,1,0:T(8,128)(2,1)S(1)} %all_to_all.10.refs_0_, bf16[2,2,256,1024]{3,2,1,0:T(8,128)(2,1)S(1)} %all_to_all.11.refs_1_, f32[2,1024]{1,0:T(2,128)S(1)} %get-tuple-element.47.refs_2_), custom_call_target="tpu_custom_call" | custom-call | flops 1000 | bytes 1000 | tf_op jit(solution)/shard_map/cross_far/pallas_call | solution.py:80
  85.1 1.5 %collective-permute-done.6.refs_1_ = bf16[256,1024]{1,0:T(8,128)(2,1)S(1)} collective-permute-done((bf16[256,1024]{1,0:T(8,128)(2,1)S(1)}, bf16[256,1024]{1,0:T(8,128)(2,1)S(1)}, u32[]{:S(2)}, u32[]{:S(2)}) %collective-permute-start.6) | collective-permute-done | bytes 524320 | tf_op jit(solution)/shard_map/ppermute | solution.py:269
  86.6 11.3 %collective-permute-done.5.refs_0_ = bf16[256,1024]{1,0:T(8,128)(2,1)S(1)} collective-permute-done((bf16[256,1024]{1,0:T(8,128)(2,1)S(1)}, bf16[256,1024]{1,0:T(8,128)(2,1)S(1)}, u32[]{:S(2)}, u32[]{:S(2)}) %collective-permute-start.5) | collective-permute-done | bytes 524320 | tf_op jit(solution)/shard_map/ppermute | solution.py:269
  97.9 0.1 gather_late.1.refs_2_
  98.0 1.5 %collective-permute-start.7 = (bf16[2,256,1024]{2,1,0:T(8,128)(2,1)S(1)}, bf16[2,256,1024]{2,1,0:T(8,128)(2,1)S(1)}, u32[]{:S(2)}, u32[]{:S(2)}) collective-permute-start(bf16[2,256,1024]{2,1,0:T(8,128)(2,1)S(1)} %gather_late.1.refs_2_), channel_id=1, source_target_pairs={{0,1},{2,3},{4,5},{6,7},{8,9},{10,11},{12,13},{14,15},{16,17},{18,... | collective-permute-start | bytes 3145736 | tf_op jit(solution)/shard_map/ppermute | solution.py:314
  99.4 2.4 %own_late.1.refs_3_ = f32[2,1024]{1,0:T(2,128)S(1)} custom-call(bf16[2,2,512,1024]{3,2,1,0:T(8,128)(2,1)S(1)} %all_to_all.10.refs_0_, bf16[2,2,256,1024]{3,2,1,0:T(8,128)(2,1)S(1)} %all_to_all.11.refs_1_, bf16[2,256,1024]{2,1,0:T(8,128)(2,1)S(1)} %gather_late.1.refs_2_, f32[2,1024]{1,0:T(2,128)S(1)} %cross_far.1.refs_3_), custom_call_target="tpu_custom_call" | custom-call | flops 1000 | bytes 1000 | tf_op jit(solution)/shard_map/own_late/pallas_call | solution.py:80
  101.8 1.4 %collective-permute-done.7.refs_4_ = bf16[2,256,1024]{2,1,0:T(8,128)(2,1)S(1)} collective-permute-done((bf16[2,256,1024]{2,1,0:T(8,128)(2,1)S(1)}, bf16[2,256,1024]{2,1,0:T(8,128)(2,1)S(1)}, u32[]{:S(2)}, u32[]{:S(2)}) %collective-permute-start.7) | collective-permute-done | bytes 1048608 | tf_op jit(solution)/shard_map/ppermute | solution.py:314
  103.2 3.0 %cross_late.1 = f32[2,1024]{1,0:T(2,128)} custom-call(bf16[2,2,512,1024]{3,2,1,0:T(8,128)(2,1)S(1)} %all_to_all.10.refs_0_, bf16[2,2,256,1024]{3,2,1,0:T(8,128)(2,1)S(1)} %all_to_all.11.refs_1_, bf16[2,256,1024]{2,1,0:T(8,128)(2,1)S(1)} %gather_late.1.refs_2_, f32[2,1024]{1,0:T(2,128)S(1)} %own_late.1.refs_3_, ...), custom_call_target="tpu_custom_call" | custom-call | flops 1000 | bytes 1000 | tf_op jit(solution)/shard_map/cross_late/pallas_call | solution.py:80
Async XLA Ops:
  0.0 1.6 %copy-start = (bf16[1024,1024]{1,0:T(8,128)(2,1)S(1)}, bf16[1024,1024]{1,0:T(8,128)(2,1)}, u32[]{:S(2)}) copy-start(bf16[1024,1024]{1,0:T(8,128)(2,1)} %emb.1) | copy-start | bytes 6291460
  1.6 0.7 copy-start.1
  4.4 23.0 %collective-permute-start.2 = (bf16[256,1024]{1,0:T(8,128)(2,1)S(1)}, bf16[256,1024]{1,0:T(8,128)(2,1)S(1)}, u32[]{:S(2)}, u32[]{:S(2)}) collective-permute-start(bf16[256,1024]{1,0:T(8,128)(2,1)S(1)} %get-tuple-element.34), channel_id=1, source_target_pairs={{0,6},{2,4},{4,2},{6,0},{8,14},{10,12},{12,10},{14,8},{1,7},{3,5},... | collective-permute-start | bytes 1572872 | tf_op jit(solution)/shard_map/ppermute | solution.py:269
  6.7 22.7 %collective-permute-start.4 = (bf16[256,1024]{1,0:T(8,128)(2,1)S(1)}, bf16[256,1024]{1,0:T(8,128)(2,1)S(1)}, u32[]{:S(2)}, u32[]{:S(2)}) collective-permute-start(bf16[256,1024]{1,0:T(8,128)(2,1)S(1)} %get-tuple-element.41), channel_id=1, source_target_pairs={{0,8},{2,10},{4,12},{6,14},{8,0},{10,2},{12,4},{14,6},{1,9},{3,11}... | collective-permute-start | bytes 1572872 | tf_op jit(solution)/shard_map/ppermute | solution.py:269
  9.4 21.4 %collective-permute-start = (bf16[256,1024]{1,0:T(8,128)(2,1)S(1)}, bf16[256,1024]{1,0:T(8,128)(2,1)S(1)}, u32[]{:S(2)}, u32[]{:S(2)}) collective-permute-start(bf16[256,1024]{1,0:T(8,128)(2,1)S(1)} %get-tuple-element.31), channel_id=1, source_target_pairs={{0,2},{2,0},{4,6},{6,4},{8,10},{10,8},{12,14},{14,12},{1,3},{3,1},... | collective-permute-start | bytes 1572872 | tf_op jit(solution)/shard_map/ppermute | solution.py:269
  9.7 40.0 %collective-permute-start.1 = (bf16[256,1024]{1,0:T(8,128)(2,1)S(1)}, bf16[256,1024]{1,0:T(8,128)(2,1)S(1)}, u32[]{:S(2)}, u32[]{:S(2)}) collective-permute-start(bf16[256,1024]{1,0:T(8,128)(2,1)S(1)} %get-tuple-element.32), channel_id=1, source_target_pairs={{0,4},{2,6},{4,0},{6,2},{8,12},{10,14},{12,8},{14,10},{1,5},{3,7},... | collective-permute-start | bytes 1572872 | tf_op jit(solution)/shard_map/ppermute | solution.py:269
  9.9 50.7 %collective-permute-start.3 = (bf16[256,1024]{1,0:T(8,128)(2,1)S(1)}, bf16[256,1024]{1,0:T(8,128)(2,1)S(1)}, u32[]{:S(2)}, u32[]{:S(2)}) collective-permute-start(bf16[256,1024]{1,0:T(8,128)(2,1)S(1)} %get-tuple-element.37), channel_id=1, source_target_pairs={{0,10},{2,8},{4,14},{6,12},{8,2},{10,0},{12,6},{14,4},{1,11},{3,9}... | collective-permute-start | bytes 1572872 | tf_op jit(solution)/shard_map/ppermute | solution.py:269
  29.4 57.1 %collective-permute-start.6 = (bf16[256,1024]{1,0:T(8,128)(2,1)S(1)}, bf16[256,1024]{1,0:T(8,128)(2,1)S(1)}, u32[]{:S(2)}, u32[]{:S(2)}) collective-permute-start(bf16[256,1024]{1,0:T(8,128)(2,1)S(1)} %get-tuple-element.46), channel_id=1, source_target_pairs={{0,14},{2,12},{4,10},{6,8},{8,6},{10,4},{12,2},{14,0},{1,15},{3,13... | collective-permute-start | bytes 1572872 | tf_op jit(solution)/shard_map/ppermute | solution.py:269
  30.7 67.2 %collective-permute-start.5 = (bf16[256,1024]{1,0:T(8,128)(2,1)S(1)}, bf16[256,1024]{1,0:T(8,128)(2,1)S(1)}, u32[]{:S(2)}, u32[]{:S(2)}) collective-permute-start(bf16[256,1024]{1,0:T(8,128)(2,1)S(1)} %get-tuple-element.45), channel_id=1, source_target_pairs={{0,12},{2,14},{4,8},{6,10},{8,4},{10,6},{12,0},{14,2},{1,13},{3,15... | collective-permute-start | bytes 1572872 | tf_op jit(solution)/shard_map/ppermute | solution.py:269
  98.0 5.3 %collective-permute-start.7 = (bf16[2,256,1024]{2,1,0:T(8,128)(2,1)S(1)}, bf16[2,256,1024]{2,1,0:T(8,128)(2,1)S(1)}, u32[]{:S(2)}, u32[]{:S(2)}) collective-permute-start(bf16[2,256,1024]{2,1,0:T(8,128)(2,1)S(1)} %gather_late.1.refs_2_), channel_id=1, source_target_pairs={{0,1},{2,3},{4,5},{6,7},{8,9},{10,11},{12,13},{14,15},{16,17},{18,... | collective-permute-start | bytes 3145736 | tf_op jit(solution)/shard_map/ppermute | solution.py:314

commit v11 on v10

--- a/solution.py
+++ b/solution.py
@@ -10,6 +10,7 @@
 CLUS_DEV = 2
 LANES = 128
 MARK = 2.0
+UNFILLED = 8.0
 BF = jnp.bfloat16
 F32 = jnp.float32
 
@@ -61,11 +62,28 @@
         out[:, LANES:] = tail
 
 
-def pack_first(steps, clusters, per_source, emb, ids, unit, tgt, *outs):
-    values = emb[...].astype(F32)
-    scale = lax.rsqrt(jnp.sum(values * values, axis=1, keepdims=True) + 1e-6)
-    unit[...] = (values * scale).astype(BF)
-    tgt[...] = targets(ids[...], clusters, per_source)
+PIECES = 4
+
+
+def pack_first(steps, clusters, per_source, emb, ids, unit, tgt, *refs):
+    outs, (raw, raw_ids, sems, ids_sem) = refs[:-4], refs[-4:]
+    size = emb.shape[0] // PIECES
+    ids_copy = pltpu.make_async_copy(ids, raw_ids, ids_sem)
+    ids_copy.start()
+    windows = [pl.ds(piece * size, size) for piece in range(PIECES)]
+    copies = [
+        pltpu.make_async_copy(emb.at[window], raw.at[window], sems.at[piece])
+        for piece, window in enumerate(windows)
+    ]
+    for copy in copies:
+        copy.start()
+    ids_copy.wait()
+    tgt[...] = targets(raw_ids[...], clusters, per_source)
+    for copy, window in zip(copies, windows):
+        copy.wait()
+        values = raw[window, :].astype(F32)
+        scale = lax.rsqrt(jnp.sum(values * values, axis=1, keepdims=True) + 1e-6)
+        unit[window, :] = (values * scale).astype(BF)
     store_blocks(unit[...], tgt[...], steps, CLUS_DEV * per_source, outs)
 
 
@@ -76,14 +94,14 @@
 VMEM = pl.BlockSpec(memory_space=pltpu.VMEM)
 
 
-def kernel_call(kernel, shapes, inputs, name, scratch=()):
+def kernel_call(kernel, shapes, inputs, name, scratch=(), place=VMEM, grant=20 * 2**20):
     return pl.pallas_call(
         kernel,
         out_shape=shapes,
-        in_specs=[VMEM] * len(inputs),
+        in_specs=[place] * len(inputs),
         out_specs=[VMEM] * len(shapes),
         scratch_shapes=scratch,
-        compiler_params=pltpu.CompilerParams(vmem_limit_bytes=20 * 2**20),
+        compiler_params=pltpu.CompilerParams(vmem_limit_bytes=grant),
         cost_estimate=pl.CostEstimate(flops=1000, bytes_accessed=1000, transcendentals=0),
         name=name,
     )(*inputs)
@@ -96,7 +114,15 @@
         functools.partial(pack_first, steps, clusters, per_source),
         shapes + [block] * len(steps),
         [emb, ids],
-        "pack_first",
+        place=pl.BlockSpec(memory_space=pl.ANY),
+        grant=50 * 2**20,
+        name="pack_first",
+        scratch=[
+            pltpu.VMEM(emb.shape, BF),
+            pltpu.VMEM(ids.shape, jnp.int32),
+            pltpu.SemaphoreType.DMA((PIECES,)),
+            pltpu.SemaphoreType.DMA,
+        ],
     )
 
 
@@ -151,6 +177,12 @@
         raise_best(bests[old], groups[new], groups[old])
 
 
+def fresh_best(rows):
+    ones = jnp.ones((8, LANES), BF)
+    heads = matmul(ones, rows[:, :LANES], ((1,), (1,)))[:1]
+    return jnp.where(heads < 100.0, F32(-1.0), F32(UNFILLED))
+
+
 def own_stage(cuts, bits, held, first, *refs):
     stages, refs = refs[:held], refs[held:]
     blocks, (send, best) = list(refs[:-2]), refs[-2:]
@@ -162,7 +194,6 @@
     base = spans[first][0]
     if held:
         best[:, :base] = before[:, :base]
-    best[:, base:] = jnp.full((CLUS_DEV, best.shape[1] - base), -1.0, F32)
     for c in range(CLUS_DEV):
         rows = [best.at[c : c + 1, a:b] for a, b in spans]
         groups = []
@@ -177,6 +208,7 @@
             group = send.at[1, c, a - base : b - base]
             gather_group(blocks[(a - base) // per : (b - base) // per], c, group, me)
             groups.append(group)
+            rows[i][...] = fresh_best(group)
             raise_best(rows[i], group, group, True)
             for j in range(i):
                 score_pair(rows, groups, i, j, bits[j], me)
@@ -201,11 +233,6 @@
                 raise_best(best.at[c : c + 1, start:base], stage.at[0, c], new.at[1, c])
 
 
-def filled_queries(rows):
-    ones = jnp.ones((8, LANES), BF)
-    return matmul(ones, rows[:, :LANES], ((1,), (1,)))[:1] < 100.0
-
-
 def gather_late(*refs):
     blocks, out = refs[:-1], refs[-1]
     for c in range(CLUS_DEV):
@@ -220,10 +247,10 @@
     last = len(spans) - 1
     start = spans[last][0]
     best[:, :start] = before[:, :start]
-    best[:, start:] = jnp.full((CLUS_DEV, best.shape[1] - start), -1.0, F32)
     for c in range(CLUS_DEV):
         rows = [best.at[c : c + 1, a:b] for a, b in spans]
         groups = [stage.at[core, c] for stage in stages] + [cat.at[c]]
+        rows[last][...] = fresh_best(groups[last])
         raise_best(rows[last], groups[last], groups[last], True)
         for i in range(last):
             score_pair(rows, groups, last, i, bits[i], me)
@@ -245,13 +272,11 @@
                 raise_best(rows[held], stage.at[0, c], cat.at[c])
             raise_best(rows[held], other.at[c], cat.at[c])
 
-    for c in range(CLUS_DEV):
-        groups = [stage.at[core, c] for stage in stages] + [cat.at[c]]
-        for (a, b), group in zip(spans, groups):
-            place = (me ^ (a // per)) & ~((b - a) // per - 1)
-            at = pl.ds(pl.multiple_of(place * per, LANES), b - a)
-            value = best[c : c + 1, a:b]
-            out[c : c + 1, at] = jnp.where(filled_queries(group), value, F32(0.0))
+    for a, b in spans:
+        place = (me ^ (a // per)) & ~((b - a) // per - 1)
+        value = best[:, a:b]
+        at = pl.ds(pl.multiple_of(place * per, LANES), b - a)
+        out[:, at] = jnp.where(value > 0.5 * UNFILLED, F32(0.0), value)
 
 
 def local(embeddings, cluster_ids):
@@ -275,17 +300,16 @@
         return lax.all_to_all(send, "blk", split_axis=0, concat_axis=0, tiled=True)
 
     arrived = {}
-    lead = [near[-1], far[0]]
+    lead = far[:1]
     unit, tgt, *packed = call_pack_first(embeddings, cluster_ids, lead, clusters, per)
-    for steps in (near[1:-1] + far[1:] + [0], []):
+    for steps in (near[1:] + far[1:] + [0], []):
         for step, block in zip(lead, packed):
             arrived[step] = to_owner(block, step) if step else block
         lead, packed = steps, call_pack_rest(unit, tgt, steps, per) if steps else []
     packed = call_pack_rest(unit, tgt, late, per)
-    for part, gate in ((slice(0, len(late) // 2), near[-1]), (slice(len(late) // 2, None), far[0])):
-        *held, arrived[gate] = lax.optimization_barrier((*packed[part], arrived[gate]))
-        for step, block in zip(late[part], held):
-            arrived[step] = to_owner(block, step)
+    *held, arrived[far[0]] = lax.optimization_barrier((*packed, arrived[far[0]]))
+    for step, block in zip(late, held):
+        arrived[step] = to_owner(block, step)
 
     send, best = kernel_call(
         functools.partial(own_stage, cuts[:2], bits, 0, 0),

time: 106 us -> 106 us (level); the launches traced: 106 us -> 105 us
  blocking collectives: 29.3 us -> 13.9 us
  waiting for transfers between devices: 47.9 us -> 60.3 us
  starting transfers between devices: 8.98 us -> 11.6 us
  local copies, waits for them, and re-layouts: 2.28 us -> 0.69 us
    all_to_all x2, blocking collectives: 29.3 us -> 13.9 us  [to_both(): return lax.all_to_all(send, 'blk', split_axis=0, concat_axis=0, tiled=True)]
    ppermute x7, waiting for transfers between devices: 46.5 us -> 59.6 us  [to_owner(): return lax.ppermute(block, 'clus', [(i, i ^ step) for i in range(owners)])]
    ppermute x7, starting transfers between devices: 7.5 us -> 10.1 us  [to_owner(): return lax.ppermute(block, 'clus', [(i, i ^ step) for i in range(owners)])]
    unnamed x4 -> x2, local copies, waits for them, and re-layouts: 2.28 us -> 0.69 us
  transfers between devices with their start and end apart: 8 -> 8, of which waited for: 6 -> 5; matrix products, arithmetic and copies ran while one was open for 0% -> 0% of each run, Pallas kernels for 12% -> 12%
where the time goes in v11:
time: 106 us; the launch traced here: 105 us
  waiting for transfers between devices  60.3 us (57%)
  Pallas kernels  18.5 us (17%)
  blocking collectives  13.9 us (13%)
  starting transfers between devices  11.6 us (11%)
    ppermute x7, waiting for transfers between devices, to_owner(): return lax.ppermute(block, 'clus', [(i, i ^ step) for i in range(owners)])  59.6 us
    pallas_call x10, Pallas kernels, kernel_call(): pl.pallas_call(kernel, out_shape=shapes, in_specs=[place] * len(inputs),...  18.5 us
    all_to_all x2, blocking collectives, to_both(): return lax.all_to_all(send, 'blk', split_axis=0, concat_axis=0, tiled=True)  13.9 us
    ppermute x7, starting transfers between devices, to_owner(): return lax.ppermute(block, 'clus', [(i, i ^ step) for i in range(owners)])  10.1 us
  transfers between devices with their start and end apart: 8, of which 5 were waited for; matrix products, arithmetic and copies ran while one was open for 0% of the time, Pallas kernels for 12%

profile of v11, /device:TPU:17, one launch (start us, length us, event | category | flops | bytes accessed | tf_op | source)
XLA Modules:
  0.0 105.1 jit_solution(17263711615333245707)
XLA Ops:
  0.0 0.0 copy-start
  0.0 0.7 copy-done
  0.7 2.6 %pack_first.1 = (bf16[1024,1024]{1,0:T(8,128)(2,1)S(1)}, s32[1,1024]{1,0:T(1,128)S(1)}, bf16[256,1024]{1,0:T(8,128)(2,1)S(1)}) custom-call(bf16[1024,1024]{1,0:T(8,128)(2,1)} %emb.1, s32[1,1024]{1,0:T(1,128)S(1)} %copy-done), custom_call_target="tpu_custom_call" | custom-call | flops 1000 | bytes 1000 | tf_op jit(solution)/shard_map/pack_first/pallas_call | solution.py:98
  3.3 0.1 collective-permute-start.4
  3.3 3.2 %pack_rest.2 = (bf16[256,1024]{1,0:T(8,128)(2,1)S(1)}, bf16[256,1024]{1,0:T(8,128)(2,1)S(1)}, bf16[256,1024]{1,0:T(8,128)(2,1)S(1)}, bf16[256,1024]{1,0:T(8,128)(2,1)S(1)}, bf16[256,1024]{1,0:T(8,128)(2,1)S(1)}) custom-call(bf16[1024,1024]{1,0:T(8,128)(2,1)S(1)} %get-tuple-element.27.unit, s32[1,1024]{1,0:T(1,128)S(1)} %get-tuple-element.28.tgt), custom_call_target="tpu_custom_call" | custom-call | flops 1000 | bytes 1000 | tf_op jit(solution)/shard_map/pack_rest/pallas_call | solution.py:98
  6.6 1.4 %collective-permute-start = (bf16[256,1024]{1,0:T(8,128)(2,1)S(1)}, bf16[256,1024]{1,0:T(8,128)(2,1)S(1)}, u32[]{:S(2)}, u32[]{:S(2)}) collective-permute-start(bf16[256,1024]{1,0:T(8,128)(2,1)S(1)} %get-tuple-element.30), channel_id=1, source_target_pairs={{0,2},{2,0},{4,6},{6,4},{8,10},{10,8},{12,14},{14,12},{1,3},{3,1},... | collective-permute-start | bytes 1572872 | tf_op jit(solution)/shard_map/ppermute | solution.py:294
  7.9 1.3 %collective-permute-start.1 = (bf16[256,1024]{1,0:T(8,128)(2,1)S(1)}, bf16[256,1024]{1,0:T(8,128)(2,1)S(1)}, u32[]{:S(2)}, u32[]{:S(2)}) collective-permute-start(bf16[256,1024]{1,0:T(8,128)(2,1)S(1)} %get-tuple-element.31), channel_id=1, source_target_pairs={{0,4},{2,6},{4,0},{6,2},{8,12},{10,14},{12,8},{14,10},{1,5},{3,7},... | collective-permute-start | bytes 1572872 | tf_op jit(solution)/shard_map/ppermute | solution.py:294
  9.2 0.1 collective-permute-start.2
  9.3 3.3 %collective-permute-start.3 = (bf16[256,1024]{1,0:T(8,128)(2,1)S(1)}, bf16[256,1024]{1,0:T(8,128)(2,1)S(1)}, u32[]{:S(2)}, u32[]{:S(2)}) collective-permute-start(bf16[256,1024]{1,0:T(8,128)(2,1)S(1)} %get-tuple-element.34), channel_id=1, source_target_pairs={{0,10},{2,8},{4,14},{6,12},{8,2},{10,0},{12,6},{14,4},{1,11},{3,9}... | collective-permute-start | bytes 1572872 | tf_op jit(solution)/shard_map/ppermute | solution.py:294
  12.6 1.4 %pack_rest.3 = (bf16[256,1024]{1,0:T(8,128)(2,1)S(1)}, bf16[256,1024]{1,0:T(8,128)(2,1)S(1)}) custom-call(bf16[1024,1024]{1,0:T(8,128)(2,1)S(1)} %get-tuple-element.27.unit, s32[1,1024]{1,0:T(1,128)S(1)} %get-tuple-element.28.tgt), custom_call_target="tpu_custom_call" | custom-call | flops 1000 | bytes 1000 | tf_op jit(solution)/shard_map/pack_rest/pallas_call | solution.py:98
  14.0 11.5 %collective-permute-done.4.refs_2_ = bf16[256,1024]{1,0:T(8,128)(2,1)S(1)} collective-permute-done((bf16[256,1024]{1,0:T(8,128)(2,1)S(1)}, bf16[256,1024]{1,0:T(8,128)(2,1)S(1)}, u32[]{:S(2)}, u32[]{:S(2)}) %collective-permute-start.4) | collective-permute-done | bytes 524320 | tf_op jit(solution)/shard_map/ppermute | solution.py:294
  25.5 3.1 %collective-permute-start.5 = (bf16[256,1024]{1,0:T(8,128)(2,1)S(1)}, bf16[256,1024]{1,0:T(8,128)(2,1)S(1)}, u32[]{:S(2)}, u32[]{:S(2)}) collective-permute-start(bf16[256,1024]{1,0:T(8,128)(2,1)S(1)} %get-tuple-element.43), channel_id=1, source_target_pairs={{0,12},{2,14},{4,8},{6,10},{8,4},{10,6},{12,0},{14,2},{1,13},{3,15... | collective-permute-start | bytes 1572872 | tf_op jit(solution)/shard_map/ppermute | solution.py:294
  28.6 0.0 collective-permute-done.refs_1_
  28.6 1.0 collective-permute-start.6
  29.6 11.9 %collective-permute-done.1.refs_2_ = bf16[256,1024]{1,0:T(8,128)(2,1)S(1)} collective-permute-done((bf16[256,1024]{1,0:T(8,128)(2,1)S(1)}, bf16[256,1024]{1,0:T(8,128)(2,1)S(1)}, u32[]{:S(2)}, u32[]{:S(2)}) %collective-permute-start.1) | collective-permute-done | bytes 524320 | tf_op jit(solution)/shard_map/ppermute | solution.py:294
  41.4 33.8 %collective-permute-done.2.refs_3_ = bf16[256,1024]{1,0:T(8,128)(2,1)S(1)} collective-permute-done((bf16[256,1024]{1,0:T(8,128)(2,1)S(1)}, bf16[256,1024]{1,0:T(8,128)(2,1)S(1)}, u32[]{:S(2)}, u32[]{:S(2)}) %collective-permute-start.2) | collective-permute-done | bytes 524320 | tf_op jit(solution)/shard_map/ppermute | solution.py:294
  75.3 1.3 %own_near.1 = (bf16[2,2,512,1024]{3,2,1,0:T(8,128)(2,1)S(1)}, f32[2,1024]{1,0:T(2,128)S(1)}) custom-call(bf16[256,1024]{1,0:T(8,128)(2,1)S(1)} %get-tuple-element.29.refs_0_, bf16[256,1024]{1,0:T(8,128)(2,1)S(1)} %collective-permute-done.refs_1_, bf16[256,1024]{1,0:T(8,128)(2,1)S(1)} %collective-permute-done.1.refs_2_, ...), custom_call_target="tpu_custom_call" | custom-call | flops 1000 | bytes 1000 | tf_op jit(solution)/shard_map/own_near/pallas_call | solution.py:98
  76.6 8.9 %all_to_all.10.refs_0_ = bf16[2,2,512,1024]{3,2,1,0:T(8,128)(2,1)S(1)} all-to-all(bf16[2,2,512,1024]{3,2,1,0:T(8,128)(2,1)S(1)} %get-tuple-element.33), channel_id=1, replica_groups=mesh['groups'=2,'clus'=8,'blk'=2] {'blk'}, dimensions={0} | all-to-all | bytes 8388608 | tf_op jit(solution)/shard_map/all_to_all | solution.py:300
  85.5 1.3 %cross_near.1.refs_1_ = f32[2,1024]{1,0:T(2,128)S(1)} custom-call(bf16[2,2,512,1024]{3,2,1,0:T(8,128)(2,1)S(1)} %all_to_all.10.refs_0_, f32[2,1024]{1,0:T(2,128)S(1)} %get-tuple-element.35.refs_1_), custom_call_target="tpu_custom_call" | custom-call | flops 1000 | bytes 1000 | tf_op jit(solution)/shard_map/cross_near/pallas_call | solution.py:98
  86.8 0.0 collective-permute-done.3.refs_3_
  86.8 1.8 %own_far.1 = (bf16[2,2,256,1024]{3,2,1,0:T(8,128)(2,1)S(1)}, f32[2,1024]{1,0:T(2,128)S(1)}) custom-call(bf16[2,2,512,1024]{3,2,1,0:T(8,128)(2,1)S(1)} %all_to_all.10.refs_0_, f32[2,1024]{1,0:T(2,128)S(1)} %cross_near.1.refs_1_, bf16[256,1024]{1,0:T(8,128)(2,1)S(1)} %collective-permute-done.4.refs_2_, bf16[256,1024]{1,0:T(8,128)(2,1)S(1)} %collective-permute-done.3.refs_3_), custom_call_target="tpu_custom_call" | custom-call | flops 1000 | bytes 1000 | tf_op jit(solution)/shard_map/own_far/pallas_call | solution.py:98
  88.7 5.1 %all_to_all.11.refs_1_ = bf16[2,2,256,1024]{3,2,1,0:T(8,128)(2,1)S(1)} all-to-all(bf16[2,2,256,1024]{3,2,1,0:T(8,128)(2,1)S(1)} %get-tuple-element.42), channel_id=1, replica_groups=mesh['groups'=2,'clus'=8,'blk'=2] {'blk'}, dimensions={0} | all-to-all | bytes 4194304 | tf_op jit(solution)/shard_map/all_to_all | solution.py:300
  93.7 1.6 %cross_far.1.refs_3_ = f32[2,1024]{1,0:T(2,128)S(1)} custom-call(bf16[2,2,512,1024]{3,2,1,0:T(8,128)(2,1)S(1)} %all_to_all.10.refs_0_, bf16[2,2,256,1024]{3,2,1,0:T(8,128)(2,1)S(1)} %all_to_all.11.refs_1_, f32[2,1024]{1,0:T(2,128)S(1)} %get-tuple-element.45.refs_2_), custom_call_target="tpu_custom_call" | custom-call | flops 1000 | bytes 1000 | tf_op jit(solution)/shard_map/cross_far/pallas_call | solution.py:98
  95.3 0.0 collective-permute-done.5.refs_0_
  95.3 2.4 %collective-permute-done.6.refs_1_ = bf16[256,1024]{1,0:T(8,128)(2,1)S(1)} collective-permute-done((bf16[256,1024]{1,0:T(8,128)(2,1)S(1)}, bf16[256,1024]{1,0:T(8,128)(2,1)S(1)}, u32[]{:S(2)}, u32[]{:S(2)}) %collective-permute-start.6) | collective-permute-done | bytes 524320 | tf_op jit(solution)/shard_map/ppermute | solution.py:294
  97.7 0.1 gather_late.1.refs_2_
  97.8 1.5 %collective-permute-start.7 = (bf16[2,256,1024]{2,1,0:T(8,128)(2,1)S(1)}, bf16[2,256,1024]{2,1,0:T(8,128)(2,1)S(1)}, u32[]{:S(2)}, u32[]{:S(2)}) collective-permute-start(bf16[2,256,1024]{2,1,0:T(8,128)(2,1)S(1)} %gather_late.1.refs_2_), channel_id=1, source_target_pairs={{0,1},{2,3},{4,5},{6,7},{8,9},{10,11},{12,13},{14,15},{16,17},{18,... | collective-permute-start | bytes 3145736 | tf_op jit(solution)/shard_map/ppermute | solution.py:338
  99.3 2.4 %own_late.1.refs_3_ = f32[2,1024]{1,0:T(2,128)S(1)} custom-call(bf16[2,2,512,1024]{3,2,1,0:T(8,128)(2,1)S(1)} %all_to_all.10.refs_0_, bf16[2,2,256,1024]{3,2,1,0:T(8,128)(2,1)S(1)} %all_to_all.11.refs_1_, bf16[2,256,1024]{2,1,0:T(8,128)(2,1)S(1)} %gather_late.1.refs_2_, f32[2,1024]{1,0:T(2,128)S(1)} %cross_far.1.refs_3_), custom_call_target="tpu_custom_call" | custom-call | flops 1000 | bytes 1000 | tf_op jit(solution)/shard_map/own_late/pallas_call | solution.py:98
  101.7 0.7 collective-permute-done.7.refs_4_
  102.4 2.8 %cross_late.1 = f32[2,1024]{1,0:T(2,128)} custom-call(bf16[2,2,512,1024]{3,2,1,0:T(8,128)(2,1)S(1)} %all_to_all.10.refs_0_, bf16[2,2,256,1024]{3,2,1,0:T(8,128)(2,1)S(1)} %all_to_all.11.refs_1_, bf16[2,256,1024]{2,1,0:T(8,128)(2,1)S(1)} %gather_late.1.refs_2_, f32[2,1024]{1,0:T(2,128)S(1)} %own_late.1.refs_3_, ...), custom_call_target="tpu_custom_call" | custom-call | flops 1000 | bytes 1000 | tf_op jit(solution)/shard_map/cross_late/pallas_call | solution.py:98
Async XLA Ops:
  0.0 0.7 copy-start
  3.3 22.3 %collective-permute-start.4 = (bf16[256,1024]{1,0:T(8,128)(2,1)S(1)}, bf16[256,1024]{1,0:T(8,128)(2,1)S(1)}, u32[]{:S(2)}, u32[]{:S(2)}) collective-permute-start(bf16[256,1024]{1,0:T(8,128)(2,1)S(1)} %get-tuple-element.39), channel_id=1, source_target_pairs={{0,8},{2,10},{4,12},{6,14},{8,0},{10,2},{12,4},{14,6},{1,9},{3,11}... | collective-permute-start | bytes 1572872 | tf_op jit(solution)/shard_map/ppermute | solution.py:294
  6.6 22.0 %collective-permute-start = (bf16[256,1024]{1,0:T(8,128)(2,1)S(1)}, bf16[256,1024]{1,0:T(8,128)(2,1)S(1)}, u32[]{:S(2)}, u32[]{:S(2)}) collective-permute-start(bf16[256,1024]{1,0:T(8,128)(2,1)S(1)} %get-tuple-element.30), channel_id=1, source_target_pairs={{0,2},{2,0},{4,6},{6,4},{8,10},{10,8},{12,14},{14,12},{1,3},{3,1},... | collective-permute-start | bytes 1572872 | tf_op jit(solution)/shard_map/ppermute | solution.py:294
  7.9 33.5 %collective-permute-start.1 = (bf16[256,1024]{1,0:T(8,128)(2,1)S(1)}, bf16[256,1024]{1,0:T(8,128)(2,1)S(1)}, u32[]{:S(2)}, u32[]{:S(2)}) collective-permute-start(bf16[256,1024]{1,0:T(8,128)(2,1)S(1)} %get-tuple-element.31), channel_id=1, source_target_pairs={{0,4},{2,6},{4,0},{6,2},{8,12},{10,14},{12,8},{14,10},{1,5},{3,7},... | collective-permute-start | bytes 1572872 | tf_op jit(solution)/shard_map/ppermute | solution.py:294
  9.2 66.1 %collective-permute-start.2 = (bf16[256,1024]{1,0:T(8,128)(2,1)S(1)}, bf16[256,1024]{1,0:T(8,128)(2,1)S(1)}, u32[]{:S(2)}, u32[]{:S(2)}) collective-permute-start(bf16[256,1024]{1,0:T(8,128)(2,1)S(1)} %get-tuple-element.32), channel_id=1, source_target_pairs={{0,6},{2,4},{4,2},{6,0},{8,14},{10,12},{12,10},{14,8},{1,7},{3,5},... | collective-permute-start | bytes 1572872 | tf_op jit(solution)/shard_map/ppermute | solution.py:294
  9.3 77.5 %collective-permute-start.3 = (bf16[256,1024]{1,0:T(8,128)(2,1)S(1)}, bf16[256,1024]{1,0:T(8,128)(2,1)S(1)}, u32[]{:S(2)}, u32[]{:S(2)}) collective-permute-start(bf16[256,1024]{1,0:T(8,128)(2,1)S(1)} %get-tuple-element.34), channel_id=1, source_target_pairs={{0,10},{2,8},{4,14},{6,12},{8,2},{10,0},{12,6},{14,4},{1,11},{3,9}... | collective-permute-start | bytes 1572872 | tf_op jit(solution)/shard_map/ppermute | solution.py:294
  25.5 69.8 %collective-permute-start.5 = (bf16[256,1024]{1,0:T(8,128)(2,1)S(1)}, bf16[256,1024]{1,0:T(8,128)(2,1)S(1)}, u32[]{:S(2)}, u32[]{:S(2)}) collective-permute-start(bf16[256,1024]{1,0:T(8,128)(2,1)S(1)} %get-tuple-element.43), channel_id=1, source_target_pairs={{0,12},{2,14},{4,8},{6,10},{8,4},{10,6},{12,0},{14,2},{1,13},{3,15... | collective-permute-start | bytes 1572872 | tf_op jit(solution)/shard_map/ppermute | solution.py:294
  28.6 69.1 %collective-permute-start.6 = (bf16[256,1024]{1,0:T(8,128)(2,1)S(1)}, bf16[256,1024]{1,0:T(8,128)(2,1)S(1)}, u32[]{:S(2)}, u32[]{:S(2)}) collective-permute-start(bf16[256,1024]{1,0:T(8,128)(2,1)S(1)} %get-tuple-element.44), channel_id=1, source_target_pairs={{0,14},{2,12},{4,10},{6,8},{8,6},{10,4},{12,2},{14,0},{1,15},{3,13... | collective-permute-start | bytes 1572872 | tf_op jit(solution)/shard_map/ppermute | solution.py:294
  97.8 4.6 %collective-permute-start.7 = (bf16[2,256,1024]{2,1,0:T(8,128)(2,1)S(1)}, bf16[2,256,1024]{2,1,0:T(8,128)(2,1)S(1)}, u32[]{:S(2)}, u32[]{:S(2)}) collective-permute-start(bf16[2,256,1024]{2,1,0:T(8,128)(2,1)S(1)} %gather_late.1.refs_2_), channel_id=1, source_target_pairs={{0,1},{2,3},{4,5},{6,7},{8,9},{10,11},{12,13},{14,15},{16,17},{18,... | collective-permute-start | bytes 3145736 | tf_op jit(solution)/shard_map/ppermute | solution.py:338

commit v12 on v11

--- a/solution.py
+++ b/solution.py
@@ -187,6 +187,7 @@
     stages, refs = refs[:held], refs[held:]
     blocks, (send, best) = list(refs[:-2]), refs[-2:]
     before = blocks.pop(0) if held else None
+    blocks.reverse()
     per = blocks[0].shape[0] // CLUS_DEV
     me = lax.axis_index("clus")
     core = lax.axis_index("blk")
@@ -314,7 +315,7 @@
     send, best = kernel_call(
         functools.partial(own_stage, cuts[:2], bits, 0, 0),
         [stage_shape(len(near)), best_shape],
-        [arrived[s] for s in near],
+        [arrived[s] for s in reversed(near)],
         "own_near",
     )
     stages = [to_both(send)]
@@ -325,7 +326,7 @@
     send, best = kernel_call(
         functools.partial(own_stage, cuts[:3], bits, 1, 1),
         [stage_shape(len(far)), best_shape],
-        stages + [best] + [arrived[s] for s in far],
+        stages + [best] + [arrived[s] for s in reversed(far)],
         "own_far",
     )
     stages.append(to_both(send))

time: 106 us -> 106 us (level)
  waiting for transfers between devices: 60.3 us -> 61.4 us
    ppermute x7, waiting for transfers between devices: 59.6 us -> 60.7 us  [to_owner(): return lax.ppermute(block, 'clus', [(i, i ^ step) for i in range(owners)])]
where the time goes in v12:
time: 106 us; the launch traced here: 105 us
  waiting for transfers between devices  61.4 us (58%)
  Pallas kernels  18.5 us (17%)
  blocking collectives  13.7 us (13%)
  starting transfers between devices  10.7 us (10%)
    ppermute x7, waiting for transfers between devices, to_owner(): return lax.ppermute(block, 'clus', [(i, i ^ step) for i in range(owners)])  60.7 us
    pallas_call x10, Pallas kernels, kernel_call(): pl.pallas_call(kernel, out_shape=shapes, in_specs=[place] * len(inputs),...  18.5 us
    all_to_all x2, blocking collectives, to_both(): return lax.all_to_all(send, 'blk', split_axis=0, concat_axis=0, tiled=True)  13.7 us
    ppermute x7, starting transfers between devices, to_owner(): return lax.ppermute(block, 'clus', [(i, i ^ step) for i in range(owners)])  9.27 us
  transfers between devices with their start and end apart: 8, of which 5 were waited for; matrix products, arithmetic and copies ran while one was open for 0% of the time, Pallas kernels for 12%

profile of v12, /device:TPU:17, one launch (start us, length us, event | category | flops | bytes accessed | tf_op | source)
XLA Modules:
  0.0 105.1 jit_solution(14862376173377216251)
XLA Ops:
  0.0 0.0 copy-start
  0.0 0.7 copy-done
  0.7 2.6 %pack_first.1 = (bf16[1024,1024]{1,0:T(8,128)(2,1)S(1)}, s32[1,1024]{1,0:T(1,128)S(1)}, bf16[256,1024]{1,0:T(8,128)(2,1)S(1)}) custom-call(bf16[1024,1024]{1,0:T(8,128)(2,1)} %emb.1, s32[1,1024]{1,0:T(1,128)S(1)} %copy-done), custom_call_target="tpu_custom_call" | custom-call | flops 1000 | bytes 1000 | tf_op jit(solution)/shard_map/pack_first/pallas_call | solution.py:98
  3.3 0.1 collective-permute-start.4
  3.3 3.2 %pack_rest.2 = (bf16[256,1024]{1,0:T(8,128)(2,1)S(1)}, bf16[256,1024]{1,0:T(8,128)(2,1)S(1)}, bf16[256,1024]{1,0:T(8,128)(2,1)S(1)}, bf16[256,1024]{1,0:T(8,128)(2,1)S(1)}, bf16[256,1024]{1,0:T(8,128)(2,1)S(1)}) custom-call(bf16[1024,1024]{1,0:T(8,128)(2,1)S(1)} %get-tuple-element.27.unit, s32[1,1024]{1,0:T(1,128)S(1)} %get-tuple-element.28.tgt), custom_call_target="tpu_custom_call" | custom-call | flops 1000 | bytes 1000 | tf_op jit(solution)/shard_map/pack_rest/pallas_call | solution.py:98
  6.6 2.4 %collective-permute-start = (bf16[256,1024]{1,0:T(8,128)(2,1)S(1)}, bf16[256,1024]{1,0:T(8,128)(2,1)S(1)}, u32[]{:S(2)}, u32[]{:S(2)}) collective-permute-start(bf16[256,1024]{1,0:T(8,128)(2,1)S(1)} %get-tuple-element.29), channel_id=1, source_target_pairs={{0,6},{2,4},{4,2},{6,0},{8,14},{10,12},{12,10},{14,8},{1,7},{3,5},... | collective-permute-start | bytes 1572872 | tf_op jit(solution)/shard_map/ppermute | solution.py:295
  8.9 0.2 collective-permute-start.1
  9.1 0.2 collective-permute-start.2
  9.3 3.3 %collective-permute-start.3 = (bf16[256,1024]{1,0:T(8,128)(2,1)S(1)}, bf16[256,1024]{1,0:T(8,128)(2,1)S(1)}, u32[]{:S(2)}, u32[]{:S(2)}) collective-permute-start(bf16[256,1024]{1,0:T(8,128)(2,1)S(1)} %get-tuple-element.34), channel_id=1, source_target_pairs={{0,10},{2,8},{4,14},{6,12},{8,2},{10,0},{12,6},{14,4},{1,11},{3,9}... | collective-permute-start | bytes 1572872 | tf_op jit(solution)/shard_map/ppermute | solution.py:295
  12.6 1.4 %pack_rest.3 = (bf16[256,1024]{1,0:T(8,128)(2,1)S(1)}, bf16[256,1024]{1,0:T(8,128)(2,1)S(1)}) custom-call(bf16[1024,1024]{1,0:T(8,128)(2,1)S(1)} %get-tuple-element.27.unit, s32[1,1024]{1,0:T(1,128)S(1)} %get-tuple-element.28.tgt), custom_call_target="tpu_custom_call" | custom-call | flops 1000 | bytes 1000 | tf_op jit(solution)/shard_map/pack_rest/pallas_call | solution.py:98
  14.0 11.5 %collective-permute-done.4.refs_3_ = bf16[256,1024]{1,0:T(8,128)(2,1)S(1)} collective-permute-done((bf16[256,1024]{1,0:T(8,128)(2,1)S(1)}, bf16[256,1024]{1,0:T(8,128)(2,1)S(1)}, u32[]{:S(2)}, u32[]{:S(2)}) %collective-permute-start.4) | collective-permute-done | bytes 524320 | tf_op jit(solution)/shard_map/ppermute | solution.py:295
  25.5 3.1 %collective-permute-start.5 = (bf16[256,1024]{1,0:T(8,128)(2,1)S(1)}, bf16[256,1024]{1,0:T(8,128)(2,1)S(1)}, u32[]{:S(2)}, u32[]{:S(2)}) collective-permute-start(bf16[256,1024]{1,0:T(8,128)(2,1)S(1)} %get-tuple-element.43), channel_id=1, source_target_pairs={{0,12},{2,14},{4,8},{6,10},{8,4},{10,6},{12,0},{14,2},{1,13},{3,15... | collective-permute-start | bytes 1572872 | tf_op jit(solution)/shard_map/ppermute | solution.py:295
  28.6 12.9 %collective-permute-done.refs_0_ = bf16[256,1024]{1,0:T(8,128)(2,1)S(1)} collective-permute-done((bf16[256,1024]{1,0:T(8,128)(2,1)S(1)}, bf16[256,1024]{1,0:T(8,128)(2,1)S(1)}, u32[]{:S(2)}, u32[]{:S(2)}) %collective-permute-start) | collective-permute-done | bytes 524320 | tf_op jit(solution)/shard_map/ppermute | solution.py:295
  41.5 0.1 collective-permute-start.6
  41.6 33.8 %collective-permute-done.1.refs_1_ = bf16[256,1024]{1,0:T(8,128)(2,1)S(1)} collective-permute-done((bf16[256,1024]{1,0:T(8,128)(2,1)S(1)}, bf16[256,1024]{1,0:T(8,128)(2,1)S(1)}, u32[]{:S(2)}, u32[]{:S(2)}) %collective-permute-start.1) | collective-permute-done | bytes 524320 | tf_op jit(solution)/shard_map/ppermute | solution.py:295
  75.3 0.0 collective-permute-done.2.refs_2_
  75.3 1.3 %own_near.1 = (bf16[2,2,512,1024]{3,2,1,0:T(8,128)(2,1)S(1)}, f32[2,1024]{1,0:T(2,128)S(1)}) custom-call(bf16[256,1024]{1,0:T(8,128)(2,1)S(1)} %collective-permute-done.refs_0_, bf16[256,1024]{1,0:T(8,128)(2,1)S(1)} %collective-permute-done.1.refs_1_, bf16[256,1024]{1,0:T(8,128)(2,1)S(1)} %collective-permute-done.2.refs_2_, ...), custom_call_target="tpu_custom_call" | custom-call | flops 1000 | bytes 1000 | tf_op jit(solution)/shard_map/own_near/pallas_call | solution.py:98
  76.7 8.6 %all_to_all.10.refs_0_ = bf16[2,2,512,1024]{3,2,1,0:T(8,128)(2,1)S(1)} all-to-all(bf16[2,2,512,1024]{3,2,1,0:T(8,128)(2,1)S(1)} %get-tuple-element.33), channel_id=1, replica_groups=mesh['groups'=2,'clus'=8,'blk'=2] {'blk'}, dimensions={0} | all-to-all | bytes 8388608 | tf_op jit(solution)/shard_map/all_to_all | solution.py:301
  85.3 1.3 %cross_near.1.refs_1_ = f32[2,1024]{1,0:T(2,128)S(1)} custom-call(bf16[2,2,512,1024]{3,2,1,0:T(8,128)(2,1)S(1)} %all_to_all.10.refs_0_, f32[2,1024]{1,0:T(2,128)S(1)} %get-tuple-element.35.refs_1_), custom_call_target="tpu_custom_call" | custom-call | flops 1000 | bytes 1000 | tf_op jit(solution)/shard_map/cross_near/pallas_call | solution.py:98
  86.6 0.0 collective-permute-done.3.refs_2_
  86.6 1.8 %own_far.1 = (bf16[2,2,256,1024]{3,2,1,0:T(8,128)(2,1)S(1)}, f32[2,1024]{1,0:T(2,128)S(1)}) custom-call(bf16[2,2,512,1024]{3,2,1,0:T(8,128)(2,1)S(1)} %all_to_all.10.refs_0_, f32[2,1024]{1,0:T(2,128)S(1)} %cross_near.1.refs_1_, bf16[256,1024]{1,0:T(8,128)(2,1)S(1)} %collective-permute-done.3.refs_2_, bf16[256,1024]{1,0:T(8,128)(2,1)S(1)} %collective-permute-done.4.refs_3_), custom_call_target="tpu_custom_call" | custom-call | flops 1000 | bytes 1000 | tf_op jit(solution)/shard_map/own_far/pallas_call | solution.py:98
  88.4 5.1 %all_to_all.11.refs_1_ = bf16[2,2,256,1024]{3,2,1,0:T(8,128)(2,1)S(1)} all-to-all(bf16[2,2,256,1024]{3,2,1,0:T(8,128)(2,1)S(1)} %get-tuple-element.42), channel_id=1, replica_groups=mesh['groups'=2,'clus'=8,'blk'=2] {'blk'}, dimensions={0} | all-to-all | bytes 4194304 | tf_op jit(solution)/shard_map/all_to_all | solution.py:301
  93.5 1.6 %cross_far.1.refs_3_ = f32[2,1024]{1,0:T(2,128)S(1)} custom-call(bf16[2,2,512,1024]{3,2,1,0:T(8,128)(2,1)S(1)} %all_to_all.10.refs_0_, bf16[2,2,256,1024]{3,2,1,0:T(8,128)(2,1)S(1)} %all_to_all.11.refs_1_, f32[2,1024]{1,0:T(2,128)S(1)} %get-tuple-element.45.refs_2_), custom_call_target="tpu_custom_call" | custom-call | flops 1000 | bytes 1000 | tf_op jit(solution)/shard_map/cross_far/pallas_call | solution.py:98
  95.1 0.0 collective-permute-done.5.refs_0_
  95.1 2.6 %collective-permute-done.6.refs_1_ = bf16[256,1024]{1,0:T(8,128)(2,1)S(1)} collective-permute-done((bf16[256,1024]{1,0:T(8,128)(2,1)S(1)}, bf16[256,1024]{1,0:T(8,128)(2,1)S(1)}, u32[]{:S(2)}, u32[]{:S(2)}) %collective-permute-start.6) | collective-permute-done | bytes 524320 | tf_op jit(solution)/shard_map/ppermute | solution.py:295
  97.7 0.1 gather_late.1.refs_2_
  97.8 1.5 %collective-permute-start.7 = (bf16[2,256,1024]{2,1,0:T(8,128)(2,1)S(1)}, bf16[2,256,1024]{2,1,0:T(8,128)(2,1)S(1)}, u32[]{:S(2)}, u32[]{:S(2)}) collective-permute-start(bf16[2,256,1024]{2,1,0:T(8,128)(2,1)S(1)} %gather_late.1.refs_2_), channel_id=1, source_target_pairs={{0,1},{2,3},{4,5},{6,7},{8,9},{10,11},{12,13},{14,15},{16,17},{18,... | collective-permute-start | bytes 3145736 | tf_op jit(solution)/shard_map/ppermute | solution.py:339
  99.3 2.4 %own_late.1.refs_3_ = f32[2,1024]{1,0:T(2,128)S(1)} custom-call(bf16[2,2,512,1024]{3,2,1,0:T(8,128)(2,1)S(1)} %all_to_all.10.refs_0_, bf16[2,2,256,1024]{3,2,1,0:T(8,128)(2,1)S(1)} %all_to_all.11.refs_1_, bf16[2,256,1024]{2,1,0:T(8,128)(2,1)S(1)} %gather_late.1.refs_2_, f32[2,1024]{1,0:T(2,128)S(1)} %cross_far.1.refs_3_), custom_call_target="tpu_custom_call" | custom-call | flops 1000 | bytes 1000 | tf_op jit(solution)/shard_map/own_late/pallas_call | solution.py:98
  101.7 0.7 collective-permute-done.7.refs_4_
  102.4 2.8 %cross_late.1 = f32[2,1024]{1,0:T(2,128)} custom-call(bf16[2,2,512,1024]{3,2,1,0:T(8,128)(2,1)S(1)} %all_to_all.10.refs_0_, bf16[2,2,256,1024]{3,2,1,0:T(8,128)(2,1)S(1)} %all_to_all.11.refs_1_, bf16[2,256,1024]{2,1,0:T(8,128)(2,1)S(1)} %gather_late.1.refs_2_, f32[2,1024]{1,0:T(2,128)S(1)} %own_late.1.refs_3_, ...), custom_call_target="tpu_custom_call" | custom-call | flops 1000 | bytes 1000 | tf_op jit(solution)/shard_map/cross_late/pallas_call | solution.py:98
Async XLA Ops:
  0.0 0.7 copy-start
  3.3 22.3 %collective-permute-start.4 = (bf16[256,1024]{1,0:T(8,128)(2,1)S(1)}, bf16[256,1024]{1,0:T(8,128)(2,1)S(1)}, u32[]{:S(2)}, u32[]{:S(2)}) collective-permute-start(bf16[256,1024]{1,0:T(8,128)(2,1)S(1)} %get-tuple-element.40), channel_id=1, source_target_pairs={{0,8},{2,10},{4,12},{6,14},{8,0},{10,2},{12,4},{14,6},{1,9},{3,11}... | collective-permute-start | bytes 1572872 | tf_op jit(solution)/shard_map/ppermute | solution.py:295
  6.6 34.9 %collective-permute-start = (bf16[256,1024]{1,0:T(8,128)(2,1)S(1)}, bf16[256,1024]{1,0:T(8,128)(2,1)S(1)}, u32[]{:S(2)}, u32[]{:S(2)}) collective-permute-start(bf16[256,1024]{1,0:T(8,128)(2,1)S(1)} %get-tuple-element.29), channel_id=1, source_target_pairs={{0,6},{2,4},{4,2},{6,0},{8,14},{10,12},{12,10},{14,8},{1,7},{3,5},... | collective-permute-start | bytes 1572872 | tf_op jit(solution)/shard_map/ppermute | solution.py:295
  8.9 66.4 %collective-permute-start.1 = (bf16[256,1024]{1,0:T(8,128)(2,1)S(1)}, bf16[256,1024]{1,0:T(8,128)(2,1)S(1)}, u32[]{:S(2)}, u32[]{:S(2)}) collective-permute-start(bf16[256,1024]{1,0:T(8,128)(2,1)S(1)} %get-tuple-element.30), channel_id=1, source_target_pairs={{0,4},{2,6},{4,0},{6,2},{8,12},{10,14},{12,8},{14,10},{1,5},{3,7},... | collective-permute-start | bytes 1572872 | tf_op jit(solution)/shard_map/ppermute | solution.py:295
  9.1 66.2 %collective-permute-start.2 = (bf16[256,1024]{1,0:T(8,128)(2,1)S(1)}, bf16[256,1024]{1,0:T(8,128)(2,1)S(1)}, u32[]{:S(2)}, u32[]{:S(2)}) collective-permute-start(bf16[256,1024]{1,0:T(8,128)(2,1)S(1)} %get-tuple-element.31), channel_id=1, source_target_pairs={{0,2},{2,0},{4,6},{6,4},{8,10},{10,8},{12,14},{14,12},{1,3},{3,1},... | collective-permute-start | bytes 1572872 | tf_op jit(solution)/shard_map/ppermute | solution.py:295
  9.3 77.3 %collective-permute-start.3 = (bf16[256,1024]{1,0:T(8,128)(2,1)S(1)}, bf16[256,1024]{1,0:T(8,128)(2,1)S(1)}, u32[]{:S(2)}, u32[]{:S(2)}) collective-permute-start(bf16[256,1024]{1,0:T(8,128)(2,1)S(1)} %get-tuple-element.34), channel_id=1, source_target_pairs={{0,10},{2,8},{4,14},{6,12},{8,2},{10,0},{12,6},{14,4},{1,11},{3,9}... | collective-permute-start | bytes 1572872 | tf_op jit(solution)/shard_map/ppermute | solution.py:295
  25.5 69.6 %collective-permute-start.5 = (bf16[256,1024]{1,0:T(8,128)(2,1)S(1)}, bf16[256,1024]{1,0:T(8,128)(2,1)S(1)}, u32[]{:S(2)}, u32[]{:S(2)}) collective-permute-start(bf16[256,1024]{1,0:T(8,128)(2,1)S(1)} %get-tuple-element.43), channel_id=1, source_target_pairs={{0,12},{2,14},{4,8},{6,10},{8,4},{10,6},{12,0},{14,2},{1,13},{3,15... | collective-permute-start | bytes 1572872 | tf_op jit(solution)/shard_map/ppermute | solution.py:295
  41.5 56.2 %collective-permute-start.6 = (bf16[256,1024]{1,0:T(8,128)(2,1)S(1)}, bf16[256,1024]{1,0:T(8,128)(2,1)S(1)}, u32[]{:S(2)}, u32[]{:S(2)}) collective-permute-start(bf16[256,1024]{1,0:T(8,128)(2,1)S(1)} %get-tuple-element.44), channel_id=1, source_target_pairs={{0,14},{2,12},{4,10},{6,8},{8,6},{10,4},{12,2},{14,0},{1,15},{3,13... | collective-permute-start | bytes 1572872 | tf_op jit(solution)/shard_map/ppermute | solution.py:295
  97.8 4.6 %collective-permute-start.7 = (bf16[2,256,1024]{2,1,0:T(8,128)(2,1)S(1)}, bf16[2,256,1024]{2,1,0:T(8,128)(2,1)S(1)}, u32[]{:S(2)}, u32[]{:S(2)}) collective-permute-start(bf16[2,256,1024]{2,1,0:T(8,128)(2,1)S(1)} %gather_late.1.refs_2_), channel_id=1, source_target_pairs={{0,1},{2,3},{4,5},{6,7},{8,9},{10,11},{12,13},{14,15},{16,17},{18,... | collective-permute-start | bytes 3145736 | tf_op jit(solution)/shard_map/ppermute | solution.py:339

commit v13 on v12

--- a/solution.py
+++ b/solution.py
@@ -250,7 +250,7 @@
     best[:, :start] = before[:, :start]
     for c in range(CLUS_DEV):
         rows = [best.at[c : c + 1, a:b] for a, b in spans]
-        groups = [stage.at[core, c] for stage in stages] + [cat.at[c]]
+        groups = [stages[0].at[core, c, a:b] for a, b in spans[:-1]] + [cat.at[c]]
         rows[last][...] = fresh_best(groups[last])
         raise_best(rows[last], groups[last], groups[last], True)
         for i in range(last):
@@ -266,12 +266,12 @@
 
     @pl.when(core == 1)
     def _():
+        start = spans[-1][0]
         for c in range(CLUS_DEV):
-            rows = [best.at[c : c + 1, a:b] for a, b in spans]
-            for row, stage in zip(rows, stages):
-                raise_best(row, other.at[c], stage.at[1, c])
-                raise_best(rows[held], stage.at[0, c], cat.at[c])
-            raise_best(rows[held], other.at[c], cat.at[c])
+            fresh = best.at[c : c + 1, start:]
+            raise_best(best.at[c : c + 1, :start], other.at[c], stages[0].at[1, c])
+            raise_best(fresh, stages[0].at[0, c], cat.at[c])
+            raise_best(fresh, other.at[c], cat.at[c])
 
     for a, b in spans:
         place = (me ^ (a // per)) & ~((b - a) // per - 1)
@@ -312,36 +312,26 @@
     for step, block in zip(late, held):
         arrived[step] = to_owner(block, step)
 
+    early = near + far
     send, best = kernel_call(
-        functools.partial(own_stage, cuts[:2], bits, 0, 0),
-        [stage_shape(len(near)), best_shape],
-        [arrived[s] for s in reversed(near)],
-        "own_near",
+        functools.partial(own_stage, cuts[:3], bits, 0, 0),
+        [stage_shape(len(early)), best_shape],
+        [arrived[s] for s in reversed(early)],
+        "own_early",
     )
     stages = [to_both(send)]
     (best,) = kernel_call(
-        functools.partial(cross_stage, cuts, 0), [best_shape], stages + [best], "cross_near"
-    )
-    arrived[far[-1]], best = lax.optimization_barrier((arrived[far[-1]], best))
-    send, best = kernel_call(
-        functools.partial(own_stage, cuts[:3], bits, 1, 1),
-        [stage_shape(len(far)), best_shape],
-        stages + [best] + [arrived[s] for s in reversed(far)],
-        "own_far",
-    )
-    stages.append(to_both(send))
-    (best,) = kernel_call(
-        functools.partial(cross_stage, cuts, 1), [best_shape], stages + [best], "cross_far"
+        functools.partial(cross_stage, cuts, 0), [best_shape], stages + [best], "cross_early"
     )
     *new, best = lax.optimization_barrier((*[arrived[s] for s in late], best))
     cat_shape = jax.ShapeDtypeStruct((CLUS_DEV, len(late) * per, width), BF)
     (cat,) = kernel_call(gather_late, [cat_shape], new, "gather_late")
     other = lax.ppermute(cat, "blk", [(0, 1)])
     (best,) = kernel_call(
-        functools.partial(own_late, cuts, bits, 2), [best_shape], stages + [cat, best], "own_late"
+        functools.partial(own_late, cuts, bits, 1), [best_shape], stages + [cat, best], "own_late"
     )
     (out,) = kernel_call(
-        functools.partial(cross_late, cuts, per, 2),
+        functools.partial(cross_late, cuts, per, 1),
         [best_shape],
         stages + [cat, best, other],
         "cross_late",

time: 106 us -> 105 us (level)
  starting transfers between devices: 10.7 us -> 15 us
  blocking collectives: 13.7 us -> 10.6 us
  waiting for transfers between devices: 61.4 us -> 60.3 us
    ppermute x7, starting transfers between devices: 9.27 us -> 13.7 us  [to_owner(): return lax.ppermute(block, 'clus', [(i, i ^ step) for i in range(owners)])]
    all_to_all x2 -> x1, blocking collectives: 13.7 us -> 10.6 us  [to_both(): return lax.all_to_all(send, 'blk', split_axis=0, concat_axis=0, tiled=True)]
    ppermute x7, waiting for transfers between devices: 60.7 us -> 59.6 us  [to_owner(): return lax.ppermute(block, 'clus', [(i, i ^ step) for i in range(owners)])]
    pallas_call x10 -> x8, Pallas kernels: 18.5 us -> 18.5 us  [kernel_call(): pl.pallas_call(kernel, out_shape=shapes, in_specs=[place] * len(inputs),...]
where the time goes in v13:
time: 105 us
  waiting for transfers between devices  60.3 us (57%)
  Pallas kernels  18.5 us (18%)
  starting transfers between devices  15 us (14%)
  blocking collectives  10.6 us (10%)
    ppermute x7, waiting for transfers between devices, to_owner(): return lax.ppermute(block, 'clus', [(i, i ^ step) for i in range(owners)])  59.6 us
    pallas_call x8, Pallas kernels, kernel_call(): pl.pallas_call(kernel, out_shape=shapes, in_specs=[place] * len(inputs),...  18.5 us
    ppermute x7, starting transfers between devices, to_owner(): return lax.ppermute(block, 'clus', [(i, i ^ step) for i in range(owners)])  13.7 us
    all_to_all x1, blocking collectives, to_both(): return lax.all_to_all(send, 'blk', split_axis=0, concat_axis=0, tiled=True)  10.6 us
  transfers between devices with their start and end apart: 8, of which 5 were waited for; matrix products, arithmetic and copies ran while one was open for 0% of the time, Pallas kernels for 12%

profile of v13, /device:TPU:17, one launch (start us, length us, event | category | flops | bytes accessed | tf_op | source)
XLA Modules:
  0.0 105.2 jit_solution(7213263119538478358)
XLA Ops:
  0.0 0.0 copy-start
  0.0 0.7 copy-done
  0.7 2.6 %pack_first.1 = (bf16[1024,1024]{1,0:T(8,128)(2,1)S(1)}, s32[1,1024]{1,0:T(1,128)S(1)}, bf16[256,1024]{1,0:T(8,128)(2,1)S(1)}) custom-call(bf16[1024,1024]{1,0:T(8,128)(2,1)} %emb.1, s32[1,1024]{1,0:T(1,128)S(1)} %copy-done), custom_call_target="tpu_custom_call" | custom-call | flops 1000 | bytes 1000 | tf_op jit(solution)/shard_map/pack_first/pallas_call | solution.py:98
  3.3 0.1 collective-permute-start.1
  3.3 3.2 %pack_rest.2 = (bf16[256,1024]{1,0:T(8,128)(2,1)S(1)}, bf16[256,1024]{1,0:T(8,128)(2,1)S(1)}, bf16[256,1024]{1,0:T(8,128)(2,1)S(1)}, bf16[256,1024]{1,0:T(8,128)(2,1)S(1)}, bf16[256,1024]{1,0:T(8,128)(2,1)S(1)}) custom-call(bf16[1024,1024]{1,0:T(8,128)(2,1)S(1)} %get-tuple-element.23.unit, s32[1,1024]{1,0:T(1,128)S(1)} %get-tuple-element.24.tgt), custom_call_target="tpu_custom_call" | custom-call | flops 1000 | bytes 1000 | tf_op jit(solution)/shard_map/pack_rest/pallas_call | solution.py:98
  6.6 3.4 %collective-permute-start = (bf16[256,1024]{1,0:T(8,128)(2,1)S(1)}, bf16[256,1024]{1,0:T(8,128)(2,1)S(1)}, u32[]{:S(2)}, u32[]{:S(2)}) collective-permute-start(bf16[256,1024]{1,0:T(8,128)(2,1)S(1)} %get-tuple-element.25), channel_id=1, source_target_pairs={{0,10},{2,8},{4,14},{6,12},{8,2},{10,0},{12,6},{14,4},{1,11},{3,9}... | collective-permute-start | bytes 1572872 | tf_op jit(solution)/shard_map/ppermute | solution.py:295
  10.0 1.2 %collective-permute-start.2 = (bf16[256,1024]{1,0:T(8,128)(2,1)S(1)}, bf16[256,1024]{1,0:T(8,128)(2,1)S(1)}, u32[]{:S(2)}, u32[]{:S(2)}) collective-permute-start(bf16[256,1024]{1,0:T(8,128)(2,1)S(1)} %get-tuple-element.30), channel_id=1, source_target_pairs={{0,6},{2,4},{4,2},{6,0},{8,14},{10,12},{12,10},{14,8},{1,7},{3,5},... | collective-permute-start | bytes 1572872 | tf_op jit(solution)/shard_map/ppermute | solution.py:295
  11.2 0.2 collective-permute-start.3
  11.4 1.2 %collective-permute-start.4 = (bf16[256,1024]{1,0:T(8,128)(2,1)S(1)}, bf16[256,1024]{1,0:T(8,128)(2,1)S(1)}, u32[]{:S(2)}, u32[]{:S(2)}) collective-permute-start(bf16[256,1024]{1,0:T(8,128)(2,1)S(1)} %get-tuple-element.32), channel_id=1, source_target_pairs={{0,2},{2,0},{4,6},{6,4},{8,10},{10,8},{12,14},{14,12},{1,3},{3,1},... | collective-permute-start | bytes 1572872 | tf_op jit(solution)/shard_map/ppermute | solution.py:295
  12.6 1.4 %pack_rest.3 = (bf16[256,1024]{1,0:T(8,128)(2,1)S(1)}, bf16[256,1024]{1,0:T(8,128)(2,1)S(1)}) custom-call(bf16[1024,1024]{1,0:T(8,128)(2,1)S(1)} %get-tuple-element.23.unit, s32[1,1024]{1,0:T(1,128)S(1)} %get-tuple-element.24.tgt), custom_call_target="tpu_custom_call" | custom-call | flops 1000 | bytes 1000 | tf_op jit(solution)/shard_map/pack_rest/pallas_call | solution.py:98
  14.0 22.7 %collective-permute-done.1.refs_1_ = bf16[256,1024]{1,0:T(8,128)(2,1)S(1)} collective-permute-done((bf16[256,1024]{1,0:T(8,128)(2,1)S(1)}, bf16[256,1024]{1,0:T(8,128)(2,1)S(1)}, u32[]{:S(2)}, u32[]{:S(2)}) %collective-permute-start.1) | collective-permute-done | bytes 524320 | tf_op jit(solution)/shard_map/ppermute | solution.py:295
  36.8 3.1 %collective-permute-start.5 = (bf16[256,1024]{1,0:T(8,128)(2,1)S(1)}, bf16[256,1024]{1,0:T(8,128)(2,1)S(1)}, u32[]{:S(2)}, u32[]{:S(2)}) collective-permute-start(bf16[256,1024]{1,0:T(8,128)(2,1)S(1)} %get-tuple-element.35), channel_id=1, source_target_pairs={{0,12},{2,14},{4,8},{6,10},{8,4},{10,6},{12,0},{14,2},{1,13},{3,15... | collective-permute-start | bytes 1572872 | tf_op jit(solution)/shard_map/ppermute | solution.py:295
  39.8 8.1 %collective-permute-done.refs_0_ = bf16[256,1024]{1,0:T(8,128)(2,1)S(1)} collective-permute-done((bf16[256,1024]{1,0:T(8,128)(2,1)S(1)}, bf16[256,1024]{1,0:T(8,128)(2,1)S(1)}, u32[]{:S(2)}, u32[]{:S(2)}) %collective-permute-start) | collective-permute-done | bytes 524320 | tf_op jit(solution)/shard_map/ppermute | solution.py:295
  48.0 4.6 %collective-permute-start.6 = (bf16[256,1024]{1,0:T(8,128)(2,1)S(1)}, bf16[256,1024]{1,0:T(8,128)(2,1)S(1)}, u32[]{:S(2)}, u32[]{:S(2)}) collective-permute-start(bf16[256,1024]{1,0:T(8,128)(2,1)S(1)} %get-tuple-element.36), channel_id=1, source_target_pairs={{0,14},{2,12},{4,10},{6,8},{8,6},{10,4},{12,2},{14,0},{1,15},{3,13... | collective-permute-start | bytes 1572872 | tf_op jit(solution)/shard_map/ppermute | solution.py:295
  52.5 0.0 collective-permute-done.2.refs_2_
  52.6 24.7 %collective-permute-done.3.refs_3_ = bf16[256,1024]{1,0:T(8,128)(2,1)S(1)} collective-permute-done((bf16[256,1024]{1,0:T(8,128)(2,1)S(1)}, bf16[256,1024]{1,0:T(8,128)(2,1)S(1)}, u32[]{:S(2)}, u32[]{:S(2)}) %collective-permute-start.3) | collective-permute-done | bytes 524320 | tf_op jit(solution)/shard_map/ppermute | solution.py:295
  77.3 0.0 collective-permute-done.4.refs_4_
  77.3 3.1 %own_early.1 = (bf16[2,2,768,1024]{3,2,1,0:T(8,128)(2,1)S(1)}, f32[2,1024]{1,0:T(2,128)S(1)}) custom-call(bf16[256,1024]{1,0:T(8,128)(2,1)S(1)} %collective-permute-done.refs_0_, bf16[256,1024]{1,0:T(8,128)(2,1)S(1)} %collective-permute-done.1.refs_1_, bf16[256,1024]{1,0:T(8,128)(2,1)S(1)} %collective-permute-done.2.refs_2_, ...), custom_call_target="tpu_custom_call" | custom-call | flops 1000 | bytes 1000 | tf_op jit(solution)/shard_map/own_early/pallas_call | solution.py:98
  80.4 10.6 %all_to_all.5.refs_0_ = bf16[2,2,768,1024]{3,2,1,0:T(8,128)(2,1)S(1)} all-to-all(bf16[2,2,768,1024]{3,2,1,0:T(8,128)(2,1)S(1)} %get-tuple-element.34), channel_id=1, replica_groups=mesh['groups'=2,'clus'=8,'blk'=2] {'blk'}, dimensions={0} | all-to-all | bytes 12582912 | tf_op jit(solution)/shard_map/all_to_all | solution.py:301
  91.0 2.7 %cross_early.1.refs_2_ = f32[2,1024]{1,0:T(2,128)S(1)} custom-call(bf16[2,2,768,1024]{3,2,1,0:T(8,128)(2,1)S(1)} %all_to_all.5.refs_0_, f32[2,1024]{1,0:T(2,128)S(1)} %get-tuple-element.37.refs_1_), custom_call_target="tpu_custom_call" | custom-call | flops 1000 | bytes 1000 | tf_op jit(solution)/shard_map/cross_early/pallas_call | solution.py:98
  93.7 0.0 collective-permute-done.5.refs_0_
  93.7 4.0 %collective-permute-done.6.refs_1_ = bf16[256,1024]{1,0:T(8,128)(2,1)S(1)} collective-permute-done((bf16[256,1024]{1,0:T(8,128)(2,1)S(1)}, bf16[256,1024]{1,0:T(8,128)(2,1)S(1)}, u32[]{:S(2)}, u32[]{:S(2)}) %collective-permute-start.6) | collective-permute-done | bytes 524320 | tf_op jit(solution)/shard_map/ppermute | solution.py:295
  97.7 0.1 gather_late.1.refs_1_
  97.8 1.3 %collective-permute-start.7 = (bf16[2,256,1024]{2,1,0:T(8,128)(2,1)S(1)}, bf16[2,256,1024]{2,1,0:T(8,128)(2,1)S(1)}, u32[]{:S(2)}, u32[]{:S(2)}) collective-permute-start(bf16[2,256,1024]{2,1,0:T(8,128)(2,1)S(1)} %gather_late.1.refs_1_), channel_id=1, source_target_pairs={{0,1},{2,3},{4,5},{6,7},{8,9},{10,11},{12,13},{14,15},{16,17},{18,... | collective-permute-start | bytes 3145736 | tf_op jit(solution)/shard_map/ppermute | solution.py:329
  99.1 2.6 %own_late.1.refs_2_ = f32[2,1024]{1,0:T(2,128)S(1)} custom-call(bf16[2,2,768,1024]{3,2,1,0:T(8,128)(2,1)S(1)} %all_to_all.5.refs_0_, bf16[2,256,1024]{2,1,0:T(8,128)(2,1)S(1)} %gather_late.1.refs_1_, f32[2,1024]{1,0:T(2,128)S(1)} %cross_early.1.refs_2_), custom_call_target="tpu_custom_call" | custom-call | flops 1000 | bytes 1000 | tf_op jit(solution)/shard_map/own_late/pallas_call | solution.py:98
  101.7 0.7 collective-permute-done.7.refs_3_
  102.4 2.8 %cross_late.1 = f32[2,1024]{1,0:T(2,128)} custom-call(bf16[2,2,768,1024]{3,2,1,0:T(8,128)(2,1)S(1)} %all_to_all.5.refs_0_, bf16[2,256,1024]{2,1,0:T(8,128)(2,1)S(1)} %gather_late.1.refs_1_, f32[2,1024]{1,0:T(2,128)S(1)} %own_late.1.refs_2_, bf16[2,256,1024]{2,1,0:T(8,128)(2,1)S(1)} %collective-permute-done.7.refs_3_), custom_call_target="tpu_custom_call" | custom-call | flops 1000 | bytes 1000 | tf_op jit(solution)/shard_map/cross_late/pallas_call | solution.py:98
Async XLA Ops:
  0.0 0.7 copy-start
  3.3 33.5 %collective-permute-start.1 = (bf16[256,1024]{1,0:T(8,128)(2,1)S(1)}, bf16[256,1024]{1,0:T(8,128)(2,1)S(1)}, u32[]{:S(2)}, u32[]{:S(2)}) collective-permute-start(bf16[256,1024]{1,0:T(8,128)(2,1)S(1)} %get-tuple-element.28), channel_id=1, source_target_pairs={{0,8},{2,10},{4,12},{6,14},{8,0},{10,2},{12,4},{14,6},{1,9},{3,11}... | collective-permute-start | bytes 1572872 | tf_op jit(solution)/shard_map/ppermute | solution.py:295
  6.6 41.4 %collective-permute-start = (bf16[256,1024]{1,0:T(8,128)(2,1)S(1)}, bf16[256,1024]{1,0:T(8,128)(2,1)S(1)}, u32[]{:S(2)}, u32[]{:S(2)}) collective-permute-start(bf16[256,1024]{1,0:T(8,128)(2,1)S(1)} %get-tuple-element.25), channel_id=1, source_target_pairs={{0,10},{2,8},{4,14},{6,12},{8,2},{10,0},{12,6},{14,4},{1,11},{3,9}... | collective-permute-start | bytes 1572872 | tf_op jit(solution)/shard_map/ppermute | solution.py:295
  10.0 42.6 %collective-permute-start.2 = (bf16[256,1024]{1,0:T(8,128)(2,1)S(1)}, bf16[256,1024]{1,0:T(8,128)(2,1)S(1)}, u32[]{:S(2)}, u32[]{:S(2)}) collective-permute-start(bf16[256,1024]{1,0:T(8,128)(2,1)S(1)} %get-tuple-element.30), channel_id=1, source_target_pairs={{0,6},{2,4},{4,2},{6,0},{8,14},{10,12},{12,10},{14,8},{1,7},{3,5},... | collective-permute-start | bytes 1572872 | tf_op jit(solution)/shard_map/ppermute | solution.py:295
  11.2 66.1 %collective-permute-start.3 = (bf16[256,1024]{1,0:T(8,128)(2,1)S(1)}, bf16[256,1024]{1,0:T(8,128)(2,1)S(1)}, u32[]{:S(2)}, u32[]{:S(2)}) collective-permute-start(bf16[256,1024]{1,0:T(8,128)(2,1)S(1)} %get-tuple-element.31), channel_id=1, source_target_pairs={{0,4},{2,6},{4,0},{6,2},{8,12},{10,14},{12,8},{14,10},{1,5},{3,7},... | collective-permute-start | bytes 1572872 | tf_op jit(solution)/shard_map/ppermute | solution.py:295
  11.4 65.9 %collective-permute-start.4 = (bf16[256,1024]{1,0:T(8,128)(2,1)S(1)}, bf16[256,1024]{1,0:T(8,128)(2,1)S(1)}, u32[]{:S(2)}, u32[]{:S(2)}) collective-permute-start(bf16[256,1024]{1,0:T(8,128)(2,1)S(1)} %get-tuple-element.32), channel_id=1, source_target_pairs={{0,2},{2,0},{4,6},{6,4},{8,10},{10,8},{12,14},{14,12},{1,3},{3,1},... | collective-permute-start | bytes 1572872 | tf_op jit(solution)/shard_map/ppermute | solution.py:295
  36.8 56.9 %collective-permute-start.5 = (bf16[256,1024]{1,0:T(8,128)(2,1)S(1)}, bf16[256,1024]{1,0:T(8,128)(2,1)S(1)}, u32[]{:S(2)}, u32[]{:S(2)}) collective-permute-start(bf16[256,1024]{1,0:T(8,128)(2,1)S(1)} %get-tuple-element.35), channel_id=1, source_target_pairs={{0,12},{2,14},{4,8},{6,10},{8,4},{10,6},{12,0},{14,2},{1,13},{3,15... | collective-permute-start | bytes 1572872 | tf_op jit(solution)/shard_map/ppermute | solution.py:295
  48.0 49.7 %collective-permute-start.6 = (bf16[256,1024]{1,0:T(8,128)(2,1)S(1)}, bf16[256,1024]{1,0:T(8,128)(2,1)S(1)}, u32[]{:S(2)}, u32[]{:S(2)}) collective-permute-start(bf16[256,1024]{1,0:T(8,128)(2,1)S(1)} %get-tuple-element.36), channel_id=1, source_target_pairs={{0,14},{2,12},{4,10},{6,8},{8,6},{10,4},{12,2},{14,0},{1,15},{3,13... | collective-permute-start | bytes 1572872 | tf_op jit(solution)/shard_map/ppermute | solution.py:295
  97.8 4.6 %collective-permute-start.7 = (bf16[2,256,1024]{2,1,0:T(8,128)(2,1)S(1)}, bf16[2,256,1024]{2,1,0:T(8,128)(2,1)S(1)}, u32[]{:S(2)}, u32[]{:S(2)}) collective-permute-start(bf16[2,256,1024]{2,1,0:T(8,128)(2,1)S(1)} %gather_late.1.refs_1_), channel_id=1, source_target_pairs={{0,1},{2,3},{4,5},{6,7},{8,9},{10,11},{12,13},{14,15},{16,17},{18,... | collective-permute-start | bytes 3145736 | tf_op jit(solution)/shard_map/ppermute | solution.py:329

commit v14 on v13

--- a/solution.py
+++ b/solution.py
@@ -256,6 +256,11 @@
         for i in range(last):
             score_pair(rows, groups, last, i, bits[i], me)
 
+    @pl.when(core == 1)
+    def _():
+        for c in range(CLUS_DEV):
+            raise_best(best.at[c : c + 1, start:], stages[0].at[0, c], cat.at[c])
+
 
 def cross_late(cuts, per, held, *refs):
     stages, (cat, before, other, out, best) = refs[:held], refs[held:]
@@ -270,7 +275,6 @@
         for c in range(CLUS_DEV):
             fresh = best.at[c : c + 1, start:]
             raise_best(best.at[c : c + 1, :start], other.at[c], stages[0].at[1, c])
-            raise_best(fresh, stages[0].at[0, c], cat.at[c])
             raise_best(fresh, other.at[c], cat.at[c])
 
     for a, b in spans:

time: 105 us -> 105 us (level)
  transfers between devices with their start and end apart: 8 -> 8, of which waited for: 5 -> 4; matrix products, arithmetic and copies ran while one was open for 0% -> 0% of each run, Pallas kernels for 12% -> 13%
where the time goes in v14:
time: 105 us
  waiting for transfers between devices  59.6 us (57%)
  Pallas kernels  18.6 us (18%)
  starting transfers between devices  15 us (14%)
  blocking collectives  10.6 us (10%)
    ppermute x7, waiting for transfers between devices, to_owner(): return lax.ppermute(block, 'clus', [(i, i ^ step) for i in range(owners)])  59.6 us
    pallas_call x8, Pallas kernels, kernel_call(): pl.pallas_call(kernel, out_shape=shapes, in_specs=[place] * len(inputs),...  18.6 us
    ppermute x7, starting transfers between devices, to_owner(): return lax.ppermute(block, 'clus', [(i, i ^ step) for i in range(owners)])  13.7 us
    all_to_all x1, blocking collectives, to_both(): return lax.all_to_all(send, 'blk', split_axis=0, concat_axis=0, tiled=True)  10.6 us
  transfers between devices with their start and end apart: 8, of which 4 were waited for; matrix products, arithmetic and copies ran while one was open for 0% of the time, Pallas kernels for 13%

profile of v14, /device:TPU:17, one launch (start us, length us, event | category | flops | bytes accessed | tf_op | source)
XLA Modules:
  0.0 104.6 jit_solution(11638211771751386968)
XLA Ops:
  0.0 0.0 copy-start
  0.0 0.7 copy-done
  0.7 2.6 %pack_first.1 = (bf16[1024,1024]{1,0:T(8,128)(2,1)S(1)}, s32[1,1024]{1,0:T(1,128)S(1)}, bf16[256,1024]{1,0:T(8,128)(2,1)S(1)}) custom-call(bf16[1024,1024]{1,0:T(8,128)(2,1)} %emb.1, s32[1,1024]{1,0:T(1,128)S(1)} %copy-done), custom_call_target="tpu_custom_call" | custom-call | flops 1000 | bytes 1000 | tf_op jit(solution)/shard_map/pack_first/pallas_call | solution.py:98
  3.3 0.1 collective-permute-start.1
  3.3 3.2 %pack_rest.2 = (bf16[256,1024]{1,0:T(8,128)(2,1)S(1)}, bf16[256,1024]{1,0:T(8,128)(2,1)S(1)}, bf16[256,1024]{1,0:T(8,128)(2,1)S(1)}, bf16[256,1024]{1,0:T(8,128)(2,1)S(1)}, bf16[256,1024]{1,0:T(8,128)(2,1)S(1)}) custom-call(bf16[1024,1024]{1,0:T(8,128)(2,1)S(1)} %get-tuple-element.23.unit, s32[1,1024]{1,0:T(1,128)S(1)} %get-tuple-element.24.tgt), custom_call_target="tpu_custom_call" | custom-call | flops 1000 | bytes 1000 | tf_op jit(solution)/shard_map/pack_rest/pallas_call | solution.py:98
  6.6 3.4 %collective-permute-start = (bf16[256,1024]{1,0:T(8,128)(2,1)S(1)}, bf16[256,1024]{1,0:T(8,128)(2,1)S(1)}, u32[]{:S(2)}, u32[]{:S(2)}) collective-permute-start(bf16[256,1024]{1,0:T(8,128)(2,1)S(1)} %get-tuple-element.25), channel_id=1, source_target_pairs={{0,10},{2,8},{4,14},{6,12},{8,2},{10,0},{12,6},{14,4},{1,11},{3,9}... | collective-permute-start | bytes 1572872 | tf_op jit(solution)/shard_map/ppermute | solution.py:299
  10.0 1.2 %collective-permute-start.2 = (bf16[256,1024]{1,0:T(8,128)(2,1)S(1)}, bf16[256,1024]{1,0:T(8,128)(2,1)S(1)}, u32[]{:S(2)}, u32[]{:S(2)}) collective-permute-start(bf16[256,1024]{1,0:T(8,128)(2,1)S(1)} %get-tuple-element.30), channel_id=1, source_target_pairs={{0,6},{2,4},{4,2},{6,0},{8,14},{10,12},{12,10},{14,8},{1,7},{3,5},... | collective-permute-start | bytes 1572872 | tf_op jit(solution)/shard_map/ppermute | solution.py:299
  11.2 0.2 collective-permute-start.3
  11.4 1.2 %collective-permute-start.4 = (bf16[256,1024]{1,0:T(8,128)(2,1)S(1)}, bf16[256,1024]{1,0:T(8,128)(2,1)S(1)}, u32[]{:S(2)}, u32[]{:S(2)}) collective-permute-start(bf16[256,1024]{1,0:T(8,128)(2,1)S(1)} %get-tuple-element.32), channel_id=1, source_target_pairs={{0,2},{2,0},{4,6},{6,4},{8,10},{10,8},{12,14},{14,12},{1,3},{3,1},... | collective-permute-start | bytes 1572872 | tf_op jit(solution)/shard_map/ppermute | solution.py:299
  12.6 1.4 %pack_rest.3 = (bf16[256,1024]{1,0:T(8,128)(2,1)S(1)}, bf16[256,1024]{1,0:T(8,128)(2,1)S(1)}) custom-call(bf16[1024,1024]{1,0:T(8,128)(2,1)S(1)} %get-tuple-element.23.unit, s32[1,1024]{1,0:T(1,128)S(1)} %get-tuple-element.24.tgt), custom_call_target="tpu_custom_call" | custom-call | flops 1000 | bytes 1000 | tf_op jit(solution)/shard_map/pack_rest/pallas_call | solution.py:98
  14.0 22.7 %collective-permute-done.1.refs_1_ = bf16[256,1024]{1,0:T(8,128)(2,1)S(1)} collective-permute-done((bf16[256,1024]{1,0:T(8,128)(2,1)S(1)}, bf16[256,1024]{1,0:T(8,128)(2,1)S(1)}, u32[]{:S(2)}, u32[]{:S(2)}) %collective-permute-start.1) | collective-permute-done | bytes 524320 | tf_op jit(solution)/shard_map/ppermute | solution.py:299
  36.8 3.1 %collective-permute-start.5 = (bf16[256,1024]{1,0:T(8,128)(2,1)S(1)}, bf16[256,1024]{1,0:T(8,128)(2,1)S(1)}, u32[]{:S(2)}, u32[]{:S(2)}) collective-permute-start(bf16[256,1024]{1,0:T(8,128)(2,1)S(1)} %get-tuple-element.35), channel_id=1, source_target_pairs={{0,12},{2,14},{4,8},{6,10},{8,4},{10,6},{12,0},{14,2},{1,13},{3,15... | collective-permute-start | bytes 1572872 | tf_op jit(solution)/shard_map/ppermute | solution.py:299
  39.8 8.1 %collective-permute-done.refs_0_ = bf16[256,1024]{1,0:T(8,128)(2,1)S(1)} collective-permute-done((bf16[256,1024]{1,0:T(8,128)(2,1)S(1)}, bf16[256,1024]{1,0:T(8,128)(2,1)S(1)}, u32[]{:S(2)}, u32[]{:S(2)}) %collective-permute-start) | collective-permute-done | bytes 524320 | tf_op jit(solution)/shard_map/ppermute | solution.py:299
  48.0 4.6 %collective-permute-start.6 = (bf16[256,1024]{1,0:T(8,128)(2,1)S(1)}, bf16[256,1024]{1,0:T(8,128)(2,1)S(1)}, u32[]{:S(2)}, u32[]{:S(2)}) collective-permute-start(bf16[256,1024]{1,0:T(8,128)(2,1)S(1)} %get-tuple-element.36), channel_id=1, source_target_pairs={{0,14},{2,12},{4,10},{6,8},{8,6},{10,4},{12,2},{14,0},{1,15},{3,13... | collective-permute-start | bytes 1572872 | tf_op jit(solution)/shard_map/ppermute | solution.py:299
  52.5 0.0 collective-permute-done.2.refs_2_
  52.6 24.7 %collective-permute-done.3.refs_3_ = bf16[256,1024]{1,0:T(8,128)(2,1)S(1)} collective-permute-done((bf16[256,1024]{1,0:T(8,128)(2,1)S(1)}, bf16[256,1024]{1,0:T(8,128)(2,1)S(1)}, u32[]{:S(2)}, u32[]{:S(2)}) %collective-permute-start.3) | collective-permute-done | bytes 524320 | tf_op jit(solution)/shard_map/ppermute | solution.py:299
  77.3 0.0 collective-permute-done.4.refs_4_
  77.3 3.1 %own_early.1 = (bf16[2,2,768,1024]{3,2,1,0:T(8,128)(2,1)S(1)}, f32[2,1024]{1,0:T(2,128)S(1)}) custom-call(bf16[256,1024]{1,0:T(8,128)(2,1)S(1)} %collective-permute-done.refs_0_, bf16[256,1024]{1,0:T(8,128)(2,1)S(1)} %collective-permute-done.1.refs_1_, bf16[256,1024]{1,0:T(8,128)(2,1)S(1)} %collective-permute-done.2.refs_2_, ...), custom_call_target="tpu_custom_call" | custom-call | flops 1000 | bytes 1000 | tf_op jit(solution)/shard_map/own_early/pallas_call | solution.py:98
  80.4 10.6 %all_to_all.5.refs_0_ = bf16[2,2,768,1024]{3,2,1,0:T(8,128)(2,1)S(1)} all-to-all(bf16[2,2,768,1024]{3,2,1,0:T(8,128)(2,1)S(1)} %get-tuple-element.34), channel_id=1, replica_groups=mesh['groups'=2,'clus'=8,'blk'=2] {'blk'}, dimensions={0} | all-to-all | bytes 12582912 | tf_op jit(solution)/shard_map/all_to_all | solution.py:305
  91.0 2.7 %cross_early.1.refs_2_ = f32[2,1024]{1,0:T(2,128)S(1)} custom-call(bf16[2,2,768,1024]{3,2,1,0:T(8,128)(2,1)S(1)} %all_to_all.5.refs_0_, f32[2,1024]{1,0:T(2,128)S(1)} %get-tuple-element.37.refs_1_), custom_call_target="tpu_custom_call" | custom-call | flops 1000 | bytes 1000 | tf_op jit(solution)/shard_map/cross_early/pallas_call | solution.py:98
  93.7 0.0 collective-permute-done.5.refs_0_
  93.7 4.0 %collective-permute-done.6.refs_1_ = bf16[256,1024]{1,0:T(8,128)(2,1)S(1)} collective-permute-done((bf16[256,1024]{1,0:T(8,128)(2,1)S(1)}, bf16[256,1024]{1,0:T(8,128)(2,1)S(1)}, u32[]{:S(2)}, u32[]{:S(2)}) %collective-permute-start.6) | collective-permute-done | bytes 524320 | tf_op jit(solution)/shard_map/ppermute | solution.py:299
  97.7 0.1 gather_late.1.refs_1_
  97.8 1.3 %collective-permute-start.7 = (bf16[2,256,1024]{2,1,0:T(8,128)(2,1)S(1)}, bf16[2,256,1024]{2,1,0:T(8,128)(2,1)S(1)}, u32[]{:S(2)}, u32[]{:S(2)}) collective-permute-start(bf16[2,256,1024]{2,1,0:T(8,128)(2,1)S(1)} %gather_late.1.refs_1_), channel_id=1, source_target_pairs={{0,1},{2,3},{4,5},{6,7},{8,9},{10,11},{12,13},{14,15},{16,17},{18,... | collective-permute-start | bytes 3145736 | tf_op jit(solution)/shard_map/ppermute | solution.py:333
  99.1 3.6 %own_late.1.refs_2_ = f32[2,1024]{1,0:T(2,128)S(1)} custom-call(bf16[2,2,768,1024]{3,2,1,0:T(8,128)(2,1)S(1)} %all_to_all.5.refs_0_, bf16[2,256,1024]{2,1,0:T(8,128)(2,1)S(1)} %gather_late.1.refs_1_, f32[2,1024]{1,0:T(2,128)S(1)} %cross_early.1.refs_2_), custom_call_target="tpu_custom_call" | custom-call | flops 1000 | bytes 1000 | tf_op jit(solution)/shard_map/own_late/pallas_call | solution.py:98
  102.7 0.0 collective-permute-done.7.refs_3_
  102.7 1.9 %cross_late.1 = f32[2,1024]{1,0:T(2,128)} custom-call(bf16[2,2,768,1024]{3,2,1,0:T(8,128)(2,1)S(1)} %all_to_all.5.refs_0_, bf16[2,256,1024]{2,1,0:T(8,128)(2,1)S(1)} %gather_late.1.refs_1_, f32[2,1024]{1,0:T(2,128)S(1)} %own_late.1.refs_2_, bf16[2,256,1024]{2,1,0:T(8,128)(2,1)S(1)} %collective-permute-done.7.refs_3_), custom_call_target="tpu_custom_call" | custom-call | flops 1000 | bytes 1000 | tf_op jit(solution)/shard_map/cross_late/pallas_call | solution.py:98
Async XLA Ops:
  0.0 0.7 copy-start
  3.3 33.5 %collective-permute-start.1 = (bf16[256,1024]{1,0:T(8,128)(2,1)S(1)}, bf16[256,1024]{1,0:T(8,128)(2,1)S(1)}, u32[]{:S(2)}, u32[]{:S(2)}) collective-permute-start(bf16[256,1024]{1,0:T(8,128)(2,1)S(1)} %get-tuple-element.28), channel_id=1, source_target_pairs={{0,8},{2,10},{4,12},{6,14},{8,0},{10,2},{12,4},{14,6},{1,9},{3,11}... | collective-permute-start | bytes 1572872 | tf_op jit(solution)/shard_map/ppermute | solution.py:299
  6.6 41.4 %collective-permute-start = (bf16[256,1024]{1,0:T(8,128)(2,1)S(1)}, bf16[256,1024]{1,0:T(8,128)(2,1)S(1)}, u32[]{:S(2)}, u32[]{:S(2)}) collective-permute-start(bf16[256,1024]{1,0:T(8,128)(2,1)S(1)} %get-tuple-element.25), channel_id=1, source_target_pairs={{0,10},{2,8},{4,14},{6,12},{8,2},{10,0},{12,6},{14,4},{1,11},{3,9}... | collective-permute-start | bytes 1572872 | tf_op jit(solution)/shard_map/ppermute | solution.py:299
  10.0 42.6 %collective-permute-start.2 = (bf16[256,1024]{1,0:T(8,128)(2,1)S(1)}, bf16[256,1024]{1,0:T(8,128)(2,1)S(1)}, u32[]{:S(2)}, u32[]{:S(2)}) collective-permute-start(bf16[256,1024]{1,0:T(8,128)(2,1)S(1)} %get-tuple-element.30), channel_id=1, source_target_pairs={{0,6},{2,4},{4,2},{6,0},{8,14},{10,12},{12,10},{14,8},{1,7},{3,5},... | collective-permute-start | bytes 1572872 | tf_op jit(solution)/shard_map/ppermute | solution.py:299
  11.2 66.1 %collective-permute-start.3 = (bf16[256,1024]{1,0:T(8,128)(2,1)S(1)}, bf16[256,1024]{1,0:T(8,128)(2,1)S(1)}, u32[]{:S(2)}, u32[]{:S(2)}) collective-permute-start(bf16[256,1024]{1,0:T(8,128)(2,1)S(1)} %get-tuple-element.31), channel_id=1, source_target_pairs={{0,4},{2,6},{4,0},{6,2},{8,12},{10,14},{12,8},{14,10},{1,5},{3,7},... | collective-permute-start | bytes 1572872 | tf_op jit(solution)/shard_map/ppermute | solution.py:299
  11.4 65.9 %collective-permute-start.4 = (bf16[256,1024]{1,0:T(8,128)(2,1)S(1)}, bf16[256,1024]{1,0:T(8,128)(2,1)S(1)}, u32[]{:S(2)}, u32[]{:S(2)}) collective-permute-start(bf16[256,1024]{1,0:T(8,128)(2,1)S(1)} %get-tuple-element.32), channel_id=1, source_target_pairs={{0,2},{2,0},{4,6},{6,4},{8,10},{10,8},{12,14},{14,12},{1,3},{3,1},... | collective-permute-start | bytes 1572872 | tf_op jit(solution)/shard_map/ppermute | solution.py:299
  36.8 56.9 %collective-permute-start.5 = (bf16[256,1024]{1,0:T(8,128)(2,1)S(1)}, bf16[256,1024]{1,0:T(8,128)(2,1)S(1)}, u32[]{:S(2)}, u32[]{:S(2)}) collective-permute-start(bf16[256,1024]{1,0:T(8,128)(2,1)S(1)} %get-tuple-element.35), channel_id=1, source_target_pairs={{0,12},{2,14},{4,8},{6,10},{8,4},{10,6},{12,0},{14,2},{1,13},{3,15... | collective-permute-start | bytes 1572872 | tf_op jit(solution)/shard_map/ppermute | solution.py:299
  48.0 49.7 %collective-permute-start.6 = (bf16[256,1024]{1,0:T(8,128)(2,1)S(1)}, bf16[256,1024]{1,0:T(8,128)(2,1)S(1)}, u32[]{:S(2)}, u32[]{:S(2)}) collective-permute-start(bf16[256,1024]{1,0:T(8,128)(2,1)S(1)} %get-tuple-element.36), channel_id=1, source_target_pairs={{0,14},{2,12},{4,10},{6,8},{8,6},{10,4},{12,2},{14,0},{1,15},{3,13... | collective-permute-start | bytes 1572872 | tf_op jit(solution)/shard_map/ppermute | solution.py:299
  97.8 4.9 %collective-permute-start.7 = (bf16[2,256,1024]{2,1,0:T(8,128)(2,1)S(1)}, bf16[2,256,1024]{2,1,0:T(8,128)(2,1)S(1)}, u32[]{:S(2)}, u32[]{:S(2)}) collective-permute-start(bf16[2,256,1024]{2,1,0:T(8,128)(2,1)S(1)} %gather_late.1.refs_1_), channel_id=1, source_target_pairs={{0,1},{2,3},{4,5},{6,7},{8,9},{10,11},{12,13},{14,15},{16,17},{18,... | collective-permute-start | bytes 3145736 | tf_op jit(solution)/shard_map/ppermute | solution.py:333

commit v15 on v14

--- a/solution.py
+++ b/solution.py
@@ -141,11 +141,12 @@
 
 def raise_best(best, keys, queries, triangular=False):
     rows = queries.shape[0]
-    for start in range(0, rows, CHUNK):
-        chunk = min(CHUNK, rows - start)
+    chunk = min(CHUNK, rows) if triangular else rows
+    for start in range(0, rows, chunk):
         count = start + chunk if triangular else keys.shape[0]
         sims = matmul(keys[:count, :], queries[start : start + chunk, :], ((1,), (1,)))
         filled = keys[:count, :LANES].astype(F32) < 1.5
+        parts = []
         for first in range(0, chunk, LANES):
             allowed = filled
             if triangular:
@@ -153,8 +154,9 @@
                     iota((count, LANES), 0) < iota((count, LANES), 1) + (start + first)
                 )
             part = jnp.where(allowed, sims[:, first : first + LANES], F32(-1.0))
-            window = slice(start + first, start + first + LANES)
-            best[:, window] = jnp.maximum(best[:, window], jnp.max(part, axis=0, keepdims=True))
+            parts.append(jnp.max(part, axis=0, keepdims=True))
+        window = slice(start, start + chunk)
+        best[:, window] = jnp.maximum(best[:, window], jnp.concatenate(parts, axis=1))
 
 
 def gather_group(blocks, cluster, out, me):
@@ -165,16 +167,18 @@
         out[rows, :] = block[cluster * per : (cluster + 1) * per, :]
 
 
-def score_pair(bests, groups, new, old, bit, me):
+def score_pairs(bests, groups, new, old, bit, me):
     later = (me & bit) == 0
 
     @pl.when(later)
     def _():
-        raise_best(bests[new], groups[old], groups[new])
+        for best, group in zip(bests, groups):
+            raise_best(best[new], group[old], group[new])
 
     @pl.when(jnp.logical_not(later))
     def _():
-        raise_best(bests[old], groups[new], groups[old])
+        for best, group in zip(bests, groups):
+            raise_best(best[old], group[new], group[old])
 
 
 def fresh_best(rows):
@@ -183,55 +187,29 @@
     return jnp.where(heads < 100.0, F32(-1.0), F32(UNFILLED))
 
 
-def own_stage(cuts, bits, held, first, *refs):
-    stages, refs = refs[:held], refs[held:]
-    blocks, (send, best) = list(refs[:-2]), refs[-2:]
-    before = blocks.pop(0) if held else None
-    blocks.reverse()
+def own_early(cuts, bits, *refs):
+    blocks, (send, best) = list(reversed(refs[:-2])), refs[-2:]
     per = blocks[0].shape[0] // CLUS_DEV
     me = lax.axis_index("clus")
-    core = lax.axis_index("blk")
     spans = list(zip(cuts, cuts[1:]))
-    base = spans[first][0]
-    if held:
-        best[:, :base] = before[:, :base]
+    bests = [[best.at[c : c + 1, a:b] for a, b in spans] for c in range(CLUS_DEV)]
+    groups = [[send.at[1, c, a:b] for a, b in spans] for c in range(CLUS_DEV)]
     for c in range(CLUS_DEV):
-        rows = [best.at[c : c + 1, a:b] for a, b in spans]
-        groups = []
-        for stage in stages:
-            start = spans[len(groups)][0]
-            end = start + stage.shape[2]
-            while len(groups) < first and spans[len(groups)][0] < end:
-                a, b = spans[len(groups)]
-                groups.append(stage.at[core, c, a - start : b - start])
-        for i in range(first, len(spans)):
-            a, b = spans[i]
-            group = send.at[1, c, a - base : b - base]
-            gather_group(blocks[(a - base) // per : (b - base) // per], c, group, me)
-            groups.append(group)
-            rows[i][...] = fresh_best(group)
-            raise_best(rows[i], group, group, True)
-            for j in range(i):
-                score_pair(rows, groups, i, j, bits[j], me)
+        for i, (a, b) in enumerate(spans):
+            gather_group(blocks[a // per : b // per], c, groups[c][i], me)
+            bests[c][i][...] = fresh_best(groups[c][i])
+            raise_best(bests[c][i], groups[c][i], groups[c][i], True)
         send[0, c] = send[1, c]
-
-
-def cross_stage(cuts, held, *refs):
-    stages, before, best = refs[: held + 1], refs[held + 1], refs[held + 2]
+    score_pairs(bests, groups, 1, 0, bits[0], me)
+
+
+def cross_early(received, before, best):
     best[...] = before[...]
 
     @pl.when(lax.axis_index("blk") == 1)
     def _():
-        new = stages[-1]
         for c in range(CLUS_DEV):
-            base = 0
-            for stage in stages:
-                end = base + stage.shape[2]
-                raise_best(best.at[c : c + 1, base:end], new.at[0, c], stage.at[1, c])
-                base = end
-            start = base - new.shape[2]
-            for stage in stages[:-1]:
-                raise_best(best.at[c : c + 1, start:base], stage.at[0, c], new.at[1, c])
+            raise_best(best.at[c : c + 1, : received.shape[2]], received.at[0, c], received.at[1, c])
 
 
 def gather_late(*refs):
@@ -240,30 +218,30 @@
         gather_group(blocks, c, out.at[c], lax.axis_index("clus"))
 
 
-def own_late(cuts, bits, held, *refs):
-    stages, (cat, before, best) = refs[:held], refs[held:]
+def own_late(cuts, bits, received, cat, before, best):
     me = lax.axis_index("clus")
     core = lax.axis_index("blk")
     spans = list(zip(cuts, cuts[1:]))
     last = len(spans) - 1
     start = spans[last][0]
     best[:, :start] = before[:, :start]
+    bests = [[best.at[c : c + 1, a:b] for a, b in spans] for c in range(CLUS_DEV)]
+    groups = [
+        [received.at[core, c, a:b] for a, b in spans[:-1]] + [cat.at[c]] for c in range(CLUS_DEV)
+    ]
     for c in range(CLUS_DEV):
-        rows = [best.at[c : c + 1, a:b] for a, b in spans]
-        groups = [stages[0].at[core, c, a:b] for a, b in spans[:-1]] + [cat.at[c]]
-        rows[last][...] = fresh_best(groups[last])
-        raise_best(rows[last], groups[last], groups[last], True)
-        for i in range(last):
-            score_pair(rows, groups, last, i, bits[i], me)
+        bests[c][last][...] = fresh_best(cat.at[c])
+        raise_best(bests[c][last], cat.at[c], cat.at[c], True)
+    for i in range(last):
+        score_pairs(bests, groups, last, i, bits[i], me)
 
     @pl.when(core == 1)
     def _():
         for c in range(CLUS_DEV):
-            raise_best(best.at[c : c + 1, start:], stages[0].at[0, c], cat.at[c])
-
-
-def cross_late(cuts, per, held, *refs):
-    stages, (cat, before, other, out, best) = refs[:held], refs[held:]
+            raise_best(bests[c][last], received.at[0, c], cat.at[c])
+
+
+def cross_late(cuts, per, received, cat, before, other, out, best):
     me = lax.axis_index("clus")
     core = lax.axis_index("blk")
     spans = list(zip(cuts, cuts[1:]))
@@ -274,7 +252,7 @@
         start = spans[-1][0]
         for c in range(CLUS_DEV):
             fresh = best.at[c : c + 1, start:]
-            raise_best(best.at[c : c + 1, :start], other.at[c], stages[0].at[1, c])
+            raise_best(best.at[c : c + 1, :start], other.at[c], received.at[1, c])
             raise_best(fresh, other.at[c], cat.at[c])
 
     for a, b in spans:
@@ -318,26 +296,24 @@
 
     early = near + far
     send, best = kernel_call(
-        functools.partial(own_stage, cuts[:3], bits, 0, 0),
+        functools.partial(own_early, cuts[:3], bits),
         [stage_shape(len(early)), best_shape],
         [arrived[s] for s in reversed(early)],
         "own_early",
     )
-    stages = [to_both(send)]
-    (best,) = kernel_call(
-        functools.partial(cross_stage, cuts, 0), [best_shape], stages + [best], "cross_early"
-    )
+    received = to_both(send)
+    (best,) = kernel_call(cross_early, [best_shape], [received, best], "cross_early")
     *new, best = lax.optimization_barrier((*[arrived[s] for s in late], best))
     cat_shape = jax.ShapeDtypeStruct((CLUS_DEV, len(late) * per, width), BF)
     (cat,) = kernel_call(gather_late, [cat_shape], new, "gather_late")
     other = lax.ppermute(cat, "blk", [(0, 1)])
     (best,) = kernel_call(
-        functools.partial(own_late, cuts, bits, 1), [best_shape], stages + [cat, best], "own_late"
+        functools.partial(own_late, cuts, bits), [best_shape], [received, cat, best], "own_late"
     )
     (out,) = kernel_call(
-        functools.partial(cross_late, cuts, per, 1),
+        functools.partial(cross_late, cuts, per),
         [best_shape],
-        stages + [cat, best, other],
+        [received, cat, best, other],
         "cross_late",
         [pltpu.VMEM((CLUS_DEV, rows), F32)],
     )

time: 105 us -> 104 us (level)
  Pallas kernels: 18.6 us -> 17.5 us
    pallas_call x8, Pallas kernels: 18.6 us -> 17.5 us  [kernel_call(): pl.pallas_call(kernel, out_shape=shapes, in_specs=[place] * len(inputs),...]
  transfers between devices with their start and end apart: 8 -> 8, of which waited for: 4 -> 5; matrix products, arithmetic and copies ran while one was open for 0% -> 0% of each run, Pallas kernels for 13% -> 12%
where the time goes in v15:
time: 104 us
  waiting for transfers between devices  60.4 us (58%)
  Pallas kernels  17.5 us (17%)
  starting transfers between devices  15 us (14%)
  blocking collectives  10.6 us (10%)
    ppermute x7, waiting for transfers between devices, to_owner(): return lax.ppermute(block, 'clus', [(i, i ^ step) for i in range(owners)])  60.1 us
    pallas_call x8, Pallas kernels, kernel_call(): pl.pallas_call(kernel, out_shape=shapes, in_specs=[place] * len(inputs),...  17.5 us
    ppermute x7, starting transfers between devices, to_owner(): return lax.ppermute(block, 'clus', [(i, i ^ step) for i in range(owners)])  13.7 us
    all_to_all x1, blocking collectives, to_both(): return lax.all_to_all(send, 'blk', split_axis=0, concat_axis=0, tiled=True)  10.6 us
  transfers between devices with their start and end apart: 8, of which 5 were waited for; matrix products, arithmetic and copies ran while one was open for 0% of the time, Pallas kernels for 12%

profile of v15, /device:TPU:17, one launch (start us, length us, event | category | flops | bytes accessed | tf_op | source)
XLA Modules:
  0.0 104.3 jit_solution(15279118855561595487)
XLA Ops:
  0.0 0.0 copy-start
  0.0 0.7 copy-done
  0.7 2.6 %pack_first.1 = (bf16[1024,1024]{1,0:T(8,128)(2,1)S(1)}, s32[1,1024]{1,0:T(1,128)S(1)}, bf16[256,1024]{1,0:T(8,128)(2,1)S(1)}) custom-call(bf16[1024,1024]{1,0:T(8,128)(2,1)} %emb.1, s32[1,1024]{1,0:T(1,128)S(1)} %copy-done), custom_call_target="tpu_custom_call" | custom-call | flops 1000 | bytes 1000 | tf_op jit(solution)/shard_map/pack_first/pallas_call | solution.py:98
  3.3 0.1 collective-permute-start.1
  3.3 3.2 %pack_rest.2 = (bf16[256,1024]{1,0:T(8,128)(2,1)S(1)}, bf16[256,1024]{1,0:T(8,128)(2,1)S(1)}, bf16[256,1024]{1,0:T(8,128)(2,1)S(1)}, bf16[256,1024]{1,0:T(8,128)(2,1)S(1)}, bf16[256,1024]{1,0:T(8,128)(2,1)S(1)}) custom-call(bf16[1024,1024]{1,0:T(8,128)(2,1)S(1)} %get-tuple-element.23.unit, s32[1,1024]{1,0:T(1,128)S(1)} %get-tuple-element.24.tgt), custom_call_target="tpu_custom_call" | custom-call | flops 1000 | bytes 1000 | tf_op jit(solution)/shard_map/pack_rest/pallas_call | solution.py:98
  6.6 3.4 %collective-permute-start = (bf16[256,1024]{1,0:T(8,128)(2,1)S(1)}, bf16[256,1024]{1,0:T(8,128)(2,1)S(1)}, u32[]{:S(2)}, u32[]{:S(2)}) collective-permute-start(bf16[256,1024]{1,0:T(8,128)(2,1)S(1)} %get-tuple-element.25), channel_id=1, source_target_pairs={{0,10},{2,8},{4,14},{6,12},{8,2},{10,0},{12,6},{14,4},{1,11},{3,9}... | collective-permute-start | bytes 1572872 | tf_op jit(solution)/shard_map/ppermute | solution.py:277
  10.0 1.2 %collective-permute-start.2 = (bf16[256,1024]{1,0:T(8,128)(2,1)S(1)}, bf16[256,1024]{1,0:T(8,128)(2,1)S(1)}, u32[]{:S(2)}, u32[]{:S(2)}) collective-permute-start(bf16[256,1024]{1,0:T(8,128)(2,1)S(1)} %get-tuple-element.30), channel_id=1, source_target_pairs={{0,6},{2,4},{4,2},{6,0},{8,14},{10,12},{12,10},{14,8},{1,7},{3,5},... | collective-permute-start | bytes 1572872 | tf_op jit(solution)/shard_map/ppermute | solution.py:277
  11.2 0.2 collective-permute-start.3
  11.4 1.2 %collective-permute-start.4 = (bf16[256,1024]{1,0:T(8,128)(2,1)S(1)}, bf16[256,1024]{1,0:T(8,128)(2,1)S(1)}, u32[]{:S(2)}, u32[]{:S(2)}) collective-permute-start(bf16[256,1024]{1,0:T(8,128)(2,1)S(1)} %get-tuple-element.32), channel_id=1, source_target_pairs={{0,2},{2,0},{4,6},{6,4},{8,10},{10,8},{12,14},{14,12},{1,3},{3,1},... | collective-permute-start | bytes 1572872 | tf_op jit(solution)/shard_map/ppermute | solution.py:277
  12.6 1.4 %pack_rest.3 = (bf16[256,1024]{1,0:T(8,128)(2,1)S(1)}, bf16[256,1024]{1,0:T(8,128)(2,1)S(1)}) custom-call(bf16[1024,1024]{1,0:T(8,128)(2,1)S(1)} %get-tuple-element.23.unit, s32[1,1024]{1,0:T(1,128)S(1)} %get-tuple-element.24.tgt), custom_call_target="tpu_custom_call" | custom-call | flops 1000 | bytes 1000 | tf_op jit(solution)/shard_map/pack_rest/pallas_call | solution.py:98
  14.0 22.7 %collective-permute-done.1.refs_1_ = bf16[256,1024]{1,0:T(8,128)(2,1)S(1)} collective-permute-done((bf16[256,1024]{1,0:T(8,128)(2,1)S(1)}, bf16[256,1024]{1,0:T(8,128)(2,1)S(1)}, u32[]{:S(2)}, u32[]{:S(2)}) %collective-permute-start.1) | collective-permute-done | bytes 524320 | tf_op jit(solution)/shard_map/ppermute | solution.py:277
  36.8 3.1 %collective-permute-start.5 = (bf16[256,1024]{1,0:T(8,128)(2,1)S(1)}, bf16[256,1024]{1,0:T(8,128)(2,1)S(1)}, u32[]{:S(2)}, u32[]{:S(2)}) collective-permute-start(bf16[256,1024]{1,0:T(8,128)(2,1)S(1)} %get-tuple-element.35), channel_id=1, source_target_pairs={{0,12},{2,14},{4,8},{6,10},{8,4},{10,6},{12,0},{14,2},{1,13},{3,15... | collective-permute-start | bytes 1572872 | tf_op jit(solution)/shard_map/ppermute | solution.py:277
  39.8 8.1 %collective-permute-done.refs_0_ = bf16[256,1024]{1,0:T(8,128)(2,1)S(1)} collective-permute-done((bf16[256,1024]{1,0:T(8,128)(2,1)S(1)}, bf16[256,1024]{1,0:T(8,128)(2,1)S(1)}, u32[]{:S(2)}, u32[]{:S(2)}) %collective-permute-start) | collective-permute-done | bytes 524320 | tf_op jit(solution)/shard_map/ppermute | solution.py:277
  48.0 4.6 %collective-permute-start.6 = (bf16[256,1024]{1,0:T(8,128)(2,1)S(1)}, bf16[256,1024]{1,0:T(8,128)(2,1)S(1)}, u32[]{:S(2)}, u32[]{:S(2)}) collective-permute-start(bf16[256,1024]{1,0:T(8,128)(2,1)S(1)} %get-tuple-element.36), channel_id=1, source_target_pairs={{0,14},{2,12},{4,10},{6,8},{8,6},{10,4},{12,2},{14,0},{1,15},{3,13... | collective-permute-start | bytes 1572872 | tf_op jit(solution)/shard_map/ppermute | solution.py:277
  52.5 0.0 collective-permute-done.2.refs_2_
  52.6 24.7 %collective-permute-done.3.refs_3_ = bf16[256,1024]{1,0:T(8,128)(2,1)S(1)} collective-permute-done((bf16[256,1024]{1,0:T(8,128)(2,1)S(1)}, bf16[256,1024]{1,0:T(8,128)(2,1)S(1)}, u32[]{:S(2)}, u32[]{:S(2)}) %collective-permute-start.3) | collective-permute-done | bytes 524320 | tf_op jit(solution)/shard_map/ppermute | solution.py:277
  77.3 0.0 collective-permute-done.4.refs_4_
  77.3 2.6 %own_early.1 = (bf16[2,2,768,1024]{3,2,1,0:T(8,128)(2,1)S(1)}, f32[2,1024]{1,0:T(2,128)S(1)}) custom-call(bf16[256,1024]{1,0:T(8,128)(2,1)S(1)} %collective-permute-done.refs_0_, bf16[256,1024]{1,0:T(8,128)(2,1)S(1)} %collective-permute-done.1.refs_1_, bf16[256,1024]{1,0:T(8,128)(2,1)S(1)} %collective-permute-done.2.refs_2_, ...), custom_call_target="tpu_custom_call" | custom-call | flops 1000 | bytes 1000 | tf_op jit(solution)/shard_map/own_early/pallas_call | solution.py:98
  79.9 10.6 %all_to_all.5.received = bf16[2,2,768,1024]{3,2,1,0:T(8,128)(2,1)S(1)} all-to-all(bf16[2,2,768,1024]{3,2,1,0:T(8,128)(2,1)S(1)} %get-tuple-element.34), channel_id=1, replica_groups=mesh['groups'=2,'clus'=8,'blk'=2] {'blk'}, dimensions={0} | all-to-all | bytes 12582912 | tf_op jit(solution)/shard_map/all_to_all | solution.py:283
  90.5 2.7 %cross_early.1.before = f32[2,1024]{1,0:T(2,128)S(1)} custom-call(bf16[2,2,768,1024]{3,2,1,0:T(8,128)(2,1)S(1)} %all_to_all.5.received, f32[2,1024]{1,0:T(2,128)S(1)} %get-tuple-element.37.before), custom_call_target="tpu_custom_call" | custom-call | flops 1000 | bytes 1000 | tf_op jit(solution)/shard_map/cross_early/pallas_call | solution.py:98
  93.2 0.0 collective-permute-done.5.refs_0_
  93.2 4.5 %collective-permute-done.6.refs_1_ = bf16[256,1024]{1,0:T(8,128)(2,1)S(1)} collective-permute-done((bf16[256,1024]{1,0:T(8,128)(2,1)S(1)}, bf16[256,1024]{1,0:T(8,128)(2,1)S(1)}, u32[]{:S(2)}, u32[]{:S(2)}) %collective-permute-start.6) | collective-permute-done | bytes 524320 | tf_op jit(solution)/shard_map/ppermute | solution.py:277
  97.7 0.1 gather_late.1.cat
  97.8 1.3 %collective-permute-start.7 = (bf16[2,256,1024]{2,1,0:T(8,128)(2,1)S(1)}, bf16[2,256,1024]{2,1,0:T(8,128)(2,1)S(1)}, u32[]{:S(2)}, u32[]{:S(2)}) collective-permute-start(bf16[2,256,1024]{2,1,0:T(8,128)(2,1)S(1)} %gather_late.1.cat), channel_id=1, source_target_pairs={{0,1},{2,3},{4,5},{6,7},{8,9},{10,11},{12,13},{14,15},{16,17},{18,... | collective-permute-start | bytes 3145736 | tf_op jit(solution)/shard_map/ppermute | solution.py:309
  99.1 3.0 %own_late.1.before = f32[2,1024]{1,0:T(2,128)S(1)} custom-call(bf16[2,2,768,1024]{3,2,1,0:T(8,128)(2,1)S(1)} %all_to_all.5.received, bf16[2,256,1024]{2,1,0:T(8,128)(2,1)S(1)} %gather_late.1.cat, f32[2,1024]{1,0:T(2,128)S(1)} %cross_early.1.before), custom_call_target="tpu_custom_call" | custom-call | flops 1000 | bytes 1000 | tf_op jit(solution)/shard_map/own_late/pallas_call | solution.py:98
  102.1 0.3 collective-permute-done.7.other
  102.4 1.9 %cross_late.1 = f32[2,1024]{1,0:T(2,128)} custom-call(bf16[2,2,768,1024]{3,2,1,0:T(8,128)(2,1)S(1)} %all_to_all.5.received, bf16[2,256,1024]{2,1,0:T(8,128)(2,1)S(1)} %gather_late.1.cat, f32[2,1024]{1,0:T(2,128)S(1)} %own_late.1.before, bf16[2,256,1024]{2,1,0:T(8,128)(2,1)S(1)} %collective-permute-done.7.other), custom_call_target="tpu_custom_call" | custom-call | flops 1000 | bytes 1000 | tf_op jit(solution)/shard_map/cross_late/pallas_call | solution.py:98
Async XLA Ops:
  0.0 0.7 copy-start
  3.3 33.5 %collective-permute-start.1 = (bf16[256,1024]{1,0:T(8,128)(2,1)S(1)}, bf16[256,1024]{1,0:T(8,128)(2,1)S(1)}, u32[]{:S(2)}, u32[]{:S(2)}) collective-permute-start(bf16[256,1024]{1,0:T(8,128)(2,1)S(1)} %get-tuple-element.28), channel_id=1, source_target_pairs={{0,8},{2,10},{4,12},{6,14},{8,0},{10,2},{12,4},{14,6},{1,9},{3,11}... | collective-permute-start | bytes 1572872 | tf_op jit(solution)/shard_map/ppermute | solution.py:277
  6.6 41.4 %collective-permute-start = (bf16[256,1024]{1,0:T(8,128)(2,1)S(1)}, bf16[256,1024]{1,0:T(8,128)(2,1)S(1)}, u32[]{:S(2)}, u32[]{:S(2)}) collective-permute-start(bf16[256,1024]{1,0:T(8,128)(2,1)S(1)} %get-tuple-element.25), channel_id=1, source_target_pairs={{0,10},{2,8},{4,14},{6,12},{8,2},{10,0},{12,6},{14,4},{1,11},{3,9}... | collective-permute-start | bytes 1572872 | tf_op jit(solution)/shard_map/ppermute | solution.py:277
  10.0 42.6 %collective-permute-start.2 = (bf16[256,1024]{1,0:T(8,128)(2,1)S(1)}, bf16[256,1024]{1,0:T(8,128)(2,1)S(1)}, u32[]{:S(2)}, u32[]{:S(2)}) collective-permute-start(bf16[256,1024]{1,0:T(8,128)(2,1)S(1)} %get-tuple-element.30), channel_id=1, source_target_pairs={{0,6},{2,4},{4,2},{6,0},{8,14},{10,12},{12,10},{14,8},{1,7},{3,5},... | collective-permute-start | bytes 1572872 | tf_op jit(solution)/shard_map/ppermute | solution.py:277
  11.2 66.1 %collective-permute-start.3 = (bf16[256,1024]{1,0:T(8,128)(2,1)S(1)}, bf16[256,1024]{1,0:T(8,128)(2,1)S(1)}, u32[]{:S(2)}, u32[]{:S(2)}) collective-permute-start(bf16[256,1024]{1,0:T(8,128)(2,1)S(1)} %get-tuple-element.31), channel_id=1, source_target_pairs={{0,4},{2,6},{4,0},{6,2},{8,12},{10,14},{12,8},{14,10},{1,5},{3,7},... | collective-permute-start | bytes 1572872 | tf_op jit(solution)/shard_map/ppermute | solution.py:277
  11.4 65.9 %collective-permute-start.4 = (bf16[256,1024]{1,0:T(8,128)(2,1)S(1)}, bf16[256,1024]{1,0:T(8,128)(2,1)S(1)}, u32[]{:S(2)}, u32[]{:S(2)}) collective-permute-start(bf16[256,1024]{1,0:T(8,128)(2,1)S(1)} %get-tuple-element.32), channel_id=1, source_target_pairs={{0,2},{2,0},{4,6},{6,4},{8,10},{10,8},{12,14},{14,12},{1,3},{3,1},... | collective-permute-start | bytes 1572872 | tf_op jit(solution)/shard_map/ppermute | solution.py:277
  36.8 56.4 %collective-permute-start.5 = (bf16[256,1024]{1,0:T(8,128)(2,1)S(1)}, bf16[256,1024]{1,0:T(8,128)(2,1)S(1)}, u32[]{:S(2)}, u32[]{:S(2)}) collective-permute-start(bf16[256,1024]{1,0:T(8,128)(2,1)S(1)} %get-tuple-element.35), channel_id=1, source_target_pairs={{0,12},{2,14},{4,8},{6,10},{8,4},{10,6},{12,0},{14,2},{1,13},{3,15... | collective-permute-start | bytes 1572872 | tf_op jit(solution)/shard_map/ppermute | solution.py:277
  48.0 49.7 %collective-permute-start.6 = (bf16[256,1024]{1,0:T(8,128)(2,1)S(1)}, bf16[256,1024]{1,0:T(8,128)(2,1)S(1)}, u32[]{:S(2)}, u32[]{:S(2)}) collective-permute-start(bf16[256,1024]{1,0:T(8,128)(2,1)S(1)} %get-tuple-element.36), channel_id=1, source_target_pairs={{0,14},{2,12},{4,10},{6,8},{8,6},{10,4},{12,2},{14,0},{1,15},{3,13... | collective-permute-start | bytes 1572872 | tf_op jit(solution)/shard_map/ppermute | solution.py:277
  97.8 4.6 %collective-permute-start.7 = (bf16[2,256,1024]{2,1,0:T(8,128)(2,1)S(1)}, bf16[2,256,1024]{2,1,0:T(8,128)(2,1)S(1)}, u32[]{:S(2)}, u32[]{:S(2)}) collective-permute-start(bf16[2,256,1024]{2,1,0:T(8,128)(2,1)S(1)} %gather_late.1.cat), channel_id=1, source_target_pairs={{0,1},{2,3},{4,5},{6,7},{8,9},{10,11},{12,13},{14,15},{16,17},{18,... | collective-permute-start | bytes 3145736 | tf_op jit(solution)/shard_map/ppermute | solution.py:309

commit v16 on v15

--- a/solution.py
+++ b/solution.py
@@ -65,8 +65,8 @@
 PIECES = 4
 
 
-def pack_first(steps, clusters, per_source, emb, ids, unit, tgt, *refs):
-    outs, (raw, raw_ids, sems, ids_sem) = refs[:-4], refs[-4:]
+def pack_first(steps, clusters, per_source, emb, ids, tgt, *refs):
+    outs, (unit, raw, raw_ids, sems, ids_sem) = refs[:-5], refs[-5:]
     size = emb.shape[0] // PIECES
     ids_copy = pltpu.make_async_copy(ids, raw_ids, ids_sem)
     ids_copy.start()
@@ -87,6 +87,13 @@
     store_blocks(unit[...], tgt[...], steps, CLUS_DEV * per_source, outs)
 
 
+def pack_second(steps, per_source, emb, tgt, unit, *outs):
+    values = emb[...].astype(F32)
+    scale = lax.rsqrt(jnp.sum(values * values, axis=1, keepdims=True) + 1e-6)
+    unit[...] = (values * scale).astype(BF)
+    store_blocks(unit[...], tgt[...], steps, CLUS_DEV * per_source, outs)
+
+
 def pack_rest(steps, per_source, unit, tgt, *outs):
     store_blocks(unit[...], tgt[...], steps, CLUS_DEV * per_source, outs)
 
@@ -109,15 +116,16 @@
 
 def call_pack_first(emb, ids, steps, clusters, per_source):
     block = jax.ShapeDtypeStruct((CLUS_DEV * per_source, emb.shape[1]), BF)
-    shapes = [jax.ShapeDtypeStruct(emb.shape, BF), jax.ShapeDtypeStruct(ids.shape, jnp.int32)]
+    shapes = [jax.ShapeDtypeStruct(ids.shape, jnp.int32)]
     return kernel_call(
         functools.partial(pack_first, steps, clusters, per_source),
         shapes + [block] * len(steps),
         [emb, ids],
         place=pl.BlockSpec(memory_space=pl.ANY),
-        grant=50 * 2**20,
+        grant=54 * 2**20,
         name="pack_first",
         scratch=[
+            pltpu.VMEM(emb.shape, BF),
             pltpu.VMEM(emb.shape, BF),
             pltpu.VMEM(ids.shape, jnp.int32),
             pltpu.SemaphoreType.DMA((PIECES,)),
@@ -218,42 +226,48 @@
         gather_group(blocks, c, out.at[c], lax.axis_index("clus"))
 
 
-def own_late(cuts, bits, received, cat, before, best):
+def own_late(cuts, bits, received, *refs):
+    cats, (before, best) = refs[:-2], refs[-2:]
     me = lax.axis_index("clus")
     core = lax.axis_index("blk")
     spans = list(zip(cuts, cuts[1:]))
     last = len(spans) - 1
+    early = last - len(cats) + 1
     start = spans[last][0]
     best[:, :start] = before[:, :start]
     bests = [[best.at[c : c + 1, a:b] for a, b in spans] for c in range(CLUS_DEV)]
     groups = [
-        [received.at[core, c, a:b] for a, b in spans[:-1]] + [cat.at[c]] for c in range(CLUS_DEV)
+        [received.at[core, c, a:b] for a, b in spans[:early]]
+        + [cat.at[c, : b - a] for cat, (a, b) in zip(cats, spans[early:])]
+        for c in range(CLUS_DEV)
     ]
     for c in range(CLUS_DEV):
-        bests[c][last][...] = fresh_best(cat.at[c])
-        raise_best(bests[c][last], cat.at[c], cat.at[c], True)
+        bests[c][last][...] = fresh_best(groups[c][last])
+        raise_best(bests[c][last], groups[c][last], groups[c][last], True)
     for i in range(last):
         score_pairs(bests, groups, last, i, bits[i], me)
 
     @pl.when(core == 1)
     def _():
         for c in range(CLUS_DEV):
-            raise_best(bests[c][last], received.at[0, c], cat.at[c])
-
-
-def cross_late(cuts, per, received, cat, before, other, out, best):
+            raise_best(bests[c][last], received.at[0, c], groups[c][last])
+
+
+def cross_late(cuts, per, count, received, *refs):
+    cats, (before, *others, out, best, keys, queries) = refs[:count], refs[count:]
     me = lax.axis_index("clus")
-    core = lax.axis_index("blk")
     spans = list(zip(cuts, cuts[1:]))
+    start = received.shape[2]
     best[...] = before[...]
 
-    @pl.when(core == 1)
-    def _():
-        start = spans[-1][0]
+    @pl.when(lax.axis_index("blk") == 1)
+    def _():
         for c in range(CLUS_DEV):
-            fresh = best.at[c : c + 1, start:]
-            raise_best(best.at[c : c + 1, :start], other.at[c], received.at[1, c])
-            raise_best(fresh, other.at[c], cat.at[c])
+            for cat, other, (a, b) in zip(cats, others, spans[-count:]):
+                keys[c, a - start : b - start, :] = other[c, : b - a, :]
+                queries[c, a - start : b - start, :] = cat[c, : b - a, :]
+            raise_best(best.at[c : c + 1, :start], keys.at[c], received.at[1, c])
+            raise_best(best.at[c : c + 1, start:], keys.at[c], queries.at[c])
 
     for a, b in spans:
         place = (me ^ (a // per)) & ~((b - a) // per - 1)
@@ -267,10 +281,10 @@
     clusters = CLUS_DEV * owners
     rows, width = embeddings.shape
     per = 2 * rows // clusters
-    bits = [owners // 2, owners // 4]
-    bounds = [0, owners // 2, owners // 2 + owners // 4, owners]
+    bits = [owners // 2, owners // 4, owners // 8]
+    bounds = [0, owners // 2, owners // 2 + owners // 4, owners - owners // 8, owners]
     cuts = [x * per for x in bounds]
-    near, far, late = [list(range(a, b)) for a, b in zip(bounds, bounds[1:])]
+    near, far, *lates = [list(range(a, b)) for a, b in zip(bounds, bounds[1:])]
     best_shape = jax.ShapeDtypeStruct((CLUS_DEV, rows), F32)
 
     def to_owner(block, step):
@@ -283,12 +297,19 @@
         return lax.all_to_all(send, "blk", split_axis=0, concat_axis=0, tiled=True)
 
     arrived = {}
-    lead = far[:1]
-    unit, tgt, *packed = call_pack_first(embeddings, cluster_ids, lead, clusters, per)
-    for steps in (near[1:] + far[1:] + [0], []):
-        for step, block in zip(lead, packed):
-            arrived[step] = to_owner(block, step) if step else block
-        lead, packed = steps, call_pack_rest(unit, tgt, steps, per) if steps else []
+    tgt, *packed = call_pack_first(embeddings, cluster_ids, far[:1], clusters, per)
+    arrived[far[0]] = to_owner(packed[0], far[0])
+    steps = near[1:] + far[1:] + [0]
+    block = jax.ShapeDtypeStruct((CLUS_DEV * per, width), BF)
+    unit, *packed = kernel_call(
+        functools.partial(pack_second, steps, per),
+        [jax.ShapeDtypeStruct(embeddings.shape, BF)] + [block] * len(steps),
+        [embeddings, tgt],
+        "pack_second",
+    )
+    for step, packed_block in zip(steps, packed):
+        arrived[step] = to_owner(packed_block, step) if step else packed_block
+    late = lates[0] + lates[1]
     packed = call_pack_rest(unit, tgt, late, per)
     *held, arrived[far[0]] = lax.optimization_barrier((*packed, arrived[far[0]]))
     for step, block in zip(late, held):
@@ -303,19 +324,26 @@
     )
     received = to_both(send)
     (best,) = kernel_call(cross_early, [best_shape], [received, best], "cross_early")
-    *new, best = lax.optimization_barrier((*[arrived[s] for s in late], best))
-    cat_shape = jax.ShapeDtypeStruct((CLUS_DEV, len(late) * per, width), BF)
-    (cat,) = kernel_call(gather_late, [cat_shape], new, "gather_late")
-    other = lax.ppermute(cat, "blk", [(0, 1)])
-    (best,) = kernel_call(
-        functools.partial(own_late, cuts, bits), [best_shape], [received, cat, best], "own_late"
-    )
+    cats, others = [], []
+    for steps, spare in zip(lates, (1, 0)):
+        *new, best = lax.optimization_barrier((*[arrived[s] for s in steps], best))
+        count = len(steps) * per
+        cat_shape = jax.ShapeDtypeStruct((CLUS_DEV, count + spare * count // 2, width), BF)
+        cats += kernel_call(gather_late, [cat_shape], new, "gather_late")
+        others.append(lax.ppermute(cats[-1], "blk", [(0, 1)]))
+        (best,) = kernel_call(
+            functools.partial(own_late, cuts[: 3 + len(cats)], bits),
+            [best_shape],
+            [received] + cats + [best],
+            "own_late",
+        )
+    late_rows = (CLUS_DEV, len(late) * per, width)
     (out,) = kernel_call(
-        functools.partial(cross_late, cuts, per),
+        functools.partial(cross_late, cuts, per, len(cats)),
         [best_shape],
-        [received, cat, best, other],
+        [received] + cats + [best] + others,
         "cross_late",
-        [pltpu.VMEM((CLUS_DEV, rows), F32)],
+        [pltpu.VMEM((CLUS_DEV, rows), F32)] + [pltpu.VMEM(late_rows, BF)] * 2,
     )
     return out
 

time: 104 us -> 108 us (1.038); the launches traced: 104 us -> 107 us
  waiting for transfers between devices: 60.4 us -> 55.6 us
  Pallas kernels: 17.5 us -> 21.7 us
  local copies, waits for them, and re-layouts: 0.69 us -> 2.27 us
  starting transfers between devices: 15 us -> 16.5 us
    ppermute x7, waiting for transfers between devices: 60.1 us -> 55.6 us  [to_owner(): return lax.ppermute(block, 'clus', [(i, i ^ step) for i in range(owners)])]
    pallas_call x8 -> x10, Pallas kernels: 17.5 us -> 21.7 us  [kernel_call(): pl.pallas_call(kernel, out_shape=shapes, in_specs=[place] * len(inputs),...]
    unnamed x2 -> x4, local copies, waits for them, and re-layouts: 0.69 us -> 2.27 us
    ppermute x1 -> x2, starting transfers between devices: 1.29 us -> 2.76 us  [local(): others.append(lax.ppermute(cats[-1], 'blk', [(0, 1)]))]
  transfers between devices with their start and end apart: 8 -> 9, of which waited for: 5 -> 3; matrix products, arithmetic and copies ran while one was open for 0% -> 0% of each run, Pallas kernels for 12% -> 15%
where the time goes in v16:
time: 108 us; the launch traced here: 107 us
  waiting for transfers between devices  55.6 us (51%)
  Pallas kernels  21.7 us (20%)
  starting transfers between devices  16.5 us (15%)
  blocking collectives  10.6 us (10%)
  local copies, waits for them, and re-layouts  2.27 us (2%)
    ppermute x7, waiting for transfers between devices, to_owner(): return lax.ppermute(block, 'clus', [(i, i ^ step) for i in range(owners)])  55.6 us
    pallas_call x10, Pallas kernels, kernel_call(): pl.pallas_call(kernel, out_shape=shapes, in_specs=[place] * len(inputs),...  21.7 us
    ppermute x7, starting transfers between devices, to_owner(): return lax.ppermute(block, 'clus', [(i, i ^ step) for i in range(owners)])  13.8 us
    all_to_all x1, blocking collectives, to_both(): return lax.all_to_all(send, 'blk', split_axis=0, concat_axis=0, tiled=True)  10.6 us
    ppermute x2, starting transfers between devices, local(): others.append(lax.ppermute(cats[-1], 'blk', [(0, 1)]))  2.76 us
    unnamed x4, local copies, waits for them, and re-layouts  2.27 us
  transfers between devices with their start and end apart: 9, of which 3 were waited for; matrix products, arithmetic and copies ran while one was open for 0% of the time, Pallas kernels for 15%

profile of v16, /device:TPU:17, one launch (start us, length us, event | category | flops | bytes accessed | tf_op | source)
XLA Modules:
  0.0 106.8 jit_solution(14160208434459085455)
XLA Ops:
  0.0 3.7 %pack_first.1 = (s32[1,1024]{1,0:T(1,128)}, bf16[256,1024]{1,0:T(8,128)(2,1)}) custom-call(bf16[1024,1024]{1,0:T(8,128)(2,1)} %emb.3, s32[1,1024]{1,0:T(1,128)} %ids.1), custom_call_target="tpu_custom_call" | custom-call | flops 1000 | bytes 1000 | tf_op jit(solution)/shard_map/pack_first/pallas_call | solution.py:105
  3.7 0.1 collective-permute-start.1
  3.8 0.0 copy-start
  3.8 1.6 %copy-done = bf16[1024,1024]{1,0:T(8,128)(2,1)S(1)} copy-done((bf16[1024,1024]{1,0:T(8,128)(2,1)S(1)}, bf16[1024,1024]{1,0:T(8,128)(2,1)}, u32[]{:S(2)}) %copy-start) | copy-done | bytes 2097176
  5.4 0.0 copy-start.1
  5.4 0.7 copy-done.1
  6.1 3.7 %pack_second.1 = (bf16[1024,1024]{1,0:T(8,128)(2,1)S(1)}, bf16[256,1024]{1,0:T(8,128)(2,1)S(1)}, bf16[256,1024]{1,0:T(8,128)(2,1)S(1)}, bf16[256,1024]{1,0:T(8,1...) custom-call(bf16[1024,1024]{1,0:T(8,128)(2,1)S(1)} %copy-done, s32[1,1024]{1,0:T(1,128)S(1)} %copy-done.1), custom_call_target="tpu_custom_call" | custom-call | flops 1000 | bytes 1000 | tf_op jit(solution)/shard_map/pack_second/pallas_call | solution.py:105
  9.8 3.4 %collective-permute-start = (bf16[256,1024]{1,0:T(8,128)(2,1)S(1)}, bf16[256,1024]{1,0:T(8,128)(2,1)S(1)}, u32[]{:S(2)}, u32[]{:S(2)}) collective-permute-start(bf16[256,1024]{1,0:T(8,128)(2,1)S(1)} %get-tuple-element.25), channel_id=1, source_target_pairs={{0,10},{2,8},{4,14},{6,12},{8,2},{10,0},{12,6},{14,4},{1,11},{3,9}... | collective-permute-start | bytes 1572872 | tf_op jit(solution)/shard_map/ppermute | solution.py:291
  13.2 1.2 %collective-permute-start.2 = (bf16[256,1024]{1,0:T(8,128)(2,1)S(1)}, bf16[256,1024]{1,0:T(8,128)(2,1)S(1)}, u32[]{:S(2)}, u32[]{:S(2)}) collective-permute-start(bf16[256,1024]{1,0:T(8,128)(2,1)S(1)} %get-tuple-element.31), channel_id=1, source_target_pairs={{0,6},{2,4},{4,2},{6,0},{8,14},{10,12},{12,10},{14,8},{1,7},{3,5},... | collective-permute-start | bytes 1572872 | tf_op jit(solution)/shard_map/ppermute | solution.py:291
  14.4 0.2 collective-permute-start.3
  14.6 1.2 %collective-permute-start.4 = (bf16[256,1024]{1,0:T(8,128)(2,1)S(1)}, bf16[256,1024]{1,0:T(8,128)(2,1)S(1)}, u32[]{:S(2)}, u32[]{:S(2)}) collective-permute-start(bf16[256,1024]{1,0:T(8,128)(2,1)S(1)} %get-tuple-element.33), channel_id=1, source_target_pairs={{0,2},{2,0},{4,6},{6,4},{8,10},{10,8},{12,14},{14,12},{1,3},{3,1},... | collective-permute-start | bytes 1572872 | tf_op jit(solution)/shard_map/ppermute | solution.py:291
  15.8 1.4 %pack_rest.1 = (bf16[256,1024]{1,0:T(8,128)(2,1)S(1)}, bf16[256,1024]{1,0:T(8,128)(2,1)S(1)}) custom-call(bf16[1024,1024]{1,0:T(8,128)(2,1)S(1)} %get-tuple-element.26.unit, s32[1,1024]{1,0:T(1,128)S(1)} %copy-done.1), custom_call_target="tpu_custom_call" | custom-call | flops 1000 | bytes 1000 | tf_op jit(solution)/shard_map/pack_rest/pallas_call | solution.py:105
  17.2 20.3 %collective-permute-done.1.refs_1_ = bf16[256,1024]{1,0:T(8,128)(2,1)S(1)} collective-permute-done((bf16[256,1024]{1,0:T(8,128)(2,1)}, bf16[256,1024]{1,0:T(8,128)(2,1)S(1)}, u32[]{:S(2)}, u32[]{:S(2)}) %collective-permute-start.1) | collective-permute-done | bytes 524320 | tf_op jit(solution)/shard_map/ppermute | solution.py:291
  37.5 3.1 %collective-permute-start.5 = (bf16[256,1024]{1,0:T(8,128)(2,1)S(1)}, bf16[256,1024]{1,0:T(8,128)(2,1)S(1)}, u32[]{:S(2)}, u32[]{:S(2)}) collective-permute-start(bf16[256,1024]{1,0:T(8,128)(2,1)S(1)} %get-tuple-element.36), channel_id=1, source_target_pairs={{0,12},{2,14},{4,8},{6,10},{8,4},{10,6},{12,0},{14,2},{1,13},{3,15... | collective-permute-start | bytes 1572872 | tf_op jit(solution)/shard_map/ppermute | solution.py:291
  40.6 8.0 %collective-permute-done.refs_0_ = bf16[256,1024]{1,0:T(8,128)(2,1)S(1)} collective-permute-done((bf16[256,1024]{1,0:T(8,128)(2,1)S(1)}, bf16[256,1024]{1,0:T(8,128)(2,1)S(1)}, u32[]{:S(2)}, u32[]{:S(2)}) %collective-permute-start) | collective-permute-done | bytes 524320 | tf_op jit(solution)/shard_map/ppermute | solution.py:291
  48.7 4.6 %collective-permute-start.6 = (bf16[256,1024]{1,0:T(8,128)(2,1)S(1)}, bf16[256,1024]{1,0:T(8,128)(2,1)S(1)}, u32[]{:S(2)}, u32[]{:S(2)}) collective-permute-start(bf16[256,1024]{1,0:T(8,128)(2,1)S(1)} %get-tuple-element.39), channel_id=1, source_target_pairs={{0,14},{2,12},{4,10},{6,8},{8,6},{10,4},{12,2},{14,0},{1,15},{3,13... | collective-permute-start | bytes 1572872 | tf_op jit(solution)/shard_map/ppermute | solution.py:291
  53.2 0.0 collective-permute-done.2.refs_2_
  53.2 27.3 %collective-permute-done.3.refs_3_ = bf16[256,1024]{1,0:T(8,128)(2,1)S(1)} collective-permute-done((bf16[256,1024]{1,0:T(8,128)(2,1)S(1)}, bf16[256,1024]{1,0:T(8,128)(2,1)S(1)}, u32[]{:S(2)}, u32[]{:S(2)}) %collective-permute-start.3) | collective-permute-done | bytes 524320 | tf_op jit(solution)/shard_map/ppermute | solution.py:291
  80.5 0.0 collective-permute-done.4.refs_4_
  80.5 2.6 %own_early.1 = (bf16[2,2,768,1024]{3,2,1,0:T(8,128)(2,1)S(1)}, f32[2,1024]{1,0:T(2,128)S(1)}) custom-call(bf16[256,1024]{1,0:T(8,128)(2,1)S(1)} %collective-permute-done.refs_0_, bf16[256,1024]{1,0:T(8,128)(2,1)S(1)} %collective-permute-done.1.refs_1_, bf16[256,1024]{1,0:T(8,128)(2,1)S(1)} %collective-permute-done.2.refs_2_, ...), custom_call_target="tpu_custom_call" | custom-call | flops 1000 | bytes 1000 | tf_op jit(solution)/shard_map/own_early/pallas_call | solution.py:105
  83.1 10.6 %all_to_all.5.received = bf16[2,2,768,1024]{3,2,1,0:T(8,128)(2,1)S(1)} all-to-all(bf16[2,2,768,1024]{3,2,1,0:T(8,128)(2,1)S(1)} %get-tuple-element.35), channel_id=1, replica_groups=mesh['groups'=2,'clus'=8,'blk'=2] {'blk'}, dimensions={0} | all-to-all | bytes 12582912 | tf_op jit(solution)/shard_map/all_to_all | solution.py:297
  93.7 2.7 %cross_early.1.refs_1_ = f32[2,1024]{1,0:T(2,128)S(1)} custom-call(bf16[2,2,768,1024]{3,2,1,0:T(8,128)(2,1)S(1)} %all_to_all.5.received, f32[2,1024]{1,0:T(2,128)S(1)} %get-tuple-element.37.before), custom_call_target="tpu_custom_call" | custom-call | flops 1000 | bytes 1000 | tf_op jit(solution)/shard_map/cross_early/pallas_call | solution.py:105
  96.4 0.0 collective-permute-done.5.refs_0_
  96.4 1.5 %collective-permute-start.7 = (bf16[2,192,1024]{2,1,0:T(8,128)(2,1)S(1)}, bf16[2,192,1024]{2,1,0:T(8,128)(2,1)S(1)}, u32[]{:S(2)}, u32[]{:S(2)}) collective-permute-start(bf16[2,192,1024]{2,1,0:T(8,128)(2,1)S(1)} %gather_late.2.refs_0_), channel_id=1, source_target_pairs={{0,1},{2,3},{4,5},{6,7},{8,9},{10,11},{12,13},{14,15},{16,17},{18,... | collective-permute-start | bytes 2359304 | tf_op jit(solution)/shard_map/ppermute | solution.py:333
  97.9 2.6 %own_late.2.refs_2_ = f32[2,1024]{1,0:T(2,128)S(1)} custom-call(bf16[2,2,768,1024]{3,2,1,0:T(8,128)(2,1)S(1)} %all_to_all.5.received, bf16[2,192,1024]{2,1,0:T(8,128)(2,1)S(1)} %gather_late.2.refs_0_, f32[2,1024]{1,0:T(2,128)S(1)} %cross_early.1.refs_1_), custom_call_target="tpu_custom_call" | custom-call | flops 1000 | bytes 1000 | tf_op jit(solution)/shard_map/own_late/pallas_call | solution.py:105
  100.5 0.0 collective-permute-done.6.refs_0_
  100.6 1.3 %collective-permute-start.8 = (bf16[2,128,1024]{2,1,0:T(8,128)(2,1)S(1)}, bf16[2,128,1024]{2,1,0:T(8,128)(2,1)S(1)}, u32[]{:S(2)}, u32[]{:S(2)}) collective-permute-start(bf16[2,128,1024]{2,1,0:T(8,128)(2,1)S(1)} %gather_late.3.refs_1_), channel_id=1, source_target_pairs={{0,1},{2,3},{4,5},{6,7},{8,9},{10,11},{12,13},{14,15},{16,17},{18,... | collective-permute-start | bytes 1572872 | tf_op jit(solution)/shard_map/ppermute | solution.py:333
  101.9 2.9 %own_late.3.refs_2_ = f32[2,1024]{1,0:T(2,128)S(1)} custom-call(bf16[2,2,768,1024]{3,2,1,0:T(8,128)(2,1)S(1)} %all_to_all.5.received, bf16[2,192,1024]{2,1,0:T(8,128)(2,1)S(1)} %gather_late.2.refs_0_, bf16[2,128,1024]{2,1,0:T(8,128)(2,1)S(1)} %gather_late.3.refs_1_, f32[2,1024]{1,0:T(2,128)S(1)} %own_late.2.refs_2_), custom_call_target="tpu_custom_call" | custom-call | flops 1000 | bytes 1000 | tf_op jit(solution)/shard_map/own_late/pallas_call | solution.py:105
  104.8 0.0 collective-permute-done.8.refs_4_
  104.8 0.0 collective-permute-done.7.refs_3_
  104.8 1.9 %cross_late.1 = f32[2,1024]{1,0:T(2,128)} custom-call(bf16[2,2,768,1024]{3,2,1,0:T(8,128)(2,1)S(1)} %all_to_all.5.received, bf16[2,192,1024]{2,1,0:T(8,128)(2,1)S(1)} %gather_late.2.refs_0_, bf16[2,128,1024]{2,1,0:T(8,128)(2,1)S(1)} %gather_late.3.refs_1_, f32[2,1024]{1,0:T(2,128)S(1)} %own_late.3.refs_2_, ...), custom_call_target="tpu_custom_call" | custom-call | flops 1000 | bytes 1000 | tf_op jit(solution)/shard_map/cross_late/pallas_call | solution.py:105
  (2 shorter events, 0.1 us)
Async XLA Ops:
  3.7 33.8 %collective-permute-start.1 = (bf16[256,1024]{1,0:T(8,128)(2,1)}, bf16[256,1024]{1,0:T(8,128)(2,1)S(1)}, u32[]{:S(2)}, u32[]{:S(2)}) collective-permute-start(bf16[256,1024]{1,0:T(8,128)(2,1)} %get-tuple-element.29), channel_id=1, source_target_pairs={{0,8},{2,10},{4,12},{6,14},{8,0},{10,2},{12,4},{14,6},{1,9},{3,11}... | collective-permute-start | bytes 1572872 | tf_op jit(solution)/shard_map/ppermute | solution.py:291
  3.8 1.6 %copy-start = (bf16[1024,1024]{1,0:T(8,128)(2,1)S(1)}, bf16[1024,1024]{1,0:T(8,128)(2,1)}, u32[]{:S(2)}) copy-start(bf16[1024,1024]{1,0:T(8,128)(2,1)} %emb.3) | copy-start | bytes 6291460
  5.4 0.7 copy-start.1
  9.8 38.9 %collective-permute-start = (bf16[256,1024]{1,0:T(8,128)(2,1)S(1)}, bf16[256,1024]{1,0:T(8,128)(2,1)S(1)}, u32[]{:S(2)}, u32[]{:S(2)}) collective-permute-start(bf16[256,1024]{1,0:T(8,128)(2,1)S(1)} %get-tuple-element.25), channel_id=1, source_target_pairs={{0,10},{2,8},{4,14},{6,12},{8,2},{10,0},{12,6},{14,4},{1,11},{3,9}... | collective-permute-start | bytes 1572872 | tf_op jit(solution)/shard_map/ppermute | solution.py:291
  13.2 40.1 %collective-permute-start.2 = (bf16[256,1024]{1,0:T(8,128)(2,1)S(1)}, bf16[256,1024]{1,0:T(8,128)(2,1)S(1)}, u32[]{:S(2)}, u32[]{:S(2)}) collective-permute-start(bf16[256,1024]{1,0:T(8,128)(2,1)S(1)} %get-tuple-element.31), channel_id=1, source_target_pairs={{0,6},{2,4},{4,2},{6,0},{8,14},{10,12},{12,10},{14,8},{1,7},{3,5},... | collective-permute-start | bytes 1572872 | tf_op jit(solution)/shard_map/ppermute | solution.py:291
  14.4 66.1 %collective-permute-start.3 = (bf16[256,1024]{1,0:T(8,128)(2,1)S(1)}, bf16[256,1024]{1,0:T(8,128)(2,1)S(1)}, u32[]{:S(2)}, u32[]{:S(2)}) collective-permute-start(bf16[256,1024]{1,0:T(8,128)(2,1)S(1)} %get-tuple-element.32), channel_id=1, source_target_pairs={{0,4},{2,6},{4,0},{6,2},{8,12},{10,14},{12,8},{14,10},{1,5},{3,7},... | collective-permute-start | bytes 1572872 | tf_op jit(solution)/shard_map/ppermute | solution.py:291
  14.6 65.9 %collective-permute-start.4 = (bf16[256,1024]{1,0:T(8,128)(2,1)S(1)}, bf16[256,1024]{1,0:T(8,128)(2,1)S(1)}, u32[]{:S(2)}, u32[]{:S(2)}) collective-permute-start(bf16[256,1024]{1,0:T(8,128)(2,1)S(1)} %get-tuple-element.33), channel_id=1, source_target_pairs={{0,2},{2,0},{4,6},{6,4},{8,10},{10,8},{12,14},{14,12},{1,3},{3,1},... | collective-permute-start | bytes 1572872 | tf_op jit(solution)/shard_map/ppermute | solution.py:291
  37.5 58.8 %collective-permute-start.5 = (bf16[256,1024]{1,0:T(8,128)(2,1)S(1)}, bf16[256,1024]{1,0:T(8,128)(2,1)S(1)}, u32[]{:S(2)}, u32[]{:S(2)}) collective-permute-start(bf16[256,1024]{1,0:T(8,128)(2,1)S(1)} %get-tuple-element.36), channel_id=1, source_target_pairs={{0,12},{2,14},{4,8},{6,10},{8,4},{10,6},{12,0},{14,2},{1,13},{3,15... | collective-permute-start | bytes 1572872 | tf_op jit(solution)/shard_map/ppermute | solution.py:291
  48.7 51.9 %collective-permute-start.6 = (bf16[256,1024]{1,0:T(8,128)(2,1)S(1)}, bf16[256,1024]{1,0:T(8,128)(2,1)S(1)}, u32[]{:S(2)}, u32[]{:S(2)}) collective-permute-start(bf16[256,1024]{1,0:T(8,128)(2,1)S(1)} %get-tuple-element.39), channel_id=1, source_target_pairs={{0,14},{2,12},{4,10},{6,8},{8,6},{10,4},{12,2},{14,0},{1,15},{3,13... | collective-permute-start | bytes 1572872 | tf_op jit(solution)/shard_map/ppermute | solution.py:291
  96.4 8.4 %collective-permute-start.7 = (bf16[2,192,1024]{2,1,0:T(8,128)(2,1)S(1)}, bf16[2,192,1024]{2,1,0:T(8,128)(2,1)S(1)}, u32[]{:S(2)}, u32[]{:S(2)}) collective-permute-start(bf16[2,192,1024]{2,1,0:T(8,128)(2,1)S(1)} %gather_late.2.refs_0_), channel_id=1, source_target_pairs={{0,1},{2,3},{4,5},{6,7},{8,9},{10,11},{12,13},{14,15},{16,17},{18,... | collective-permute-start | bytes 2359304 | tf_op jit(solution)/shard_map/ppermute | solution.py:333
  100.6 4.2 %collective-permute-start.8 = (bf16[2,128,1024]{2,1,0:T(8,128)(2,1)S(1)}, bf16[2,128,1024]{2,1,0:T(8,128)(2,1)S(1)}, u32[]{:S(2)}, u32[]{:S(2)}) collective-permute-start(bf16[2,128,1024]{2,1,0:T(8,128)(2,1)S(1)} %gather_late.3.refs_1_), channel_id=1, source_target_pairs={{0,1},{2,3},{4,5},{6,7},{8,9},{10,11},{12,13},{14,15},{16,17},{18,... | collective-permute-start | bytes 1572872 | tf_op jit(solution)/shard_map/ppermute | solution.py:333

commit v17 on v15

--- a/solution.py
+++ b/solution.py
@@ -66,10 +66,8 @@
 
 
 def pack_first(steps, clusters, per_source, emb, ids, unit, tgt, *refs):
-    outs, (raw, raw_ids, sems, ids_sem) = refs[:-4], refs[-4:]
+    outs, (raw, sems) = refs[:-2], refs[-2:]
     size = emb.shape[0] // PIECES
-    ids_copy = pltpu.make_async_copy(ids, raw_ids, ids_sem)
-    ids_copy.start()
     windows = [pl.ds(piece * size, size) for piece in range(PIECES)]
     copies = [
         pltpu.make_async_copy(emb.at[window], raw.at[window], sems.at[piece])
@@ -77,8 +75,7 @@
     ]
     for copy in copies:
         copy.start()
-    ids_copy.wait()
-    tgt[...] = targets(raw_ids[...], clusters, per_source)
+    tgt[...] = targets(ids[...], clusters, per_source)
     for copy, window in zip(copies, windows):
         copy.wait()
         values = raw[window, :].astype(F32)
@@ -94,11 +91,11 @@
 VMEM = pl.BlockSpec(memory_space=pltpu.VMEM)
 
 
-def kernel_call(kernel, shapes, inputs, name, scratch=(), place=VMEM, grant=20 * 2**20):
+def kernel_call(kernel, shapes, inputs, name, scratch=(), places=None, grant=20 * 2**20):
     return pl.pallas_call(
         kernel,
         out_shape=shapes,
-        in_specs=[place] * len(inputs),
+        in_specs=places or [VMEM] * len(inputs),
         out_specs=[VMEM] * len(shapes),
         scratch_shapes=scratch,
         compiler_params=pltpu.CompilerParams(vmem_limit_bytes=grant),
@@ -114,14 +111,12 @@
         functools.partial(pack_first, steps, clusters, per_source),
         shapes + [block] * len(steps),
         [emb, ids],
-        place=pl.BlockSpec(memory_space=pl.ANY),
+        places=[pl.BlockSpec(memory_space=pl.ANY), VMEM],
         grant=50 * 2**20,
         name="pack_first",
         scratch=[
             pltpu.VMEM(emb.shape, BF),
-            pltpu.VMEM(ids.shape, jnp.int32),
             pltpu.SemaphoreType.DMA((PIECES,)),
-            pltpu.SemaphoreType.DMA,
         ],
     )
 
@@ -232,8 +227,8 @@
     for c in range(CLUS_DEV):
         bests[c][last][...] = fresh_best(cat.at[c])
         raise_best(bests[c][last], cat.at[c], cat.at[c], True)
-    for i in range(last):
-        score_pairs(bests, groups, last, i, bits[i], me)
+    score_pairs(bests, groups, last, 0, bits[0], me)
+    score_pairs(bests, groups, 1, last, bits[1], me)
 
     @pl.when(core == 1)
     def _():
@@ -241,7 +236,7 @@
             raise_best(bests[c][last], received.at[0, c], cat.at[c])
 
 
-def cross_late(cuts, per, received, cat, before, other, out, best):
+def cross_late(cuts, starts, per, received, cat, before, other, out, best):
     me = lax.axis_index("clus")
     core = lax.axis_index("blk")
     spans = list(zip(cuts, cuts[1:]))
@@ -255,8 +250,8 @@
             raise_best(best.at[c : c + 1, :start], other.at[c], received.at[1, c])
             raise_best(fresh, other.at[c], cat.at[c])
 
-    for a, b in spans:
-        place = (me ^ (a // per)) & ~((b - a) // per - 1)
+    for (a, b), first in zip(spans, starts):
+        place = (me ^ first) & ~((b - a) // per - 1)
         value = best[:, a:b]
         at = pl.ds(pl.multiple_of(place * per, LANES), b - a)
         out[:, at] = jnp.where(value > 0.5 * UNFILLED, F32(0.0), value)
@@ -268,9 +263,10 @@
     rows, width = embeddings.shape
     per = 2 * rows // clusters
     bits = [owners // 2, owners // 4]
-    bounds = [0, owners // 2, owners // 2 + owners // 4, owners]
-    cuts = [x * per for x in bounds]
-    near, far, late = [list(range(a, b)) for a, b in zip(bounds, bounds[1:])]
+    half, rest = owners // 2, owners - owners // 4
+    near, far, late = [list(range(*x)) for x in ((0, half), (rest, owners), (half, rest))]
+    starts = [near[0], far[0], late[0]]
+    cuts = [0, half * per, rest * per, rows]
     best_shape = jax.ShapeDtypeStruct((CLUS_DEV, rows), F32)
 
     def to_owner(block, step):
@@ -311,7 +307,7 @@
         functools.partial(own_late, cuts, bits), [best_shape], [received, cat, best], "own_late"
     )
     (out,) = kernel_call(
-        functools.partial(cross_late, cuts, per),
+        functools.partial(cross_late, cuts, starts, per),
         [best_shape],
         [received, cat, best, other],
         "cross_late",

time: 104 us -> 107 us (1.029)
  the two profiles are of different devices: /device:TPU:17 before, /device:TPU:1 now
where the time goes in v17:
time: 107 us
  starting transfers between devices  44.8 us (42%)
  waiting for transfers between devices  22 us (21%)
  blocking collectives  21.6 us (20%)
  Pallas kernels  17.5 us (16%)
    ppermute x7, starting transfers between devices, to_owner(): return lax.ppermute(block, 'clus', [(i, i ^ step) for i in range(owners)])  43.5 us
    all_to_all x1, blocking collectives, to_both(): return lax.all_to_all(send, 'blk', split_axis=0, concat_axis=0, tiled=True)  21.6 us
    ppermute x7, waiting for transfers between devices, to_owner(): return lax.ppermute(block, 'clus', [(i, i ^ step) for i in range(owners)])  21.5 us
    pallas_call x8, Pallas kernels, kernel_call(): pl.pallas_call(kernel, out_shape=shapes, in_specs=places or [VMEM] * len(...  17.5 us
  transfers between devices with their start and end apart: 8, of which 4 were waited for; matrix products, arithmetic and copies ran while one was open for 0% of the time, Pallas kernels for 12%

profile of v17, /device:TPU:1, one launch (start us, length us, event | category | flops | bytes accessed | tf_op | source)
XLA Modules:
  0.0 106.6 jit_solution(4174057691372757205)
XLA Ops:
  0.0 0.0 copy-start
  0.0 0.7 copy-done
  0.7 2.6 %pack_first.1 = (bf16[1024,1024]{1,0:T(8,128)(2,1)S(1)}, s32[1,1024]{1,0:T(1,128)S(1)}, bf16[256,1024]{1,0:T(8,128)(2,1)S(1)}) custom-call(bf16[1024,1024]{1,0:T(8,128)(2,1)} %emb.1, s32[1,1024]{1,0:T(1,128)S(1)} %copy-done), custom_call_target="tpu_custom_call" | custom-call | flops 1000 | bytes 1000 | tf_op jit(solution)/shard_map/pack_first/pallas_call | solution.py:95
  3.3 4.2 %collective-permute-start.1 = (bf16[256,1024]{1,0:T(8,128)(2,1)S(1)}, bf16[256,1024]{1,0:T(8,128)(2,1)S(1)}, u32[]{:S(2)}, u32[]{:S(2)}) collective-permute-start(bf16[256,1024]{1,0:T(8,128)(2,1)S(1)} %get-tuple-element.28), channel_id=1, source_target_pairs={{0,12},{2,14},{4,8},{6,10},{8,4},{10,6},{12,0},{14,2},{1,13},{3,15... | collective-permute-start | bytes 1572872 | tf_op jit(solution)/shard_map/ppermute | solution.py:273
  7.5 3.2 %pack_rest.2 = (bf16[256,1024]{1,0:T(8,128)(2,1)S(1)}, bf16[256,1024]{1,0:T(8,128)(2,1)S(1)}, bf16[256,1024]{1,0:T(8,128)(2,1)S(1)}, bf16[256,1024]{1,0:T(8,128)(2,1)S(1)}, bf16[256,1024]{1,0:T(8,128)(2,1)S(1)}) custom-call(bf16[1024,1024]{1,0:T(8,128)(2,1)S(1)} %get-tuple-element.23.unit, s32[1,1024]{1,0:T(1,128)S(1)} %get-tuple-element.24.tgt), custom_call_target="tpu_custom_call" | custom-call | flops 1000 | bytes 1000 | tf_op jit(solution)/shard_map/pack_rest/pallas_call | solution.py:95
  10.7 1.0 collective-permute-start
  11.8 0.0 collective-permute-start.2
  11.8 1.5 %collective-permute-start.3 = (bf16[256,1024]{1,0:T(8,128)(2,1)S(1)}, bf16[256,1024]{1,0:T(8,128)(2,1)S(1)}, u32[]{:S(2)}, u32[]{:S(2)}) collective-permute-start(bf16[256,1024]{1,0:T(8,128)(2,1)S(1)} %get-tuple-element.31), channel_id=1, source_target_pairs={{0,4},{2,6},{4,0},{6,2},{8,12},{10,14},{12,8},{14,10},{1,5},{3,7},... | collective-permute-start | bytes 1572872 | tf_op jit(solution)/shard_map/ppermute | solution.py:273
  13.3 1.1 %collective-permute-start.4 = (bf16[256,1024]{1,0:T(8,128)(2,1)S(1)}, bf16[256,1024]{1,0:T(8,128)(2,1)S(1)}, u32[]{:S(2)}, u32[]{:S(2)}) collective-permute-start(bf16[256,1024]{1,0:T(8,128)(2,1)S(1)} %get-tuple-element.32), channel_id=1, source_target_pairs={{0,2},{2,0},{4,6},{6,4},{8,10},{10,8},{12,14},{14,12},{1,3},{3,1},... | collective-permute-start | bytes 1572872 | tf_op jit(solution)/shard_map/ppermute | solution.py:273
  14.4 1.4 %pack_rest.3 = (bf16[256,1024]{1,0:T(8,128)(2,1)S(1)}, bf16[256,1024]{1,0:T(8,128)(2,1)S(1)}) custom-call(bf16[1024,1024]{1,0:T(8,128)(2,1)S(1)} %get-tuple-element.23.unit, s32[1,1024]{1,0:T(1,128)S(1)} %get-tuple-element.24.tgt), custom_call_target="tpu_custom_call" | custom-call | flops 1000 | bytes 1000 | tf_op jit(solution)/shard_map/pack_rest/pallas_call | solution.py:95
  15.8 3.4 %collective-permute-done.1.refs_1_ = bf16[256,1024]{1,0:T(8,128)(2,1)S(1)} collective-permute-done((bf16[256,1024]{1,0:T(8,128)(2,1)S(1)}, bf16[256,1024]{1,0:T(8,128)(2,1)S(1)}, u32[]{:S(2)}, u32[]{:S(2)}) %collective-permute-start.1) | collective-permute-done | bytes 524320 | tf_op jit(solution)/shard_map/ppermute | solution.py:273
  19.2 22.5 %collective-permute-start.5 = (bf16[256,1024]{1,0:T(8,128)(2,1)S(1)}, bf16[256,1024]{1,0:T(8,128)(2,1)S(1)}, u32[]{:S(2)}, u32[]{:S(2)}) collective-permute-start(bf16[256,1024]{1,0:T(8,128)(2,1)S(1)} %get-tuple-element.35), channel_id=1, source_target_pairs={{0,8},{2,10},{4,12},{6,14},{8,0},{10,2},{12,4},{14,6},{1,9},{3,11}... | collective-permute-start | bytes 1572872 | tf_op jit(solution)/shard_map/ppermute | solution.py:273
  41.7 0.0 collective-permute-done.refs_0_
  41.7 13.1 %collective-permute-start.6 = (bf16[256,1024]{1,0:T(8,128)(2,1)S(1)}, bf16[256,1024]{1,0:T(8,128)(2,1)S(1)}, u32[]{:S(2)}, u32[]{:S(2)}) collective-permute-start(bf16[256,1024]{1,0:T(8,128)(2,1)S(1)} %get-tuple-element.36), channel_id=1, source_target_pairs={{0,10},{2,8},{4,14},{6,12},{8,2},{10,0},{12,6},{14,4},{1,11},{3,9}... | collective-permute-start | bytes 1572872 | tf_op jit(solution)/shard_map/ppermute | solution.py:273
  54.8 0.0 collective-permute-done.2.refs_2_
  54.8 0.0 collective-permute-done.3.refs_3_
  54.8 0.0 collective-permute-done.4.refs_4_
  54.9 2.6 %own_early.1 = (bf16[2,2,768,1024]{3,2,1,0:T(8,128)(2,1)S(1)}, f32[2,1024]{1,0:T(2,128)S(1)}) custom-call(bf16[256,1024]{1,0:T(8,128)(2,1)S(1)} %collective-permute-done.refs_0_, bf16[256,1024]{1,0:T(8,128)(2,1)S(1)} %collective-permute-done.1.refs_1_, bf16[256,1024]{1,0:T(8,128)(2,1)S(1)} %collective-permute-done.2.refs_2_, ...), custom_call_target="tpu_custom_call" | custom-call | flops 1000 | bytes 1000 | tf_op jit(solution)/shard_map/own_early/pallas_call | solution.py:95
  57.5 21.6 %all_to_all.5.received = bf16[2,2,768,1024]{3,2,1,0:T(8,128)(2,1)S(1)} all-to-all(bf16[2,2,768,1024]{3,2,1,0:T(8,128)(2,1)S(1)} %get-tuple-element.34), channel_id=1, replica_groups=mesh['groups'=2,'clus'=8,'blk'=2] {'blk'}, dimensions={0} | all-to-all | bytes 12582912 | tf_op jit(solution)/shard_map/all_to_all | solution.py:279
  79.1 2.7 %cross_early.1.before = f32[2,1024]{1,0:T(2,128)S(1)} custom-call(bf16[2,2,768,1024]{3,2,1,0:T(8,128)(2,1)S(1)} %all_to_all.5.received, f32[2,1024]{1,0:T(2,128)S(1)} %get-tuple-element.37.before), custom_call_target="tpu_custom_call" | custom-call | flops 1000 | bytes 1000 | tf_op jit(solution)/shard_map/cross_early/pallas_call | solution.py:95
  81.7 5.9 %collective-permute-done.5.refs_0_ = bf16[256,1024]{1,0:T(8,128)(2,1)S(1)} collective-permute-done((bf16[256,1024]{1,0:T(8,128)(2,1)S(1)}, bf16[256,1024]{1,0:T(8,128)(2,1)S(1)}, u32[]{:S(2)}, u32[]{:S(2)}) %collective-permute-start.5) | collective-permute-done | bytes 524320 | tf_op jit(solution)/shard_map/ppermute | solution.py:273
  87.7 12.2 %collective-permute-done.6.refs_1_ = bf16[256,1024]{1,0:T(8,128)(2,1)S(1)} collective-permute-done((bf16[256,1024]{1,0:T(8,128)(2,1)S(1)}, bf16[256,1024]{1,0:T(8,128)(2,1)S(1)}, u32[]{:S(2)}, u32[]{:S(2)}) %collective-permute-start.6) | collective-permute-done | bytes 524320 | tf_op jit(solution)/shard_map/ppermute | solution.py:273
  99.8 0.1 gather_late.1.cat
  99.9 1.3 %collective-permute-start.7 = (bf16[2,256,1024]{2,1,0:T(8,128)(2,1)S(1)}, bf16[2,256,1024]{2,1,0:T(8,128)(2,1)S(1)}, u32[]{:S(2)}, u32[]{:S(2)}) collective-permute-start(bf16[2,256,1024]{2,1,0:T(8,128)(2,1)S(1)} %gather_late.1.cat), channel_id=1, source_target_pairs={{0,1},{2,3},{4,5},{6,7},{8,9},{10,11},{12,13},{14,15},{16,17},{18,... | collective-permute-start | bytes 3145736 | tf_op jit(solution)/shard_map/ppermute | solution.py:305
  101.2 2.9 %own_late.1.before = f32[2,1024]{1,0:T(2,128)S(1)} custom-call(bf16[2,2,768,1024]{3,2,1,0:T(8,128)(2,1)S(1)} %all_to_all.5.received, bf16[2,256,1024]{2,1,0:T(8,128)(2,1)S(1)} %gather_late.1.cat, f32[2,1024]{1,0:T(2,128)S(1)} %cross_early.1.before), custom_call_target="tpu_custom_call" | custom-call | flops 1000 | bytes 1000 | tf_op jit(solution)/shard_map/own_late/pallas_call | solution.py:95
  104.2 0.5 collective-permute-done.7.other
  104.7 1.9 %cross_late.1 = f32[2,1024]{1,0:T(2,128)} custom-call(bf16[2,2,768,1024]{3,2,1,0:T(8,128)(2,1)S(1)} %all_to_all.5.received, bf16[2,256,1024]{2,1,0:T(8,128)(2,1)S(1)} %gather_late.1.cat, f32[2,1024]{1,0:T(2,128)S(1)} %own_late.1.before, bf16[2,256,1024]{2,1,0:T(8,128)(2,1)S(1)} %collective-permute-done.7.other), custom_call_target="tpu_custom_call" | custom-call | flops 1000 | bytes 1000 | tf_op jit(solution)/shard_map/cross_late/pallas_call | solution.py:95
Async XLA Ops:
  0.0 0.7 copy-start
  3.3 16.0 %collective-permute-start.1 = (bf16[256,1024]{1,0:T(8,128)(2,1)S(1)}, bf16[256,1024]{1,0:T(8,128)(2,1)S(1)}, u32[]{:S(2)}, u32[]{:S(2)}) collective-permute-start(bf16[256,1024]{1,0:T(8,128)(2,1)S(1)} %get-tuple-element.28), channel_id=1, source_target_pairs={{0,12},{2,14},{4,8},{6,10},{8,4},{10,6},{12,0},{14,2},{1,13},{3,15... | collective-permute-start | bytes 1572872 | tf_op jit(solution)/shard_map/ppermute | solution.py:273
  10.7 31.0 %collective-permute-start = (bf16[256,1024]{1,0:T(8,128)(2,1)S(1)}, bf16[256,1024]{1,0:T(8,128)(2,1)S(1)}, u32[]{:S(2)}, u32[]{:S(2)}) collective-permute-start(bf16[256,1024]{1,0:T(8,128)(2,1)S(1)} %get-tuple-element.25), channel_id=1, source_target_pairs={{0,14},{2,12},{4,10},{6,8},{8,6},{10,4},{12,2},{14,0},{1,15},{3,13... | collective-permute-start | bytes 1572872 | tf_op jit(solution)/shard_map/ppermute | solution.py:273
  11.8 43.1 %collective-permute-start.2 = (bf16[256,1024]{1,0:T(8,128)(2,1)S(1)}, bf16[256,1024]{1,0:T(8,128)(2,1)S(1)}, u32[]{:S(2)}, u32[]{:S(2)}) collective-permute-start(bf16[256,1024]{1,0:T(8,128)(2,1)S(1)} %get-tuple-element.30), channel_id=1, source_target_pairs={{0,6},{2,4},{4,2},{6,0},{8,14},{10,12},{12,10},{14,8},{1,7},{3,5},... | collective-permute-start | bytes 1572872 | tf_op jit(solution)/shard_map/ppermute | solution.py:273
  11.8 43.1 %collective-permute-start.3 = (bf16[256,1024]{1,0:T(8,128)(2,1)S(1)}, bf16[256,1024]{1,0:T(8,128)(2,1)S(1)}, u32[]{:S(2)}, u32[]{:S(2)}) collective-permute-start(bf16[256,1024]{1,0:T(8,128)(2,1)S(1)} %get-tuple-element.31), channel_id=1, source_target_pairs={{0,4},{2,6},{4,0},{6,2},{8,12},{10,14},{12,8},{14,10},{1,5},{3,7},... | collective-permute-start | bytes 1572872 | tf_op jit(solution)/shard_map/ppermute | solution.py:273
  13.3 41.6 %collective-permute-start.4 = (bf16[256,1024]{1,0:T(8,128)(2,1)S(1)}, bf16[256,1024]{1,0:T(8,128)(2,1)S(1)}, u32[]{:S(2)}, u32[]{:S(2)}) collective-permute-start(bf16[256,1024]{1,0:T(8,128)(2,1)S(1)} %get-tuple-element.32), channel_id=1, source_target_pairs={{0,2},{2,0},{4,6},{6,4},{8,10},{10,8},{12,14},{14,12},{1,3},{3,1},... | collective-permute-start | bytes 1572872 | tf_op jit(solution)/shard_map/ppermute | solution.py:273
  19.2 68.4 %collective-permute-start.5 = (bf16[256,1024]{1,0:T(8,128)(2,1)S(1)}, bf16[256,1024]{1,0:T(8,128)(2,1)S(1)}, u32[]{:S(2)}, u32[]{:S(2)}) collective-permute-start(bf16[256,1024]{1,0:T(8,128)(2,1)S(1)} %get-tuple-element.35), channel_id=1, source_target_pairs={{0,8},{2,10},{4,12},{6,14},{8,0},{10,2},{12,4},{14,6},{1,9},{3,11}... | collective-permute-start | bytes 1572872 | tf_op jit(solution)/shard_map/ppermute | solution.py:273
  41.7 58.1 %collective-permute-start.6 = (bf16[256,1024]{1,0:T(8,128)(2,1)S(1)}, bf16[256,1024]{1,0:T(8,128)(2,1)S(1)}, u32[]{:S(2)}, u32[]{:S(2)}) collective-permute-start(bf16[256,1024]{1,0:T(8,128)(2,1)S(1)} %get-tuple-element.36), channel_id=1, source_target_pairs={{0,10},{2,8},{4,14},{6,12},{8,2},{10,0},{12,6},{14,4},{1,11},{3,9}... | collective-permute-start | bytes 1572872 | tf_op jit(solution)/shard_map/ppermute | solution.py:273
  99.9 4.8 %collective-permute-start.7 = (bf16[2,256,1024]{2,1,0:T(8,128)(2,1)S(1)}, bf16[2,256,1024]{2,1,0:T(8,128)(2,1)S(1)}, u32[]{:S(2)}, u32[]{:S(2)}) collective-permute-start(bf16[2,256,1024]{2,1,0:T(8,128)(2,1)S(1)} %gather_late.1.cat), channel_id=1, source_target_pairs={{0,1},{2,3},{4,5},{6,7},{8,9},{10,11},{12,13},{14,15},{16,17},{18,... | collective-permute-start | bytes 3145736 | tf_op jit(solution)/shard_map/ppermute | solution.py:305

commit v18 on v17

--- a/solution.py
+++ b/solution.py
@@ -183,8 +183,10 @@
 
 
 def own_early(cuts, bits, *refs):
-    blocks, (send, best) = list(reversed(refs[:-2])), refs[-2:]
+    blocks, (send, best) = refs[:-2], refs[-2:]
     per = blocks[0].shape[0] // CLUS_DEV
+    near = cuts[1] // per
+    blocks = blocks[near - 1 :: -1] + blocks[near:]
     me = lax.axis_index("clus")
     spans = list(zip(cuts, cuts[1:]))
     bests = [[best.at[c : c + 1, a:b] for a, b in spans] for c in range(CLUS_DEV)]
@@ -294,7 +296,7 @@
     send, best = kernel_call(
         functools.partial(own_early, cuts[:3], bits),
         [stage_shape(len(early)), best_shape],
-        [arrived[s] for s in reversed(early)],
+        [arrived[s] for s in near[::-1] + far],
         "own_early",
     )
     received = to_both(send)

time: 107 us -> 107 us (level)
  waiting for transfers between devices: 22 us -> 55.8 us
  starting transfers between devices: 44.8 us -> 21.8 us
  blocking collectives: 21.6 us -> 10.9 us
    ppermute x7, waiting for transfers between devices: 21.5 us -> 55.2 us  [to_owner(): return lax.ppermute(block, 'clus', [(i, i ^ step) for i in range(owners)])]
    ppermute x7, starting transfers between devices: 43.5 us -> 20.5 us  [to_owner(): return lax.ppermute(block, 'clus', [(i, i ^ step) for i in range(owners)])]
    all_to_all x1, blocking collectives: 21.6 us -> 10.9 us  [to_both(): return lax.all_to_all(send, 'blk', split_axis=0, concat_axis=0, tiled=True)]
  transfers between devices with their start and end apart: 8 -> 8, of which waited for: 4 -> 7; matrix products, arithmetic and copies ran while one was open for 0% -> 0% of each run, Pallas kernels for 12% -> 12%
where the time goes in v18:
time: 107 us
  waiting for transfers between devices  55.8 us (52%)
  starting transfers between devices  21.8 us (20%)
  Pallas kernels  17.4 us (16%)
  blocking collectives  10.9 us (10%)
    ppermute x7, waiting for transfers between devices, to_owner(): return lax.ppermute(block, 'clus', [(i, i ^ step) for i in range(owners)])  55.2 us
    ppermute x7, starting transfers between devices, to_owner(): return lax.ppermute(block, 'clus', [(i, i ^ step) for i in range(owners)])  20.5 us
    pallas_call x8, Pallas kernels, kernel_call(): pl.pallas_call(kernel, out_shape=shapes, in_specs=places or [VMEM] * len(...  17.4 us
    all_to_all x1, blocking collectives, to_both(): return lax.all_to_all(send, 'blk', split_axis=0, concat_axis=0, tiled=True)  10.9 us
  transfers between devices with their start and end apart: 8, of which 7 were waited for; matrix products, arithmetic and copies ran while one was open for 0% of the time, Pallas kernels for 12%

profile of v18, /device:TPU:1, one launch (start us, length us, event | category | flops | bytes accessed | tf_op | source)
XLA Modules:
  0.0 106.7 jit_solution(12701445411883376006)
XLA Ops:
  0.0 0.0 copy-start
  0.0 0.7 copy-done
  0.7 2.6 %pack_first.1 = (bf16[1024,1024]{1,0:T(8,128)(2,1)S(1)}, s32[1,1024]{1,0:T(1,128)S(1)}, bf16[256,1024]{1,0:T(8,128)(2,1)S(1)}) custom-call(bf16[1024,1024]{1,0:T(8,128)(2,1)} %emb.1, s32[1,1024]{1,0:T(1,128)S(1)} %copy-done), custom_call_target="tpu_custom_call" | custom-call | flops 1000 | bytes 1000 | tf_op jit(solution)/shard_map/pack_first/pallas_call | solution.py:95
  3.3 4.2 %collective-permute-start.3 = (bf16[256,1024]{1,0:T(8,128)(2,1)S(1)}, bf16[256,1024]{1,0:T(8,128)(2,1)S(1)}, u32[]{:S(2)}, u32[]{:S(2)}) collective-permute-start(bf16[256,1024]{1,0:T(8,128)(2,1)S(1)} %get-tuple-element.31), channel_id=1, source_target_pairs={{0,12},{2,14},{4,8},{6,10},{8,4},{10,6},{12,0},{14,2},{1,13},{3,15... | collective-permute-start | bytes 1572872 | tf_op jit(solution)/shard_map/ppermute | solution.py:275
  7.5 3.2 %pack_rest.2 = (bf16[256,1024]{1,0:T(8,128)(2,1)S(1)}, bf16[256,1024]{1,0:T(8,128)(2,1)S(1)}, bf16[256,1024]{1,0:T(8,128)(2,1)S(1)}, bf16[256,1024]{1,0:T(8,128)(2,1)S(1)}, bf16[256,1024]{1,0:T(8,128)(2,1)S(1)}) custom-call(bf16[1024,1024]{1,0:T(8,128)(2,1)S(1)} %get-tuple-element.23.unit, s32[1,1024]{1,0:T(1,128)S(1)} %get-tuple-element.24.tgt), custom_call_target="tpu_custom_call" | custom-call | flops 1000 | bytes 1000 | tf_op jit(solution)/shard_map/pack_rest/pallas_call | solution.py:95
  10.7 0.3 collective-permute-start
  11.0 2.2 %collective-permute-start.1 = (bf16[256,1024]{1,0:T(8,128)(2,1)S(1)}, bf16[256,1024]{1,0:T(8,128)(2,1)S(1)}, u32[]{:S(2)}, u32[]{:S(2)}) collective-permute-start(bf16[256,1024]{1,0:T(8,128)(2,1)S(1)} %get-tuple-element.26), channel_id=1, source_target_pairs={{0,4},{2,6},{4,0},{6,2},{8,12},{10,14},{12,8},{14,10},{1,5},{3,7},... | collective-permute-start | bytes 1572872 | tf_op jit(solution)/shard_map/ppermute | solution.py:275
  13.2 0.2 collective-permute-start.2
  13.4 1.0 collective-permute-start.4
  14.4 1.4 %pack_rest.3 = (bf16[256,1024]{1,0:T(8,128)(2,1)S(1)}, bf16[256,1024]{1,0:T(8,128)(2,1)S(1)}) custom-call(bf16[1024,1024]{1,0:T(8,128)(2,1)S(1)} %get-tuple-element.23.unit, s32[1,1024]{1,0:T(1,128)S(1)} %get-tuple-element.24.tgt), custom_call_target="tpu_custom_call" | custom-call | flops 1000 | bytes 1000 | tf_op jit(solution)/shard_map/pack_rest/pallas_call | solution.py:95
  15.8 3.4 %collective-permute-done.3.refs_4_ = bf16[256,1024]{1,0:T(8,128)(2,1)S(1)} collective-permute-done((bf16[256,1024]{1,0:T(8,128)(2,1)S(1)}, bf16[256,1024]{1,0:T(8,128)(2,1)S(1)}, u32[]{:S(2)}, u32[]{:S(2)}) %collective-permute-start.3) | collective-permute-done | bytes 524320 | tf_op jit(solution)/shard_map/ppermute | solution.py:275
  19.2 11.3 %collective-permute-start.5 = (bf16[256,1024]{1,0:T(8,128)(2,1)S(1)}, bf16[256,1024]{1,0:T(8,128)(2,1)S(1)}, u32[]{:S(2)}, u32[]{:S(2)}) collective-permute-start(bf16[256,1024]{1,0:T(8,128)(2,1)S(1)} %get-tuple-element.35), channel_id=1, source_target_pairs={{0,8},{2,10},{4,12},{6,14},{8,0},{10,2},{12,4},{14,6},{1,9},{3,11}... | collective-permute-start | bytes 1572872 | tf_op jit(solution)/shard_map/ppermute | solution.py:275
  30.5 1.7 %collective-permute-done.refs_0_ = bf16[256,1024]{1,0:T(8,128)(2,1)S(1)} collective-permute-done((bf16[256,1024]{1,0:T(8,128)(2,1)S(1)}, bf16[256,1024]{1,0:T(8,128)(2,1)S(1)}, u32[]{:S(2)}, u32[]{:S(2)}) %collective-permute-start) | collective-permute-done | bytes 524320 | tf_op jit(solution)/shard_map/ppermute | solution.py:275
  32.2 1.3 %collective-permute-start.6 = (bf16[256,1024]{1,0:T(8,128)(2,1)S(1)}, bf16[256,1024]{1,0:T(8,128)(2,1)S(1)}, u32[]{:S(2)}, u32[]{:S(2)}) collective-permute-start(bf16[256,1024]{1,0:T(8,128)(2,1)S(1)} %get-tuple-element.36), channel_id=1, source_target_pairs={{0,10},{2,8},{4,14},{6,12},{8,2},{10,0},{12,6},{14,4},{1,11},{3,9}... | collective-permute-start | bytes 1572872 | tf_op jit(solution)/shard_map/ppermute | solution.py:275
  33.5 9.7 %collective-permute-done.1.refs_1_ = bf16[256,1024]{1,0:T(8,128)(2,1)S(1)} collective-permute-done((bf16[256,1024]{1,0:T(8,128)(2,1)S(1)}, bf16[256,1024]{1,0:T(8,128)(2,1)S(1)}, u32[]{:S(2)}, u32[]{:S(2)}) %collective-permute-start.1) | collective-permute-done | bytes 524320 | tf_op jit(solution)/shard_map/ppermute | solution.py:275
  43.2 0.0 collective-permute-done.2.refs_2_
  43.2 10.6 %collective-permute-done.4.refs_5_ = bf16[256,1024]{1,0:T(8,128)(2,1)S(1)} collective-permute-done((bf16[256,1024]{1,0:T(8,128)(2,1)S(1)}, bf16[256,1024]{1,0:T(8,128)(2,1)S(1)}, u32[]{:S(2)}, u32[]{:S(2)}) %collective-permute-start.4) | collective-permute-done | bytes 524320 | tf_op jit(solution)/shard_map/ppermute | solution.py:275
  53.8 2.6 %own_early.1 = (bf16[2,2,768,1024]{3,2,1,0:T(8,128)(2,1)S(1)}, f32[2,1024]{1,0:T(2,128)S(1)}) custom-call(bf16[256,1024]{1,0:T(8,128)(2,1)S(1)} %collective-permute-done.refs_0_, bf16[256,1024]{1,0:T(8,128)(2,1)S(1)} %collective-permute-done.1.refs_1_, bf16[256,1024]{1,0:T(8,128)(2,1)S(1)} %collective-permute-done.2.refs_2_, ...), custom_call_target="tpu_custom_call" | custom-call | flops 1000 | bytes 1000 | tf_op jit(solution)/shard_map/own_early/pallas_call | solution.py:95
  56.4 10.9 %all_to_all.5.received = bf16[2,2,768,1024]{3,2,1,0:T(8,128)(2,1)S(1)} all-to-all(bf16[2,2,768,1024]{3,2,1,0:T(8,128)(2,1)S(1)} %get-tuple-element.34), channel_id=1, replica_groups=mesh['groups'=2,'clus'=8,'blk'=2] {'blk'}, dimensions={0} | all-to-all | bytes 12582912 | tf_op jit(solution)/shard_map/all_to_all | solution.py:281
  67.3 2.7 %cross_early.1.before = f32[2,1024]{1,0:T(2,128)S(1)} custom-call(bf16[2,2,768,1024]{3,2,1,0:T(8,128)(2,1)S(1)} %all_to_all.5.received, f32[2,1024]{1,0:T(2,128)S(1)} %get-tuple-element.37.before), custom_call_target="tpu_custom_call" | custom-call | flops 1000 | bytes 1000 | tf_op jit(solution)/shard_map/cross_early/pallas_call | solution.py:95
  70.0 17.7 %collective-permute-done.5.refs_0_ = bf16[256,1024]{1,0:T(8,128)(2,1)S(1)} collective-permute-done((bf16[256,1024]{1,0:T(8,128)(2,1)S(1)}, bf16[256,1024]{1,0:T(8,128)(2,1)S(1)}, u32[]{:S(2)}, u32[]{:S(2)}) %collective-permute-start.5) | collective-permute-done | bytes 524320 | tf_op jit(solution)/shard_map/ppermute | solution.py:275
  87.7 12.2 %collective-permute-done.6.refs_1_ = bf16[256,1024]{1,0:T(8,128)(2,1)S(1)} collective-permute-done((bf16[256,1024]{1,0:T(8,128)(2,1)S(1)}, bf16[256,1024]{1,0:T(8,128)(2,1)S(1)}, u32[]{:S(2)}, u32[]{:S(2)}) %collective-permute-start.6) | collective-permute-done | bytes 524320 | tf_op jit(solution)/shard_map/ppermute | solution.py:275
  99.9 0.1 gather_late.1.cat
  100.0 1.3 %collective-permute-start.7 = (bf16[2,256,1024]{2,1,0:T(8,128)(2,1)S(1)}, bf16[2,256,1024]{2,1,0:T(8,128)(2,1)S(1)}, u32[]{:S(2)}, u32[]{:S(2)}) collective-permute-start(bf16[2,256,1024]{2,1,0:T(8,128)(2,1)S(1)} %gather_late.1.cat), channel_id=1, source_target_pairs={{0,1},{2,3},{4,5},{6,7},{8,9},{10,11},{12,13},{14,15},{16,17},{18,... | collective-permute-start | bytes 3145736 | tf_op jit(solution)/shard_map/ppermute | solution.py:307
  101.3 2.9 %own_late.1.before = f32[2,1024]{1,0:T(2,128)S(1)} custom-call(bf16[2,2,768,1024]{3,2,1,0:T(8,128)(2,1)S(1)} %all_to_all.5.received, bf16[2,256,1024]{2,1,0:T(8,128)(2,1)S(1)} %gather_late.1.cat, f32[2,1024]{1,0:T(2,128)S(1)} %cross_early.1.before), custom_call_target="tpu_custom_call" | custom-call | flops 1000 | bytes 1000 | tf_op jit(solution)/shard_map/own_late/pallas_call | solution.py:95
  104.2 0.5 collective-permute-done.7.other
  104.8 1.9 %cross_late.1 = f32[2,1024]{1,0:T(2,128)} custom-call(bf16[2,2,768,1024]{3,2,1,0:T(8,128)(2,1)S(1)} %all_to_all.5.received, bf16[2,256,1024]{2,1,0:T(8,128)(2,1)S(1)} %gather_late.1.cat, f32[2,1024]{1,0:T(2,128)S(1)} %own_late.1.before, bf16[2,256,1024]{2,1,0:T(8,128)(2,1)S(1)} %collective-permute-done.7.other), custom_call_target="tpu_custom_call" | custom-call | flops 1000 | bytes 1000 | tf_op jit(solution)/shard_map/cross_late/pallas_call | solution.py:95
Async XLA Ops:
  0.0 0.7 copy-start
  3.3 16.0 %collective-permute-start.3 = (bf16[256,1024]{1,0:T(8,128)(2,1)S(1)}, bf16[256,1024]{1,0:T(8,128)(2,1)S(1)}, u32[]{:S(2)}, u32[]{:S(2)}) collective-permute-start(bf16[256,1024]{1,0:T(8,128)(2,1)S(1)} %get-tuple-element.31), channel_id=1, source_target_pairs={{0,12},{2,14},{4,8},{6,10},{8,4},{10,6},{12,0},{14,2},{1,13},{3,15... | collective-permute-start | bytes 1572872 | tf_op jit(solution)/shard_map/ppermute | solution.py:275
  10.7 21.5 %collective-permute-start = (bf16[256,1024]{1,0:T(8,128)(2,1)S(1)}, bf16[256,1024]{1,0:T(8,128)(2,1)S(1)}, u32[]{:S(2)}, u32[]{:S(2)}) collective-permute-start(bf16[256,1024]{1,0:T(8,128)(2,1)S(1)} %get-tuple-element.25), channel_id=1, source_target_pairs={{0,6},{2,4},{4,2},{6,0},{8,14},{10,12},{12,10},{14,8},{1,7},{3,5},... | collective-permute-start | bytes 1572872 | tf_op jit(solution)/shard_map/ppermute | solution.py:275
  11.0 32.2 %collective-permute-start.1 = (bf16[256,1024]{1,0:T(8,128)(2,1)S(1)}, bf16[256,1024]{1,0:T(8,128)(2,1)S(1)}, u32[]{:S(2)}, u32[]{:S(2)}) collective-permute-start(bf16[256,1024]{1,0:T(8,128)(2,1)S(1)} %get-tuple-element.26), channel_id=1, source_target_pairs={{0,4},{2,6},{4,0},{6,2},{8,12},{10,14},{12,8},{14,10},{1,5},{3,7},... | collective-permute-start | bytes 1572872 | tf_op jit(solution)/shard_map/ppermute | solution.py:275
  13.2 30.0 %collective-permute-start.2 = (bf16[256,1024]{1,0:T(8,128)(2,1)S(1)}, bf16[256,1024]{1,0:T(8,128)(2,1)S(1)}, u32[]{:S(2)}, u32[]{:S(2)}) collective-permute-start(bf16[256,1024]{1,0:T(8,128)(2,1)S(1)} %get-tuple-element.27), channel_id=1, source_target_pairs={{0,2},{2,0},{4,6},{6,4},{8,10},{10,8},{12,14},{14,12},{1,3},{3,1},... | collective-permute-start | bytes 1572872 | tf_op jit(solution)/shard_map/ppermute | solution.py:275
  13.4 40.3 %collective-permute-start.4 = (bf16[256,1024]{1,0:T(8,128)(2,1)S(1)}, bf16[256,1024]{1,0:T(8,128)(2,1)S(1)}, u32[]{:S(2)}, u32[]{:S(2)}) collective-permute-start(bf16[256,1024]{1,0:T(8,128)(2,1)S(1)} %get-tuple-element.33), channel_id=1, source_target_pairs={{0,14},{2,12},{4,10},{6,8},{8,6},{10,4},{12,2},{14,0},{1,15},{3,13... | collective-permute-start | bytes 1572872 | tf_op jit(solution)/shard_map/ppermute | solution.py:275
  19.2 68.5 %collective-permute-start.5 = (bf16[256,1024]{1,0:T(8,128)(2,1)S(1)}, bf16[256,1024]{1,0:T(8,128)(2,1)S(1)}, u32[]{:S(2)}, u32[]{:S(2)}) collective-permute-start(bf16[256,1024]{1,0:T(8,128)(2,1)S(1)} %get-tuple-element.35), channel_id=1, source_target_pairs={{0,8},{2,10},{4,12},{6,14},{8,0},{10,2},{12,4},{14,6},{1,9},{3,11}... | collective-permute-start | bytes 1572872 | tf_op jit(solution)/shard_map/ppermute | solution.py:275
  32.2 67.7 %collective-permute-start.6 = (bf16[256,1024]{1,0:T(8,128)(2,1)S(1)}, bf16[256,1024]{1,0:T(8,128)(2,1)S(1)}, u32[]{:S(2)}, u32[]{:S(2)}) collective-permute-start(bf16[256,1024]{1,0:T(8,128)(2,1)S(1)} %get-tuple-element.36), channel_id=1, source_target_pairs={{0,10},{2,8},{4,14},{6,12},{8,2},{10,0},{12,6},{14,4},{1,11},{3,9}... | collective-permute-start | bytes 1572872 | tf_op jit(solution)/shard_map/ppermute | solution.py:275
  100.0 4.8 %collective-permute-start.7 = (bf16[2,256,1024]{2,1,0:T(8,128)(2,1)S(1)}, bf16[2,256,1024]{2,1,0:T(8,128)(2,1)S(1)}, u32[]{:S(2)}, u32[]{:S(2)}) collective-permute-start(bf16[2,256,1024]{2,1,0:T(8,128)(2,1)S(1)} %gather_late.1.cat), channel_id=1, source_target_pairs={{0,1},{2,3},{4,5},{6,7},{8,9},{10,11},{12,13},{14,15},{16,17},{18,... | collective-permute-start | bytes 3145736 | tf_op jit(solution)/shard_map/ppermute | solution.py:307

commit v19 on v15

--- a/solution.py
+++ b/solution.py
@@ -188,7 +188,7 @@
 
 
 def own_early(cuts, bits, *refs):
-    blocks, (send, best) = list(reversed(refs[:-2])), refs[-2:]
+    blocks, (send, best) = refs[:-2], refs[-2:]
     per = blocks[0].shape[0] // CLUS_DEV
     me = lax.axis_index("clus")
     spans = list(zip(cuts, cuts[1:]))
@@ -283,14 +283,16 @@
         return lax.all_to_all(send, "blk", split_axis=0, concat_axis=0, tiled=True)
 
     arrived = {}
-    lead = far[:1]
+    lead = [near[-1], far[0]]
     unit, tgt, *packed = call_pack_first(embeddings, cluster_ids, lead, clusters, per)
-    for steps in (near[1:] + far[1:] + [0], []):
+    for steps in (near[1:-1] + far[1:] + [0], []):
         for step, block in zip(lead, packed):
             arrived[step] = to_owner(block, step) if step else block
         lead, packed = steps, call_pack_rest(unit, tgt, steps, per) if steps else []
     packed = call_pack_rest(unit, tgt, late, per)
-    *held, arrived[far[0]] = lax.optimization_barrier((*packed, arrived[far[0]]))
+    *held, arrived[near[-1]], arrived[far[0]] = lax.optimization_barrier(
+        (*packed, arrived[near[-1]], arrived[far[0]])
+    )
     for step, block in zip(late, held):
         arrived[step] = to_owner(block, step)
 
@@ -298,7 +300,7 @@
     send, best = kernel_call(
         functools.partial(own_early, cuts[:3], bits),
         [stage_shape(len(early)), best_shape],
-        [arrived[s] for s in reversed(early)],
+        [arrived[s] for s in early],
         "own_early",
     )
     received = to_both(send)

time: 104 us -> 105 us (level)
  blocking collectives: 10.6 us -> 33.1 us
  waiting for transfers between devices: 60.4 us -> 44.4 us
  starting transfers between devices: 15 us -> 8.8 us
    all_to_all x1, blocking collectives: 10.6 us -> 33.1 us  [to_both(): return lax.all_to_all(send, 'blk', split_axis=0, concat_axis=0, tiled=True)]
    ppermute x7, waiting for transfers between devices: 60.1 us -> 43.4 us  [to_owner(): return lax.ppermute(block, 'clus', [(i, i ^ step) for i in range(owners)])]
    ppermute x7, starting transfers between devices: 13.7 us -> 7.51 us  [to_owner(): return lax.ppermute(block, 'clus', [(i, i ^ step) for i in range(owners)])]
  transfers between devices with their start and end apart: 8 -> 8, of which waited for: 5 -> 6; matrix products, arithmetic and copies ran while one was open for 0% -> 0% of each run, Pallas kernels for 12% -> 12%
where the time goes in v19:
time: 105 us
  waiting for transfers between devices  44.4 us (42%)
  blocking collectives  33.1 us (32%)
  Pallas kernels  17.5 us (17%)
  starting transfers between devices  8.8 us (8%)
    ppermute x7, waiting for transfers between devices, to_owner(): return lax.ppermute(block, 'clus', [(i, i ^ step) for i in range(owners)])  43.4 us
    all_to_all x1, blocking collectives, to_both(): return lax.all_to_all(send, 'blk', split_axis=0, concat_axis=0, tiled=True)  33.1 us
    pallas_call x8, Pallas kernels, kernel_call(): pl.pallas_call(kernel, out_shape=shapes, in_specs=[place] * len(inputs),...  17.5 us
    ppermute x7, starting transfers between devices, to_owner(): return lax.ppermute(block, 'clus', [(i, i ^ step) for i in range(owners)])  7.51 us
  transfers between devices with their start and end apart: 8, of which 6 were waited for; matrix products, arithmetic and copies ran while one was open for 0% of the time, Pallas kernels for 12%

profile of v19, /device:TPU:17, one launch (start us, length us, event | category | flops | bytes accessed | tf_op | source)
XLA Modules:
  0.0 104.5 jit_solution(1787001222725667063)
XLA Ops:
  0.0 0.0 copy-start
  0.0 0.7 copy-done
  0.7 3.2 %pack_first.1 = (bf16[1024,1024]{1,0:T(8,128)(2,1)S(1)}, s32[1,1024]{1,0:T(1,128)S(1)}, bf16[256,1024]{1,0:T(8,128)(2,1)S(1)}, bf16[256,1024]{1,0:T(8,128)(2,1)S(1)}) custom-call(bf16[1024,1024]{1,0:T(8,128)(2,1)} %emb.1, s32[1,1024]{1,0:T(1,128)S(1)} %copy-done), custom_call_target="tpu_custom_call" | custom-call | flops 1000 | bytes 1000 | tf_op jit(solution)/shard_map/pack_first/pallas_call | solution.py:98
  3.9 2.3 %collective-permute-start.2 = (bf16[256,1024]{1,0:T(8,128)(2,1)S(1)}, bf16[256,1024]{1,0:T(8,128)(2,1)S(1)}, u32[]{:S(2)}, u32[]{:S(2)}) collective-permute-start(bf16[256,1024]{1,0:T(8,128)(2,1)S(1)} %get-tuple-element.31), channel_id=1, source_target_pairs={{0,6},{2,4},{4,2},{6,0},{8,14},{10,12},{12,10},{14,8},{1,7},{3,5},... | collective-permute-start | bytes 1572872 | tf_op jit(solution)/shard_map/ppermute | solution.py:277
  6.2 0.1 collective-permute-start.3
  6.3 2.6 %pack_rest.2 = (bf16[256,1024]{1,0:T(8,128)(2,1)S(1)}, bf16[256,1024]{1,0:T(8,128)(2,1)S(1)}, bf16[256,1024]{1,0:T(8,128)(2,1)S(1)}, bf16[256,1024]{1,0:T(8,128)(2,1)S(1)}) custom-call(bf16[1024,1024]{1,0:T(8,128)(2,1)S(1)} %get-tuple-element.24.unit, s32[1,1024]{1,0:T(1,128)S(1)} %get-tuple-element.25.tgt), custom_call_target="tpu_custom_call" | custom-call | flops 1000 | bytes 1000 | tf_op jit(solution)/shard_map/pack_rest/pallas_call | solution.py:98
  8.9 0.3 collective-permute-start
  9.2 0.1 collective-permute-start.1
  9.3 3.3 %collective-permute-start.4 = (bf16[256,1024]{1,0:T(8,128)(2,1)S(1)}, bf16[256,1024]{1,0:T(8,128)(2,1)S(1)}, u32[]{:S(2)}, u32[]{:S(2)}) collective-permute-start(bf16[256,1024]{1,0:T(8,128)(2,1)S(1)} %get-tuple-element.35), channel_id=1, source_target_pairs={{0,10},{2,8},{4,14},{6,12},{8,2},{10,0},{12,6},{14,4},{1,11},{3,9}... | collective-permute-start | bytes 1572872 | tf_op jit(solution)/shard_map/ppermute | solution.py:277
  12.6 1.4 %pack_rest.3 = (bf16[256,1024]{1,0:T(8,128)(2,1)S(1)}, bf16[256,1024]{1,0:T(8,128)(2,1)S(1)}) custom-call(bf16[1024,1024]{1,0:T(8,128)(2,1)S(1)} %get-tuple-element.24.unit, s32[1,1024]{1,0:T(1,128)S(1)} %get-tuple-element.25.tgt), custom_call_target="tpu_custom_call" | custom-call | flops 1000 | bytes 1000 | tf_op jit(solution)/shard_map/pack_rest/pallas_call | solution.py:98
  14.1 12.8 %collective-permute-done.2.refs_3_ = bf16[256,1024]{1,0:T(8,128)(2,1)S(1)} collective-permute-done((bf16[256,1024]{1,0:T(8,128)(2,1)S(1)}, bf16[256,1024]{1,0:T(8,128)(2,1)S(1)}, u32[]{:S(2)}, u32[]{:S(2)}) %collective-permute-start.2) | collective-permute-done | bytes 524320 | tf_op jit(solution)/shard_map/ppermute | solution.py:277
  26.8 2.1 %collective-permute-done.3.refs_4_ = bf16[256,1024]{1,0:T(8,128)(2,1)S(1)} collective-permute-done((bf16[256,1024]{1,0:T(8,128)(2,1)S(1)}, bf16[256,1024]{1,0:T(8,128)(2,1)S(1)}, u32[]{:S(2)}, u32[]{:S(2)}) %collective-permute-start.3) | collective-permute-done | bytes 524320 | tf_op jit(solution)/shard_map/ppermute | solution.py:277
  28.9 1.3 %collective-permute-start.5 = (bf16[256,1024]{1,0:T(8,128)(2,1)S(1)}, bf16[256,1024]{1,0:T(8,128)(2,1)S(1)}, u32[]{:S(2)}, u32[]{:S(2)}) collective-permute-start(bf16[256,1024]{1,0:T(8,128)(2,1)S(1)} %get-tuple-element.37), channel_id=1, source_target_pairs={{0,12},{2,14},{4,8},{6,10},{8,4},{10,6},{12,0},{14,2},{1,13},{3,15... | collective-permute-start | bytes 1572872 | tf_op jit(solution)/shard_map/ppermute | solution.py:277
  30.2 0.1 collective-permute-start.6
  30.3 0.0 collective-permute-done.refs_1_
  30.3 18.9 %collective-permute-done.1.refs_2_ = bf16[256,1024]{1,0:T(8,128)(2,1)S(1)} collective-permute-done((bf16[256,1024]{1,0:T(8,128)(2,1)S(1)}, bf16[256,1024]{1,0:T(8,128)(2,1)S(1)}, u32[]{:S(2)}, u32[]{:S(2)}) %collective-permute-start.1) | collective-permute-done | bytes 524320 | tf_op jit(solution)/shard_map/ppermute | solution.py:277
  49.2 2.2 %collective-permute-done.4.refs_5_ = bf16[256,1024]{1,0:T(8,128)(2,1)S(1)} collective-permute-done((bf16[256,1024]{1,0:T(8,128)(2,1)S(1)}, bf16[256,1024]{1,0:T(8,128)(2,1)S(1)}, u32[]{:S(2)}, u32[]{:S(2)}) %collective-permute-start.4) | collective-permute-done | bytes 524320 | tf_op jit(solution)/shard_map/ppermute | solution.py:277
  51.4 2.6 %own_early.1 = (bf16[2,2,768,1024]{3,2,1,0:T(8,128)(2,1)S(1)}, f32[2,1024]{1,0:T(2,128)S(1)}) custom-call(bf16[256,1024]{1,0:T(8,128)(2,1)S(1)} %get-tuple-element.26.refs_0_, bf16[256,1024]{1,0:T(8,128)(2,1)S(1)} %collective-permute-done.refs_1_, bf16[256,1024]{1,0:T(8,128)(2,1)S(1)} %collective-permute-done.1.refs_2_, ...), custom_call_target="tpu_custom_call" | custom-call | flops 1000 | bytes 1000 | tf_op jit(solution)/shard_map/own_early/pallas_call | solution.py:98
  54.0 33.1 %all_to_all.5.received = bf16[2,2,768,1024]{3,2,1,0:T(8,128)(2,1)S(1)} all-to-all(bf16[2,2,768,1024]{3,2,1,0:T(8,128)(2,1)S(1)} %get-tuple-element.36), channel_id=1, replica_groups=mesh['groups'=2,'clus'=8,'blk'=2] {'blk'}, dimensions={0} | all-to-all | bytes 12582912 | tf_op jit(solution)/shard_map/all_to_all | solution.py:283
  87.1 2.7 %cross_early.1.before = f32[2,1024]{1,0:T(2,128)S(1)} custom-call(bf16[2,2,768,1024]{3,2,1,0:T(8,128)(2,1)S(1)} %all_to_all.5.received, f32[2,1024]{1,0:T(2,128)S(1)} %get-tuple-element.39.before), custom_call_target="tpu_custom_call" | custom-call | flops 1000 | bytes 1000 | tf_op jit(solution)/shard_map/cross_early/pallas_call | solution.py:98
  89.8 0.0 collective-permute-done.5.refs_0_
  89.8 7.5 %collective-permute-done.6.refs_1_ = bf16[256,1024]{1,0:T(8,128)(2,1)S(1)} collective-permute-done((bf16[256,1024]{1,0:T(8,128)(2,1)S(1)}, bf16[256,1024]{1,0:T(8,128)(2,1)S(1)}, u32[]{:S(2)}, u32[]{:S(2)}) %collective-permute-start.6) | collective-permute-done | bytes 524320 | tf_op jit(solution)/shard_map/ppermute | solution.py:277
  97.3 0.1 gather_late.1.cat
  97.4 1.3 %collective-permute-start.7 = (bf16[2,256,1024]{2,1,0:T(8,128)(2,1)S(1)}, bf16[2,256,1024]{2,1,0:T(8,128)(2,1)S(1)}, u32[]{:S(2)}, u32[]{:S(2)}) collective-permute-start(bf16[2,256,1024]{2,1,0:T(8,128)(2,1)S(1)} %gather_late.1.cat), channel_id=1, source_target_pairs={{0,1},{2,3},{4,5},{6,7},{8,9},{10,11},{12,13},{14,15},{16,17},{18,... | collective-permute-start | bytes 3145736 | tf_op jit(solution)/shard_map/ppermute | solution.py:311
  98.7 3.0 %own_late.1.before = f32[2,1024]{1,0:T(2,128)S(1)} custom-call(bf16[2,2,768,1024]{3,2,1,0:T(8,128)(2,1)S(1)} %all_to_all.5.received, bf16[2,256,1024]{2,1,0:T(8,128)(2,1)S(1)} %gather_late.1.cat, f32[2,1024]{1,0:T(2,128)S(1)} %cross_early.1.before), custom_call_target="tpu_custom_call" | custom-call | flops 1000 | bytes 1000 | tf_op jit(solution)/shard_map/own_late/pallas_call | solution.py:98
  101.7 1.0 collective-permute-done.7.other
  102.6 1.9 %cross_late.1 = f32[2,1024]{1,0:T(2,128)} custom-call(bf16[2,2,768,1024]{3,2,1,0:T(8,128)(2,1)S(1)} %all_to_all.5.received, bf16[2,256,1024]{2,1,0:T(8,128)(2,1)S(1)} %gather_late.1.cat, f32[2,1024]{1,0:T(2,128)S(1)} %own_late.1.before, bf16[2,256,1024]{2,1,0:T(8,128)(2,1)S(1)} %collective-permute-done.7.other), custom_call_target="tpu_custom_call" | custom-call | flops 1000 | bytes 1000 | tf_op jit(solution)/shard_map/cross_late/pallas_call | solution.py:98
Async XLA Ops:
  0.0 0.7 copy-start
  3.9 22.9 %collective-permute-start.2 = (bf16[256,1024]{1,0:T(8,128)(2,1)S(1)}, bf16[256,1024]{1,0:T(8,128)(2,1)S(1)}, u32[]{:S(2)}, u32[]{:S(2)}) collective-permute-start(bf16[256,1024]{1,0:T(8,128)(2,1)S(1)} %get-tuple-element.31), channel_id=1, source_target_pairs={{0,6},{2,4},{4,2},{6,0},{8,14},{10,12},{12,10},{14,8},{1,7},{3,5},... | collective-permute-start | bytes 1572872 | tf_op jit(solution)/shard_map/ppermute | solution.py:277
  6.2 22.7 %collective-permute-start.3 = (bf16[256,1024]{1,0:T(8,128)(2,1)S(1)}, bf16[256,1024]{1,0:T(8,128)(2,1)S(1)}, u32[]{:S(2)}, u32[]{:S(2)}) collective-permute-start(bf16[256,1024]{1,0:T(8,128)(2,1)S(1)} %get-tuple-element.32), channel_id=1, source_target_pairs={{0,8},{2,10},{4,12},{6,14},{8,0},{10,2},{12,4},{14,6},{1,9},{3,11}... | collective-permute-start | bytes 1572872 | tf_op jit(solution)/shard_map/ppermute | solution.py:277
  8.9 21.4 %collective-permute-start = (bf16[256,1024]{1,0:T(8,128)(2,1)S(1)}, bf16[256,1024]{1,0:T(8,128)(2,1)S(1)}, u32[]{:S(2)}, u32[]{:S(2)}) collective-permute-start(bf16[256,1024]{1,0:T(8,128)(2,1)S(1)} %get-tuple-element.27), channel_id=1, source_target_pairs={{0,2},{2,0},{4,6},{6,4},{8,10},{10,8},{12,14},{14,12},{1,3},{3,1},... | collective-permute-start | bytes 1572872 | tf_op jit(solution)/shard_map/ppermute | solution.py:277
  9.2 40.0 %collective-permute-start.1 = (bf16[256,1024]{1,0:T(8,128)(2,1)S(1)}, bf16[256,1024]{1,0:T(8,128)(2,1)S(1)}, u32[]{:S(2)}, u32[]{:S(2)}) collective-permute-start(bf16[256,1024]{1,0:T(8,128)(2,1)S(1)} %get-tuple-element.28), channel_id=1, source_target_pairs={{0,4},{2,6},{4,0},{6,2},{8,12},{10,14},{12,8},{14,10},{1,5},{3,7},... | collective-permute-start | bytes 1572872 | tf_op jit(solution)/shard_map/ppermute | solution.py:277
  9.3 42.0 %collective-permute-start.4 = (bf16[256,1024]{1,0:T(8,128)(2,1)S(1)}, bf16[256,1024]{1,0:T(8,128)(2,1)S(1)}, u32[]{:S(2)}, u32[]{:S(2)}) collective-permute-start(bf16[256,1024]{1,0:T(8,128)(2,1)S(1)} %get-tuple-element.35), channel_id=1, source_target_pairs={{0,10},{2,8},{4,14},{6,12},{8,2},{10,0},{12,6},{14,4},{1,11},{3,9}... | collective-permute-start | bytes 1572872 | tf_op jit(solution)/shard_map/ppermute | solution.py:277
  28.9 60.9 %collective-permute-start.5 = (bf16[256,1024]{1,0:T(8,128)(2,1)S(1)}, bf16[256,1024]{1,0:T(8,128)(2,1)S(1)}, u32[]{:S(2)}, u32[]{:S(2)}) collective-permute-start(bf16[256,1024]{1,0:T(8,128)(2,1)S(1)} %get-tuple-element.37), channel_id=1, source_target_pairs={{0,12},{2,14},{4,8},{6,10},{8,4},{10,6},{12,0},{14,2},{1,13},{3,15... | collective-permute-start | bytes 1572872 | tf_op jit(solution)/shard_map/ppermute | solution.py:277
  30.2 67.1 %collective-permute-start.6 = (bf16[256,1024]{1,0:T(8,128)(2,1)S(1)}, bf16[256,1024]{1,0:T(8,128)(2,1)S(1)}, u32[]{:S(2)}, u32[]{:S(2)}) collective-permute-start(bf16[256,1024]{1,0:T(8,128)(2,1)S(1)} %get-tuple-element.38), channel_id=1, source_target_pairs={{0,14},{2,12},{4,10},{6,8},{8,6},{10,4},{12,2},{14,0},{1,15},{3,13... | collective-permute-start | bytes 1572872 | tf_op jit(solution)/shard_map/ppermute | solution.py:277
  97.4 5.3 %collective-permute-start.7 = (bf16[2,256,1024]{2,1,0:T(8,128)(2,1)S(1)}, bf16[2,256,1024]{2,1,0:T(8,128)(2,1)S(1)}, u32[]{:S(2)}, u32[]{:S(2)}) collective-permute-start(bf16[2,256,1024]{2,1,0:T(8,128)(2,1)S(1)} %gather_late.1.cat), channel_id=1, source_target_pairs={{0,1},{2,3},{4,5},{6,7},{8,9},{10,11},{12,13},{14,15},{16,17},{18,... | collective-permute-start | bytes 3145736 | tf_op jit(solution)/shard_map/ppermute | solution.py:311

commit v20 on v15

--- a/solution.py
+++ b/solution.py
@@ -218,8 +218,14 @@
         gather_group(blocks, c, out.at[c], lax.axis_index("clus"))
 
 
-def own_late(cuts, bits, received, cat, before, best):
+def own_late(cuts, bits, received, first, second, before, cat, best):
     me = lax.axis_index("clus")
+    size = second.shape[1]
+    swapped = (me & (bits[-1] // 2)) != 0
+    for half, swap in ((first, swapped), (second, jnp.logical_not(swapped))):
+        rows = pl.ds(pl.multiple_of(jnp.where(swap, size, 0), size), size)
+        for c in range(CLUS_DEV):
+            cat[c, rows, :] = half[c, :size, :]
     core = lax.axis_index("blk")
     spans = list(zip(cuts, cuts[1:]))
     last = len(spans) - 1
@@ -241,7 +247,7 @@
             raise_best(bests[c][last], received.at[0, c], cat.at[c])
 
 
-def cross_late(cuts, per, received, cat, before, other, out, best):
+def cross_late(cuts, per, received, cat, before, first, second, out, best, keys):
     me = lax.axis_index("clus")
     core = lax.axis_index("blk")
     spans = list(zip(cuts, cuts[1:]))
@@ -250,10 +256,13 @@
     @pl.when(core == 1)
     def _():
         start = spans[-1][0]
+        size = second.shape[1]
         for c in range(CLUS_DEV):
+            keys[c, :size, :] = first[c, :size, :]
+            keys[c, size:, :] = second[c]
             fresh = best.at[c : c + 1, start:]
-            raise_best(best.at[c : c + 1, :start], other.at[c], received.at[1, c])
-            raise_best(fresh, other.at[c], cat.at[c])
+            raise_best(best.at[c : c + 1, :start], keys.at[c], received.at[1, c])
+            raise_best(fresh, keys.at[c], cat.at[c])
 
     for a, b in spans:
         place = (me ^ (a // per)) & ~((b - a) // per - 1)
@@ -303,19 +312,31 @@
     )
     received = to_both(send)
     (best,) = kernel_call(cross_early, [best_shape], [received, best], "cross_early")
-    *new, best = lax.optimization_barrier((*[arrived[s] for s in late], best))
-    cat_shape = jax.ShapeDtypeStruct((CLUS_DEV, len(late) * per, width), BF)
-    (cat,) = kernel_call(gather_late, [cat_shape], new, "gather_late")
-    other = lax.ppermute(cat, "blk", [(0, 1)])
-    (best,) = kernel_call(
-        functools.partial(own_late, cuts, bits), [best_shape], [received, cat, best], "own_late"
+    count = len(late) // 2
+    size = count * per
+    count = len(late) // 2
+    size = count * per
+    halves, others = [], []
+    for steps, spare in ((late[:count], size // 2), (late[count:], 0)):
+        *new, best = lax.optimization_barrier((*[arrived[s] for s in steps], best))
+        half_shape = jax.ShapeDtypeStruct((CLUS_DEV, size + spare, width), BF)
+        (half,) = kernel_call(gather_late, [half_shape], new, "gather_late")
+        others.append(lax.ppermute(half, "blk", [(0, 1)]))
+        half, best = lax.optimization_barrier((half, best))
+        halves.append(half)
+    cat_shape = jax.ShapeDtypeStruct((CLUS_DEV, 2 * size, width), BF)
+    cat, best = kernel_call(
+        functools.partial(own_late, cuts, bits),
+        [cat_shape, best_shape],
+        [received] + halves + [best],
+        "own_late",
     )
     (out,) = kernel_call(
         functools.partial(cross_late, cuts, per),
         [best_shape],
-        [received, cat, best, other],
+        [received, cat, best] + others,
         "cross_late",
-        [pltpu.VMEM((CLUS_DEV, rows), F32)],
+        [pltpu.VMEM((CLUS_DEV, rows), F32), pltpu.VMEM(cat_shape.shape, BF)],
     )
     return out
 

time: 104 us -> 104 us (level)
  waiting for transfers between devices: 60.4 us -> 58.9 us
  starting transfers between devices: 15 us -> 16.3 us
    ppermute x7, waiting for transfers between devices: 60.1 us -> 58.9 us  [to_owner(): return lax.ppermute(block, 'clus', [(i, i ^ step) for i in range(owners)])]
    ppermute x1 -> x2, starting transfers between devices: 1.29 us -> 2.58 us  [local(): others.append(lax.ppermute(half, 'blk', [(0, 1)]))]
    pallas_call x8 -> x9, Pallas kernels: 17.5 us -> 17.5 us  [kernel_call(): pl.pallas_call(kernel, out_shape=shapes, in_specs=[place] * len(inputs),...]
  transfers between devices with their start and end apart: 8 -> 9, of which waited for: 5 -> 4; matrix products, arithmetic and copies ran while one was open for 0% -> 0% of each run, Pallas kernels for 12% -> 13%
where the time goes in v20:
time: 104 us
  waiting for transfers between devices  58.9 us (57%)
  Pallas kernels  17.5 us (17%)
  starting transfers between devices  16.3 us (16%)
  blocking collectives  10.6 us (10%)
    ppermute x7, waiting for transfers between devices, to_owner(): return lax.ppermute(block, 'clus', [(i, i ^ step) for i in range(owners)])  58.9 us
    pallas_call x9, Pallas kernels, kernel_call(): pl.pallas_call(kernel, out_shape=shapes, in_specs=[place] * len(inputs),...  17.5 us
    ppermute x7, starting transfers between devices, to_owner(): return lax.ppermute(block, 'clus', [(i, i ^ step) for i in range(owners)])  13.7 us
    all_to_all x1, blocking collectives, to_both(): return lax.all_to_all(send, 'blk', split_axis=0, concat_axis=0, tiled=True)  10.6 us
    ppermute x2, starting transfers between devices, local(): others.append(lax.ppermute(half, 'blk', [(0, 1)]))  2.58 us
  transfers between devices with their start and end apart: 9, of which 4 were waited for; matrix products, arithmetic and copies ran while one was open for 0% of the time, Pallas kernels for 13%

profile of v20, /device:TPU:17, one launch (start us, length us, event | category | flops | bytes accessed | tf_op | source)
XLA Modules:
  0.0 104.1 jit_solution(3794397349853928040)
XLA Ops:
  0.0 0.0 copy-start
  0.0 0.7 copy-done
  0.7 2.6 %pack_first.1 = (bf16[1024,1024]{1,0:T(8,128)(2,1)S(1)}, s32[1,1024]{1,0:T(1,128)S(1)}, bf16[256,1024]{1,0:T(8,128)(2,1)S(1)}) custom-call(bf16[1024,1024]{1,0:T(8,128)(2,1)} %emb.1, s32[1,1024]{1,0:T(1,128)S(1)} %copy-done), custom_call_target="tpu_custom_call" | custom-call | flops 1000 | bytes 1000 | tf_op jit(solution)/shard_map/pack_first/pallas_call | solution.py:98
  3.3 0.1 collective-permute-start.1
  3.3 3.2 %pack_rest.2 = (bf16[256,1024]{1,0:T(8,128)(2,1)S(1)}, bf16[256,1024]{1,0:T(8,128)(2,1)S(1)}, bf16[256,1024]{1,0:T(8,128)(2,1)S(1)}, bf16[256,1024]{1,0:T(8,128)(2,1)S(1)}, bf16[256,1024]{1,0:T(8,128)(2,1)S(1)}) custom-call(bf16[1024,1024]{1,0:T(8,128)(2,1)S(1)} %get-tuple-element.30.unit, s32[1,1024]{1,0:T(1,128)S(1)} %get-tuple-element.31.tgt), custom_call_target="tpu_custom_call" | custom-call | flops 1000 | bytes 1000 | tf_op jit(solution)/shard_map/pack_rest/pallas_call | solution.py:98
  6.6 3.4 %collective-permute-start = (bf16[256,1024]{1,0:T(8,128)(2,1)S(1)}, bf16[256,1024]{1,0:T(8,128)(2,1)S(1)}, u32[]{:S(2)}, u32[]{:S(2)}) collective-permute-start(bf16[256,1024]{1,0:T(8,128)(2,1)S(1)} %get-tuple-element.32), channel_id=1, source_target_pairs={{0,10},{2,8},{4,14},{6,12},{8,2},{10,0},{12,6},{14,4},{1,11},{3,9}... | collective-permute-start | bytes 1572872 | tf_op jit(solution)/shard_map/ppermute | solution.py:286
  10.0 1.2 %collective-permute-start.2 = (bf16[256,1024]{1,0:T(8,128)(2,1)S(1)}, bf16[256,1024]{1,0:T(8,128)(2,1)S(1)}, u32[]{:S(2)}, u32[]{:S(2)}) collective-permute-start(bf16[256,1024]{1,0:T(8,128)(2,1)S(1)} %get-tuple-element.37), channel_id=1, source_target_pairs={{0,6},{2,4},{4,2},{6,0},{8,14},{10,12},{12,10},{14,8},{1,7},{3,5},... | collective-permute-start | bytes 1572872 | tf_op jit(solution)/shard_map/ppermute | solution.py:286
  11.2 0.2 collective-permute-start.3
  11.4 1.2 %collective-permute-start.4 = (bf16[256,1024]{1,0:T(8,128)(2,1)S(1)}, bf16[256,1024]{1,0:T(8,128)(2,1)S(1)}, u32[]{:S(2)}, u32[]{:S(2)}) collective-permute-start(bf16[256,1024]{1,0:T(8,128)(2,1)S(1)} %get-tuple-element.39), channel_id=1, source_target_pairs={{0,2},{2,0},{4,6},{6,4},{8,10},{10,8},{12,14},{14,12},{1,3},{3,1},... | collective-permute-start | bytes 1572872 | tf_op jit(solution)/shard_map/ppermute | solution.py:286
  12.6 1.4 %pack_rest.3 = (bf16[256,1024]{1,0:T(8,128)(2,1)S(1)}, bf16[256,1024]{1,0:T(8,128)(2,1)S(1)}) custom-call(bf16[1024,1024]{1,0:T(8,128)(2,1)S(1)} %get-tuple-element.30.unit, s32[1,1024]{1,0:T(1,128)S(1)} %get-tuple-element.31.tgt), custom_call_target="tpu_custom_call" | custom-call | flops 1000 | bytes 1000 | tf_op jit(solution)/shard_map/pack_rest/pallas_call | solution.py:98
  14.0 22.7 %collective-permute-done.1.refs_1_ = bf16[256,1024]{1,0:T(8,128)(2,1)S(1)} collective-permute-done((bf16[256,1024]{1,0:T(8,128)(2,1)S(1)}, bf16[256,1024]{1,0:T(8,128)(2,1)S(1)}, u32[]{:S(2)}, u32[]{:S(2)}) %collective-permute-start.1) | collective-permute-done | bytes 524320 | tf_op jit(solution)/shard_map/ppermute | solution.py:286
  36.8 3.1 %collective-permute-start.5 = (bf16[256,1024]{1,0:T(8,128)(2,1)S(1)}, bf16[256,1024]{1,0:T(8,128)(2,1)S(1)}, u32[]{:S(2)}, u32[]{:S(2)}) collective-permute-start(bf16[256,1024]{1,0:T(8,128)(2,1)S(1)} %get-tuple-element.42), channel_id=1, source_target_pairs={{0,12},{2,14},{4,8},{6,10},{8,4},{10,6},{12,0},{14,2},{1,13},{3,15... | collective-permute-start | bytes 1572872 | tf_op jit(solution)/shard_map/ppermute | solution.py:286
  39.8 8.1 %collective-permute-done.refs_0_ = bf16[256,1024]{1,0:T(8,128)(2,1)S(1)} collective-permute-done((bf16[256,1024]{1,0:T(8,128)(2,1)S(1)}, bf16[256,1024]{1,0:T(8,128)(2,1)S(1)}, u32[]{:S(2)}, u32[]{:S(2)}) %collective-permute-start) | collective-permute-done | bytes 524320 | tf_op jit(solution)/shard_map/ppermute | solution.py:286
  48.0 4.6 %collective-permute-start.6 = (bf16[256,1024]{1,0:T(8,128)(2,1)S(1)}, bf16[256,1024]{1,0:T(8,128)(2,1)S(1)}, u32[]{:S(2)}, u32[]{:S(2)}) collective-permute-start(bf16[256,1024]{1,0:T(8,128)(2,1)S(1)} %get-tuple-element.47), channel_id=1, source_target_pairs={{0,14},{2,12},{4,10},{6,8},{8,6},{10,4},{12,2},{14,0},{1,15},{3,13... | collective-permute-start | bytes 1572872 | tf_op jit(solution)/shard_map/ppermute | solution.py:286
  52.5 0.0 collective-permute-done.2.refs_2_
  52.6 24.7 %collective-permute-done.3.refs_3_ = bf16[256,1024]{1,0:T(8,128)(2,1)S(1)} collective-permute-done((bf16[256,1024]{1,0:T(8,128)(2,1)S(1)}, bf16[256,1024]{1,0:T(8,128)(2,1)S(1)}, u32[]{:S(2)}, u32[]{:S(2)}) %collective-permute-start.3) | collective-permute-done | bytes 524320 | tf_op jit(solution)/shard_map/ppermute | solution.py:286
  77.3 0.0 collective-permute-done.4.refs_4_
  77.3 2.6 %own_early.1 = (bf16[2,2,768,1024]{3,2,1,0:T(8,128)(2,1)S(1)}, f32[2,1024]{1,0:T(2,128)S(1)}) custom-call(bf16[256,1024]{1,0:T(8,128)(2,1)S(1)} %collective-permute-done.refs_0_, bf16[256,1024]{1,0:T(8,128)(2,1)S(1)} %collective-permute-done.1.refs_1_, bf16[256,1024]{1,0:T(8,128)(2,1)S(1)} %collective-permute-done.2.refs_2_, ...), custom_call_target="tpu_custom_call" | custom-call | flops 1000 | bytes 1000 | tf_op jit(solution)/shard_map/own_early/pallas_call | solution.py:98
  79.9 10.6 %all_to_all.5.received = bf16[2,2,768,1024]{3,2,1,0:T(8,128)(2,1)S(1)} all-to-all(bf16[2,2,768,1024]{3,2,1,0:T(8,128)(2,1)S(1)} %get-tuple-element.41), channel_id=1, replica_groups=mesh['groups'=2,'clus'=8,'blk'=2] {'blk'}, dimensions={0} | all-to-all | bytes 12582912 | tf_op jit(solution)/shard_map/all_to_all | solution.py:292
  90.5 2.6 %cross_early.1.before = f32[2,1024]{1,0:T(2,128)S(1)} custom-call(bf16[2,2,768,1024]{3,2,1,0:T(8,128)(2,1)S(1)} %all_to_all.5.received, f32[2,1024]{1,0:T(2,128)S(1)} %get-tuple-element.43.before), custom_call_target="tpu_custom_call" | custom-call | flops 1000 | bytes 1000 | tf_op jit(solution)/shard_map/cross_early/pallas_call | solution.py:98
  93.1 0.0 collective-permute-done.5.refs_0_
  93.2 1.3 %collective-permute-start.7 = (bf16[2,192,1024]{2,1,0:T(8,128)(2,1)S(1)}, bf16[2,192,1024]{2,1,0:T(8,128)(2,1)S(1)}, u32[]{:S(2)}, u32[]{:S(2)}) collective-permute-start(bf16[2,192,1024]{2,1,0:T(8,128)(2,1)S(1)} %gather_late.2.first), channel_id=1, source_target_pairs={{0,1},{2,3},{4,5},{6,7},{8,9},{10,11},{12,13},{14,15},{16,17},{18,... | collective-permute-start | bytes 2359304 | tf_op jit(solution)/shard_map/ppermute | solution.py:324
  94.5 3.3 %collective-permute-done.6.refs_0_ = bf16[256,1024]{1,0:T(8,128)(2,1)S(1)} collective-permute-done((bf16[256,1024]{1,0:T(8,128)(2,1)S(1)}, bf16[256,1024]{1,0:T(8,128)(2,1)S(1)}, u32[]{:S(2)}, u32[]{:S(2)}) %collective-permute-start.6) | collective-permute-done | bytes 524320 | tf_op jit(solution)/shard_map/ppermute | solution.py:286
  97.8 1.3 %collective-permute-start.8 = (bf16[2,128,1024]{2,1,0:T(8,128)(2,1)S(1)}, bf16[2,128,1024]{2,1,0:T(8,128)(2,1)S(1)}, u32[]{:S(2)}, u32[]{:S(2)}) collective-permute-start(bf16[2,128,1024]{2,1,0:T(8,128)(2,1)S(1)} %gather_late.3.second), channel_id=1, source_target_pairs={{0,1},{2,3},{4,5},{6,7},{8,9},{10,11},{12,13},{14,15},{16,17},{18,... | collective-permute-start | bytes 1572872 | tf_op jit(solution)/shard_map/ppermute | solution.py:324
  99.1 3.1 %own_late.1 = (bf16[2,256,1024]{2,1,0:T(8,128)(2,1)S(1)}, f32[2,1024]{1,0:T(2,128)S(1)}) custom-call(bf16[2,2,768,1024]{3,2,1,0:T(8,128)(2,1)S(1)} %all_to_all.5.received, bf16[2,192,1024]{2,1,0:T(8,128)(2,1)S(1)} %gather_late.2.first, bf16[2,128,1024]{2,1,0:T(8,128)(2,1)S(1)} %gather_late.3.second, f32[2,1024]{1,0:T(2,128)S(1)} %cross_early.1.before), custom_call_target="tpu_custom_call" | custom-call | flops 1000 | bytes 1000 | tf_op jit(solution)/shard_map/own_late/pallas_call | solution.py:98
  102.2 0.0 collective-permute-done.8.second
  102.2 0.0 collective-permute-done.7.first
  102.2 1.9 %cross_late.1 = f32[2,1024]{1,0:T(2,128)} custom-call(bf16[2,2,768,1024]{3,2,1,0:T(8,128)(2,1)S(1)} %all_to_all.5.received, bf16[2,256,1024]{2,1,0:T(8,128)(2,1)S(1)} %get-tuple-element.53.cat, f32[2,1024]{1,0:T(2,128)S(1)} %get-tuple-element.54.before, bf16[2,192,1024]{2,1,0:T(8,128)(2,1)S(1)} %collective-permute-done.7.first, ...), custom_call_target="tpu_custom_call" | custom-call | flops 1000 | bytes 1000 | tf_op jit(solution)/shard_map/cross_late/pallas_call | solution.py:98
  (2 shorter events, 0.1 us)
Async XLA Ops:
  0.0 0.7 copy-start
  3.3 33.5 %collective-permute-start.1 = (bf16[256,1024]{1,0:T(8,128)(2,1)S(1)}, bf16[256,1024]{1,0:T(8,128)(2,1)S(1)}, u32[]{:S(2)}, u32[]{:S(2)}) collective-permute-start(bf16[256,1024]{1,0:T(8,128)(2,1)S(1)} %get-tuple-element.35), channel_id=1, source_target_pairs={{0,8},{2,10},{4,12},{6,14},{8,0},{10,2},{12,4},{14,6},{1,9},{3,11}... | collective-permute-start | bytes 1572872 | tf_op jit(solution)/shard_map/ppermute | solution.py:286
  6.6 41.4 %collective-permute-start = (bf16[256,1024]{1,0:T(8,128)(2,1)S(1)}, bf16[256,1024]{1,0:T(8,128)(2,1)S(1)}, u32[]{:S(2)}, u32[]{:S(2)}) collective-permute-start(bf16[256,1024]{1,0:T(8,128)(2,1)S(1)} %get-tuple-element.32), channel_id=1, source_target_pairs={{0,10},{2,8},{4,14},{6,12},{8,2},{10,0},{12,6},{14,4},{1,11},{3,9}... | collective-permute-start | bytes 1572872 | tf_op jit(solution)/shard_map/ppermute | solution.py:286
  10.0 42.6 %collective-permute-start.2 = (bf16[256,1024]{1,0:T(8,128)(2,1)S(1)}, bf16[256,1024]{1,0:T(8,128)(2,1)S(1)}, u32[]{:S(2)}, u32[]{:S(2)}) collective-permute-start(bf16[256,1024]{1,0:T(8,128)(2,1)S(1)} %get-tuple-element.37), channel_id=1, source_target_pairs={{0,6},{2,4},{4,2},{6,0},{8,14},{10,12},{12,10},{14,8},{1,7},{3,5},... | collective-permute-start | bytes 1572872 | tf_op jit(solution)/shard_map/ppermute | solution.py:286
  11.2 66.1 %collective-permute-start.3 = (bf16[256,1024]{1,0:T(8,128)(2,1)S(1)}, bf16[256,1024]{1,0:T(8,128)(2,1)S(1)}, u32[]{:S(2)}, u32[]{:S(2)}) collective-permute-start(bf16[256,1024]{1,0:T(8,128)(2,1)S(1)} %get-tuple-element.38), channel_id=1, source_target_pairs={{0,4},{2,6},{4,0},{6,2},{8,12},{10,14},{12,8},{14,10},{1,5},{3,7},... | collective-permute-start | bytes 1572872 | tf_op jit(solution)/shard_map/ppermute | solution.py:286
  11.4 65.9 %collective-permute-start.4 = (bf16[256,1024]{1,0:T(8,128)(2,1)S(1)}, bf16[256,1024]{1,0:T(8,128)(2,1)S(1)}, u32[]{:S(2)}, u32[]{:S(2)}) collective-permute-start(bf16[256,1024]{1,0:T(8,128)(2,1)S(1)} %get-tuple-element.39), channel_id=1, source_target_pairs={{0,2},{2,0},{4,6},{6,4},{8,10},{10,8},{12,14},{14,12},{1,3},{3,1},... | collective-permute-start | bytes 1572872 | tf_op jit(solution)/shard_map/ppermute | solution.py:286
  36.8 56.4 %collective-permute-start.5 = (bf16[256,1024]{1,0:T(8,128)(2,1)S(1)}, bf16[256,1024]{1,0:T(8,128)(2,1)S(1)}, u32[]{:S(2)}, u32[]{:S(2)}) collective-permute-start(bf16[256,1024]{1,0:T(8,128)(2,1)S(1)} %get-tuple-element.42), channel_id=1, source_target_pairs={{0,12},{2,14},{4,8},{6,10},{8,4},{10,6},{12,0},{14,2},{1,13},{3,15... | collective-permute-start | bytes 1572872 | tf_op jit(solution)/shard_map/ppermute | solution.py:286
  48.0 49.7 %collective-permute-start.6 = (bf16[256,1024]{1,0:T(8,128)(2,1)S(1)}, bf16[256,1024]{1,0:T(8,128)(2,1)S(1)}, u32[]{:S(2)}, u32[]{:S(2)}) collective-permute-start(bf16[256,1024]{1,0:T(8,128)(2,1)S(1)} %get-tuple-element.47), channel_id=1, source_target_pairs={{0,14},{2,12},{4,10},{6,8},{8,6},{10,4},{12,2},{14,0},{1,15},{3,13... | collective-permute-start | bytes 1572872 | tf_op jit(solution)/shard_map/ppermute | solution.py:286
  93.2 9.0 %collective-permute-start.7 = (bf16[2,192,1024]{2,1,0:T(8,128)(2,1)S(1)}, bf16[2,192,1024]{2,1,0:T(8,128)(2,1)S(1)}, u32[]{:S(2)}, u32[]{:S(2)}) collective-permute-start(bf16[2,192,1024]{2,1,0:T(8,128)(2,1)S(1)} %gather_late.2.first), channel_id=1, source_target_pairs={{0,1},{2,3},{4,5},{6,7},{8,9},{10,11},{12,13},{14,15},{16,17},{18,... | collective-permute-start | bytes 2359304 | tf_op jit(solution)/shard_map/ppermute | solution.py:324
  97.8 4.4 %collective-permute-start.8 = (bf16[2,128,1024]{2,1,0:T(8,128)(2,1)S(1)}, bf16[2,128,1024]{2,1,0:T(8,128)(2,1)S(1)}, u32[]{:S(2)}, u32[]{:S(2)}) collective-permute-start(bf16[2,128,1024]{2,1,0:T(8,128)(2,1)S(1)} %gather_late.3.second), channel_id=1, source_target_pairs={{0,1},{2,3},{4,5},{6,7},{8,9},{10,11},{12,13},{14,15},{16,17},{18,... | collective-permute-start | bytes 1572872 | tf_op jit(solution)/shard_map/ppermute | solution.py:324

commit v21 on v20

--- a/solution.py
+++ b/solution.py
@@ -159,6 +159,15 @@
         best[:, window] = jnp.maximum(best[:, window], jnp.concatenate(parts, axis=1))
 
 
+def raise_wide(best, keys, queries, unfilled):
+    sims = matmul(queries[...], keys[...], ((1,), (1,)))
+    sims = jnp.where(unfilled > 1.0, F32(-1.0), sims)
+    top = sims[:, :LANES]
+    for first in range(LANES, sims.shape[1], LANES):
+        top = jnp.maximum(top, sims[:, first : first + LANES])
+    best[...] = jnp.maximum(best[...], jnp.max(top.T, axis=0, keepdims=True))
+
+
 def gather_group(blocks, cluster, out, me):
     per = blocks[0].shape[0] // CLUS_DEV
     for step, block in enumerate(blocks):
@@ -203,7 +212,9 @@
     score_pairs(bests, groups, 1, 0, bits[0], me)
 
 
-def cross_early(received, before, best):
+def cross_early(received, before, best, unfilled):
+    for c in range(CLUS_DEV):
+        unfilled[c : c + 1, :] = fresh_best(received.at[0, c])
     best[...] = before[...]
 
     @pl.when(lax.axis_index("blk") == 1)
@@ -218,7 +229,7 @@
         gather_group(blocks, c, out.at[c], lax.axis_index("clus"))
 
 
-def own_late(cuts, bits, received, first, second, before, cat, best):
+def own_late(cuts, bits, received, first, second, before, unfilled, cat, best):
     me = lax.axis_index("clus")
     size = second.shape[1]
     swapped = (me & (bits[-1] // 2)) != 0
@@ -244,7 +255,7 @@
     @pl.when(core == 1)
     def _():
         for c in range(CLUS_DEV):
-            raise_best(bests[c][last], received.at[0, c], cat.at[c])
+            raise_wide(bests[c][last], received.at[0, c], cat.at[c], unfilled[c : c + 1, :])
 
 
 def cross_late(cuts, per, received, cat, before, first, second, out, best, keys):
@@ -311,7 +322,8 @@
         "own_early",
     )
     received = to_both(send)
-    (best,) = kernel_call(cross_early, [best_shape], [received, best], "cross_early")
+    flags = jax.ShapeDtypeStruct((CLUS_DEV, cuts[2]), F32)
+    best, unfilled = kernel_call(cross_early, [best_shape, flags], [received, best], "cross_early")
     count = len(late) // 2
     size = count * per
     count = len(late) // 2
@@ -328,7 +340,7 @@
     cat, best = kernel_call(
         functools.partial(own_late, cuts, bits),
         [cat_shape, best_shape],
-        [received] + halves + [best],
+        [received] + halves + [best, unfilled],
         "own_late",
     )
     (out,) = kernel_call(

time: 104 us -> 104 us (level)
  no operation moved by 1% of the time
where the time goes in v21:
time: 104 us
  waiting for transfers between devices  58.6 us (56%)
  Pallas kernels  17.7 us (17%)
  starting transfers between devices  16.5 us (16%)
  blocking collectives  10.6 us (10%)
    ppermute x7, waiting for transfers between devices, to_owner(): return lax.ppermute(block, 'clus', [(i, i ^ step) for i in range(owners)])  58.6 us
    pallas_call x9, Pallas kernels, kernel_call(): pl.pallas_call(kernel, out_shape=shapes, in_specs=[place] * len(inputs),...  17.7 us
    ppermute x7, starting transfers between devices, to_owner(): return lax.ppermute(block, 'clus', [(i, i ^ step) for i in range(owners)])  13.7 us
    all_to_all x1, blocking collectives, to_both(): return lax.all_to_all(send, 'blk', split_axis=0, concat_axis=0, tiled=True)  10.6 us
    ppermute x2, starting transfers between devices, local(): others.append(lax.ppermute(half, 'blk', [(0, 1)]))  2.76 us
  transfers between devices with their start and end apart: 9, of which 4 were waited for; matrix products, arithmetic and copies ran while one was open for 0% of the time, Pallas kernels for 13%

profile of v21, /device:TPU:17, one launch (start us, length us, event | category | flops | bytes accessed | tf_op | source)
XLA Modules:
  0.0 104.2 jit_solution(12489625877270262830)
XLA Ops:
  0.0 0.0 copy-start
  0.0 0.7 copy-done
  0.7 2.6 %pack_first.1 = (bf16[1024,1024]{1,0:T(8,128)(2,1)S(1)}, s32[1,1024]{1,0:T(1,128)S(1)}, bf16[256,1024]{1,0:T(8,128)(2,1)S(1)}) custom-call(bf16[1024,1024]{1,0:T(8,128)(2,1)} %emb.1, s32[1,1024]{1,0:T(1,128)S(1)} %copy-done), custom_call_target="tpu_custom_call" | custom-call | flops 1000 | bytes 1000 | tf_op jit(solution)/shard_map/pack_first/pallas_call | solution.py:98
  3.3 0.1 collective-permute-start.1
  3.3 3.2 %pack_rest.2 = (bf16[256,1024]{1,0:T(8,128)(2,1)S(1)}, bf16[256,1024]{1,0:T(8,128)(2,1)S(1)}, bf16[256,1024]{1,0:T(8,128)(2,1)S(1)}, bf16[256,1024]{1,0:T(8,128)(2,1)S(1)}, bf16[256,1024]{1,0:T(8,128)(2,1)S(1)}) custom-call(bf16[1024,1024]{1,0:T(8,128)(2,1)S(1)} %get-tuple-element.32.unit, s32[1,1024]{1,0:T(1,128)S(1)} %get-tuple-element.33.tgt), custom_call_target="tpu_custom_call" | custom-call | flops 1000 | bytes 1000 | tf_op jit(solution)/shard_map/pack_rest/pallas_call | solution.py:98
  6.6 3.4 %collective-permute-start = (bf16[256,1024]{1,0:T(8,128)(2,1)S(1)}, bf16[256,1024]{1,0:T(8,128)(2,1)S(1)}, u32[]{:S(2)}, u32[]{:S(2)}) collective-permute-start(bf16[256,1024]{1,0:T(8,128)(2,1)S(1)} %get-tuple-element.34), channel_id=1, source_target_pairs={{0,10},{2,8},{4,14},{6,12},{8,2},{10,0},{12,6},{14,4},{1,11},{3,9}... | collective-permute-start | bytes 1572872 | tf_op jit(solution)/shard_map/ppermute | solution.py:297
  10.0 1.2 %collective-permute-start.2 = (bf16[256,1024]{1,0:T(8,128)(2,1)S(1)}, bf16[256,1024]{1,0:T(8,128)(2,1)S(1)}, u32[]{:S(2)}, u32[]{:S(2)}) collective-permute-start(bf16[256,1024]{1,0:T(8,128)(2,1)S(1)} %get-tuple-element.39), channel_id=1, source_target_pairs={{0,6},{2,4},{4,2},{6,0},{8,14},{10,12},{12,10},{14,8},{1,7},{3,5},... | collective-permute-start | bytes 1572872 | tf_op jit(solution)/shard_map/ppermute | solution.py:297
  11.2 0.2 collective-permute-start.3
  11.4 1.2 %collective-permute-start.4 = (bf16[256,1024]{1,0:T(8,128)(2,1)S(1)}, bf16[256,1024]{1,0:T(8,128)(2,1)S(1)}, u32[]{:S(2)}, u32[]{:S(2)}) collective-permute-start(bf16[256,1024]{1,0:T(8,128)(2,1)S(1)} %get-tuple-element.41), channel_id=1, source_target_pairs={{0,2},{2,0},{4,6},{6,4},{8,10},{10,8},{12,14},{14,12},{1,3},{3,1},... | collective-permute-start | bytes 1572872 | tf_op jit(solution)/shard_map/ppermute | solution.py:297
  12.6 1.4 %pack_rest.3 = (bf16[256,1024]{1,0:T(8,128)(2,1)S(1)}, bf16[256,1024]{1,0:T(8,128)(2,1)S(1)}) custom-call(bf16[1024,1024]{1,0:T(8,128)(2,1)S(1)} %get-tuple-element.32.unit, s32[1,1024]{1,0:T(1,128)S(1)} %get-tuple-element.33.tgt), custom_call_target="tpu_custom_call" | custom-call | flops 1000 | bytes 1000 | tf_op jit(solution)/shard_map/pack_rest/pallas_call | solution.py:98
  14.0 22.7 %collective-permute-done.1.refs_1_ = bf16[256,1024]{1,0:T(8,128)(2,1)S(1)} collective-permute-done((bf16[256,1024]{1,0:T(8,128)(2,1)S(1)}, bf16[256,1024]{1,0:T(8,128)(2,1)S(1)}, u32[]{:S(2)}, u32[]{:S(2)}) %collective-permute-start.1) | collective-permute-done | bytes 524320 | tf_op jit(solution)/shard_map/ppermute | solution.py:297
  36.8 3.1 %collective-permute-start.5 = (bf16[256,1024]{1,0:T(8,128)(2,1)S(1)}, bf16[256,1024]{1,0:T(8,128)(2,1)S(1)}, u32[]{:S(2)}, u32[]{:S(2)}) collective-permute-start(bf16[256,1024]{1,0:T(8,128)(2,1)S(1)} %get-tuple-element.44), channel_id=1, source_target_pairs={{0,12},{2,14},{4,8},{6,10},{8,4},{10,6},{12,0},{14,2},{1,13},{3,15... | collective-permute-start | bytes 1572872 | tf_op jit(solution)/shard_map/ppermute | solution.py:297
  39.8 8.1 %collective-permute-done.refs_0_ = bf16[256,1024]{1,0:T(8,128)(2,1)S(1)} collective-permute-done((bf16[256,1024]{1,0:T(8,128)(2,1)S(1)}, bf16[256,1024]{1,0:T(8,128)(2,1)S(1)}, u32[]{:S(2)}, u32[]{:S(2)}) %collective-permute-start) | collective-permute-done | bytes 524320 | tf_op jit(solution)/shard_map/ppermute | solution.py:297
  48.0 4.6 %collective-permute-start.6 = (bf16[256,1024]{1,0:T(8,128)(2,1)S(1)}, bf16[256,1024]{1,0:T(8,128)(2,1)S(1)}, u32[]{:S(2)}, u32[]{:S(2)}) collective-permute-start(bf16[256,1024]{1,0:T(8,128)(2,1)S(1)} %get-tuple-element.50), channel_id=1, source_target_pairs={{0,14},{2,12},{4,10},{6,8},{8,6},{10,4},{12,2},{14,0},{1,15},{3,13... | collective-permute-start | bytes 1572872 | tf_op jit(solution)/shard_map/ppermute | solution.py:297
  52.5 0.0 collective-permute-done.2.refs_2_
  52.6 24.7 %collective-permute-done.3.refs_3_ = bf16[256,1024]{1,0:T(8,128)(2,1)S(1)} collective-permute-done((bf16[256,1024]{1,0:T(8,128)(2,1)S(1)}, bf16[256,1024]{1,0:T(8,128)(2,1)S(1)}, u32[]{:S(2)}, u32[]{:S(2)}) %collective-permute-start.3) | collective-permute-done | bytes 524320 | tf_op jit(solution)/shard_map/ppermute | solution.py:297
  77.3 0.0 collective-permute-done.4.refs_4_
  77.3 2.6 %own_early.1 = (bf16[2,2,768,1024]{3,2,1,0:T(8,128)(2,1)S(1)}, f32[2,1024]{1,0:T(2,128)S(1)}) custom-call(bf16[256,1024]{1,0:T(8,128)(2,1)S(1)} %collective-permute-done.refs_0_, bf16[256,1024]{1,0:T(8,128)(2,1)S(1)} %collective-permute-done.1.refs_1_, bf16[256,1024]{1,0:T(8,128)(2,1)S(1)} %collective-permute-done.2.refs_2_, ...), custom_call_target="tpu_custom_call" | custom-call | flops 1000 | bytes 1000 | tf_op jit(solution)/shard_map/own_early/pallas_call | solution.py:98
  79.9 10.6 %all_to_all.5.received = bf16[2,2,768,1024]{3,2,1,0:T(8,128)(2,1)S(1)} all-to-all(bf16[2,2,768,1024]{3,2,1,0:T(8,128)(2,1)S(1)} %get-tuple-element.43), channel_id=1, replica_groups=mesh['groups'=2,'clus'=8,'blk'=2] {'blk'}, dimensions={0} | all-to-all | bytes 12582912 | tf_op jit(solution)/shard_map/all_to_all | solution.py:303
  90.5 2.9 %cross_early.1 = (f32[2,1024]{1,0:T(2,128)S(1)}, f32[2,768]{1,0:T(2,128)S(1)}) custom-call(bf16[2,2,768,1024]{3,2,1,0:T(8,128)(2,1)S(1)} %all_to_all.5.received, f32[2,1024]{1,0:T(2,128)S(1)} %get-tuple-element.45.before), custom_call_target="tpu_custom_call" | custom-call | flops 1000 | bytes 1000 | tf_op jit(solution)/shard_map/cross_early/pallas_call | solution.py:98
  93.4 0.0 collective-permute-done.5.refs_0_
  93.4 1.3 %collective-permute-start.7 = (bf16[2,192,1024]{2,1,0:T(8,128)(2,1)S(1)}, bf16[2,192,1024]{2,1,0:T(8,128)(2,1)S(1)}, u32[]{:S(2)}, u32[]{:S(2)}) collective-permute-start(bf16[2,192,1024]{2,1,0:T(8,128)(2,1)S(1)} %gather_late.2.first), channel_id=1, source_target_pairs={{0,1},{2,3},{4,5},{6,7},{8,9},{10,11},{12,13},{14,15},{16,17},{18,... | collective-permute-start | bytes 2359304 | tf_op jit(solution)/shard_map/ppermute | solution.py:336
  94.7 3.0 %collective-permute-done.6.refs_0_ = bf16[256,1024]{1,0:T(8,128)(2,1)S(1)} collective-permute-done((bf16[256,1024]{1,0:T(8,128)(2,1)S(1)}, bf16[256,1024]{1,0:T(8,128)(2,1)S(1)}, u32[]{:S(2)}, u32[]{:S(2)}) %collective-permute-start.6) | collective-permute-done | bytes 524320 | tf_op jit(solution)/shard_map/ppermute | solution.py:297
  97.8 1.5 %collective-permute-start.8 = (bf16[2,128,1024]{2,1,0:T(8,128)(2,1)S(1)}, bf16[2,128,1024]{2,1,0:T(8,128)(2,1)S(1)}, u32[]{:S(2)}, u32[]{:S(2)}) collective-permute-start(bf16[2,128,1024]{2,1,0:T(8,128)(2,1)S(1)} %gather_late.3.second), channel_id=1, source_target_pairs={{0,1},{2,3},{4,5},{6,7},{8,9},{10,11},{12,13},{14,15},{16,17},{18,... | collective-permute-start | bytes 1572872 | tf_op jit(solution)/shard_map/ppermute | solution.py:336
  99.2 3.0 %own_late.1 = (bf16[2,256,1024]{2,1,0:T(8,128)(2,1)S(1)}, f32[2,1024]{1,0:T(2,128)S(1)}) custom-call(bf16[2,2,768,1024]{3,2,1,0:T(8,128)(2,1)S(1)} %all_to_all.5.received, bf16[2,192,1024]{2,1,0:T(8,128)(2,1)S(1)} %gather_late.2.first, bf16[2,128,1024]{2,1,0:T(8,128)(2,1)S(1)} %gather_late.3.second, f32[2,1024]{1,0:T(2,128)S(1)} %get-tuple-element.55.before, ...), custom_call_target="tpu_custom_call" | custom-call | flops 1000 | bytes 1000 | tf_op jit(solution)/shard_map/own_late/pallas_call | solution.py:98
  102.2 0.0 collective-permute-done.8.second
  102.2 0.0 collective-permute-done.7.first
  102.3 1.9 %cross_late.1 = f32[2,1024]{1,0:T(2,128)} custom-call(bf16[2,2,768,1024]{3,2,1,0:T(8,128)(2,1)S(1)} %all_to_all.5.received, bf16[2,256,1024]{2,1,0:T(8,128)(2,1)S(1)} %get-tuple-element.57.cat, f32[2,1024]{1,0:T(2,128)S(1)} %get-tuple-element.58.before, bf16[2,192,1024]{2,1,0:T(8,128)(2,1)S(1)} %collective-permute-done.7.first, ...), custom_call_target="tpu_custom_call" | custom-call | flops 1000 | bytes 1000 | tf_op jit(solution)/shard_map/cross_late/pallas_call | solution.py:98
  (2 shorter events, 0.1 us)
Async XLA Ops:
  0.0 0.7 copy-start
  3.3 33.5 %collective-permute-start.1 = (bf16[256,1024]{1,0:T(8,128)(2,1)S(1)}, bf16[256,1024]{1,0:T(8,128)(2,1)S(1)}, u32[]{:S(2)}, u32[]{:S(2)}) collective-permute-start(bf16[256,1024]{1,0:T(8,128)(2,1)S(1)} %get-tuple-element.37), channel_id=1, source_target_pairs={{0,8},{2,10},{4,12},{6,14},{8,0},{10,2},{12,4},{14,6},{1,9},{3,11}... | collective-permute-start | bytes 1572872 | tf_op jit(solution)/shard_map/ppermute | solution.py:297
  6.6 41.4 %collective-permute-start = (bf16[256,1024]{1,0:T(8,128)(2,1)S(1)}, bf16[256,1024]{1,0:T(8,128)(2,1)S(1)}, u32[]{:S(2)}, u32[]{:S(2)}) collective-permute-start(bf16[256,1024]{1,0:T(8,128)(2,1)S(1)} %get-tuple-element.34), channel_id=1, source_target_pairs={{0,10},{2,8},{4,14},{6,12},{8,2},{10,0},{12,6},{14,4},{1,11},{3,9}... | collective-permute-start | bytes 1572872 | tf_op jit(solution)/shard_map/ppermute | solution.py:297
  10.0 42.6 %collective-permute-start.2 = (bf16[256,1024]{1,0:T(8,128)(2,1)S(1)}, bf16[256,1024]{1,0:T(8,128)(2,1)S(1)}, u32[]{:S(2)}, u32[]{:S(2)}) collective-permute-start(bf16[256,1024]{1,0:T(8,128)(2,1)S(1)} %get-tuple-element.39), channel_id=1, source_target_pairs={{0,6},{2,4},{4,2},{6,0},{8,14},{10,12},{12,10},{14,8},{1,7},{3,5},... | collective-permute-start | bytes 1572872 | tf_op jit(solution)/shard_map/ppermute | solution.py:297
  11.2 66.1 %collective-permute-start.3 = (bf16[256,1024]{1,0:T(8,128)(2,1)S(1)}, bf16[256,1024]{1,0:T(8,128)(2,1)S(1)}, u32[]{:S(2)}, u32[]{:S(2)}) collective-permute-start(bf16[256,1024]{1,0:T(8,128)(2,1)S(1)} %get-tuple-element.40), channel_id=1, source_target_pairs={{0,4},{2,6},{4,0},{6,2},{8,12},{10,14},{12,8},{14,10},{1,5},{3,7},... | collective-permute-start | bytes 1572872 | tf_op jit(solution)/shard_map/ppermute | solution.py:297
  11.4 65.9 %collective-permute-start.4 = (bf16[256,1024]{1,0:T(8,128)(2,1)S(1)}, bf16[256,1024]{1,0:T(8,128)(2,1)S(1)}, u32[]{:S(2)}, u32[]{:S(2)}) collective-permute-start(bf16[256,1024]{1,0:T(8,128)(2,1)S(1)} %get-tuple-element.41), channel_id=1, source_target_pairs={{0,2},{2,0},{4,6},{6,4},{8,10},{10,8},{12,14},{14,12},{1,3},{3,1},... | collective-permute-start | bytes 1572872 | tf_op jit(solution)/shard_map/ppermute | solution.py:297
  36.8 56.6 %collective-permute-start.5 = (bf16[256,1024]{1,0:T(8,128)(2,1)S(1)}, bf16[256,1024]{1,0:T(8,128)(2,1)S(1)}, u32[]{:S(2)}, u32[]{:S(2)}) collective-permute-start(bf16[256,1024]{1,0:T(8,128)(2,1)S(1)} %get-tuple-element.44), channel_id=1, source_target_pairs={{0,12},{2,14},{4,8},{6,10},{8,4},{10,6},{12,0},{14,2},{1,13},{3,15... | collective-permute-start | bytes 1572872 | tf_op jit(solution)/shard_map/ppermute | solution.py:297
  48.0 49.7 %collective-permute-start.6 = (bf16[256,1024]{1,0:T(8,128)(2,1)S(1)}, bf16[256,1024]{1,0:T(8,128)(2,1)S(1)}, u32[]{:S(2)}, u32[]{:S(2)}) collective-permute-start(bf16[256,1024]{1,0:T(8,128)(2,1)S(1)} %get-tuple-element.50), channel_id=1, source_target_pairs={{0,14},{2,12},{4,10},{6,8},{8,6},{10,4},{12,2},{14,0},{1,15},{3,13... | collective-permute-start | bytes 1572872 | tf_op jit(solution)/shard_map/ppermute | solution.py:297
  93.4 8.8 %collective-permute-start.7 = (bf16[2,192,1024]{2,1,0:T(8,128)(2,1)S(1)}, bf16[2,192,1024]{2,1,0:T(8,128)(2,1)S(1)}, u32[]{:S(2)}, u32[]{:S(2)}) collective-permute-start(bf16[2,192,1024]{2,1,0:T(8,128)(2,1)S(1)} %gather_late.2.first), channel_id=1, source_target_pairs={{0,1},{2,3},{4,5},{6,7},{8,9},{10,11},{12,13},{14,15},{16,17},{18,... | collective-permute-start | bytes 2359304 | tf_op jit(solution)/shard_map/ppermute | solution.py:336
  97.8 4.5 %collective-permute-start.8 = (bf16[2,128,1024]{2,1,0:T(8,128)(2,1)S(1)}, bf16[2,128,1024]{2,1,0:T(8,128)(2,1)S(1)}, u32[]{:S(2)}, u32[]{:S(2)}) collective-permute-start(bf16[2,128,1024]{2,1,0:T(8,128)(2,1)S(1)} %gather_late.3.second), channel_id=1, source_target_pairs={{0,1},{2,3},{4,5},{6,7},{8,9},{10,11},{12,13},{14,15},{16,17},{18,... | collective-permute-start | bytes 1572872 | tf_op jit(solution)/shard_map/ppermute | solution.py:336

commit v22 on v15

--- a/solution.py
+++ b/solution.py
@@ -62,14 +62,12 @@
         out[:, LANES:] = tail
 
 
-PIECES = 4
+PIECES = 8
 
 
 def pack_first(steps, clusters, per_source, emb, ids, unit, tgt, *refs):
-    outs, (raw, raw_ids, sems, ids_sem) = refs[:-4], refs[-4:]
+    outs, (raw, sems) = refs[:-2], refs[-2:]
     size = emb.shape[0] // PIECES
-    ids_copy = pltpu.make_async_copy(ids, raw_ids, ids_sem)
-    ids_copy.start()
     windows = [pl.ds(piece * size, size) for piece in range(PIECES)]
     copies = [
         pltpu.make_async_copy(emb.at[window], raw.at[window], sems.at[piece])
@@ -77,8 +75,7 @@
     ]
     for copy in copies:
         copy.start()
-    ids_copy.wait()
-    tgt[...] = targets(raw_ids[...], clusters, per_source)
+    tgt[...] = targets(ids[...], clusters, per_source)
     for copy, window in zip(copies, windows):
         copy.wait()
         values = raw[window, :].astype(F32)
@@ -94,11 +91,11 @@
 VMEM = pl.BlockSpec(memory_space=pltpu.VMEM)
 
 
-def kernel_call(kernel, shapes, inputs, name, scratch=(), place=VMEM, grant=20 * 2**20):
+def kernel_call(kernel, shapes, inputs, name, scratch=(), places=None, grant=20 * 2**20):
     return pl.pallas_call(
         kernel,
         out_shape=shapes,
-        in_specs=[place] * len(inputs),
+        in_specs=places or [VMEM] * len(inputs),
         out_specs=[VMEM] * len(shapes),
         scratch_shapes=scratch,
         compiler_params=pltpu.CompilerParams(vmem_limit_bytes=grant),
@@ -114,14 +111,12 @@
         functools.partial(pack_first, steps, clusters, per_source),
         shapes + [block] * len(steps),
         [emb, ids],
-        place=pl.BlockSpec(memory_space=pl.ANY),
+        places=[pl.BlockSpec(memory_space=pl.ANY), VMEM],
         grant=50 * 2**20,
         name="pack_first",
         scratch=[
             pltpu.VMEM(emb.shape, BF),
-            pltpu.VMEM(ids.shape, jnp.int32),
             pltpu.SemaphoreType.DMA((PIECES,)),
-            pltpu.SemaphoreType.DMA,
         ],
     )
 

time: 104 us -> 105 us (level)
  no operation moved by 1% of the time
where the time goes in v22:
time: 105 us
  waiting for transfers between devices  60.4 us (58%)
  Pallas kernels  17.8 us (17%)
  starting transfers between devices  15 us (14%)
  blocking collectives  10.6 us (10%)
    ppermute x7, waiting for transfers between devices, to_owner(): return lax.ppermute(block, 'clus', [(i, i ^ step) for i in range(owners)])  60.1 us
    pallas_call x8, Pallas kernels, kernel_call(): pl.pallas_call(kernel, out_shape=shapes, in_specs=places or [VMEM] * len(...  17.8 us
    ppermute x7, starting transfers between devices, to_owner(): return lax.ppermute(block, 'clus', [(i, i ^ step) for i in range(owners)])  13.7 us
    all_to_all x1, blocking collectives, to_both(): return lax.all_to_all(send, 'blk', split_axis=0, concat_axis=0, tiled=True)  10.6 us
  transfers between devices with their start and end apart: 8, of which 5 were waited for; matrix products, arithmetic and copies ran while one was open for 0% of the time, Pallas kernels for 12%

profile of v22, /device:TPU:17, one launch (start us, length us, event | category | flops | bytes accessed | tf_op | source)
XLA Modules:
  0.0 104.6 jit_solution(6051984199880170511)
XLA Ops:
  0.0 0.0 copy-start
  0.0 0.7 copy-done
  0.7 2.9 %pack_first.1 = (bf16[1024,1024]{1,0:T(8,128)(2,1)S(1)}, s32[1,1024]{1,0:T(1,128)S(1)}, bf16[256,1024]{1,0:T(8,128)(2,1)S(1)}) custom-call(bf16[1024,1024]{1,0:T(8,128)(2,1)} %emb.1, s32[1,1024]{1,0:T(1,128)S(1)} %copy-done), custom_call_target="tpu_custom_call" | custom-call | flops 1000 | bytes 1000 | tf_op jit(solution)/shard_map/pack_first/pallas_call | solution.py:95
  3.5 0.1 collective-permute-start.1
  3.6 3.2 %pack_rest.2 = (bf16[256,1024]{1,0:T(8,128)(2,1)S(1)}, bf16[256,1024]{1,0:T(8,128)(2,1)S(1)}, bf16[256,1024]{1,0:T(8,128)(2,1)S(1)}, bf16[256,1024]{1,0:T(8,128)(2,1)S(1)}, bf16[256,1024]{1,0:T(8,128)(2,1)S(1)}) custom-call(bf16[1024,1024]{1,0:T(8,128)(2,1)S(1)} %get-tuple-element.23.unit, s32[1,1024]{1,0:T(1,128)S(1)} %get-tuple-element.24.tgt), custom_call_target="tpu_custom_call" | custom-call | flops 1000 | bytes 1000 | tf_op jit(solution)/shard_map/pack_rest/pallas_call | solution.py:95
  6.9 3.4 %collective-permute-start = (bf16[256,1024]{1,0:T(8,128)(2,1)S(1)}, bf16[256,1024]{1,0:T(8,128)(2,1)S(1)}, u32[]{:S(2)}, u32[]{:S(2)}) collective-permute-start(bf16[256,1024]{1,0:T(8,128)(2,1)S(1)} %get-tuple-element.25), channel_id=1, source_target_pairs={{0,10},{2,8},{4,14},{6,12},{8,2},{10,0},{12,6},{14,4},{1,11},{3,9}... | collective-permute-start | bytes 1572872 | tf_op jit(solution)/shard_map/ppermute | solution.py:272
  10.3 1.2 %collective-permute-start.2 = (bf16[256,1024]{1,0:T(8,128)(2,1)S(1)}, bf16[256,1024]{1,0:T(8,128)(2,1)S(1)}, u32[]{:S(2)}, u32[]{:S(2)}) collective-permute-start(bf16[256,1024]{1,0:T(8,128)(2,1)S(1)} %get-tuple-element.30), channel_id=1, source_target_pairs={{0,6},{2,4},{4,2},{6,0},{8,14},{10,12},{12,10},{14,8},{1,7},{3,5},... | collective-permute-start | bytes 1572872 | tf_op jit(solution)/shard_map/ppermute | solution.py:272
  11.5 0.2 collective-permute-start.3
  11.7 1.2 %collective-permute-start.4 = (bf16[256,1024]{1,0:T(8,128)(2,1)S(1)}, bf16[256,1024]{1,0:T(8,128)(2,1)S(1)}, u32[]{:S(2)}, u32[]{:S(2)}) collective-permute-start(bf16[256,1024]{1,0:T(8,128)(2,1)S(1)} %get-tuple-element.32), channel_id=1, source_target_pairs={{0,2},{2,0},{4,6},{6,4},{8,10},{10,8},{12,14},{14,12},{1,3},{3,1},... | collective-permute-start | bytes 1572872 | tf_op jit(solution)/shard_map/ppermute | solution.py:272
  12.9 1.4 %pack_rest.3 = (bf16[256,1024]{1,0:T(8,128)(2,1)S(1)}, bf16[256,1024]{1,0:T(8,128)(2,1)S(1)}) custom-call(bf16[1024,1024]{1,0:T(8,128)(2,1)S(1)} %get-tuple-element.23.unit, s32[1,1024]{1,0:T(1,128)S(1)} %get-tuple-element.24.tgt), custom_call_target="tpu_custom_call" | custom-call | flops 1000 | bytes 1000 | tf_op jit(solution)/shard_map/pack_rest/pallas_call | solution.py:95
  14.3 22.7 %collective-permute-done.1.refs_1_ = bf16[256,1024]{1,0:T(8,128)(2,1)S(1)} collective-permute-done((bf16[256,1024]{1,0:T(8,128)(2,1)S(1)}, bf16[256,1024]{1,0:T(8,128)(2,1)S(1)}, u32[]{:S(2)}, u32[]{:S(2)}) %collective-permute-start.1) | collective-permute-done | bytes 524320 | tf_op jit(solution)/shard_map/ppermute | solution.py:272
  37.0 3.1 %collective-permute-start.5 = (bf16[256,1024]{1,0:T(8,128)(2,1)S(1)}, bf16[256,1024]{1,0:T(8,128)(2,1)S(1)}, u32[]{:S(2)}, u32[]{:S(2)}) collective-permute-start(bf16[256,1024]{1,0:T(8,128)(2,1)S(1)} %get-tuple-element.35), channel_id=1, source_target_pairs={{0,12},{2,14},{4,8},{6,10},{8,4},{10,6},{12,0},{14,2},{1,13},{3,15... | collective-permute-start | bytes 1572872 | tf_op jit(solution)/shard_map/ppermute | solution.py:272
  40.1 8.1 %collective-permute-done.refs_0_ = bf16[256,1024]{1,0:T(8,128)(2,1)S(1)} collective-permute-done((bf16[256,1024]{1,0:T(8,128)(2,1)S(1)}, bf16[256,1024]{1,0:T(8,128)(2,1)S(1)}, u32[]{:S(2)}, u32[]{:S(2)}) %collective-permute-start) | collective-permute-done | bytes 524320 | tf_op jit(solution)/shard_map/ppermute | solution.py:272
  48.3 4.6 %collective-permute-start.6 = (bf16[256,1024]{1,0:T(8,128)(2,1)S(1)}, bf16[256,1024]{1,0:T(8,128)(2,1)S(1)}, u32[]{:S(2)}, u32[]{:S(2)}) collective-permute-start(bf16[256,1024]{1,0:T(8,128)(2,1)S(1)} %get-tuple-element.36), channel_id=1, source_target_pairs={{0,14},{2,12},{4,10},{6,8},{8,6},{10,4},{12,2},{14,0},{1,15},{3,13... | collective-permute-start | bytes 1572872 | tf_op jit(solution)/shard_map/ppermute | solution.py:272
  52.8 0.0 collective-permute-done.2.refs_2_
  52.8 24.7 %collective-permute-done.3.refs_3_ = bf16[256,1024]{1,0:T(8,128)(2,1)S(1)} collective-permute-done((bf16[256,1024]{1,0:T(8,128)(2,1)S(1)}, bf16[256,1024]{1,0:T(8,128)(2,1)S(1)}, u32[]{:S(2)}, u32[]{:S(2)}) %collective-permute-start.3) | collective-permute-done | bytes 524320 | tf_op jit(solution)/shard_map/ppermute | solution.py:272
  77.6 0.0 collective-permute-done.4.refs_4_
  77.6 2.6 %own_early.1 = (bf16[2,2,768,1024]{3,2,1,0:T(8,128)(2,1)S(1)}, f32[2,1024]{1,0:T(2,128)S(1)}) custom-call(bf16[256,1024]{1,0:T(8,128)(2,1)S(1)} %collective-permute-done.refs_0_, bf16[256,1024]{1,0:T(8,128)(2,1)S(1)} %collective-permute-done.1.refs_1_, bf16[256,1024]{1,0:T(8,128)(2,1)S(1)} %collective-permute-done.2.refs_2_, ...), custom_call_target="tpu_custom_call" | custom-call | flops 1000 | bytes 1000 | tf_op jit(solution)/shard_map/own_early/pallas_call | solution.py:95
  80.2 10.6 %all_to_all.5.received = bf16[2,2,768,1024]{3,2,1,0:T(8,128)(2,1)S(1)} all-to-all(bf16[2,2,768,1024]{3,2,1,0:T(8,128)(2,1)S(1)} %get-tuple-element.34), channel_id=1, replica_groups=mesh['groups'=2,'clus'=8,'blk'=2] {'blk'}, dimensions={0} | all-to-all | bytes 12582912 | tf_op jit(solution)/shard_map/all_to_all | solution.py:278
  90.8 2.7 %cross_early.1.before = f32[2,1024]{1,0:T(2,128)S(1)} custom-call(bf16[2,2,768,1024]{3,2,1,0:T(8,128)(2,1)S(1)} %all_to_all.5.received, f32[2,1024]{1,0:T(2,128)S(1)} %get-tuple-element.37.before), custom_call_target="tpu_custom_call" | custom-call | flops 1000 | bytes 1000 | tf_op jit(solution)/shard_map/cross_early/pallas_call | solution.py:95
  93.5 0.0 collective-permute-done.5.refs_0_
  93.5 4.5 %collective-permute-done.6.refs_1_ = bf16[256,1024]{1,0:T(8,128)(2,1)S(1)} collective-permute-done((bf16[256,1024]{1,0:T(8,128)(2,1)S(1)}, bf16[256,1024]{1,0:T(8,128)(2,1)S(1)}, u32[]{:S(2)}, u32[]{:S(2)}) %collective-permute-start.6) | collective-permute-done | bytes 524320 | tf_op jit(solution)/shard_map/ppermute | solution.py:272
  98.0 0.1 gather_late.1.cat
  98.1 1.3 %collective-permute-start.7 = (bf16[2,256,1024]{2,1,0:T(8,128)(2,1)S(1)}, bf16[2,256,1024]{2,1,0:T(8,128)(2,1)S(1)}, u32[]{:S(2)}, u32[]{:S(2)}) collective-permute-start(bf16[2,256,1024]{2,1,0:T(8,128)(2,1)S(1)} %gather_late.1.cat), channel_id=1, source_target_pairs={{0,1},{2,3},{4,5},{6,7},{8,9},{10,11},{12,13},{14,15},{16,17},{18,... | collective-permute-start | bytes 3145736 | tf_op jit(solution)/shard_map/ppermute | solution.py:304
  99.4 3.0 %own_late.1.before = f32[2,1024]{1,0:T(2,128)S(1)} custom-call(bf16[2,2,768,1024]{3,2,1,0:T(8,128)(2,1)S(1)} %all_to_all.5.received, bf16[2,256,1024]{2,1,0:T(8,128)(2,1)S(1)} %gather_late.1.cat, f32[2,1024]{1,0:T(2,128)S(1)} %cross_early.1.before), custom_call_target="tpu_custom_call" | custom-call | flops 1000 | bytes 1000 | tf_op jit(solution)/shard_map/own_late/pallas_call | solution.py:95
  102.4 0.3 collective-permute-done.7.other
  102.7 1.9 %cross_late.1 = f32[2,1024]{1,0:T(2,128)} custom-call(bf16[2,2,768,1024]{3,2,1,0:T(8,128)(2,1)S(1)} %all_to_all.5.received, bf16[2,256,1024]{2,1,0:T(8,128)(2,1)S(1)} %gather_late.1.cat, f32[2,1024]{1,0:T(2,128)S(1)} %own_late.1.before, bf16[2,256,1024]{2,1,0:T(8,128)(2,1)S(1)} %collective-permute-done.7.other), custom_call_target="tpu_custom_call" | custom-call | flops 1000 | bytes 1000 | tf_op jit(solution)/shard_map/cross_late/pallas_call | solution.py:95
Async XLA Ops:
  0.0 0.7 copy-start
  3.5 33.5 %collective-permute-start.1 = (bf16[256,1024]{1,0:T(8,128)(2,1)S(1)}, bf16[256,1024]{1,0:T(8,128)(2,1)S(1)}, u32[]{:S(2)}, u32[]{:S(2)}) collective-permute-start(bf16[256,1024]{1,0:T(8,128)(2,1)S(1)} %get-tuple-element.28), channel_id=1, source_target_pairs={{0,8},{2,10},{4,12},{6,14},{8,0},{10,2},{12,4},{14,6},{1,9},{3,11}... | collective-permute-start | bytes 1572872 | tf_op jit(solution)/shard_map/ppermute | solution.py:272
  6.9 41.4 %collective-permute-start = (bf16[256,1024]{1,0:T(8,128)(2,1)S(1)}, bf16[256,1024]{1,0:T(8,128)(2,1)S(1)}, u32[]{:S(2)}, u32[]{:S(2)}) collective-permute-start(bf16[256,1024]{1,0:T(8,128)(2,1)S(1)} %get-tuple-element.25), channel_id=1, source_target_pairs={{0,10},{2,8},{4,14},{6,12},{8,2},{10,0},{12,6},{14,4},{1,11},{3,9}... | collective-permute-start | bytes 1572872 | tf_op jit(solution)/shard_map/ppermute | solution.py:272
  10.3 42.6 %collective-permute-start.2 = (bf16[256,1024]{1,0:T(8,128)(2,1)S(1)}, bf16[256,1024]{1,0:T(8,128)(2,1)S(1)}, u32[]{:S(2)}, u32[]{:S(2)}) collective-permute-start(bf16[256,1024]{1,0:T(8,128)(2,1)S(1)} %get-tuple-element.30), channel_id=1, source_target_pairs={{0,6},{2,4},{4,2},{6,0},{8,14},{10,12},{12,10},{14,8},{1,7},{3,5},... | collective-permute-start | bytes 1572872 | tf_op jit(solution)/shard_map/ppermute | solution.py:272
  11.5 66.1 %collective-permute-start.3 = (bf16[256,1024]{1,0:T(8,128)(2,1)S(1)}, bf16[256,1024]{1,0:T(8,128)(2,1)S(1)}, u32[]{:S(2)}, u32[]{:S(2)}) collective-permute-start(bf16[256,1024]{1,0:T(8,128)(2,1)S(1)} %get-tuple-element.31), channel_id=1, source_target_pairs={{0,4},{2,6},{4,0},{6,2},{8,12},{10,14},{12,8},{14,10},{1,5},{3,7},... | collective-permute-start | bytes 1572872 | tf_op jit(solution)/shard_map/ppermute | solution.py:272
  11.7 65.9 %collective-permute-start.4 = (bf16[256,1024]{1,0:T(8,128)(2,1)S(1)}, bf16[256,1024]{1,0:T(8,128)(2,1)S(1)}, u32[]{:S(2)}, u32[]{:S(2)}) collective-permute-start(bf16[256,1024]{1,0:T(8,128)(2,1)S(1)} %get-tuple-element.32), channel_id=1, source_target_pairs={{0,2},{2,0},{4,6},{6,4},{8,10},{10,8},{12,14},{14,12},{1,3},{3,1},... | collective-permute-start | bytes 1572872 | tf_op jit(solution)/shard_map/ppermute | solution.py:272
  37.0 56.4 %collective-permute-start.5 = (bf16[256,1024]{1,0:T(8,128)(2,1)S(1)}, bf16[256,1024]{1,0:T(8,128)(2,1)S(1)}, u32[]{:S(2)}, u32[]{:S(2)}) collective-permute-start(bf16[256,1024]{1,0:T(8,128)(2,1)S(1)} %get-tuple-element.35), channel_id=1, source_target_pairs={{0,12},{2,14},{4,8},{6,10},{8,4},{10,6},{12,0},{14,2},{1,13},{3,15... | collective-permute-start | bytes 1572872 | tf_op jit(solution)/shard_map/ppermute | solution.py:272
  48.3 49.7 %collective-permute-start.6 = (bf16[256,1024]{1,0:T(8,128)(2,1)S(1)}, bf16[256,1024]{1,0:T(8,128)(2,1)S(1)}, u32[]{:S(2)}, u32[]{:S(2)}) collective-permute-start(bf16[256,1024]{1,0:T(8,128)(2,1)S(1)} %get-tuple-element.36), channel_id=1, source_target_pairs={{0,14},{2,12},{4,10},{6,8},{8,6},{10,4},{12,2},{14,0},{1,15},{3,13... | collective-permute-start | bytes 1572872 | tf_op jit(solution)/shard_map/ppermute | solution.py:272
  98.1 4.6 %collective-permute-start.7 = (bf16[2,256,1024]{2,1,0:T(8,128)(2,1)S(1)}, bf16[2,256,1024]{2,1,0:T(8,128)(2,1)S(1)}, u32[]{:S(2)}, u32[]{:S(2)}) collective-permute-start(bf16[2,256,1024]{2,1,0:T(8,128)(2,1)S(1)} %gather_late.1.cat), channel_id=1, source_target_pairs={{0,1},{2,3},{4,5},{6,7},{8,9},{10,11},{12,13},{14,15},{16,17},{18,... | collective-permute-start | bytes 3145736 | tf_op jit(solution)/shard_map/ppermute | solution.py:304
